TPU v7x, 128 devices: a whole 4x4x4 slice. The times are simulated.
128 devices in a mesh: side: 2 (over core), dom: 64 (over z, y, x).
Axes of the slice: x: 4, y: 4, z: 4, core: 2. Of those that a mesh axis runs over, the one named last changes fastest.
Arguments:
- features: bfloat16 [2, 16384, 1024], P('side', 'dom'), may hold values from -6 to 6
- live_rows: int32 [2, 64], P('side', 'dom'), may hold values from 128 to 256, as said below
- listed: int32 [2, 64, 8, 2], P('side', 'dom'), may hold values from 0 to 1, as said below
- counts: int32 [2, 16384, 2048], P('side', 'dom'), may hold values from 0 to 3, as said below
- cotangent: bfloat16 [2, 16384, 1024], P('side', 'dom'), may hold values from -6 to 6
- q_weight: bfloat16 [1024, 2048], replicated, may hold values from -0.1875 to 0.1875
- q_bias: float32 [2048], replicated, may hold values from -3 to 3
- self_weight: bfloat16 [1024, 1024], replicated, may hold values from -0.109375 to 0.109375
- nb_weight: bfloat16 [2048, 1024], replicated, may hold values from -0.109375 to 0.109375
- out_bias: float32 [1024], replicated, may hold values from -3 to 3
Outputs:
- embedded: bfloat16 [2, 16384, 1024], P('side', 'dom')
- grad_features: bfloat16 [2, 16384, 1024], P('side', 'dom')
Inputs may be any that keep to these rules, and one draw needn't show every extreme that they name: `live_rows`: live rows come first on each device; user devices (group 0) hold one half to three quarters of 256 live rows, item devices three quarters to all. listed[s, j, o, b] is 1 when device (s, j) reads block b of device (1 - s, j - o), positions taken modulo the devices of a group; every block is read by 2 to 4 of the 8 devices that may read it; a device reads at most 1 block of one source, and in every draw some device reads exactly 1 block of some source. `counts`: mostly zero.
All inputs are finite; a program needn't handle non-finite values.
Results may differ from a plain program's by a relative error of at most 0.028.
The roundings to bfloat16 on the way count: a program that leaves them out, or rounds other values in their place, can miss the bound.
Values may be sent and summed in bfloat16 or wider, within the bound.
No kernel may reach another device: no remote copies, remote signals or barrier semaphores. Data moves between devices by JAX's collectives and lax.ppermute only.
A program may use at most 128 MiB of HBM per device.

v0:
```python
import jax
import jax.numpy as jnp
from jax import lax
from jax.sharding import PartitionSpec as P

epsilon = 1e-06


def partner_2(block, axis, stride):
    count = lax.axis_size(axis)
    route = []
    for low in range(count):
        high = low | 1 << stride
        if high != low and high < count:
            route += [(low, high), (high, low)]
    return lax.ppermute(block, axis, route)


def shifted(value, axis, steps):
    count = lax.axis_size(axis)
    pairs = [(source, (source + steps) % count) for source in range(count)]
    return lax.ppermute(value, axis, pairs)


def neighbour_rows(features, live_count, q_weight, q_bias):
    row_count = features.shape[0]
    pre_act = jnp.dot(features, q_weight, preferred_element_type=jnp.float32) + q_bias
    keep_rows = (jnp.arange(row_count, dtype=jnp.int32) < live_count)[:, None]
    message = jnp.where(keep_rows, jnp.maximum(pre_act, 0.0), 0.0).astype(jnp.bfloat16)
    return (pre_act, message)


def tile_weights(table, lists, source_live):
    reach, block_count = lists.shape
    row_count = table.shape[0]
    block_rows = row_count // block_count
    listed_cols = jnp.repeat(lists, block_rows, axis=1)
    living = (jnp.arange(row_count, dtype=jnp.int32)[None, :] < source_live[:, None]).astype(
        jnp.int32
    )
    chosen = (listed_cols * living).reshape(1, reach * row_count)
    return (table * chosen).astype(jnp.float32).astype(jnp.bfloat16)


def layer_forward(features, live_count, weight_tiles, messages, self_weight, nb_weight, out_bias):
    row_count = features.shape[0]
    degree = 1.0 + jnp.sum(weight_tiles.astype(jnp.float32), axis=1, keepdims=True)
    summed = jnp.dot(
        weight_tiles, messages.reshape(-1, messages.shape[-1]), preferred_element_type=jnp.float32
    )
    pooled = (summed / degree).astype(jnp.bfloat16)
    pre_act = jnp.dot(features, self_weight, preferred_element_type=jnp.float32)
    pre_act = pre_act + jnp.dot(pooled, nb_weight, preferred_element_type=jnp.float32) + out_bias
    activated = jnp.maximum(pre_act, 0.0)
    inv_norm = lax.rsqrt(jnp.mean(activated * activated, axis=1, keepdims=True) + epsilon)
    keep_rows = (jnp.arange(row_count, dtype=jnp.int32) < live_count)[:, None]
    embedded = jnp.where(keep_rows, activated * inv_norm, 0.0).astype(jnp.bfloat16)
    return (embedded, pre_act, activated, inv_norm, degree, keep_rows)


def layer_backward(
    cotangent, keep_rows, pre_act, activated, inv_norm, degree, self_weight, nb_weight
):
    width = activated.shape[1]
    upstream = jnp.where(keep_rows, cotangent.astype(jnp.float32), 0.0)
    inner = jnp.sum(upstream * activated, axis=1, keepdims=True) / width
    grad_act = inv_norm * upstream - activated * inv_norm * inv_norm * inv_norm * inner
    grad_pre = jnp.where(pre_act > 0, grad_act, 0.0).astype(jnp.bfloat16)
    contract = (((1,), (1,)), ((), ()))
    grad_self = lax.dot_general(grad_pre, self_weight, contract, preferred_element_type=jnp.float32)
    grad_nb = lax.dot_general(grad_pre, nb_weight, contract, preferred_element_type=jnp.float32)
    grad_pooled = (grad_nb / degree).astype(jnp.bfloat16)
    return (grad_self, grad_pooled)


def finish_owner(grad_message, keep_rows, neighbour_pre, grad_self, q_weight):
    grad_neighbour = jnp.where(keep_rows & (neighbour_pre > 0), grad_message, 0.0).astype(
        jnp.bfloat16
    )
    contract = (((1,), (1,)), ((), ()))
    total = grad_self + lax.dot_general(
        grad_neighbour, q_weight, contract, preferred_element_type=jnp.float32
    )
    return jnp.where(keep_rows, total, 0.0).astype(jnp.bfloat16)


def block_slots(row_flags):
    block_count = row_flags.shape[0]
    most = (block_count + 1) // 2
    before = jnp.cumsum(row_flags) - 1
    slot_ids = jnp.arange(most, dtype=jnp.int32)[:, None]
    hits = (row_flags[None, :] == 1) & (before[None, :] == slot_ids)
    chosen = jnp.sum(
        hits.astype(jnp.int32) * jnp.arange(block_count, dtype=jnp.int32)[None, :], axis=1
    )
    return (chosen, jnp.any(hits, axis=1))


def local(
    features,
    live_rows,
    listed,
    counts,
    cotangent,
    q_weight,
    q_bias,
    self_weight,
    nb_weight,
    out_bias,
):
    own_rows = features[0]
    own_live = live_rows[0, 0]
    lists = listed[0, 0]
    table = counts[0]
    upstream = cotangent[0]
    row_count, width = own_rows.shape
    hidden = q_weight.shape[1]
    reach, block_count = lists.shape
    block_rows = row_count // block_count
    levels = reach.bit_length() - 1
    neighbour_pre, message = neighbour_rows(own_rows, own_live, q_weight, q_bias)
    live_vector = live_rows.reshape(1)
    partner, partner_live = partner_2((own_rows, live_vector), "side", 0)
    carried = partner.shape[1]
    lists_window = listed[0]
    for depth_level in range(levels):
        fetched = shifted(lists_window, "dom", -(1 << depth_level))
        lists_window = jnp.concatenate([lists_window, fetched], axis=0)
    partner_blocks = partner.reshape(block_count, block_rows, carried)
    sender_slots = []
    reader_slots = []
    pieces = [partner]
    lives = [partner_live]
    for offset in range(1, reach):
        target_row = lists_window[offset][offset]
        send_block, send_valid = block_slots(target_row)
        sender_slots.append((send_block, send_valid))
        packed = jnp.where(send_valid[:, None, None], partner_blocks[send_block], 0)
        arrived, arrived_live = shifted((packed, partner_live), "dom", offset)
        take_block, take_valid = block_slots(lists[offset])
        reader_slots.append((take_block, take_valid))
        cleaned = jnp.where(take_valid[:, None, None], arrived, 0)
        placed = jnp.zeros_like(partner_blocks).at[take_block].add(cleaned)
        pieces.append(placed.reshape(row_count, carried))
        lives.append(arrived_live)
    window = jnp.stack(pieces)
    window_live = jnp.concatenate(lives)
    pre_window = (
        jnp.dot(window.reshape(-1, width), q_weight, preferred_element_type=jnp.float32) + q_bias
    )
    keep_window = (jnp.arange(row_count, dtype=jnp.int32)[None, :] < window_live[:, None]).reshape(
        -1, 1
    )
    messages = jnp.where(keep_window, jnp.maximum(pre_window, 0.0), 0.0).astype(jnp.bfloat16)
    messages = messages.reshape(reach, row_count, hidden)
    weight_tiles = tile_weights(table, lists, window_live)
    outcome = layer_forward(
        own_rows, own_live, weight_tiles, messages, self_weight, nb_weight, out_bias
    )
    embedded, pre_act, activated, inv_norm, degree, keep_rows = outcome
    grad_self, grad_pooled = layer_backward(
        upstream, keep_rows, pre_act, activated, inv_norm, degree, self_weight, nb_weight
    )
    returned = lax.dot_general(
        weight_tiles, grad_pooled, (((0,), (0,)), ((), ())), preferred_element_type=jnp.float32
    ).reshape(reach, row_count, hidden)
    total = returned[0].reshape(block_count, block_rows, hidden)
    for offset in range(1, reach):
        take_block, take_valid = reader_slots[offset - 1]
        own_part = returned[offset].reshape(block_count, block_rows, hidden)[take_block]
        packed = jnp.where(take_valid[:, None, None], own_part, 0.0)
        back = shifted(packed, "dom", -offset)
        send_block, send_valid = sender_slots[offset - 1]
        total = total.at[send_block].add(jnp.where(send_valid[:, None, None], back, 0.0))
    total = total.reshape(row_count, hidden)
    grad_message = partner_2(total, "side", 0)
    grad_rows = finish_owner(grad_message, keep_rows, neighbour_pre, grad_self, q_weight)
    return (embedded[None], grad_rows[None])


def solution(mesh):
    return jax.shard_map(
        local,
        mesh=mesh,
        in_specs=(
            P("side", "dom", None),
            P("side", "dom"),
            P("side", "dom", None, None),
            P("side", "dom", None),
            P("side", "dom", None),
            P(),
            P(),
            P(),
            P(),
            P(),
        ),
        out_specs=(P("side", "dom", None), P("side", "dom", None)),
        check_vma=False,
    )
```

profile of v0, /device:TPU:7, one launch (start us, length us, event | category | flops | bytes accessed | tf_op | source)
XLA Modules:
  0.0 365.2 jit_solution(77717222674297851)
XLA Ops:
  27.5 3.0 collective-permute-start.1
  30.5 1.6 collective-permute-start.3
  34.5 4.4 %collective-permute-start.5 = (s32[1]{0:T(128)}, s32[1]{0:T(128)}, u32[]{:S(2)}, u32[]{:S(2)}) collective-permute-start(s32[1]{0:T(128)} %collective-permute-done), channel_id=1, source_target_pairs={{0,5},{1,6},{2,7},{3,8},{4,9},{5,10},{6,11},{7,12},{8,13},{9,14},{... | collective-permute-start | bytes 20 | tf_op jit(solution)/shard_map/ppermute | solution.py:22
  38.9 1.7 collective-permute-start.6
  43.2 3.9 %collective-permute-done.6 = s32[1]{0:T(128)} collective-permute-done((s32[1]{0:T(128)}, s32[1]{0:T(128)}, u32[]{:S(2)}, u32[]{:S(2)}) %collective-permute-start.6) | collective-permute-done | bytes 36 | tf_op jit(solution)/shard_map/ppermute | solution.py:22
  47.0 2.9 collective-permute-done.7
  49.9 5.1 %concatenate.66 = s32[8]{0:T(128)S(1)} concatenate(s32[1]{0:T(128)} %collective-permute-done, s32[1]{0:T(128)} %collective-permute-done.1, s32[1]{0:T(128)} %collective-permute-done.2, s32[1]{0:T(128)} %collective-permute-done.3, s32[1]{0:T(128)} %collective-permute-done.4, s32[1]{0:T(128)} %collective-permute-done.5, s32[1]{0:T(128)} %collective-permute-done.6, ...), dimensions={0} | concatenate | bytes 64 | tf_op jit(solution)/shard_map/concatenate | solution.py:147
  55.2 2.8 convert_reduce_fusion
  60.5 2.6 collective-permute-start.11
  68.9 3.1 collective-permute-start.14
  87.2 4.6 %dynamic-slice_select_fusion.7 = (bf16[1,128,1024]{2,1,0:T(8,128)(2,1)S(1)}, bf16[1,128,1024]{2,1,0:T(8,128)(2,1)S(1)}, bf16[1,128,1024]{2,1,0:T(8,128)(2,1)S(1)...) fusion(bf16[2,128,1024]{2,1,0:T(8,128)(2,1)S(1)} %bitcast.297, ...), kind=kLoop, calls=%fused_computation.64 | loop fusion | flops 917504 | bytes 3670051 | tf_op jit(solution)/shard_map/jit(_where)/select_n | solution.py:138
  91.8 3.6 collective-permute-start.10
  96.7 2.7 collective-permute-start.16
  107.2 2.1 collective-permute-done.15
  110.8 8.2 %collective-permute-done.16 = bf16[1,128,1024]{2,1,0:T(8,128)(2,1)S(1)} collective-permute-done((bf16[1,128,1024]{2,1,0:T(8,128)(2,1)S(1)}, bf16[1,128,1024]{2,1,0:T(8,128)(2,1)S(1)}, u32[]{:S(2)}, u32[]{:S(2)}) %collective-permute-start.16) | collective-permute-done | bytes 262176 | tf_op jit(solution)/shard_map/ppermute | solution.py:22
  121.9 1.7 collective-permute-done.18
  125.0 1.9 copy-done.6
  126.9 15.5 %fusion.8 = bf16[256,2048]{1,0:T(8,128)(2,1)} fusion(bf16[256,2048]{1,0:T(8,128)(2,1)S(1)} %copy-done.1, f32[2048]{0:T(1024)S(1)} %copy-done.9, pred[2048]{0:T(1024)(128)(4,1)S(1)} %lt.102, bf16[2048,1024]{1,0:T(8,128)(2,1)} %bitcast.316, bf16[1024,2048]{1,0:T(8,128)(2,1)} %param.43, f32[256]{0:T(256)S(1)} %broadcast_add_fusion), kind=kOutput, calls=%fused_computation.9 | convolution fusion | flops 10755244032 | bytes 10497024 | tf_op jit(solution)/shard_map/dot_general | solution.py:48
  142.4 3.8 %fusion.57 = f32[256,1024]{1,0:T(8,128)S(1)} fusion(bf16[256,2048]{1,0:T(8,128)(2,1)} %fusion.8, bf16[2048,1024]{1,0:T(8,128)(2,1)} %param.46), kind=kOutput, calls=%fused_computation.205 | convolution fusion | flops 1073741824 | bytes 6291456 | tf_op jit(solution)/shard_map/dot_general | solution.py:53
  146.3 1.8 fusion.31
  148.2 12.0 %fusion.58 = f32[2048,2048]{1,0:T(8,128)} fusion(bf16[256,2048]{1,0:T(8,128)(2,1)S(1)} %copy-done.1, bf16[2048,1024]{1,0:T(8,128)(2,1)} %param.46, f32[256]{0:T(256)S(1)} %broadcast_add_fusion, f32[256,1024]{1,0:T(8,128)} %get-tuple-element.389, bf16[1,256,1024]{2,1,0:T(8,128)(2,1)} %param.42, f32[256]{0:T(256)S(1)} %broadcast_multiply_fusion, ...), kind=kOutput, calls=%fused_computation.206 | convolution fusion | flops 3225419776 | bytes 23596288 | tf_op jit(solution)/shard_map/dot_general | solution.py:164
  160.2 6.4 %fusion.56 = (f32[256,2048]{1,0:T(8,128)S(1)}, f32[256,2048]{1,0:T(8,128)S(1)}, f32[256,2048]{1,0:T(8,128)S(1)}, f32[256,2048]{1,0:T(8,128)S(1)}, f32[256,2048]{...) fusion(f32[2048,2048]{1,0:T(8,128)} %fusion.58), kind=kLoop, calls=%fused_computation.203 | loop fusion | bytes 33554432 | tf_op jit(solution)/shard_map/slice | solution.py:170
  167.4 4.7 %collective-permute-start.19 = (f32[1,128,2048]{2,1,0:T(8,128)S(1)}, f32[1,128,2048]{2,1,0:T(8,128)S(1)}, u32[]{:S(2)}, u32[]{:S(2)}) collective-permute-start(f32[1,128,2048]{2,1,0:T(8,128)S(1)} %dynamic-slice_select_fusion.6), channel_id=1, source_target_pairs={{0,63},{1,0},{2,1},{3,2},{4,3},{5,4},{6,5},{7,6},{8,7},{9,8},{10,9... | collective-permute-start | bytes 3145736 | tf_op jit(solution)/shard_map/ppermute | solution.py:22
  172.9 19.5 %collective-permute-start.20 = (f32[1,128,2048]{2,1,0:T(8,128)S(1)}, f32[1,128,2048]{2,1,0:T(8,128)S(1)}, u32[]{:S(2)}, u32[]{:S(2)}) collective-permute-start(f32[1,128,2048]{2,1,0:T(8,128)S(1)} %dynamic-slice_select_fusion.5), channel_id=1, source_target_pairs={{0,62},{1,63},{2,0},{3,1},{4,2},{5,3},{6,4},{7,5},{8,6},{9,7},{10,... | collective-permute-start | bytes 3145736 | tf_op jit(solution)/shard_map/ppermute | solution.py:22
  196.2 13.1 %collective-permute-done.19 = f32[1,128,2048]{2,1,0:T(8,128)S(1)} collective-permute-done((f32[1,128,2048]{2,1,0:T(8,128)S(1)}, f32[1,128,2048]{2,1,0:T(8,128)S(1)}, u32[]{:S(2)}, u32[]{:S(2)}) %collective-permute-start.19) | collective-permute-done | bytes 1048608 | tf_op jit(solution)/shard_map/ppermute | solution.py:22
  209.3 25.0 %collective-permute-start.24 = (f32[1,128,2048]{2,1,0:T(8,128)S(1)}, f32[1,128,2048]{2,1,0:T(8,128)S(1)}, u32[]{:S(2)}, u32[]{:S(2)}) collective-permute-start(f32[1,128,2048]{2,1,0:T(8,128)S(1)} %dynamic-slice_select_fusion.1), channel_id=1, source_target_pairs={{0,58},{1,59},{2,60},{3,61},{4,62},{5,63},{6,0},{7,1},{8,2},{9,3},... | collective-permute-start | bytes 3145736 | tf_op jit(solution)/shard_map/ppermute | solution.py:22
  235.8 9.1 %collective-permute-done.20 = f32[1,128,2048]{2,1,0:T(8,128)S(1)} collective-permute-done((f32[1,128,2048]{2,1,0:T(8,128)S(1)}, f32[1,128,2048]{2,1,0:T(8,128)S(1)}, u32[]{:S(2)}, u32[]{:S(2)}) %collective-permute-start.20) | collective-permute-done | bytes 1048608 | tf_op jit(solution)/shard_map/ppermute | solution.py:22
  244.9 1.6 fusion.20
  246.5 16.0 %collective-permute-done.21 = f32[1,128,2048]{2,1,0:T(8,128)S(1)} collective-permute-done((f32[1,128,2048]{2,1,0:T(8,128)S(1)}, f32[1,128,2048]{2,1,0:T(8,128)S(1)}, u32[]{:S(2)}, u32[]{:S(2)}) %collective-permute-start.21) | collective-permute-done | bytes 1048608 | tf_op jit(solution)/shard_map/ppermute | solution.py:22
  264.0 83.8 %collective-permute-done.22 = f32[1,128,2048]{2,1,0:T(8,128)S(1)} collective-permute-done((f32[1,128,2048]{2,1,0:T(8,128)S(1)}, f32[1,128,2048]{2,1,0:T(8,128)S(1)}, u32[]{:S(2)}, u32[]{:S(2)}) %collective-permute-start.22) | collective-permute-done | bytes 1048608 | tf_op jit(solution)/shard_map/ppermute | solution.py:22
  356.1 2.0 fusion.53
  358.1 7.1 %fusion.18 = bf16[1,256,1024]{2,1,0:T(8,128)(2,1)} fusion(f32[256,1024]{1,0:T(8,128)} %fusion.53, bf16[1024,2048]{1,0:T(8,128)(2,1)} %param.43, bf16[256,2048]{1,0:T(8,128)(2,1)S(1)} %collective-permute-done.26, f32[2048]{0:T(1024)S(1)} %copy-done.9, pred[256]{0:T(512)(128)(4,1)S(1)} %iota_compare_fusion.1, bf16[1,256,1024]{2,1,0:T(8,128)(2,1)} %param.38), kind=kOutput, calls=%fused_computation.31 | convolution fusion | flops 2150367232 | bytes 7348480 | tf_op jit(solution)/shard_map/dot_general | solution.py:81
  (145 shorter events, 59.2 us)
Async XLA Ops:
  0.6 145.6 %copy-start = (bf16[1024,1024]{1,0:T(8,128)(2,1)S(1)}, bf16[1024,1024]{1,0:T(8,128)(2,1)}, u32[]{:S(2)}) copy-start(bf16[1024,1024]{1,0:T(8,128)(2,1)} %param.45) | copy-start | bytes 6291460
  0.6 63.1 %copy-start.7 = (s32[3]{0:T(128)S(1)}, s32[3]{0:T(128)}, u32[]{:S(2)}) copy-start(s32[3]{0:T(128)} %constant.348.clone.1) | copy-start | bytes 40
  0.7 59.8 %copy-start.5 = (s32[1,1,8,2]{2,3,1,0:T(2,128)S(1)}, s32[1,1,8,2]{2,3,1,0:T(2,128)}, u32[]{:S(2)}) copy-start(s32[1,1,8,2]{2,3,1,0:T(2,128)} %param.40) | copy-start | bytes 196
  0.7 57.3 %collective-permute-start.9 = (s32[1,8,2]{1,2,0:T(2,128)}, s32[1,8,2]{1,2,0:T(2,128)S(1)}, u32[]{:S(2)}, u32[]{:S(2)}) collective-permute-start(s32[1,8,2]{1,2,0:T(2,128)} %bitcast.312), channel_id=1, source_target_pairs={{0,63},{1,0},{2,1},{3,2},{4,3},{5,4},{6,5},{7,6},{8,7},{9,8},{10,9... | collective-permute-start | bytes 200 | tf_op jit(solution)/shard_map/ppermute | solution.py:22
  1.3 85.9 %collective-permute-start.8 = (bf16[256,1024]{1,0:T(8,128)(2,1)}, bf16[256,1024]{1,0:T(8,128)(2,1)S(1)}, u32[]{:S(2)}, u32[]{:S(2)}) collective-permute-start(bf16[256,1024]{1,0:T(8,128)(2,1)} %bitcast.331), channel_id=1, source_target_pairs={{0,64},{64,0},{1,65},{65,1},{2,66},{66,2},{3,67},{67,3},{4,68},{68... | collective-permute-start | bytes 1572872 | tf_op jit(solution)/shard_map/ppermute | solution.py:16
  2.2 25.2 %collective-permute-start = (s32[1]{0:T(128)}, s32[1]{0:T(128)}, u32[]{:S(2)}, u32[]{:S(2)}) collective-permute-start(s32[1]{0:T(128)} %bitcast.3), channel_id=1, source_target_pairs={{0,64},{64,0},{1,65},{65,1},{2,66},{66,2},{3,67},{67,3},{4,68},{68... | collective-permute-start | bytes 20 | tf_op jit(solution)/shard_map/ppermute | solution.py:16
  27.5 4.6 %collective-permute-start.1 = (s32[1]{0:T(128)}, s32[1]{0:T(128)}, u32[]{:S(2)}, u32[]{:S(2)}) collective-permute-start(s32[1]{0:T(128)} %collective-permute-done), channel_id=1, source_target_pairs={{0,1},{1,2},{2,3},{3,4},{4,5},{5,6},{6,7},{7,8},{8,9},{9,10},{10,1... | collective-permute-start | bytes 20 | tf_op jit(solution)/shard_map/ppermute | solution.py:22
  30.5 4.1 %collective-permute-start.2 = (s32[1]{0:T(128)}, s32[1]{0:T(128)}, u32[]{:S(2)}, u32[]{:S(2)}) collective-permute-start(s32[1]{0:T(128)} %collective-permute-done), channel_id=1, source_target_pairs={{0,2},{1,3},{2,4},{3,5},{4,6},{5,7},{6,8},{7,9},{8,10},{9,11},{10,... | collective-permute-start | bytes 20 | tf_op jit(solution)/shard_map/ppermute | solution.py:22
  30.5 8.4 %collective-permute-start.3 = (s32[1]{0:T(128)}, s32[1]{0:T(128)}, u32[]{:S(2)}, u32[]{:S(2)}) collective-permute-start(s32[1]{0:T(128)} %collective-permute-done), channel_id=1, source_target_pairs={{0,3},{1,4},{2,5},{3,6},{4,7},{5,8},{6,9},{7,10},{8,11},{9,12},{10... | collective-permute-start | bytes 20 | tf_op jit(solution)/shard_map/ppermute | solution.py:22
  32.1 9.6 %collective-permute-start.4 = (s32[1]{0:T(128)}, s32[1]{0:T(128)}, u32[]{:S(2)}, u32[]{:S(2)}) collective-permute-start(s32[1]{0:T(128)} %collective-permute-done), channel_id=1, source_target_pairs={{0,4},{1,5},{2,6},{3,7},{4,8},{5,9},{6,10},{7,11},{8,12},{9,13},{1... | collective-permute-start | bytes 20 | tf_op jit(solution)/shard_map/ppermute | solution.py:22
  34.5 8.6 %collective-permute-start.5 = (s32[1]{0:T(128)}, s32[1]{0:T(128)}, u32[]{:S(2)}, u32[]{:S(2)}) collective-permute-start(s32[1]{0:T(128)} %collective-permute-done), channel_id=1, source_target_pairs={{0,5},{1,6},{2,7},{3,8},{4,9},{5,10},{6,11},{7,12},{8,13},{9,14},{... | collective-permute-start | bytes 20 | tf_op jit(solution)/shard_map/ppermute | solution.py:22
  38.9 8.1 %collective-permute-start.6 = (s32[1]{0:T(128)}, s32[1]{0:T(128)}, u32[]{:S(2)}, u32[]{:S(2)}) collective-permute-start(s32[1]{0:T(128)} %collective-permute-done), channel_id=1, source_target_pairs={{0,6},{1,7},{2,8},{3,9},{4,10},{5,11},{6,12},{7,13},{8,14},{9,15},... | collective-permute-start | bytes 20 | tf_op jit(solution)/shard_map/ppermute | solution.py:22
  41.7 8.2 %collective-permute-start.7 = (s32[1]{0:T(128)}, s32[1]{0:T(128)}, u32[]{:S(2)}, u32[]{:S(2)}) collective-permute-start(s32[1]{0:T(128)} %collective-permute-done), channel_id=1, source_target_pairs={{0,7},{1,8},{2,9},{3,10},{4,11},{5,12},{6,13},{7,14},{8,15},{9,16}... | collective-permute-start | bytes 20 | tf_op jit(solution)/shard_map/ppermute | solution.py:22
  60.5 4.9 %collective-permute-start.11 = (s32[2,8,2]{1,2,0:T(2,128)S(1)}, s32[2,8,2]{1,2,0:T(2,128)S(1)}, u32[]{:S(2)}, u32[]{:S(2)}) collective-permute-start(s32[2,8,2]{1,2,0:T(2,128)S(1)} %pad_add_fusion.1), channel_id=1, source_target_pairs={{0,62},{1,63},{2,0},{3,1},{4,2},{5,3},{6,4},{7,5},{8,6},{9,7},{10,... | collective-permute-start | bytes 392 | tf_op jit(solution)/shard_map/ppermute | solution.py:22
  68.9 5.7 %collective-permute-start.14 = (s32[4,8,2]{1,2,0:T(2,128)S(1)}, s32[4,8,2]{1,2,0:T(2,128)S(1)}, u32[]{:S(2)}, u32[]{:S(2)}) collective-permute-start(s32[4,8,2]{1,2,0:T(2,128)S(1)} %pad_add_fusion), channel_id=1, source_target_pairs={{0,60},{1,61},{2,62},{3,63},{4,0},{5,1},{6,2},{7,3},{8,4},{9,5},{1... | collective-permute-start | bytes 776 | tf_op jit(solution)/shard_map/ppermute | solution.py:22
  91.8 8.2 %collective-permute-start.10 = (bf16[1,128,1024]{2,1,0:T(8,128)(2,1)S(1)}, bf16[1,128,1024]{2,1,0:T(8,128)(2,1)S(1)}, u32[]{:S(2)}, u32[]{:S(2)}) collective-permute-start(bf16[1,128,1024]{2,1,0:T(8,128)(2,1)S(1)} %get-tuple-element.382), channel_id=1, source_target_pairs={{0,1},{1,2},{2,3},{3,4},{4,5},{5,6},{6,7},{7,8},{8,9},{9,10},{10,1... | collective-permute-start | bytes 786440 | tf_op jit(solution)/shard_map/ppermute | solution.py:22
  96.1 6.8 %collective-permute-start.12 = (bf16[1,128,1024]{2,1,0:T(8,128)(2,1)S(1)}, bf16[1,128,1024]{2,1,0:T(8,128)(2,1)S(1)}, u32[]{:S(2)}, u32[]{:S(2)}) collective-permute-start(bf16[1,128,1024]{2,1,0:T(8,128)(2,1)S(1)} %get-tuple-element.381), channel_id=1, source_target_pairs={{0,2},{1,3},{2,4},{3,5},{4,6},{5,7},{6,8},{7,9},{8,10},{9,11},{10,... | collective-permute-start | bytes 786440 | tf_op jit(solution)/shard_map/ppermute | solution.py:22
  96.6 9.2 %collective-permute-start.13 = (bf16[1,128,1024]{2,1,0:T(8,128)(2,1)S(1)}, bf16[1,128,1024]{2,1,0:T(8,128)(2,1)S(1)}, u32[]{:S(2)}, u32[]{:S(2)}) collective-permute-start(bf16[1,128,1024]{2,1,0:T(8,128)(2,1)S(1)} %get-tuple-element.380), channel_id=1, source_target_pairs={{0,3},{1,4},{2,5},{3,6},{4,7},{5,8},{6,9},{7,10},{8,11},{9,12},{10... | collective-permute-start | bytes 786440 | tf_op jit(solution)/shard_map/ppermute | solution.py:22
  96.6 12.7 %collective-permute-start.15 = (bf16[1,128,1024]{2,1,0:T(8,128)(2,1)S(1)}, bf16[1,128,1024]{2,1,0:T(8,128)(2,1)S(1)}, u32[]{:S(2)}, u32[]{:S(2)}) collective-permute-start(bf16[1,128,1024]{2,1,0:T(8,128)(2,1)S(1)} %get-tuple-element.379), channel_id=1, source_target_pairs={{0,4},{1,5},{2,6},{3,7},{4,8},{5,9},{6,10},{7,11},{8,12},{9,13},{1... | collective-permute-start | bytes 786440 | tf_op jit(solution)/shard_map/ppermute | solution.py:22
  96.7 22.3 %collective-permute-start.16 = (bf16[1,128,1024]{2,1,0:T(8,128)(2,1)S(1)}, bf16[1,128,1024]{2,1,0:T(8,128)(2,1)S(1)}, u32[]{:S(2)}, u32[]{:S(2)}) collective-permute-start(bf16[1,128,1024]{2,1,0:T(8,128)(2,1)S(1)} %get-tuple-element.378), channel_id=1, source_target_pairs={{0,5},{1,6},{2,7},{3,8},{4,9},{5,10},{6,11},{7,12},{8,13},{9,14},{... | collective-permute-start | bytes 786440 | tf_op jit(solution)/shard_map/ppermute | solution.py:22
  100.1 20.4 %collective-permute-start.17 = (bf16[1,128,1024]{2,1,0:T(8,128)(2,1)S(1)}, bf16[1,128,1024]{2,1,0:T(8,128)(2,1)S(1)}, u32[]{:S(2)}, u32[]{:S(2)}) collective-permute-start(bf16[1,128,1024]{2,1,0:T(8,128)(2,1)S(1)} %get-tuple-element.377), channel_id=1, source_target_pairs={{0,6},{1,7},{2,8},{3,9},{4,10},{5,11},{6,12},{7,13},{8,14},{9,15},... | collective-permute-start | bytes 786440 | tf_op jit(solution)/shard_map/ppermute | solution.py:22
  102.9 20.6 %collective-permute-start.18 = (bf16[1,128,1024]{2,1,0:T(8,128)(2,1)S(1)}, bf16[1,128,1024]{2,1,0:T(8,128)(2,1)S(1)}, u32[]{:S(2)}, u32[]{:S(2)}) collective-permute-start(bf16[1,128,1024]{2,1,0:T(8,128)(2,1)S(1)} %get-tuple-element.376), channel_id=1, source_target_pairs={{0,7},{1,8},{2,9},{3,10},{4,11},{5,12},{6,13},{7,14},{8,15},{9,16}... | collective-permute-start | bytes 786440 | tf_op jit(solution)/shard_map/ppermute | solution.py:22
  121.8 5.1 %copy-start.1 = (bf16[256,2048]{1,0:T(8,128)(2,1)S(1)}, bf16[256,2048]{1,0:T(8,128)(2,1)}, u32[]{:S(2)}) copy-start(bf16[256,2048]{1,0:T(8,128)(2,1)} %get-tuple-element.367) | copy-start | bytes 3145732
  121.8 5.1 %copy-start.9 = (f32[2048]{0:T(1024)S(1)}, f32[2048]{0:T(1024)}, u32[]{:S(2)}) copy-start(f32[2048]{0:T(1024)} %param.44) | copy-start | bytes 24580
  167.4 41.9 %collective-permute-start.19 = (f32[1,128,2048]{2,1,0:T(8,128)S(1)}, f32[1,128,2048]{2,1,0:T(8,128)S(1)}, u32[]{:S(2)}, u32[]{:S(2)}) collective-permute-start(f32[1,128,2048]{2,1,0:T(8,128)S(1)} %dynamic-slice_select_fusion.6), channel_id=1, source_target_pairs={{0,63},{1,0},{2,1},{3,2},{4,3},{5,4},{6,5},{7,6},{8,7},{9,8},{10,9... | collective-permute-start | bytes 3145736 | tf_op jit(solution)/shard_map/ppermute | solution.py:22
  172.9 72.1 %collective-permute-start.20 = (f32[1,128,2048]{2,1,0:T(8,128)S(1)}, f32[1,128,2048]{2,1,0:T(8,128)S(1)}, u32[]{:S(2)}, u32[]{:S(2)}) collective-permute-start(f32[1,128,2048]{2,1,0:T(8,128)S(1)} %dynamic-slice_select_fusion.5), channel_id=1, source_target_pairs={{0,62},{1,63},{2,0},{3,1},{4,2},{5,3},{6,4},{7,5},{8,6},{9,7},{10,... | collective-permute-start | bytes 3145736 | tf_op jit(solution)/shard_map/ppermute | solution.py:22
  193.1 69.4 %collective-permute-start.21 = (f32[1,128,2048]{2,1,0:T(8,128)S(1)}, f32[1,128,2048]{2,1,0:T(8,128)S(1)}, u32[]{:S(2)}, u32[]{:S(2)}) collective-permute-start(f32[1,128,2048]{2,1,0:T(8,128)S(1)} %dynamic-slice_select_fusion.4), channel_id=1, source_target_pairs={{0,61},{1,62},{2,63},{3,0},{4,1},{5,2},{6,3},{7,4},{8,5},{9,6},{10... | collective-permute-start | bytes 3145736 | tf_op jit(solution)/shard_map/ppermute | solution.py:22
  193.8 154.0 %collective-permute-start.22 = (f32[1,128,2048]{2,1,0:T(8,128)S(1)}, f32[1,128,2048]{2,1,0:T(8,128)S(1)}, u32[]{:S(2)}, u32[]{:S(2)}) collective-permute-start(f32[1,128,2048]{2,1,0:T(8,128)S(1)} %dynamic-slice_select_fusion.3), channel_id=1, source_target_pairs={{0,60},{1,61},{2,62},{3,63},{4,0},{5,1},{6,2},{7,3},{8,4},{9,5},{1... | collective-permute-start | bytes 3145736 | tf_op jit(solution)/shard_map/ppermute | solution.py:22
  194.7 154.6 %collective-permute-start.23 = (f32[1,128,2048]{2,1,0:T(8,128)S(1)}, f32[1,128,2048]{2,1,0:T(8,128)S(1)}, u32[]{:S(2)}, u32[]{:S(2)}) collective-permute-start(f32[1,128,2048]{2,1,0:T(8,128)S(1)} %dynamic-slice_select_fusion.2), channel_id=1, source_target_pairs={{0,59},{1,60},{2,61},{3,62},{4,63},{5,0},{6,1},{7,2},{8,3},{9,4},{... | collective-permute-start | bytes 3145736 | tf_op jit(solution)/shard_map/ppermute | solution.py:22
  209.3 141.5 %collective-permute-start.24 = (f32[1,128,2048]{2,1,0:T(8,128)S(1)}, f32[1,128,2048]{2,1,0:T(8,128)S(1)}, u32[]{:S(2)}, u32[]{:S(2)}) collective-permute-start(f32[1,128,2048]{2,1,0:T(8,128)S(1)} %dynamic-slice_select_fusion.1), channel_id=1, source_target_pairs={{0,58},{1,59},{2,60},{3,61},{4,62},{5,63},{6,0},{7,1},{8,2},{9,3},... | collective-permute-start | bytes 3145736 | tf_op jit(solution)/shard_map/ppermute | solution.py:22
  244.9 107.4 %collective-permute-start.25 = (f32[1,128,2048]{2,1,0:T(8,128)S(1)}, f32[1,128,2048]{2,1,0:T(8,128)S(1)}, u32[]{:S(2)}, u32[]{:S(2)}) collective-permute-start(f32[1,128,2048]{2,1,0:T(8,128)S(1)} %dynamic-slice_select_fusion), channel_id=1, source_target_pairs={{0,57},{1,58},{2,59},{3,60},{4,61},{5,62},{6,63},{7,0},{8,1},{9,2}... | collective-permute-start | bytes 3145736 | tf_op jit(solution)/shard_map/ppermute | solution.py:22
  354.0 4.1 %collective-permute-start.26 = (bf16[256,2048]{1,0:T(8,128)(2,1)S(1)}, bf16[256,2048]{1,0:T(8,128)(2,1)S(1)}, u32[]{:S(2)}, u32[]{:S(2)}) collective-permute-start(bf16[256,2048]{1,0:T(8,128)(2,1)S(1)} %bitcast_convert_fusion), channel_id=1, source_target_pairs={{0,64},{64,0},{1,65},{65,1},{2,66},{66,2},{3,67},{67,3},{4,68},{68... | collective-permute-start | bytes 3145736 | tf_op jit(solution)/shard_map/ppermute | solution.py:16
  (6 other events, 17.0 us)
where the time goes:
time: 366 us; the launch traced here: 365 us
  waiting for transfers between devices  146 us (40%)
  starting transfers between devices  79.2 us (22%)
  other arithmetic  52.5 us (14%)
  matrix products  42.3 us (12%)
  between operations  28.5 us (8%)
  local copies, waits for them, and re-layouts  17 us (5%)
    ppermute x24, waiting for transfers between devices, shifted(): return lax.ppermute(value, axis, pairs)  146 us
    ppermute x24, starting transfers between devices, shifted(): return lax.ppermute(value, axis, pairs)  77.4 us
    dot_general x1, matrix products, layer_forward(): jnp.dot(weight_tiles, messages.reshape(-1, messages.shape[-1]), preferred...  15.5 us
    dot_general x1, matrix products, local(): lax.dot_general(weight_tiles, grad_pooled, (((0,), (0,)), ((), ())), pref...  12 us
    scatter-add x7, other arithmetic, local(): total.at[send_block].add(jnp.where(send_valid[:, None, None], back, 0.0))  10.5 us
    scatter-add x7, other arithmetic, local(): placed = jnp.zeros_like(partner_blocks).at[take_block].add(cleaned)  9.12 us
  transfers between devices with their start and end apart: 27, of which 14 were waited for; matrix products, arithmetic and copies ran while one was open for 15% of the time, Pallas kernels for 0%

commit v1 on v0

v1 whole, which is shorter than its diff:
```python
import jax
import jax.numpy as jnp
from jax import lax
from jax.experimental import pallas as pl
from jax.experimental.pallas import tpu as pltpu
from jax.sharding import PartitionSpec as P

EPS = 1e-06
DEAD = 16384.0
LIMIT = 8192.0
F32 = jnp.float32
BF16 = jnp.bfloat16
VMEM = pl.BlockSpec(memory_space=pltpu.VMEM)
SMEM = pl.BlockSpec(memory_space=pltpu.SMEM)


def dot(a, b, ca=1, cb=0):
    return lax.dot_general(a, b, (((ca,), (cb,)), ((), ())), preferred_element_type=F32)


def call(kernel, outs, ins, in_specs=None, scratch=(), limit=24, flops=0):
    return pl.pallas_call(
        kernel,
        out_shape=[jax.ShapeDtypeStruct(s, d) for s, d in outs],
        in_specs=in_specs or [VMEM] * len(ins),
        out_specs=[VMEM] * len(outs),
        scratch_shapes=list(scratch),
        compiler_params=pltpu.CompilerParams(vmem_limit_bytes=limit << 20),
        cost_estimate=pl.CostEstimate(flops=flops, bytes_accessed=1 << 20, transcendentals=0),
    )(*ins)


def route(x, shift):
    count = lax.axis_size("dom")
    pairs = [
        (s * count + j, (1 - s) * count + (j + shift) % count)
        for s in range(2)
        for j in range(count)
    ]
    return lax.ppermute(x, ("side", "dom"), pairs)


def pick_kernel(block, live_ref, wanted_ref, x_ref, *outs):
    live = live_ref[0]
    for o, out in enumerate(outs):
        start = wanted_ref[o] * block
        row = lax.broadcasted_iota(jnp.int32, (block, 1), 0) + start
        x = x_ref[pl.ds(pl.multiple_of(start, block), block), :].astype(F32)
        out[...] = jnp.where(row < live, x, DEAD).astype(BF16)


def tiles_kernel(block, lists_ref, counts_ref, x_ref, sw_ref, tiles_ref, tiles_t_ref, self_ref):
    reach = tiles_ref.shape[1] // block
    for o in range(reach):
        first = counts_ref[:, o * 2 * block : (o * 2 + 1) * block]
        second = counts_ref[:, (o * 2 + 1) * block : (o * 2 + 2) * block]
        tile = (first * lists_ref[o, 0] + second * lists_ref[o, 1]).astype(F32)
        tiles_ref[:, o * block : (o + 1) * block] = tile.astype(BF16)
        tiles_t_ref[o * block : (o + 1) * block, :] = tile.T.astype(BF16)
    self_ref[...] = dot(x_ref[...], sw_ref[...])


def message_kernel(block, first, last, *refs):
    size = len(range(first, last))
    blocks = refs[:size]
    q_ref, qb_ref, tiles_ref, acc_in, deg_in, msg_ref, acc_ref, deg_ref = refs[size:]
    x = jnp.concatenate([b[...] for b in blocks], axis=0)
    keep = x[:, :128].astype(F32) < LIMIT
    tiles = tiles_ref[:, first * block : last * block]
    deg_ref[...] = deg_in[...] + dot(tiles, jnp.where(keep, 1.0, 0.0).astype(BF16))
    keep = keep[:, :1]
    hidden = q_ref.shape[1]
    step = 512
    for n in range(hidden // step):
        cols = slice(n * step, (n + 1) * step)
        pre = dot(x, q_ref[:, cols]) + qb_ref[:, cols]
        msg = jnp.where(keep, jnp.maximum(pre, 0.0), 0.0).astype(BF16)
        msg_ref[:, cols] = msg
        acc_ref[:, cols] = acc_in[:, cols] + dot(tiles, msg)


def layer_kernel(
    live_ref, acc_ref, deg_ref, self_ref, up_ref, sw_ref, nb_ref, ob_ref,
    emb_ref, gself_ref, gpool_ref, pre_ref,
):
    rows, width = self_ref.shape
    inv_deg = 1.0 / (1.0 + deg_ref[:, :1])
    pooled = (acc_ref[...] * inv_deg).astype(BF16)
    step = 512
    for n in range(width // step):
        cols = slice(n * step, (n + 1) * step)
        pre_ref[:, cols] = self_ref[:, cols] + dot(pooled, nb_ref[:, cols]) + ob_ref[:, cols]
    pre = pre_ref[...]
    act = jnp.maximum(pre, 0.0)
    inv = lax.rsqrt(jnp.mean(act * act, axis=1, keepdims=True) + EPS)
    keep = lax.broadcasted_iota(jnp.int32, (rows, 1), 0) < live_ref[0]
    emb_ref[...] = jnp.where(keep, act * inv, 0.0).astype(BF16)
    up = jnp.where(keep, up_ref[...].astype(F32), 0.0)
    inner = jnp.sum(up * act, axis=1, keepdims=True) / width
    g = inv * up - act * (inv * inv * inv * inner)
    g = jnp.where(pre > 0, g, 0.0).astype(BF16)
    for n in range(nb_ref.shape[0] // step):
        cols = slice(n * step, (n + 1) * step)
        gpool_ref[:, cols] = (dot(g, nb_ref[cols, :], 1, 1) * inv_deg).astype(BF16)
    for n in range(width // step):
        cols = slice(n * step, (n + 1) * step)
        gself_ref[:, cols] = dot(g, sw_ref[cols, :], 1, 1)


def back_kernel(block, first, last, skip, *refs):
    size = last - first
    tt_ref, gpool_ref, msg_ref, q_ref = refs[:4]
    outs = refs[4 : 4 + size]
    gn_ref = refs[4 + size]
    tt = tt_ref[first * block : last * block, :]
    step = 512
    for n in range(gpool_ref.shape[1] // step):
        cols = slice(n * step, (n + 1) * step)
        g = dot(tt, gpool_ref[:, cols])
        live = msg_ref[skip * block : (skip + size) * block, cols].astype(F32) > 0
        gn_ref[:, cols] = jnp.where(live, g, 0.0).astype(BF16)
    gn = gn_ref[...]
    for n in range(q_ref.shape[0] // step):
        cols = slice(n * step, (n + 1) * step)
        part = dot(gn, q_ref[cols, :], 1, 1).astype(BF16)
        for i, out in enumerate(outs):
            out[:, cols] = part[i * block : (i + 1) * block]


def finish_kernel(block, live_ref, wanted_ref, gself_ref, *refs):
    parts, (out_ref, sum_ref) = refs[:-2], refs[-2:]
    sum_ref[...] = gself_ref[...]
    for o, part in enumerate(parts):
        at = pl.ds(pl.multiple_of(wanted_ref[o] * block, block), block)
        sum_ref[at, :] += part[...].astype(F32)
    keep = lax.broadcasted_iota(jnp.int32, (sum_ref.shape[0], 1), 0) < live_ref[0]
    out_ref[...] = jnp.where(keep, sum_ref[...], 0.0).astype(BF16)


def local(x, live, listed, counts, cotangent, q, qb, sw, nb, ob):
    x, lists, counts, up = x[0], listed[0, 0], counts[0], cotangent[0]
    live = live.reshape(1)
    rows, width = x.shape
    hidden = q.shape[1]
    reach, block_count = lists.shape
    block = rows // block_count
    qb, ob = qb[None], ob[None]
    second = lists[:, 1]
    row = jnp.pad(second, (0, 128 - reach))[None]
    wanted = jnp.concatenate([route(row, -o)[0, o : o + 1] for o in range(reach)])
    sent = call(
        lambda *r: pick_kernel(block, *r),
        [((block, width), BF16)] * reach,
        (live, wanted, x),
        [SMEM, SMEM, VMEM],
    )
    got = [route(b, o) for o, b in enumerate(sent)]
    tiles, tiles_t, self_pre = call(
        lambda *r: tiles_kernel(block, *r),
        [((rows, reach * block), BF16), ((reach * block, rows), BF16), ((rows, width), F32)],
        (lists, counts, x, sw),
        [SMEM] + [VMEM] * 3,
        flops=2 * rows * width * width,
    )
    acc = jnp.zeros((rows, hidden), F32)
    deg = jnp.zeros((rows, 128), F32)
    messages = {}
    for first, last in ((0, 4), (4, 8)):
        size = last - first
        msg, acc, deg = call(
            lambda *r, f=first, l=last: message_kernel(block, f, l, *r),
            [((size * block, hidden), BF16), ((rows, hidden), F32), ((rows, 128), F32)],
            (*got[first:last], q, qb, tiles, acc, deg),
            flops=2 * size * block * hidden * (width + rows),
        )
        for o in range(first, last):
            messages[o] = (msg, o - first)
    emb, gself, gpool = call(
        layer_kernel,
        [((rows, width), BF16), ((rows, width), F32), ((rows, hidden), BF16)],
        (live, acc, deg, self_pre, up, sw, nb, ob),
        [SMEM] + [VMEM] * 7,
        scratch=[pltpu.VMEM((rows, width), F32)],
        flops=2 * rows * width * (2 * hidden + width),
    )
    back = [None] * reach
    for first, last in ((6, 8), (4, 6), (2, 4), (0, 2)):
        size = last - first
        msg, skip = messages[first]
        parts = call(
            lambda *r, f=first, l=last, k=skip: back_kernel(block, f, l, k, *r),
            [((block, width), BF16)] * size,
            (tiles_t, gpool, msg, q),
            scratch=[pltpu.VMEM((size * block, hidden), BF16)],
            flops=2 * size * block * hidden * (width + rows),
        )
        for i, part in enumerate(parts):
            back[first + i] = route(part, -(first + i))
    (grad,) = call(
        lambda *r: finish_kernel(block, *r),
        [((rows, width), BF16)],
        (live, wanted, gself, *back),
        [SMEM, SMEM] + [VMEM] * (1 + reach),
        scratch=[pltpu.VMEM((rows, width), F32)],
    )
    return emb[None], grad[None]


def solution(mesh):
    data = P("side", "dom", None)
    return jax.shard_map(
        local,
        mesh=mesh,
        in_specs=(
            data,
            P("side", "dom"),
            P("side", "dom", None, None),
            data,
            data,
            P(),
            P(),
            P(),
            P(),
            P(),
        ),
        out_specs=(data, data),
        check_vma=False,
    )
```

time: 366 us -> 134 us (0.37)
  waiting for transfers between devices: 146 us -> 29 us
  other arithmetic: 52.5 us -> 0 us
  matrix products: 42.3 us -> 0 us
  between operations: 28.5 us -> 1.55 us
  Pallas kernels: 0 us -> 21.2 us
  starting transfers between devices: 79.2 us -> 64.9 us
    ppermute x27 -> x24, waiting for transfers between devices: 146 us -> 29 us  [route(): return lax.ppermute(x, ('side', 'dom'), pairs)]
    dot_general x6 -> x0, matrix products: 42.3 us -> none  [the longest x1 15.5 us: layer_forward(): jnp.dot(weight_tiles, messages.reshape(-1, messages.shape[-1]), preferred...]
    pallas_call x0 -> x10, Pallas kernels: none -> 21.2 us  [call(): pl.pallas_call(kernel, out_shape=[jax.ShapeDtypeStruct(s, d) for s, d in...]
    scatter-add x14 -> x0, other arithmetic: 19.6 us -> none  [the longest x7 10.5 us: local(): total.at[send_block].add(jnp.where(send_valid[:, None, None], back, 0.0))]
    ppermute x27 -> x24, starting transfers between devices: 79.2 us -> 64.9 us  [route(): return lax.ppermute(x, ('side', 'dom'), pairs)]
    select_n x8 -> x0, other arithmetic: 9.64 us -> none  [the longest x7 5.01 us: local(): packed = jnp.where(take_valid[:, None, None], own_part, 0.0)]
    reduce_sum x9 -> x0, other arithmetic: 8.33 us -> none  [the longest x8 5.51 us: block_slots(): jnp.sum(hits.astype(jnp.int32) * jnp.arange(block_count, dtype=jnp.int32)...]
    another operation x18 -> x0, other arithmetic: 6.29 us -> none
  transfers between devices with their start and end apart: 27 -> 24, of which waited for: 14 -> 5; matrix products, arithmetic and copies ran while one was open for 15% -> 4% of each run, Pallas kernels for 0% -> 7%
where the time goes in v1:
time: 134 us; the launch traced here: 133 us
  starting transfers between devices  64.9 us (48%)
  waiting for transfers between devices  29 us (22%)
  Pallas kernels  21.2 us (16%)
  local copies, waits for them, and re-layouts  16.3 us (12%)
  between operations  1.55 us (1%)
    ppermute x24, starting transfers between devices, route(): return lax.ppermute(x, ('side', 'dom'), pairs)  64.9 us
    ppermute x24, waiting for transfers between devices, route(): return lax.ppermute(x, ('side', 'dom'), pairs)  29 us
    pallas_call x10, Pallas kernels, call(): pl.pallas_call(kernel, out_shape=[jax.ShapeDtypeStruct(s, d) for s, d in...  21.2 us
    unnamed x20, local copies, waits for them, and re-layouts  5.89 us
    concatenate x1, local copies, waits for them, and re-layouts, local(): wanted = jnp.concatenate([route(row, -o)[0, o:o + 1] for o in range(reach)])  4.5 us
    slice x7, local copies, waits for them, and re-layouts, local(): wanted = jnp.concatenate([route(row, -o)[0, o:o + 1] for o in range(reach)])  4.21 us
  transfers between devices with their start and end apart: 24, of which 5 were waited for; matrix products, arithmetic and copies ran while one was open for 4% of the time, Pallas kernels for 7%

profile of v1, /device:TPU:7, one launch (start us, length us, event | category | flops | bytes accessed | tf_op | source)
XLA Modules:
  0.0 132.9 jit_solution(10963254300822071168)
XLA Ops:
  1.3 6.7 %collective-permute-start.7 = (s32[1,128]{1,0:T(1,128)S(1)}, s32[1,128]{1,0:T(1,128)S(1)}, u32[]{:S(2)}, u32[]{:S(2)}) collective-permute-start(s32[1,128]{1,0:T(1,128)S(1)} %pad_bitcast_fusion), channel_id=1, source_target_pairs={{0,121},{1,122},{2,123},{3,124},{4,125},{5,126},{6,127},{7,64},{8,... | collective-permute-start | bytes 1544 | tf_op jit(solution)/shard_map/ppermute | solution.py:40
  8.0 2.5 %collective-permute-start.6 = (s32[1,128]{1,0:T(1,128)S(1)}, s32[1,128]{1,0:T(1,128)S(1)}, u32[]{:S(2)}, u32[]{:S(2)}) collective-permute-start(s32[1,128]{1,0:T(1,128)S(1)} %pad_bitcast_fusion), channel_id=1, source_target_pairs={{0,122},{1,123},{2,124},{3,125},{4,126},{5,127},{6,64},{7,65},{8,6... | collective-permute-start | bytes 1544 | tf_op jit(solution)/shard_map/ppermute | solution.py:40
  10.5 1.2 collective-permute-start.4
  11.7 5.0 %collective-permute-start.3 = (s32[1,128]{1,0:T(1,128)S(1)}, s32[1,128]{1,0:T(1,128)S(1)}, u32[]{:S(2)}, u32[]{:S(2)}) collective-permute-start(s32[1,128]{1,0:T(1,128)S(1)} %pad_bitcast_fusion), channel_id=1, source_target_pairs={{0,125},{1,126},{2,127},{3,64},{4,65},{5,66},{6,67},{7,68},{8,69},... | collective-permute-start | bytes 1544 | tf_op jit(solution)/shard_map/ppermute | solution.py:40
  21.5 1.3 %collective-permute-done.2 = s32[1,128]{1,0:T(1,128)S(1)} collective-permute-done((s32[1,128]{1,0:T(1,128)S(1)}, s32[1,128]{1,0:T(1,128)S(1)}, u32[]{:S(2)}, u32[]{:S(2)}) %collective-permute-start.2) | collective-permute-done | bytes 544 | tf_op jit(solution)/shard_map/ppermute | solution.py:40
  24.0 4.5 %concatenate.3.r_1_ = s32[8]{0:T(128)S(1)} concatenate(s32[1]{0:T(128)S(1)} %bitcast.35, s32[1]{0:T(128)} %bitcast.5, s32[1]{0:T(128)} %bitcast.6, s32[1]{0:T(128)} %bitcast.7, s32[1]{0:T(128)} %bitcast.8, s32[1]{0:T(128)} %bitcast.9, s32[1]{0:T(128)} %bitcast.10, s32[1]{0:T(128)} %bitcast.11), dimensions={0} | concatenate | bytes 64 | tf_op jit(solution)/shard_map/concatenate | solution.py:150
  28.5 1.0 copy-done.5
  30.5 2.1 %collective-permute-start.13 = (bf16[128,1024]{1,0:T(8,128)(2,1)S(1)}, bf16[128,1024]{1,0:T(8,128)(2,1)S(1)}, u32[]{:S(2)}, u32[]{:S(2)}) collective-permute-start(bf16[128,1024]{1,0:T(8,128)(2,1)S(1)} %get-tuple-element.36), channel_id=1, source_target_pairs={{0,65},{1,66},{2,67},{3,68},{4,69},{5,70},{6,71},{7,72},{8,73},{9,... | collective-permute-start | bytes 786440 | tf_op jit(solution)/shard_map/ppermute | solution.py:40
  32.6 2.0 %collective-permute-start.14 = (bf16[128,1024]{1,0:T(8,128)(2,1)S(1)}, bf16[128,1024]{1,0:T(8,128)(2,1)S(1)}, u32[]{:S(2)}, u32[]{:S(2)}) collective-permute-start(bf16[128,1024]{1,0:T(8,128)(2,1)S(1)} %get-tuple-element.37), channel_id=1, source_target_pairs={{0,66},{1,67},{2,68},{3,69},{4,70},{5,71},{6,72},{7,73},{8,74},{9,... | collective-permute-start | bytes 786440 | tf_op jit(solution)/shard_map/ppermute | solution.py:40
  35.4 6.2 %collective-permute-start.9 = (bf16[128,1024]{1,0:T(8,128)(2,1)S(1)}, bf16[128,1024]{1,0:T(8,128)(2,1)S(1)}, u32[]{:S(2)}, u32[]{:S(2)}) collective-permute-start(bf16[128,1024]{1,0:T(8,128)(2,1)S(1)} %get-tuple-element.31), channel_id=1, source_target_pairs={{0,69},{1,70},{2,71},{3,72},{4,73},{5,74},{6,75},{7,76},{8,77},{9,... | collective-permute-start | bytes 786440 | tf_op jit(solution)/shard_map/ppermute | solution.py:40
  41.6 1.2 collective-permute-start.10
  43.0 15.3 %collective-permute-start.11 = (bf16[128,1024]{1,0:T(8,128)(2,1)S(1)}, bf16[128,1024]{1,0:T(8,128)(2,1)S(1)}, u32[]{:S(2)}, u32[]{:S(2)}) collective-permute-start(bf16[128,1024]{1,0:T(8,128)(2,1)S(1)} %get-tuple-element.33), channel_id=1, source_target_pairs={{0,71},{1,72},{2,73},{3,74},{4,75},{5,76},{6,77},{7,78},{8,79},{9,... | collective-permute-start | bytes 786440 | tf_op jit(solution)/shard_map/ppermute | solution.py:40
  58.3 1.6 %copy-done.1 = bf16[1024,1024]{1,0:T(8,128)(2,1)S(1)} copy-done((bf16[1024,1024]{1,0:T(8,128)(2,1)S(1)}, bf16[1024,1024]{1,0:T(8,128)(2,1)}, u32[]{:S(2)}) %copy-start.1) | copy-done | bytes 2097176
  59.9 1.6 %copy-done.4 = s32[1,256,2048]{2,1,0:T(8,128)S(1)} copy-done((s32[1,256,2048]{2,1,0:T(8,128)S(1)}, s32[1,256,2048]{2,1,0:T(8,128)}, u32[]{:S(2)}) %copy-start.4) | copy-done | bytes 2097176
  61.5 1.0 copy-done.6
  62.5 1.4 %shard_map.114 = (bf16[256,1024]{1,0:T(8,128)(2,1)S(1)}, bf16[1024,256]{1,0:T(8,128)(2,1)S(1)}, f32[256,1024]{1,0:T(8,128)S(1)}) custom-call(s32[8,2]{1,0:T(8,128)S(1)} %copy.12.r_0_, s32[256,2048]{1,0:T(8,128)S(1)} %bitcast.25, bf16[256,1024]{1,0:T(8,128)(2,1)S(1)} %bitcast.27, bf16[1024,1024]{1,0:T(8,128)(2,1)S(1)} %copy-done.1), custom_call_target="tpu_custom_call" | custom-call | flops 536870912 | bytes 1048576 | tf_op jit(solution)/shard_map/pallas_call | solution.py:22
  64.8 3.4 %shard_map.115 = (bf16[512,2048]{1,0:T(8,128)(2,1)S(1)}, f32[256,2048]{1,0:T(8,128)S(1)}, f32[256,128]{1,0:T(8,128)S(1)}) custom-call(bf16[128,1024]{1,0:T(8,128)(2,1)S(1)} %collective-permute-done.12.r_0_, bf16[128,1024]{1,0:T(8,128)(2,1)S(1)} %collective-permute-done.13.r_1_, bf16[128,1024]{1,0:T(8,128)(2,1)S(1)} %collective-permute-done.14.r_2_, ...), custom_call_target="tpu_custom_call" | custom-call | flops 2684354560 | bytes 1048576 | tf_op jit(solution)/shard_map/pallas_call | solution.py:22
  68.2 3.4 %shard_map.116 = (bf16[512,2048]{1,0:T(8,128)(2,1)S(1)}, f32[256,2048]{1,0:T(8,128)S(1)}, f32[256,128]{1,0:T(8,128)S(1)}) custom-call(bf16[128,1024]{1,0:T(8,128)(2,1)S(1)} %collective-permute-done.8.r_0_, bf16[128,1024]{1,0:T(8,128)(2,1)S(1)} %collective-permute-done.9.r_1_, bf16[128,1024]{1,0:T(8,128)(2,1)S(1)} %collective-permute-done.10.r_2_, ...), custom_call_target="tpu_custom_call" | custom-call | flops 2684354560 | bytes 1048576 | tf_op jit(solution)/shard_map/pallas_call | solution.py:22
  71.6 4.1 %shard_map.117 = (bf16[256,1024]{1,0:T(8,128)(2,1)}, f32[256,1024]{1,0:T(8,128)S(1)}, bf16[256,2048]{1,0:T(8,128)(2,1)S(1)}) custom-call(s32[1]{0:T(128)} %bitcast.23.live_ref, f32[256,2048]{1,0:T(8,128)S(1)} %get-tuple-element.41.acc_ref, f32[256,128]{1,0:T(8,128)S(1)} %get-tuple-element.42.deg_ref, f32[256,1024]{1,0:T(8,128)S(1)} %get-tuple-element.43.self_ref, ...), custom_call_target="tpu_custom_call" | custom-call | flops 2684354560 | bytes 1048576 | tf_op jit(solution)/shard_map/pallas_call | solution.py:22
  75.7 1.5 %shard_map.121 = (bf16[128,1024]{1,0:T(8,128)(2,1)S(1)}, bf16[128,1024]{1,0:T(8,128)(2,1)S(1)}) custom-call(bf16[1024,256]{1,0:T(8,128)(2,1)S(1)} %get-tuple-element.46.r_0_, bf16[256,2048]{1,0:T(8,128)(2,1)S(1)} %get-tuple-element.47.r_1_, bf16[512,2048]{1,0:T(8,128)(2,1)S(1)} %get-tuple-element.53.r_2_, bf16[1024,2048]{1,0:T(8,128)(2,1)S(1)} %copy-done), custom_call_target="tpu_custom_call" | custom-call | flops 1342177280 | bytes 1048576 | tf_op jit(solution)/shard_map/pallas_call | solution.py:22
  77.2 6.9 %collective-permute-start.22 = (bf16[128,1024]{1,0:T(8,128)(2,1)S(1)}, bf16[128,1024]{1,0:T(8,128)(2,1)S(1)}, u32[]{:S(2)}, u32[]{:S(2)}) collective-permute-start(bf16[128,1024]{1,0:T(8,128)(2,1)S(1)} %get-tuple-element.56), channel_id=1, source_target_pairs={{0,122},{1,123},{2,124},{3,125},{4,126},{5,127},{6,64},{7,65},{8,6... | collective-permute-start | bytes 786440 | tf_op jit(solution)/shard_map/ppermute | solution.py:40
  84.2 3.6 %collective-permute-start.23 = (bf16[128,1024]{1,0:T(8,128)(2,1)S(1)}, bf16[128,1024]{1,0:T(8,128)(2,1)S(1)}, u32[]{:S(2)}, u32[]{:S(2)}) collective-permute-start(bf16[128,1024]{1,0:T(8,128)(2,1)S(1)} %get-tuple-element.57), channel_id=1, source_target_pairs={{0,121},{1,122},{2,123},{3,124},{4,125},{5,126},{6,127},{7,64},{8,... | collective-permute-start | bytes 786440 | tf_op jit(solution)/shard_map/ppermute | solution.py:40
  87.8 1.5 %shard_map.120 = (bf16[128,1024]{1,0:T(8,128)(2,1)S(1)}, bf16[128,1024]{1,0:T(8,128)(2,1)S(1)}) custom-call(bf16[1024,256]{1,0:T(8,128)(2,1)S(1)} %get-tuple-element.46.r_0_, bf16[256,2048]{1,0:T(8,128)(2,1)S(1)} %get-tuple-element.47.r_1_, bf16[512,2048]{1,0:T(8,128)(2,1)S(1)} %get-tuple-element.53.r_2_, bf16[1024,2048]{1,0:T(8,128)(2,1)S(1)} %copy-done), custom_call_target="tpu_custom_call" | custom-call | flops 1342177280 | bytes 1048576 | tf_op jit(solution)/shard_map/pallas_call | solution.py:22
  90.0 1.5 %shard_map.119 = (bf16[128,1024]{1,0:T(8,128)(2,1)S(1)}, bf16[128,1024]{1,0:T(8,128)(2,1)S(1)}) custom-call(bf16[1024,256]{1,0:T(8,128)(2,1)S(1)} %get-tuple-element.46.r_0_, bf16[256,2048]{1,0:T(8,128)(2,1)S(1)} %get-tuple-element.47.r_1_, bf16[512,2048]{1,0:T(8,128)(2,1)S(1)} %get-tuple-element.48.r_2_, bf16[1024,2048]{1,0:T(8,128)(2,1)S(1)} %copy-done), custom_call_target="tpu_custom_call" | custom-call | flops 1342177280 | bytes 1048576 | tf_op jit(solution)/shard_map/pallas_call | solution.py:22
  91.5 4.4 %collective-permute-start.18 = (bf16[128,1024]{1,0:T(8,128)(2,1)S(1)}, bf16[128,1024]{1,0:T(8,128)(2,1)S(1)}, u32[]{:S(2)}, u32[]{:S(2)}) collective-permute-start(bf16[128,1024]{1,0:T(8,128)(2,1)S(1)} %get-tuple-element.51), channel_id=1, source_target_pairs={{0,126},{1,127},{2,64},{3,65},{4,66},{5,67},{6,68},{7,69},{8,70},{... | collective-permute-start | bytes 786440 | tf_op jit(solution)/shard_map/ppermute | solution.py:40
  96.0 1.5 %shard_map.118 = (bf16[128,1024]{1,0:T(8,128)(2,1)S(1)}, bf16[128,1024]{1,0:T(8,128)(2,1)S(1)}) custom-call(bf16[1024,256]{1,0:T(8,128)(2,1)S(1)} %get-tuple-element.46.r_0_, bf16[256,2048]{1,0:T(8,128)(2,1)S(1)} %get-tuple-element.47.r_1_, bf16[512,2048]{1,0:T(8,128)(2,1)S(1)} %get-tuple-element.48.r_2_, bf16[1024,2048]{1,0:T(8,128)(2,1)S(1)} %copy-done), custom_call_target="tpu_custom_call" | custom-call | flops 1342177280 | bytes 1048576 | tf_op jit(solution)/shard_map/pallas_call | solution.py:22
  97.5 5.0 %collective-permute-start.19 = (bf16[128,1024]{1,0:T(8,128)(2,1)S(1)}, bf16[128,1024]{1,0:T(8,128)(2,1)S(1)}, u32[]{:S(2)}, u32[]{:S(2)}) collective-permute-start(bf16[128,1024]{1,0:T(8,128)(2,1)S(1)} %get-tuple-element.52), channel_id=1, source_target_pairs={{0,125},{1,126},{2,127},{3,64},{4,65},{5,66},{6,67},{7,68},{8,69},... | collective-permute-start | bytes 786440 | tf_op jit(solution)/shard_map/ppermute | solution.py:40
  102.5 3.9 %collective-permute-done.23.r_10_ = bf16[128,1024]{1,0:T(8,128)(2,1)S(1)} collective-permute-done((bf16[128,1024]{1,0:T(8,128)(2,1)S(1)}, bf16[128,1024]{1,0:T(8,128)(2,1)S(1)}, u32[]{:S(2)}, u32[]{:S(2)}) %collective-permute-start.23) | collective-permute-done | bytes 262176 | tf_op jit(solution)/shard_map/ppermute | solution.py:40
  106.5 14.1 %collective-permute-done.20.r_7_ = bf16[128,1024]{1,0:T(8,128)(2,1)S(1)} collective-permute-done((bf16[128,1024]{1,0:T(8,128)(2,1)S(1)}, bf16[128,1024]{1,0:T(8,128)(2,1)S(1)}, u32[]{:S(2)}, u32[]{:S(2)}) %collective-permute-start.20) | collective-permute-done | bytes 262176 | tf_op jit(solution)/shard_map/ppermute | solution.py:40
  120.6 1.0 collective-permute-start.17
  121.6 9.4 %collective-permute-done.17.r_4_ = bf16[128,1024]{1,0:T(8,128)(2,1)S(1)} collective-permute-done((bf16[128,1024]{1,0:T(8,128)(2,1)S(1)}, bf16[128,1024]{1,0:T(8,128)(2,1)S(1)}, u32[]{:S(2)}, u32[]{:S(2)}) %collective-permute-start.17) | collective-permute-done | bytes 262176 | tf_op jit(solution)/shard_map/ppermute | solution.py:40
  131.0 1.9 %shard_map.122 = bf16[256,1024]{1,0:T(8,128)(2,1)} custom-call(s32[1]{0:T(128)} %bitcast.24.r_0_, s32[8]{0:T(128)S(1)} %concatenate.3.r_1_, f32[256,1024]{1,0:T(8,128)S(1)} %get-tuple-element.45.r_2_, bf16[128,1024]{1,0:T(8,128)(2,1)S(1)} %collective-permute-done.16.r_3_, bf16[128,1024]{1,0:T(8,128)(2,1)S(1)} %collective-permute-done.17.r_4_, ...), custom_call_target="tpu_custom_call" | custom-call | bytes 1048576 | tf_op jit(solution)/shard_map/pallas_call | solution.py:22
  (59 shorter events, 9.5 us)
Async XLA Ops:
  1.3 16.0 %collective-permute-start.7 = (s32[1,128]{1,0:T(1,128)S(1)}, s32[1,128]{1,0:T(1,128)S(1)}, u32[]{:S(2)}, u32[]{:S(2)}) collective-permute-start(s32[1,128]{1,0:T(1,128)S(1)} %pad_bitcast_fusion), channel_id=1, source_target_pairs={{0,121},{1,122},{2,123},{3,124},{4,125},{5,126},{6,127},{7,64},{8,... | collective-permute-start | bytes 1544 | tf_op jit(solution)/shard_map/ppermute | solution.py:40
  8.0 10.1 %collective-permute-start.6 = (s32[1,128]{1,0:T(1,128)S(1)}, s32[1,128]{1,0:T(1,128)S(1)}, u32[]{:S(2)}, u32[]{:S(2)}) collective-permute-start(s32[1,128]{1,0:T(1,128)S(1)} %pad_bitcast_fusion), channel_id=1, source_target_pairs={{0,122},{1,123},{2,124},{3,125},{4,126},{5,127},{6,64},{7,65},{8,6... | collective-permute-start | bytes 1544 | tf_op jit(solution)/shard_map/ppermute | solution.py:40
  10.5 8.0 %collective-permute-start.5 = (s32[1,128]{1,0:T(1,128)S(1)}, s32[1,128]{1,0:T(1,128)S(1)}, u32[]{:S(2)}, u32[]{:S(2)}) collective-permute-start(s32[1,128]{1,0:T(1,128)S(1)} %pad_bitcast_fusion), channel_id=1, source_target_pairs={{0,123},{1,124},{2,125},{3,126},{4,127},{5,64},{6,65},{7,66},{8,67... | collective-permute-start | bytes 1544 | tf_op jit(solution)/shard_map/ppermute | solution.py:40
  10.5 9.7 %collective-permute-start.4 = (s32[1,128]{1,0:T(1,128)S(1)}, s32[1,128]{1,0:T(1,128)S(1)}, u32[]{:S(2)}, u32[]{:S(2)}) collective-permute-start(s32[1,128]{1,0:T(1,128)S(1)} %pad_bitcast_fusion), channel_id=1, source_target_pairs={{0,124},{1,125},{2,126},{3,127},{4,64},{5,65},{6,66},{7,67},{8,68}... | collective-permute-start | bytes 1544 | tf_op jit(solution)/shard_map/ppermute | solution.py:40
  11.7 9.1 %collective-permute-start.3 = (s32[1,128]{1,0:T(1,128)S(1)}, s32[1,128]{1,0:T(1,128)S(1)}, u32[]{:S(2)}, u32[]{:S(2)}) collective-permute-start(s32[1,128]{1,0:T(1,128)S(1)} %pad_bitcast_fusion), channel_id=1, source_target_pairs={{0,125},{1,126},{2,127},{3,64},{4,65},{5,66},{6,67},{7,68},{8,69},... | collective-permute-start | bytes 1544 | tf_op jit(solution)/shard_map/ppermute | solution.py:40
  17.4 5.4 %collective-permute-start.2 = (s32[1,128]{1,0:T(1,128)S(1)}, s32[1,128]{1,0:T(1,128)S(1)}, u32[]{:S(2)}, u32[]{:S(2)}) collective-permute-start(s32[1,128]{1,0:T(1,128)S(1)} %pad_bitcast_fusion), channel_id=1, source_target_pairs={{0,126},{1,127},{2,64},{3,65},{4,66},{5,67},{6,68},{7,69},{8,70},{... | collective-permute-start | bytes 1544 | tf_op jit(solution)/shard_map/ppermute | solution.py:40
  18.1 5.3 %collective-permute-start.1 = (s32[1,128]{1,0:T(1,128)S(1)}, s32[1,128]{1,0:T(1,128)S(1)}, u32[]{:S(2)}, u32[]{:S(2)}) collective-permute-start(s32[1,128]{1,0:T(1,128)S(1)} %pad_bitcast_fusion), channel_id=1, source_target_pairs={{0,127},{1,64},{2,65},{3,66},{4,67},{5,68},{6,69},{7,70},{8,71},{9... | collective-permute-start | bytes 1544 | tf_op jit(solution)/shard_map/ppermute | solution.py:40
  18.5 5.4 %collective-permute-start = (s32[1,128]{1,0:T(1,128)S(1)}, s32[1,128]{1,0:T(1,128)S(1)}, u32[]{:S(2)}, u32[]{:S(2)}) collective-permute-start(s32[1,128]{1,0:T(1,128)S(1)} %pad_bitcast_fusion), channel_id=1, source_target_pairs={{0,64},{1,65},{2,66},{3,67},{4,68},{5,69},{6,70},{7,71},{8,72},{9,... | collective-permute-start | bytes 1544 | tf_op jit(solution)/shard_map/ppermute | solution.py:40
  28.5 1.0 copy-start.5
  30.4 5.0 %collective-permute-start.12 = (bf16[128,1024]{1,0:T(8,128)(2,1)S(1)}, bf16[128,1024]{1,0:T(8,128)(2,1)S(1)}, u32[]{:S(2)}, u32[]{:S(2)}) collective-permute-start(bf16[128,1024]{1,0:T(8,128)(2,1)S(1)} %get-tuple-element.35), channel_id=1, source_target_pairs={{0,64},{1,65},{2,66},{3,67},{4,68},{5,69},{6,70},{7,71},{8,72},{9,... | collective-permute-start | bytes 786440 | tf_op jit(solution)/shard_map/ppermute | solution.py:40
  30.5 11.1 %collective-permute-start.13 = (bf16[128,1024]{1,0:T(8,128)(2,1)S(1)}, bf16[128,1024]{1,0:T(8,128)(2,1)S(1)}, u32[]{:S(2)}, u32[]{:S(2)}) collective-permute-start(bf16[128,1024]{1,0:T(8,128)(2,1)S(1)} %get-tuple-element.36), channel_id=1, source_target_pairs={{0,65},{1,66},{2,67},{3,68},{4,69},{5,70},{6,71},{7,72},{8,73},{9,... | collective-permute-start | bytes 786440 | tf_op jit(solution)/shard_map/ppermute | solution.py:40
  32.6 10.4 %collective-permute-start.14 = (bf16[128,1024]{1,0:T(8,128)(2,1)S(1)}, bf16[128,1024]{1,0:T(8,128)(2,1)S(1)}, u32[]{:S(2)}, u32[]{:S(2)}) collective-permute-start(bf16[128,1024]{1,0:T(8,128)(2,1)S(1)} %get-tuple-element.37), channel_id=1, source_target_pairs={{0,66},{1,67},{2,68},{3,69},{4,70},{5,71},{6,72},{7,73},{8,74},{9,... | collective-permute-start | bytes 786440 | tf_op jit(solution)/shard_map/ppermute | solution.py:40
  34.6 29.3 %collective-permute-start.15 = (bf16[128,1024]{1,0:T(8,128)(2,1)S(1)}, bf16[128,1024]{1,0:T(8,128)(2,1)S(1)}, u32[]{:S(2)}, u32[]{:S(2)}) collective-permute-start(bf16[128,1024]{1,0:T(8,128)(2,1)S(1)} %get-tuple-element.38), channel_id=1, source_target_pairs={{0,67},{1,68},{2,69},{3,70},{4,71},{5,72},{6,73},{7,74},{8,75},{9,... | collective-permute-start | bytes 786440 | tf_op jit(solution)/shard_map/ppermute | solution.py:40
  35.4 32.8 %collective-permute-start.8 = (bf16[128,1024]{1,0:T(8,128)(2,1)S(1)}, bf16[128,1024]{1,0:T(8,128)(2,1)S(1)}, u32[]{:S(2)}, u32[]{:S(2)}) collective-permute-start(bf16[128,1024]{1,0:T(8,128)(2,1)S(1)} %get-tuple-element.30), channel_id=1, source_target_pairs={{0,68},{1,69},{2,70},{3,71},{4,72},{5,73},{6,74},{7,75},{8,76},{9,... | collective-permute-start | bytes 786440 | tf_op jit(solution)/shard_map/ppermute | solution.py:40
  35.4 32.8 %collective-permute-start.9 = (bf16[128,1024]{1,0:T(8,128)(2,1)S(1)}, bf16[128,1024]{1,0:T(8,128)(2,1)S(1)}, u32[]{:S(2)}, u32[]{:S(2)}) collective-permute-start(bf16[128,1024]{1,0:T(8,128)(2,1)S(1)} %get-tuple-element.31), channel_id=1, source_target_pairs={{0,69},{1,70},{2,71},{3,72},{4,73},{5,74},{6,75},{7,76},{8,77},{9,... | collective-permute-start | bytes 786440 | tf_op jit(solution)/shard_map/ppermute | solution.py:40
  41.6 26.5 %collective-permute-start.10 = (bf16[128,1024]{1,0:T(8,128)(2,1)S(1)}, bf16[128,1024]{1,0:T(8,128)(2,1)S(1)}, u32[]{:S(2)}, u32[]{:S(2)}) collective-permute-start(bf16[128,1024]{1,0:T(8,128)(2,1)S(1)} %get-tuple-element.32), channel_id=1, source_target_pairs={{0,70},{1,71},{2,72},{3,73},{4,74},{5,75},{6,76},{7,77},{8,78},{9,... | collective-permute-start | bytes 786440 | tf_op jit(solution)/shard_map/ppermute | solution.py:40
  43.0 25.2 %collective-permute-start.11 = (bf16[128,1024]{1,0:T(8,128)(2,1)S(1)}, bf16[128,1024]{1,0:T(8,128)(2,1)S(1)}, u32[]{:S(2)}, u32[]{:S(2)}) collective-permute-start(bf16[128,1024]{1,0:T(8,128)(2,1)S(1)} %get-tuple-element.33), channel_id=1, source_target_pairs={{0,71},{1,72},{2,73},{3,74},{4,75},{5,76},{6,77},{7,78},{8,79},{9,... | collective-permute-start | bytes 786440 | tf_op jit(solution)/shard_map/ppermute | solution.py:40
  58.3 1.6 %copy-start.1 = (bf16[1024,1024]{1,0:T(8,128)(2,1)S(1)}, bf16[1024,1024]{1,0:T(8,128)(2,1)}, u32[]{:S(2)}) copy-start(bf16[1024,1024]{1,0:T(8,128)(2,1)} %sw_ref.1) | copy-start | bytes 6291460
  59.9 1.6 %copy-start.4 = (s32[1,256,2048]{2,1,0:T(8,128)S(1)}, s32[1,256,2048]{2,1,0:T(8,128)}, u32[]{:S(2)}) copy-start(s32[1,256,2048]{2,1,0:T(8,128)} %param.13) | copy-start | bytes 6291460
  62.5 2.2 %copy-start = (bf16[1024,2048]{1,0:T(8,128)(2,1)S(1)}, bf16[1024,2048]{1,0:T(8,128)(2,1)}, u32[]{:S(2)}) copy-start(bf16[1024,2048]{1,0:T(8,128)(2,1)} %r_3_.9) | copy-start | bytes 12582916
  68.2 3.4 %copy-start.2 = (bf16[1024,1024]{1,0:T(8,128)(2,1)S(1)}, bf16[1024,1024]{1,0:T(8,128)(2,1)}, u32[]{:S(2)}) copy-start(bf16[1024,1024]{1,0:T(8,128)(2,1)} %sw_ref.1) | copy-start | bytes 6291460
  68.2 3.4 %copy-start.3 = (bf16[2048,1024]{1,0:T(8,128)(2,1)S(1)}, bf16[2048,1024]{1,0:T(8,128)(2,1)}, u32[]{:S(2)}) copy-start(bf16[2048,1024]{1,0:T(8,128)(2,1)} %nb_ref.1) | copy-start | bytes 12582916
  68.2 3.4 %copy-start.7 = (bf16[1,256,1024]{2,1,0:T(8,128)(2,1)S(1)}, bf16[1,256,1024]{2,1,0:T(8,128)(2,1)}, u32[]{:S(2)}) copy-start(bf16[1,256,1024]{2,1,0:T(8,128)(2,1)} %param.14) | copy-start | bytes 1572868
  68.2 3.4 %copy-start.8 = (f32[1024]{0:T(1024)S(1)}, f32[1024]{0:T(1024)}, u32[]{:S(2)}) copy-start(f32[1024]{0:T(1024)} %param.19) | copy-start | bytes 12292
  77.2 20.3 %collective-permute-start.22 = (bf16[128,1024]{1,0:T(8,128)(2,1)S(1)}, bf16[128,1024]{1,0:T(8,128)(2,1)S(1)}, u32[]{:S(2)}, u32[]{:S(2)}) collective-permute-start(bf16[128,1024]{1,0:T(8,128)(2,1)S(1)} %get-tuple-element.56), channel_id=1, source_target_pairs={{0,122},{1,123},{2,124},{3,125},{4,126},{5,127},{6,64},{7,65},{8,6... | collective-permute-start | bytes 786440 | tf_op jit(solution)/shard_map/ppermute | solution.py:40
  84.2 22.2 %collective-permute-start.23 = (bf16[128,1024]{1,0:T(8,128)(2,1)S(1)}, bf16[128,1024]{1,0:T(8,128)(2,1)S(1)}, u32[]{:S(2)}, u32[]{:S(2)}) collective-permute-start(bf16[128,1024]{1,0:T(8,128)(2,1)S(1)} %get-tuple-element.57), channel_id=1, source_target_pairs={{0,121},{1,122},{2,123},{3,124},{4,125},{5,126},{6,127},{7,64},{8,... | collective-permute-start | bytes 786440 | tf_op jit(solution)/shard_map/ppermute | solution.py:40
  89.3 31.3 %collective-permute-start.20 = (bf16[128,1024]{1,0:T(8,128)(2,1)S(1)}, bf16[128,1024]{1,0:T(8,128)(2,1)S(1)}, u32[]{:S(2)}, u32[]{:S(2)}) collective-permute-start(bf16[128,1024]{1,0:T(8,128)(2,1)S(1)} %get-tuple-element.54), channel_id=1, source_target_pairs={{0,124},{1,125},{2,126},{3,127},{4,64},{5,65},{6,66},{7,67},{8,68}... | collective-permute-start | bytes 786440 | tf_op jit(solution)/shard_map/ppermute | solution.py:40
  89.4 32.2 %collective-permute-start.21 = (bf16[128,1024]{1,0:T(8,128)(2,1)S(1)}, bf16[128,1024]{1,0:T(8,128)(2,1)S(1)}, u32[]{:S(2)}, u32[]{:S(2)}) collective-permute-start(bf16[128,1024]{1,0:T(8,128)(2,1)S(1)} %get-tuple-element.55), channel_id=1, source_target_pairs={{0,123},{1,124},{2,125},{3,126},{4,127},{5,64},{6,65},{7,66},{8,67... | collective-permute-start | bytes 786440 | tf_op jit(solution)/shard_map/ppermute | solution.py:40
  91.5 30.1 %collective-permute-start.18 = (bf16[128,1024]{1,0:T(8,128)(2,1)S(1)}, bf16[128,1024]{1,0:T(8,128)(2,1)S(1)}, u32[]{:S(2)}, u32[]{:S(2)}) collective-permute-start(bf16[128,1024]{1,0:T(8,128)(2,1)S(1)} %get-tuple-element.51), channel_id=1, source_target_pairs={{0,126},{1,127},{2,64},{3,65},{4,66},{5,67},{6,68},{7,69},{8,70},{... | collective-permute-start | bytes 786440 | tf_op jit(solution)/shard_map/ppermute | solution.py:40
  97.5 24.1 %collective-permute-start.19 = (bf16[128,1024]{1,0:T(8,128)(2,1)S(1)}, bf16[128,1024]{1,0:T(8,128)(2,1)S(1)}, u32[]{:S(2)}, u32[]{:S(2)}) collective-permute-start(bf16[128,1024]{1,0:T(8,128)(2,1)S(1)} %get-tuple-element.52), channel_id=1, source_target_pairs={{0,125},{1,126},{2,127},{3,64},{4,65},{5,66},{6,67},{7,68},{8,69},... | collective-permute-start | bytes 786440 | tf_op jit(solution)/shard_map/ppermute | solution.py:40
  106.4 15.2 %collective-permute-start.16 = (bf16[128,1024]{1,0:T(8,128)(2,1)S(1)}, bf16[128,1024]{1,0:T(8,128)(2,1)S(1)}, u32[]{:S(2)}, u32[]{:S(2)}) collective-permute-start(bf16[128,1024]{1,0:T(8,128)(2,1)S(1)} %get-tuple-element.49), channel_id=1, source_target_pairs={{0,64},{1,65},{2,66},{3,67},{4,68},{5,69},{6,70},{7,71},{8,72},{9,... | collective-permute-start | bytes 786440 | tf_op jit(solution)/shard_map/ppermute | solution.py:40
  120.6 10.4 %collective-permute-start.17 = (bf16[128,1024]{1,0:T(8,128)(2,1)S(1)}, bf16[128,1024]{1,0:T(8,128)(2,1)S(1)}, u32[]{:S(2)}, u32[]{:S(2)}) collective-permute-start(bf16[128,1024]{1,0:T(8,128)(2,1)S(1)} %get-tuple-element.50), channel_id=1, source_target_pairs={{0,127},{1,64},{2,65},{3,66},{4,67},{5,68},{6,69},{7,70},{8,71},{9... | collective-permute-start | bytes 786440 | tf_op jit(solution)/shard_map/ppermute | solution.py:40
  (2 other events, 1.9 us)

commit v2 on v1

--- a/solution.py
+++ b/solution.py
@@ -8,6 +8,7 @@
 EPS = 1e-06
 DEAD = 16384.0
 LIMIT = 8192.0
+LINE = 4
 F32 = jnp.float32
 BF16 = jnp.bfloat16
 VMEM = pl.BlockSpec(memory_space=pltpu.VMEM)
@@ -30,7 +31,7 @@
     )(*ins)
 
 
-def route(x, shift):
+def swap_rows(x, shift):
     count = lax.axis_size("dom")
     pairs = [
         (s * count + j, (1 - s) * count + (j + shift) % count)
@@ -40,34 +41,78 @@
     return lax.ppermute(x, ("side", "dom"), pairs)
 
 
-def pick_kernel(block, live_ref, wanted_ref, x_ref, *outs):
-    live = live_ref[0]
-    for o, out in enumerate(outs):
-        start = wanted_ref[o] * block
-        row = lax.broadcasted_iota(jnp.int32, (block, 1), 0) + start
-        x = x_ref[pl.ds(pl.multiple_of(start, block), block), :].astype(F32)
-        out[...] = jnp.where(row < live, x, DEAD).astype(BF16)
-
-
-def tiles_kernel(block, lists_ref, counts_ref, x_ref, sw_ref, tiles_ref, tiles_t_ref, self_ref):
-    reach = tiles_ref.shape[1] // block
-    for o in range(reach):
-        first = counts_ref[:, o * 2 * block : (o * 2 + 1) * block]
-        second = counts_ref[:, (o * 2 + 1) * block : (o * 2 + 2) * block]
-        tile = (first * lists_ref[o, 0] + second * lists_ref[o, 1]).astype(F32)
-        tiles_ref[:, o * block : (o + 1) * block] = tile.astype(BF16)
-        tiles_t_ref[o * block : (o + 1) * block, :] = tile.T.astype(BF16)
+def along(x, d):
+    count = lax.axis_size("dom")
+    pairs = [(j, j // LINE * LINE + (j + d) % LINE) for j in range(count)]
+    return lax.ppermute(x, "dom", pairs)
+
+
+def near(p, d):
+    return jnp.where(p >= d, d + LINE, d)
+
+
+def far(p, d):
+    return jnp.where(p >= d, d, d + LINE)
+
+
+def at_block(index, block):
+    return pl.ds(pl.multiple_of(index * block, block), block)
+
+
+def pick_near_kernel(block, place_ref, m1, m2, m3, below_ref, *outs):
+    for d, (meta, out) in enumerate(zip((m1, m2, m3), outs), 1):
+        p = lax.rem(place_ref[0] + d, LINE)
+        out[...] = below_ref[at_block(meta[0, near(p, d)], block), :]
+
+
+def pick_far_kernel(block, place_ref, m1, m2, m3, same_ref, below_ref, *outs):
+    for d, (meta, out) in enumerate(zip((m1, m2, m3), outs), 1):
+        p = lax.rem(place_ref[0] + d, LINE)
+        at = at_block(meta[0, far(p, d)], block)
+
+        @pl.when(p >= d)
+        def _():
+            out[...] = same_ref[at, :]
+
+        @pl.when(p < d)
+        def _():
+            out[...] = below_ref[at, :]
+
+
+def slots(p):
+    return [0, LINE] + [near(p, d) for d in range(1, LINE)] + [far(p, d) for d in range(1, LINE)]
+
+
+def tiles_kernel(block, place_ref, lists_ref, counts_ref, x_ref, sw_ref, tiles_ref, tiles_t_ref, self_ref):
+    for i, o in enumerate(slots(place_ref[0])):
+        first, second = lists_ref[o, 0], lists_ref[o, 1]
+        at = pl.ds(pl.multiple_of((o * 2 + second) * block, block), block)
+        tile = (counts_ref[:, at] * (first + second)).astype(F32)
+        tiles_ref[:, i * block : (i + 1) * block] = tile.astype(BF16)
+        tiles_t_ref[i * block : (i + 1) * block, :] = tile.T.astype(BF16)
     self_ref[...] = dot(x_ref[...], sw_ref[...])
 
 
 def message_kernel(block, first, last, *refs):
-    size = len(range(first, last))
-    blocks = refs[:size]
-    q_ref, qb_ref, tiles_ref, acc_in, deg_in, msg_ref, acc_ref, deg_ref = refs[size:]
-    x = jnp.concatenate([b[...] for b in blocks], axis=0)
+    size = last - first
+    if first == 0:
+        lists_ref, same_ref, below_ref = refs[:3]
+        held = [same_ref[at_block(lists_ref[0, 1], block), :]]
+        held += [below_ref[at_block(lists_ref[LINE, 1], block), :]]
+        refs = refs[3:]
+        held += [b[...] for b in refs[: size - 2]]
+        refs = refs[size - 2 :]
+    else:
+        held = [b[...] for b in refs[:size]]
+        refs = refs[size:]
+    q_ref, qb_ref, tiles_ref = refs[:3]
+    acc_in, deg_in = refs[3:5] if first else (None, None)
+    msg_ref, acc_ref, deg_ref = refs[-3:]
+    x = jnp.concatenate(held, axis=0)
     keep = x[:, :128].astype(F32) < LIMIT
     tiles = tiles_ref[:, first * block : last * block]
-    deg_ref[...] = deg_in[...] + dot(tiles, jnp.where(keep, 1.0, 0.0).astype(BF16))
+    deg = dot(tiles, jnp.where(keep, 1.0, 0.0).astype(BF16))
+    deg_ref[...] = deg + deg_in[...] if first else deg
     keep = keep[:, :1]
     hidden = q_ref.shape[1]
     step = 512
@@ -76,7 +121,8 @@
         pre = dot(x, q_ref[:, cols]) + qb_ref[:, cols]
         msg = jnp.where(keep, jnp.maximum(pre, 0.0), 0.0).astype(BF16)
         msg_ref[:, cols] = msg
-        acc_ref[:, cols] = acc_in[:, cols] + dot(tiles, msg)
+        acc = dot(tiles, msg)
+        acc_ref[:, cols] = acc + acc_in[:, cols] if first else acc
 
 
 def layer_kernel(
@@ -127,14 +173,39 @@
             out[:, cols] = part[i * block : (i + 1) * block]
 
 
-def finish_kernel(block, live_ref, wanted_ref, gself_ref, *refs):
-    parts, (out_ref, sum_ref) = refs[:-2], refs[-2:]
-    sum_ref[...] = gself_ref[...]
-    for o, part in enumerate(parts):
-        at = pl.ds(pl.multiple_of(wanted_ref[o] * block, block), block)
-        sum_ref[at, :] += part[...].astype(F32)
-    keep = lax.broadcasted_iota(jnp.int32, (sum_ref.shape[0], 1), 0) < live_ref[0]
-    out_ref[...] = jnp.where(keep, sum_ref[...], 0.0).astype(BF16)
+def sum_far_kernel(block, place_ref, lists_ref, m1, m2, m3, own_ref, c1, c2, c3, same_ref, below_ref, same, below):
+    same[...] = jnp.zeros_like(same)
+    below[...] = jnp.zeros_like(below)
+    same[at_block(lists_ref[0, 1], block), :] = own_ref[...].astype(F32)
+    for d, (meta, part) in enumerate(zip((m1, m2, m3), (c1, c2, c3)), 1):
+        p = lax.rem(place_ref[0] + d, LINE)
+        at = at_block(meta[0, far(p, d)], block)
+
+        @pl.when(p >= d)
+        def _():
+            same[at, :] += part[...].astype(F32)
+
+        @pl.when(p < d)
+        def _():
+            below[at, :] += part[...].astype(F32)
+
+    same_ref[...] = same[...].astype(BF16)
+    below_ref[...] = below[...].astype(BF16)
+
+
+def sum_near_kernel(block, place_ref, lists_ref, m1, m2, m3, own_ref, d1, d2, d3, out_ref, total):
+    total[...] = jnp.zeros_like(total)
+    total[at_block(lists_ref[LINE, 1], block), :] = own_ref[...].astype(F32)
+    for d, (meta, part) in enumerate(zip((m1, m2, m3), (d1, d2, d3)), 1):
+        p = lax.rem(place_ref[0] + d, LINE)
+        total[at_block(meta[0, near(p, d)], block), :] += part[...].astype(F32)
+    out_ref[...] = total[...].astype(BF16)
+
+
+def finish_kernel(live_ref, gself_ref, a_ref, b_ref, c_ref, out_ref):
+    total = gself_ref[...] + a_ref[...].astype(F32) + b_ref[...].astype(F32) + c_ref[...].astype(F32)
+    keep = lax.broadcasted_iota(jnp.int32, (total.shape[0], 1), 0) < live_ref[0]
+    out_ref[...] = jnp.where(keep, total, 0.0).astype(BF16)
 
 
 def local(x, live, listed, counts, cotangent, q, qb, sw, nb, ob):
@@ -145,36 +216,50 @@
     reach, block_count = lists.shape
     block = rows // block_count
     qb, ob = qb[None], ob[None]
-    second = lists[:, 1]
-    row = jnp.pad(second, (0, 128 - reach))[None]
-    wanted = jnp.concatenate([route(row, -o)[0, o : o + 1] for o in range(reach)])
-    sent = call(
-        lambda *r: pick_kernel(block, *r),
-        [((block, width), BF16)] * reach,
-        (live, wanted, x),
-        [SMEM, SMEM, VMEM],
-    )
-    got = [route(b, o) for o, b in enumerate(sent)]
+    place = (lax.axis_index("dom") % LINE).astype(jnp.int32).reshape(1)
+    keep = lax.broadcasted_iota(jnp.int32, (rows, 1), 0) < live[0]
+    marked = jnp.where(keep, x, jnp.asarray(DEAD, BF16))
+    row = jnp.pad(lists[:, 1], (0, 128 - reach))[None]
+    below = swap_rows(marked, LINE)
+    same = swap_rows(marked, 0)
+    metas = [along(row, -d) for d in range(1, LINE)]
+    below2 = swap_rows(marked, 2 * LINE)
+    one = ((block, width), BF16)
+    three = [SMEM] * 4
+    picked = call(
+        lambda *r: pick_near_kernel(block, *r), [one] * 3, (place, *metas, below), three + [VMEM]
+    )
+    got_near = [along(b, d) for d, b in enumerate(picked, 1)]
+    picked = call(
+        lambda *r: pick_far_kernel(block, *r),
+        [one] * 3,
+        (place, *metas, same, below2),
+        three + [VMEM] * 2,
+    )
+    got_far = [along(b, d) for d, b in enumerate(picked, 1)]
     tiles, tiles_t, self_pre = call(
         lambda *r: tiles_kernel(block, *r),
         [((rows, reach * block), BF16), ((reach * block, rows), BF16), ((rows, width), F32)],
-        (lists, counts, x, sw),
-        [SMEM] + [VMEM] * 3,
+        (place, lists, counts, x, sw),
+        [SMEM] * 2 + [VMEM] * 3,
         flops=2 * rows * width * width,
     )
-    acc = jnp.zeros((rows, hidden), F32)
-    deg = jnp.zeros((rows, 128), F32)
-    messages = {}
-    for first, last in ((0, 4), (4, 8)):
+    split = 2 + LINE - 1
+
+    def message(first, last, ins, specs):
         size = last - first
-        msg, acc, deg = call(
-            lambda *r, f=first, l=last: message_kernel(block, f, l, *r),
+        return call(
+            lambda *r: message_kernel(block, first, last, *r),
             [((size * block, hidden), BF16), ((rows, hidden), F32), ((rows, 128), F32)],
-            (*got[first:last], q, qb, tiles, acc, deg),
+            ins,
+            specs,
             flops=2 * size * block * hidden * (width + rows),
         )
-        for o in range(first, last):
-            messages[o] = (msg, o - first)
+
+    msg_a, acc, deg = message(
+        0, split, (lists, same, below, *got_near, q, qb, tiles), [SMEM] + [VMEM] * 8
+    )
+    msg_b, acc, deg = message(split, reach, (*got_far, q, qb, tiles, acc, deg), [VMEM] * 8)
     emb, gself, gpool = call(
         layer_kernel,
         [((rows, width), BF16), ((rows, width), F32), ((rows, hidden), BF16)],
@@ -183,25 +268,41 @@
         scratch=[pltpu.VMEM((rows, width), F32)],
         flops=2 * rows * width * (2 * hidden + width),
     )
-    back = [None] * reach
-    for first, last in ((6, 8), (4, 6), (2, 4), (0, 2)):
+
+    def back(first, last, msg, skip):
         size = last - first
-        msg, skip = messages[first]
-        parts = call(
-            lambda *r, f=first, l=last, k=skip: back_kernel(block, f, l, k, *r),
-            [((block, width), BF16)] * size,
+        return call(
+            lambda *r: back_kernel(block, first, last, skip, *r),
+            [one] * size,
             (tiles_t, gpool, msg, q),
             scratch=[pltpu.VMEM((size * block, hidden), BF16)],
             flops=2 * size * block * hidden * (width + rows),
         )
-        for i, part in enumerate(parts):
-            back[first + i] = route(part, -(first + i))
+
+    back_far = [along(b, -d) for d, b in enumerate(back(split, reach, msg_b, 0), 1)]
+    back_near = [along(b, -d) for d, b in enumerate(back(2, split, msg_a, 2), 1)]
+    own_same, own_below = back(0, 2, msg_a, 0)
+    two = ((rows, width), BF16)
+    total = pltpu.VMEM((rows, width), F32)
+    sum_same, sum_below2 = call(
+        lambda *r: sum_far_kernel(block, *r),
+        [two, two],
+        (place, lists, *metas, own_same, *back_far),
+        [SMEM] * 5 + [VMEM] * 4,
+        scratch=[total, total],
+    )
+    g_below2 = swap_rows(sum_below2, -2 * LINE)
+    g_same = swap_rows(sum_same, 0)
+    (sum_below,) = call(
+        lambda *r: sum_near_kernel(block, *r),
+        [two],
+        (place, lists, *metas, own_below, *back_near),
+        [SMEM] * 5 + [VMEM] * 4,
+        scratch=[total],
+    )
+    g_below = swap_rows(sum_below, -LINE)
     (grad,) = call(
-        lambda *r: finish_kernel(block, *r),
-        [((rows, width), BF16)],
-        (live, wanted, gself, *back),
-        [SMEM, SMEM] + [VMEM] * (1 + reach),
-        scratch=[pltpu.VMEM((rows, width), F32)],
+        finish_kernel, [two], (live, gself, g_same, g_below, g_below2), [SMEM] + [VMEM] * 4
     )
     return emb[None], grad[None]
 

time: 134 us -> 109 us (0.81)
  the two profiles are of different devices: /device:TPU:7 before, /device:TPU:1 now
where the time goes in v2:
time: 109 us; the launch traced here: 108 us
  waiting for transfers between devices  40.9 us (38%)
  starting transfers between devices  35.3 us (32%)
  Pallas kernels  23.2 us (21%)
  local copies, waits for them, and re-layouts  5.69 us (5%)
  other arithmetic  1.96 us (2%)
  between operations  1.46 us (1%)
    pallas_call x12, Pallas kernels, call(): pl.pallas_call(kernel, out_shape=[jax.ShapeDtypeStruct(s, d) for s, d in...  23.2 us
    ppermute x15, starting transfers between devices, along(): return lax.ppermute(x, 'dom', pairs)  22.2 us
    ppermute x6, waiting for transfers between devices, swap_rows(): return lax.ppermute(x, ('side', 'dom'), pairs)  20.6 us
    ppermute x15, waiting for transfers between devices, along(): return lax.ppermute(x, 'dom', pairs)  20.2 us
    ppermute x6, starting transfers between devices, swap_rows(): return lax.ppermute(x, ('side', 'dom'), pairs)  13 us
    unnamed x18, local copies, waits for them, and re-layouts  4.25 us
  transfers between devices with their start and end apart: 21, of which 12 were waited for; matrix products, arithmetic and copies ran while one was open for 1% of the time, Pallas kernels for 12%

profile of v2, /device:TPU:1, one launch (start us, length us, event | category | flops | bytes accessed | tf_op | source)
XLA Modules:
  0.0 108.4 jit_solution(14506289395096304543)
XLA Ops:
  1.3 2.0 %broadcast_select_fusion = bf16[256,1024]{1,0:T(8,128)(2,1)} fusion(pred[256]{0:T(512)(128)(4,1)S(1)} %iota_compare_fusion, bf16[1,256,1024]{2,1,0:T(8,128)(2,1)} %param.10), kind=kLoop, calls=%fused_computation | loop fusion | flops 262144 | bytes 1048832 | tf_op jit(solution)/shard_map/jit(_where)/select_n | solution.py:221
  3.2 2.7 %collective-permute-start.8 = (bf16[256,1024]{1,0:T(8,128)(2,1)}, bf16[256,1024]{1,0:T(8,128)(2,1)S(1)}, u32[]{:S(2)}, u32[]{:S(2)}) collective-permute-start(bf16[256,1024]{1,0:T(8,128)(2,1)} %broadcast_select_fusion), channel_id=1, source_target_pairs={{0,68},{1,69},{2,70},{3,71},{4,72},{5,73},{6,74},{7,75},{8,76},{9,... | collective-permute-start | bytes 1572872 | tf_op jit(solution)/shard_map/ppermute | solution.py:41
  5.9 2.3 %collective-permute-start.4 = (bf16[256,1024]{1,0:T(8,128)(2,1)}, bf16[256,1024]{1,0:T(8,128)(2,1)S(1)}, u32[]{:S(2)}, u32[]{:S(2)}) collective-permute-start(bf16[256,1024]{1,0:T(8,128)(2,1)} %broadcast_select_fusion), channel_id=1, source_target_pairs={{0,72},{1,73},{2,74},{3,75},{4,76},{5,77},{6,78},{7,79},{8,80},{9,... | collective-permute-start | bytes 1572872 | tf_op jit(solution)/shard_map/ppermute | solution.py:41
  9.6 1.2 %collective-permute-start.2 = (s32[1,128]{1,0:T(1,128)S(1)}, s32[1,128]{1,0:T(1,128)S(1)}, u32[]{:S(2)}, u32[]{:S(2)}) collective-permute-start(s32[1,128]{1,0:T(1,128)S(1)} %pad_bitcast_fusion), channel_id=1, source_target_pairs={{0,1},{1,2},{2,3},{3,0},{4,5},{5,6},{6,7},{7,4},{8,9},{9,10},{10,1... | collective-permute-start | bytes 1544 | tf_op jit(solution)/shard_map/ppermute | solution.py:47
  10.8 2.5 %collective-permute-start.1 = (s32[1,128]{1,0:T(1,128)S(1)}, s32[1,128]{1,0:T(1,128)S(1)}, u32[]{:S(2)}, u32[]{:S(2)}) collective-permute-start(s32[1,128]{1,0:T(1,128)S(1)} %pad_bitcast_fusion), channel_id=1, source_target_pairs={{0,2},{1,3},{2,0},{3,1},{4,6},{5,7},{6,4},{7,5},{8,10},{9,11},{10,... | collective-permute-start | bytes 1544 | tf_op jit(solution)/shard_map/ppermute | solution.py:47
  13.5 1.3 %collective-permute-start = (s32[1,128]{1,0:T(1,128)S(1)}, s32[1,128]{1,0:T(1,128)S(1)}, u32[]{:S(2)}, u32[]{:S(2)}) collective-permute-start(s32[1,128]{1,0:T(1,128)S(1)} %pad_bitcast_fusion), channel_id=1, source_target_pairs={{0,3},{1,0},{2,1},{3,2},{4,7},{5,4},{6,5},{7,6},{8,11},{9,8},{10,9... | collective-permute-start | bytes 1544 | tf_op jit(solution)/shard_map/ppermute | solution.py:47
  15.0 1.2 %collective-permute-done.r_1_.r_2_ = s32[1,128]{1,0:T(1,128)S(1)} collective-permute-done((s32[1,128]{1,0:T(1,128)S(1)}, s32[1,128]{1,0:T(1,128)S(1)}, u32[]{:S(2)}, u32[]{:S(2)}) %collective-permute-start) | collective-permute-done | bytes 544 | tf_op jit(solution)/shard_map/ppermute | solution.py:47
  16.2 6.5 %collective-permute-done.8.r_4_.r_2_ = bf16[256,1024]{1,0:T(8,128)(2,1)S(1)} collective-permute-done((bf16[256,1024]{1,0:T(8,128)(2,1)}, bf16[256,1024]{1,0:T(8,128)(2,1)S(1)}, u32[]{:S(2)}, u32[]{:S(2)}) %collective-permute-start.8) | collective-permute-done | bytes 524320 | tf_op jit(solution)/shard_map/ppermute | solution.py:41
  23.3 1.3 %collective-permute-start.9 = (bf16[128,1024]{1,0:T(8,128)(2,1)S(1)}, bf16[128,1024]{1,0:T(8,128)(2,1)S(1)}, u32[]{:S(2)}, u32[]{:S(2)}) collective-permute-start(bf16[128,1024]{1,0:T(8,128)(2,1)S(1)} %get-tuple-element.34), channel_id=1, source_target_pairs={{0,1},{1,2},{2,3},{3,0},{4,5},{5,6},{6,7},{7,4},{8,9},{9,10},{10,1... | collective-permute-start | bytes 786440 | tf_op jit(solution)/shard_map/ppermute | solution.py:47
  24.6 2.5 %collective-permute-start.10 = (bf16[128,1024]{1,0:T(8,128)(2,1)S(1)}, bf16[128,1024]{1,0:T(8,128)(2,1)S(1)}, u32[]{:S(2)}, u32[]{:S(2)}) collective-permute-start(bf16[128,1024]{1,0:T(8,128)(2,1)S(1)} %get-tuple-element.35), channel_id=1, source_target_pairs={{0,2},{1,3},{2,0},{3,1},{4,6},{5,7},{6,4},{7,5},{8,10},{9,11},{10,... | collective-permute-start | bytes 786440 | tf_op jit(solution)/shard_map/ppermute | solution.py:47
  28.9 1.6 %copy-done.1 = bf16[1024,1024]{1,0:T(8,128)(2,1)S(1)} copy-done((bf16[1024,1024]{1,0:T(8,128)(2,1)S(1)}, bf16[1024,1024]{1,0:T(8,128)(2,1)}, u32[]{:S(2)}) %copy-start.1) | copy-done | bytes 2097176
  30.5 1.6 %copy-done.4 = s32[1,256,2048]{2,1,0:T(8,128)S(1)} copy-done((s32[1,256,2048]{2,1,0:T(8,128)S(1)}, s32[1,256,2048]{2,1,0:T(8,128)}, u32[]{:S(2)}) %copy-start.4) | copy-done | bytes 2097176
  33.2 1.3 %shard_map.114 = (bf16[256,1024]{1,0:T(8,128)(2,1)S(1)}, bf16[1024,256]{1,0:T(8,128)(2,1)S(1)}, f32[256,1024]{1,0:T(8,128)S(1)}) custom-call(s32[1]{0:T(128)} %bitcast.1.r_0_, s32[8,2]{1,0:T(8,128)S(1)} %copy.12.r_1_.r_0_, s32[256,2048]{1,0:T(8,128)S(1)} %bitcast.19, bf16[256,1024]{1,0:T(8,128)(2,1)S(1)} %bitcast.20, bf16[1024,1024]{1,0:T(8,128)(2,1)S(1)} %copy-done.1), custom_call_target="tpu_custom_call" | custom-call | flops 536870912 | bytes 1048576 | tf_op jit(solution)/shard_map/pallas_call | solution.py:23
  34.5 1.4 %collective-permute-done.4.r_5_ = bf16[256,1024]{1,0:T(8,128)(2,1)S(1)} collective-permute-done((bf16[256,1024]{1,0:T(8,128)(2,1)}, bf16[256,1024]{1,0:T(8,128)(2,1)S(1)}, u32[]{:S(2)}, u32[]{:S(2)}) %collective-permute-start.4) | collective-permute-done | bytes 524320 | tf_op jit(solution)/shard_map/ppermute | solution.py:41
  36.6 1.3 %collective-permute-start.5 = (bf16[128,1024]{1,0:T(8,128)(2,1)S(1)}, bf16[128,1024]{1,0:T(8,128)(2,1)S(1)}, u32[]{:S(2)}, u32[]{:S(2)}) collective-permute-start(bf16[128,1024]{1,0:T(8,128)(2,1)S(1)} %get-tuple-element.30), channel_id=1, source_target_pairs={{0,1},{1,2},{2,3},{3,0},{4,5},{5,6},{6,7},{7,4},{8,9},{9,10},{10,1... | collective-permute-start | bytes 786440 | tf_op jit(solution)/shard_map/ppermute | solution.py:47
  37.9 2.4 %collective-permute-start.6 = (bf16[128,1024]{1,0:T(8,128)(2,1)S(1)}, bf16[128,1024]{1,0:T(8,128)(2,1)S(1)}, u32[]{:S(2)}, u32[]{:S(2)}) collective-permute-start(bf16[128,1024]{1,0:T(8,128)(2,1)S(1)} %get-tuple-element.31), channel_id=1, source_target_pairs={{0,2},{1,3},{2,0},{3,1},{4,6},{5,7},{6,4},{7,5},{8,10},{9,11},{10,... | collective-permute-start | bytes 786440 | tf_op jit(solution)/shard_map/ppermute | solution.py:47
  41.5 4.6 %shard_map.116 = (bf16[640,2048]{1,0:T(8,128)(2,1)S(1)}, f32[256,2048]{1,0:T(8,128)S(1)}, f32[256,128]{1,0:T(8,128)S(1)}) custom-call(s32[8,2]{1,0:T(8,128)S(1)} %copy.12.r_1_.r_0_, bf16[256,1024]{1,0:T(8,128)(2,1)S(1)} %collective-permute-done.3.r_4_.r_1_, bf16[256,1024]{1,0:T(8,128)(2,1)S(1)} %collective-permute-done.8.r_4_.r_2_, ...), custom_call_target="tpu_custom_call" | custom-call | flops 3355443200 | bytes 1048576 | tf_op jit(solution)/shard_map/pallas_call | solution.py:23
  46.1 5.8 %collective-permute-done.6.r_1_ = bf16[128,1024]{1,0:T(8,128)(2,1)S(1)} collective-permute-done((bf16[128,1024]{1,0:T(8,128)(2,1)S(1)}, bf16[128,1024]{1,0:T(8,128)(2,1)S(1)}, u32[]{:S(2)}, u32[]{:S(2)}) %collective-permute-start.6) | collective-permute-done | bytes 262176 | tf_op jit(solution)/shard_map/ppermute | solution.py:47
  52.0 2.9 %shard_map.117 = (bf16[384,2048]{1,0:T(8,128)(2,1)S(1)}, f32[256,2048]{1,0:T(8,128)S(1)}, f32[256,128]{1,0:T(8,128)S(1)}) custom-call(bf16[128,1024]{1,0:T(8,128)(2,1)S(1)} %collective-permute-done.5.r_0_, bf16[128,1024]{1,0:T(8,128)(2,1)S(1)} %collective-permute-done.6.r_1_, bf16[128,1024]{1,0:T(8,128)(2,1)S(1)} %collective-permute-done.7.r_2_, ...), custom_call_target="tpu_custom_call" | custom-call | flops 2013265920 | bytes 1048576 | tf_op jit(solution)/shard_map/pallas_call | solution.py:23
  54.9 4.1 %shard_map.118 = (bf16[256,1024]{1,0:T(8,128)(2,1)}, f32[256,1024]{1,0:T(8,128)S(1)}, bf16[256,2048]{1,0:T(8,128)(2,1)S(1)}) custom-call(s32[1]{0:T(128)} %bitcast.16.live_ref, f32[256,2048]{1,0:T(8,128)S(1)} %get-tuple-element.39.acc_ref, f32[256,128]{1,0:T(8,128)S(1)} %get-tuple-element.40.deg_ref, f32[256,1024]{1,0:T(8,128)S(1)} %get-tuple-element.41.self_ref, ...), custom_call_target="tpu_custom_call" | custom-call | flops 2684354560 | bytes 1048576 | tf_op jit(solution)/shard_map/pallas_call | solution.py:23
  59.0 2.2 %shard_map.122 = (bf16[128,1024]{1,0:T(8,128)(2,1)S(1)}, bf16[128,1024]{1,0:T(8,128)(2,1)S(1)}, bf16[128,1024]{1,0:T(8,128)(2,1)S(1)}) custom-call(bf16[1024,256]{1,0:T(8,128)(2,1)S(1)} %get-tuple-element.44.r_0_, bf16[256,2048]{1,0:T(8,128)(2,1)S(1)} %get-tuple-element.45.r_1_, bf16[640,2048]{1,0:T(8,128)(2,1)S(1)} %get-tuple-element.46.r_2_, ...), custom_call_target="tpu_custom_call" | custom-call | flops 2013265920 | bytes 1048576 | tf_op jit(solution)/shard_map/pallas_call | solution.py:23
  61.2 2.8 %collective-permute-start.16 = (bf16[128,1024]{1,0:T(8,128)(2,1)S(1)}, bf16[128,1024]{1,0:T(8,128)(2,1)S(1)}, u32[]{:S(2)}, u32[]{:S(2)}) collective-permute-start(bf16[128,1024]{1,0:T(8,128)(2,1)S(1)} %get-tuple-element.54), channel_id=1, source_target_pairs={{0,3},{1,0},{2,1},{3,2},{4,7},{5,4},{6,5},{7,6},{8,11},{9,8},{10,9... | collective-permute-start | bytes 786440 | tf_op jit(solution)/shard_map/ppermute | solution.py:47
  64.1 2.2 %shard_map.120 = (bf16[128,1024]{1,0:T(8,128)(2,1)S(1)}, bf16[128,1024]{1,0:T(8,128)(2,1)S(1)}, bf16[128,1024]{1,0:T(8,128)(2,1)S(1)}) custom-call(bf16[1024,256]{1,0:T(8,128)(2,1)S(1)} %get-tuple-element.44.r_0_, bf16[256,2048]{1,0:T(8,128)(2,1)S(1)} %get-tuple-element.45.r_1_, bf16[384,2048]{1,0:T(8,128)(2,1)S(1)} %get-tuple-element.48.r_2_, ...), custom_call_target="tpu_custom_call" | custom-call | flops 2013265920 | bytes 1048576 | tf_op jit(solution)/shard_map/pallas_call | solution.py:23
  67.2 2.2 %collective-permute-start.12 = (bf16[128,1024]{1,0:T(8,128)(2,1)S(1)}, bf16[128,1024]{1,0:T(8,128)(2,1)S(1)}, u32[]{:S(2)}, u32[]{:S(2)}) collective-permute-start(bf16[128,1024]{1,0:T(8,128)(2,1)S(1)} %get-tuple-element.49), channel_id=1, source_target_pairs={{0,3},{1,0},{2,1},{3,2},{4,7},{5,4},{6,5},{7,6},{8,11},{9,8},{10,9... | collective-permute-start | bytes 786440 | tf_op jit(solution)/shard_map/ppermute | solution.py:47
  69.3 1.6 %collective-permute-start.13 = (bf16[128,1024]{1,0:T(8,128)(2,1)S(1)}, bf16[128,1024]{1,0:T(8,128)(2,1)S(1)}, u32[]{:S(2)}, u32[]{:S(2)}) collective-permute-start(bf16[128,1024]{1,0:T(8,128)(2,1)S(1)} %get-tuple-element.50), channel_id=1, source_target_pairs={{0,2},{1,3},{2,0},{3,1},{4,6},{5,7},{6,4},{7,5},{8,10},{9,11},{10,... | collective-permute-start | bytes 786440 | tf_op jit(solution)/shard_map/ppermute | solution.py:47
  70.9 2.2 %collective-permute-done.16.r_6_ = bf16[128,1024]{1,0:T(8,128)(2,1)S(1)} collective-permute-done((bf16[128,1024]{1,0:T(8,128)(2,1)S(1)}, bf16[128,1024]{1,0:T(8,128)(2,1)S(1)}, u32[]{:S(2)}, u32[]{:S(2)}) %collective-permute-start.16) | collective-permute-done | bytes 262176 | tf_op jit(solution)/shard_map/ppermute | solution.py:47
  73.1 1.6 %shard_map.119 = (bf16[128,1024]{1,0:T(8,128)(2,1)S(1)}, bf16[128,1024]{1,0:T(8,128)(2,1)S(1)}) custom-call(bf16[1024,256]{1,0:T(8,128)(2,1)S(1)} %get-tuple-element.44.r_0_, bf16[256,2048]{1,0:T(8,128)(2,1)S(1)} %get-tuple-element.45.r_1_, bf16[640,2048]{1,0:T(8,128)(2,1)S(1)} %get-tuple-element.46.r_2_, bf16[1024,2048]{1,0:T(8,128)(2,1)S(1)} %copy-done), custom_call_target="tpu_custom_call" | custom-call | flops 1342177280 | bytes 1048576 | tf_op jit(solution)/shard_map/pallas_call | solution.py:23
  74.7 5.7 %collective-permute-done.18.r_8_ = bf16[128,1024]{1,0:T(8,128)(2,1)S(1)} collective-permute-done((bf16[128,1024]{1,0:T(8,128)(2,1)S(1)}, bf16[128,1024]{1,0:T(8,128)(2,1)S(1)}, u32[]{:S(2)}, u32[]{:S(2)}) %collective-permute-start.18) | collective-permute-done | bytes 262176 | tf_op jit(solution)/shard_map/ppermute | solution.py:47
  81.3 4.3 %collective-permute-start.19 = (bf16[256,1024]{1,0:T(8,128)(2,1)S(1)}, bf16[256,1024]{1,0:T(8,128)(2,1)S(1)}, u32[]{:S(2)}, u32[]{:S(2)}) collective-permute-start(bf16[256,1024]{1,0:T(8,128)(2,1)S(1)} %shard_map.123), channel_id=1, source_target_pairs={{0,124},{1,125},{2,126},{3,127},{4,64},{5,65},{6,66},{7,67},{8,68}... | collective-permute-start | bytes 1572872 | tf_op jit(solution)/shard_map/ppermute | solution.py:41
  85.9 4.6 %collective-permute-done.14.r_8_ = bf16[128,1024]{1,0:T(8,128)(2,1)S(1)} collective-permute-done((bf16[128,1024]{1,0:T(8,128)(2,1)S(1)}, bf16[128,1024]{1,0:T(8,128)(2,1)S(1)}, u32[]{:S(2)}, u32[]{:S(2)}) %collective-permute-start.14) | collective-permute-done | bytes 262176 | tf_op jit(solution)/shard_map/ppermute | solution.py:47
  92.2 2.4 %collective-permute-start.20 = (bf16[256,1024]{1,0:T(8,128)(2,1)S(1)}, bf16[256,1024]{1,0:T(8,128)(2,1)S(1)}, u32[]{:S(2)}, u32[]{:S(2)}) collective-permute-start(bf16[256,1024]{1,0:T(8,128)(2,1)S(1)} %get-tuple-element.57), channel_id=1, source_target_pairs={{0,120},{1,121},{2,122},{3,123},{4,124},{5,125},{6,126},{7,127},{8... | collective-permute-start | bytes 1572872 | tf_op jit(solution)/shard_map/ppermute | solution.py:41
  95.7 11.6 %collective-permute-done.20.c_ref = bf16[256,1024]{1,0:T(8,128)(2,1)S(1)} collective-permute-done((bf16[256,1024]{1,0:T(8,128)(2,1)S(1)}, bf16[256,1024]{1,0:T(8,128)(2,1)S(1)}, u32[]{:S(2)}, u32[]{:S(2)}) %collective-permute-start.20) | collective-permute-done | bytes 524320 | tf_op jit(solution)/shard_map/ppermute | solution.py:41
  (45 shorter events, 13.4 us)
Async XLA Ops:
  3.2 19.4 %collective-permute-start.8 = (bf16[256,1024]{1,0:T(8,128)(2,1)}, bf16[256,1024]{1,0:T(8,128)(2,1)S(1)}, u32[]{:S(2)}, u32[]{:S(2)}) collective-permute-start(bf16[256,1024]{1,0:T(8,128)(2,1)} %broadcast_select_fusion), channel_id=1, source_target_pairs={{0,68},{1,69},{2,70},{3,71},{4,72},{5,73},{6,74},{7,75},{8,76},{9,... | collective-permute-start | bytes 1572872 | tf_op jit(solution)/shard_map/ppermute | solution.py:41
  5.9 30.0 %collective-permute-start.4 = (bf16[256,1024]{1,0:T(8,128)(2,1)}, bf16[256,1024]{1,0:T(8,128)(2,1)S(1)}, u32[]{:S(2)}, u32[]{:S(2)}) collective-permute-start(bf16[256,1024]{1,0:T(8,128)(2,1)} %broadcast_select_fusion), channel_id=1, source_target_pairs={{0,72},{1,73},{2,74},{3,75},{4,76},{5,77},{6,78},{7,79},{8,80},{9,... | collective-permute-start | bytes 1572872 | tf_op jit(solution)/shard_map/ppermute | solution.py:41
  8.3 27.7 %collective-permute-start.3 = (bf16[256,1024]{1,0:T(8,128)(2,1)}, bf16[256,1024]{1,0:T(8,128)(2,1)S(1)}, u32[]{:S(2)}, u32[]{:S(2)}) collective-permute-start(bf16[256,1024]{1,0:T(8,128)(2,1)} %broadcast_select_fusion), channel_id=1, source_target_pairs={{0,64},{1,65},{2,66},{3,67},{4,68},{5,69},{6,70},{7,71},{8,72},{9,... | collective-permute-start | bytes 1572872 | tf_op jit(solution)/shard_map/ppermute | solution.py:41
  9.6 3.9 %collective-permute-start.2 = (s32[1,128]{1,0:T(1,128)S(1)}, s32[1,128]{1,0:T(1,128)S(1)}, u32[]{:S(2)}, u32[]{:S(2)}) collective-permute-start(s32[1,128]{1,0:T(1,128)S(1)} %pad_bitcast_fusion), channel_id=1, source_target_pairs={{0,1},{1,2},{2,3},{3,0},{4,5},{5,6},{6,7},{7,4},{8,9},{9,10},{10,1... | collective-permute-start | bytes 1544 | tf_op jit(solution)/shard_map/ppermute | solution.py:47
  10.8 4.2 %collective-permute-start.1 = (s32[1,128]{1,0:T(1,128)S(1)}, s32[1,128]{1,0:T(1,128)S(1)}, u32[]{:S(2)}, u32[]{:S(2)}) collective-permute-start(s32[1,128]{1,0:T(1,128)S(1)} %pad_bitcast_fusion), channel_id=1, source_target_pairs={{0,2},{1,3},{2,0},{3,1},{4,6},{5,7},{6,4},{7,5},{8,10},{9,11},{10,... | collective-permute-start | bytes 1544 | tf_op jit(solution)/shard_map/ppermute | solution.py:47
  13.5 2.7 %collective-permute-start = (s32[1,128]{1,0:T(1,128)S(1)}, s32[1,128]{1,0:T(1,128)S(1)}, u32[]{:S(2)}, u32[]{:S(2)}) collective-permute-start(s32[1,128]{1,0:T(1,128)S(1)} %pad_bitcast_fusion), channel_id=1, source_target_pairs={{0,3},{1,0},{2,1},{3,2},{4,7},{5,4},{6,5},{7,6},{8,11},{9,8},{10,9... | collective-permute-start | bytes 1544 | tf_op jit(solution)/shard_map/ppermute | solution.py:47
  23.3 17.0 %collective-permute-start.9 = (bf16[128,1024]{1,0:T(8,128)(2,1)S(1)}, bf16[128,1024]{1,0:T(8,128)(2,1)S(1)}, u32[]{:S(2)}, u32[]{:S(2)}) collective-permute-start(bf16[128,1024]{1,0:T(8,128)(2,1)S(1)} %get-tuple-element.34), channel_id=1, source_target_pairs={{0,1},{1,2},{2,3},{3,0},{4,5},{5,6},{6,7},{7,4},{8,9},{9,10},{10,1... | collective-permute-start | bytes 786440 | tf_op jit(solution)/shard_map/ppermute | solution.py:47
  24.6 16.9 %collective-permute-start.10 = (bf16[128,1024]{1,0:T(8,128)(2,1)S(1)}, bf16[128,1024]{1,0:T(8,128)(2,1)S(1)}, u32[]{:S(2)}, u32[]{:S(2)}) collective-permute-start(bf16[128,1024]{1,0:T(8,128)(2,1)S(1)} %get-tuple-element.35), channel_id=1, source_target_pairs={{0,2},{1,3},{2,0},{3,1},{4,6},{5,7},{6,4},{7,5},{8,10},{9,11},{10,... | collective-permute-start | bytes 786440 | tf_op jit(solution)/shard_map/ppermute | solution.py:47
  27.0 14.5 %collective-permute-start.11 = (bf16[128,1024]{1,0:T(8,128)(2,1)S(1)}, bf16[128,1024]{1,0:T(8,128)(2,1)S(1)}, u32[]{:S(2)}, u32[]{:S(2)}) collective-permute-start(bf16[128,1024]{1,0:T(8,128)(2,1)S(1)} %get-tuple-element.36), channel_id=1, source_target_pairs={{0,3},{1,0},{2,1},{3,2},{4,7},{5,4},{6,5},{7,6},{8,11},{9,8},{10,9... | collective-permute-start | bytes 786440 | tf_op jit(solution)/shard_map/ppermute | solution.py:47
  28.9 1.6 %copy-start.1 = (bf16[1024,1024]{1,0:T(8,128)(2,1)S(1)}, bf16[1024,1024]{1,0:T(8,128)(2,1)}, u32[]{:S(2)}) copy-start(bf16[1024,1024]{1,0:T(8,128)(2,1)} %sw_ref.1) | copy-start | bytes 6291460
  30.5 1.6 %copy-start.4 = (s32[1,256,2048]{2,1,0:T(8,128)S(1)}, s32[1,256,2048]{2,1,0:T(8,128)}, u32[]{:S(2)}) copy-start(s32[1,256,2048]{2,1,0:T(8,128)} %param.13) | copy-start | bytes 6291460
  32.1 1.0 copy-start.5
  33.2 8.3 %copy-start = (bf16[1024,2048]{1,0:T(8,128)(2,1)S(1)}, bf16[1024,2048]{1,0:T(8,128)(2,1)}, u32[]{:S(2)}) copy-start(bf16[1024,2048]{1,0:T(8,128)(2,1)} %r_3_.7) | copy-start | bytes 12582916
  33.2 8.3 %copy-start.7 = (f32[2048]{0:T(1024)S(1)}, f32[2048]{0:T(1024)}, u32[]{:S(2)}) copy-start(f32[2048]{0:T(1024)} %param.16) | copy-start | bytes 24580
  36.6 9.5 %collective-permute-start.5 = (bf16[128,1024]{1,0:T(8,128)(2,1)S(1)}, bf16[128,1024]{1,0:T(8,128)(2,1)S(1)}, u32[]{:S(2)}, u32[]{:S(2)}) collective-permute-start(bf16[128,1024]{1,0:T(8,128)(2,1)S(1)} %get-tuple-element.30), channel_id=1, source_target_pairs={{0,1},{1,2},{2,3},{3,0},{4,5},{5,6},{6,7},{7,4},{8,9},{9,10},{10,1... | collective-permute-start | bytes 786440 | tf_op jit(solution)/shard_map/ppermute | solution.py:47
  37.9 14.1 %collective-permute-start.6 = (bf16[128,1024]{1,0:T(8,128)(2,1)S(1)}, bf16[128,1024]{1,0:T(8,128)(2,1)S(1)}, u32[]{:S(2)}, u32[]{:S(2)}) collective-permute-start(bf16[128,1024]{1,0:T(8,128)(2,1)S(1)} %get-tuple-element.31), channel_id=1, source_target_pairs={{0,2},{1,3},{2,0},{3,1},{4,6},{5,7},{6,4},{7,5},{8,10},{9,11},{10,... | collective-permute-start | bytes 786440 | tf_op jit(solution)/shard_map/ppermute | solution.py:47
  40.3 11.6 %collective-permute-start.7 = (bf16[128,1024]{1,0:T(8,128)(2,1)S(1)}, bf16[128,1024]{1,0:T(8,128)(2,1)S(1)}, u32[]{:S(2)}, u32[]{:S(2)}) collective-permute-start(bf16[128,1024]{1,0:T(8,128)(2,1)S(1)} %get-tuple-element.32), channel_id=1, source_target_pairs={{0,3},{1,0},{2,1},{3,2},{4,7},{5,4},{6,5},{7,6},{8,11},{9,8},{10,9... | collective-permute-start | bytes 786440 | tf_op jit(solution)/shard_map/ppermute | solution.py:47
  52.0 2.9 %copy-start.2 = (bf16[1024,1024]{1,0:T(8,128)(2,1)S(1)}, bf16[1024,1024]{1,0:T(8,128)(2,1)}, u32[]{:S(2)}) copy-start(bf16[1024,1024]{1,0:T(8,128)(2,1)} %sw_ref.1) | copy-start | bytes 6291460
  52.0 2.9 %copy-start.3 = (bf16[2048,1024]{1,0:T(8,128)(2,1)S(1)}, bf16[2048,1024]{1,0:T(8,128)(2,1)}, u32[]{:S(2)}) copy-start(bf16[2048,1024]{1,0:T(8,128)(2,1)} %nb_ref.1) | copy-start | bytes 12582916
  52.0 2.9 %copy-start.6 = (bf16[1,256,1024]{2,1,0:T(8,128)(2,1)S(1)}, bf16[1,256,1024]{2,1,0:T(8,128)(2,1)}, u32[]{:S(2)}) copy-start(bf16[1,256,1024]{2,1,0:T(8,128)(2,1)} %param.14) | copy-start | bytes 1572868
  52.0 2.9 %copy-start.8 = (f32[1024]{0:T(1024)S(1)}, f32[1024]{0:T(1024)}, u32[]{:S(2)}) copy-start(f32[1024]{0:T(1024)} %param.19) | copy-start | bytes 12292
  61.2 11.9 %collective-permute-start.16 = (bf16[128,1024]{1,0:T(8,128)(2,1)S(1)}, bf16[128,1024]{1,0:T(8,128)(2,1)S(1)}, u32[]{:S(2)}, u32[]{:S(2)}) collective-permute-start(bf16[128,1024]{1,0:T(8,128)(2,1)S(1)} %get-tuple-element.54), channel_id=1, source_target_pairs={{0,3},{1,0},{2,1},{3,2},{4,7},{5,4},{6,5},{7,6},{8,11},{9,8},{10,9... | collective-permute-start | bytes 786440 | tf_op jit(solution)/shard_map/ppermute | solution.py:47
  64.0 10.7 %collective-permute-start.17 = (bf16[128,1024]{1,0:T(8,128)(2,1)S(1)}, bf16[128,1024]{1,0:T(8,128)(2,1)S(1)}, u32[]{:S(2)}, u32[]{:S(2)}) collective-permute-start(bf16[128,1024]{1,0:T(8,128)(2,1)S(1)} %get-tuple-element.55), channel_id=1, source_target_pairs={{0,2},{1,3},{2,0},{3,1},{4,6},{5,7},{6,4},{7,5},{8,10},{9,11},{10,... | collective-permute-start | bytes 786440 | tf_op jit(solution)/shard_map/ppermute | solution.py:47
  66.4 14.0 %collective-permute-start.18 = (bf16[128,1024]{1,0:T(8,128)(2,1)S(1)}, bf16[128,1024]{1,0:T(8,128)(2,1)S(1)}, u32[]{:S(2)}, u32[]{:S(2)}) collective-permute-start(bf16[128,1024]{1,0:T(8,128)(2,1)S(1)} %get-tuple-element.56), channel_id=1, source_target_pairs={{0,1},{1,2},{2,3},{3,0},{4,5},{5,6},{6,7},{7,4},{8,9},{9,10},{10,1... | collective-permute-start | bytes 786440 | tf_op jit(solution)/shard_map/ppermute | solution.py:47
  67.2 18.7 %collective-permute-start.12 = (bf16[128,1024]{1,0:T(8,128)(2,1)S(1)}, bf16[128,1024]{1,0:T(8,128)(2,1)S(1)}, u32[]{:S(2)}, u32[]{:S(2)}) collective-permute-start(bf16[128,1024]{1,0:T(8,128)(2,1)S(1)} %get-tuple-element.49), channel_id=1, source_target_pairs={{0,3},{1,0},{2,1},{3,2},{4,7},{5,4},{6,5},{7,6},{8,11},{9,8},{10,9... | collective-permute-start | bytes 786440 | tf_op jit(solution)/shard_map/ppermute | solution.py:47
  69.3 16.6 %collective-permute-start.13 = (bf16[128,1024]{1,0:T(8,128)(2,1)S(1)}, bf16[128,1024]{1,0:T(8,128)(2,1)S(1)}, u32[]{:S(2)}, u32[]{:S(2)}) collective-permute-start(bf16[128,1024]{1,0:T(8,128)(2,1)S(1)} %get-tuple-element.50), channel_id=1, source_target_pairs={{0,2},{1,3},{2,0},{3,1},{4,6},{5,7},{6,4},{7,5},{8,10},{9,11},{10,... | collective-permute-start | bytes 786440 | tf_op jit(solution)/shard_map/ppermute | solution.py:47
  73.1 17.3 %collective-permute-start.14 = (bf16[128,1024]{1,0:T(8,128)(2,1)S(1)}, bf16[128,1024]{1,0:T(8,128)(2,1)S(1)}, u32[]{:S(2)}, u32[]{:S(2)}) collective-permute-start(bf16[128,1024]{1,0:T(8,128)(2,1)S(1)} %get-tuple-element.51), channel_id=1, source_target_pairs={{0,1},{1,2},{2,3},{3,0},{4,5},{5,6},{6,7},{7,4},{8,9},{9,10},{10,1... | collective-permute-start | bytes 786440 | tf_op jit(solution)/shard_map/ppermute | solution.py:47
  81.3 14.4 %collective-permute-start.19 = (bf16[256,1024]{1,0:T(8,128)(2,1)S(1)}, bf16[256,1024]{1,0:T(8,128)(2,1)S(1)}, u32[]{:S(2)}, u32[]{:S(2)}) collective-permute-start(bf16[256,1024]{1,0:T(8,128)(2,1)S(1)} %shard_map.123), channel_id=1, source_target_pairs={{0,124},{1,125},{2,126},{3,127},{4,64},{5,65},{6,66},{7,67},{8,68}... | collective-permute-start | bytes 1572872 | tf_op jit(solution)/shard_map/ppermute | solution.py:41
  91.5 4.2 %collective-permute-start.15 = (bf16[256,1024]{1,0:T(8,128)(2,1)S(1)}, bf16[256,1024]{1,0:T(8,128)(2,1)S(1)}, u32[]{:S(2)}, u32[]{:S(2)}) collective-permute-start(bf16[256,1024]{1,0:T(8,128)(2,1)S(1)} %get-tuple-element.52), channel_id=1, source_target_pairs={{0,64},{1,65},{2,66},{3,67},{4,68},{5,69},{6,70},{7,71},{8,72},{9,... | collective-permute-start | bytes 1572872 | tf_op jit(solution)/shard_map/ppermute | solution.py:41
  92.2 15.1 %collective-permute-start.20 = (bf16[256,1024]{1,0:T(8,128)(2,1)S(1)}, bf16[256,1024]{1,0:T(8,128)(2,1)S(1)}, u32[]{:S(2)}, u32[]{:S(2)}) collective-permute-start(bf16[256,1024]{1,0:T(8,128)(2,1)S(1)} %get-tuple-element.57), channel_id=1, source_target_pairs={{0,120},{1,121},{2,122},{3,123},{4,124},{5,125},{6,126},{7,127},{8... | collective-permute-start | bytes 1572872 | tf_op jit(solution)/shard_map/ppermute | solution.py:41

commit v3 on v2

--- a/solution.py
+++ b/solution.py
@@ -12,6 +12,7 @@
 F32 = jnp.float32
 BF16 = jnp.bfloat16
 VMEM = pl.BlockSpec(memory_space=pltpu.VMEM)
+HELD = pl.BlockSpec(memory_space=pl.ANY)
 SMEM = pl.BlockSpec(memory_space=pltpu.SMEM)
 
 
@@ -59,7 +60,7 @@
     return pl.ds(pl.multiple_of(index * block, block), block)
 
 
-def pick_near_kernel(block, place_ref, m1, m2, m3, below_ref, *outs):
+def pick_near_kernel(block, place_ref, m1, m2, m3, below_ref, _, *outs):
     for d, (meta, out) in enumerate(zip((m1, m2, m3), outs), 1):
         p = lax.rem(place_ref[0] + d, LINE)
         out[...] = below_ref[at_block(meta[0, near(p, d)], block), :]
@@ -223,11 +224,19 @@
     below = swap_rows(marked, LINE)
     same = swap_rows(marked, 0)
     metas = [along(row, -d) for d in range(1, LINE)]
-    below2 = swap_rows(marked, 2 * LINE)
+    later, *metas = lax.optimization_barrier((marked, *metas))
+    below2 = swap_rows(later, 2 * LINE)
     one = ((block, width), BF16)
     three = [SMEM] * 4
+    tiles, tiles_t, self_pre = call(
+        lambda *r: tiles_kernel(block, *r),
+        [((rows, reach * block), BF16), ((reach * block, rows), BF16), ((rows, width), F32)],
+        (place, lists, counts, x, sw),
+        [SMEM] * 2 + [VMEM] * 3,
+        flops=2 * rows * width * width,
+    )
     picked = call(
-        lambda *r: pick_near_kernel(block, *r), [one] * 3, (place, *metas, below), three + [VMEM]
+        lambda *r: pick_near_kernel(block, *r), [one] * 3, (place, *metas, below, tiles), three + [VMEM, HELD]
     )
     got_near = [along(b, d) for d, b in enumerate(picked, 1)]
     picked = call(
@@ -237,13 +246,6 @@
         three + [VMEM] * 2,
     )
     got_far = [along(b, d) for d, b in enumerate(picked, 1)]
-    tiles, tiles_t, self_pre = call(
-        lambda *r: tiles_kernel(block, *r),
-        [((rows, reach * block), BF16), ((reach * block, rows), BF16), ((rows, width), F32)],
-        (place, lists, counts, x, sw),
-        [SMEM] * 2 + [VMEM] * 3,
-        flops=2 * rows * width * width,
-    )
     split = 2 + LINE - 1
 
     def message(first, last, ins, specs):

time: 109 us -> 110 us (level)
  the two profiles are of different devices: /device:TPU:1 before, /device:TPU:57 now
where the time goes in v3:
time: 110 us
  waiting for transfers between devices  47.3 us (43%)
  starting transfers between devices  31.1 us (28%)
  Pallas kernels  23.2 us (21%)
  local copies, waits for them, and re-layouts  5.69 us (5%)
  between operations  1.46 us (1%)
  other arithmetic  1.16 us (1%)
    ppermute x15, waiting for transfers between devices, along(): return lax.ppermute(x, 'dom', pairs)  26.3 us
    pallas_call x12, Pallas kernels, call(): pl.pallas_call(kernel, out_shape=[jax.ShapeDtypeStruct(s, d) for s, d in...  23.2 us
    ppermute x6, waiting for transfers between devices, swap_rows(): return lax.ppermute(x, ('side', 'dom'), pairs)  20.9 us
    ppermute x15, starting transfers between devices, along(): return lax.ppermute(x, 'dom', pairs)  20.1 us
    ppermute x6, starting transfers between devices, swap_rows(): return lax.ppermute(x, ('side', 'dom'), pairs)  10.9 us
    unnamed x18, local copies, waits for them, and re-layouts  4.25 us
  transfers between devices with their start and end apart: 21, of which 11 were waited for; matrix products, arithmetic and copies ran while one was open for 1% of the time, Pallas kernels for 12%

profile of v3, /device:TPU:57, one launch (start us, length us, event | category | flops | bytes accessed | tf_op | source)
XLA Modules:
  0.0 109.8 jit_solution(4282440714497873393)
XLA Ops:
  1.3 1.2 %broadcast_select_fusion = bf16[256,1024]{1,0:T(8,128)(2,1)S(1)} fusion(pred[256]{0:T(512)(128)(4,1)S(1)} %iota_compare_fusion, bf16[1,256,1024]{2,1,0:T(8,128)(2,1)} %param.10), kind=kLoop, calls=%fused_computation | loop fusion | flops 262144 | bytes 1048832 | tf_op jit(solution)/shard_map/jit(_where)/select_n | solution.py:222
  2.5 1.9 %collective-permute-start.8 = (bf16[256,1024]{1,0:T(8,128)(2,1)S(1)}, bf16[256,1024]{1,0:T(8,128)(2,1)S(1)}, u32[]{:S(2)}, u32[]{:S(2)}) collective-permute-start(bf16[256,1024]{1,0:T(8,128)(2,1)S(1)} %broadcast_select_fusion), channel_id=1, source_target_pairs={{0,68},{1,69},{2,70},{3,71},{4,72},{5,73},{6,74},{7,75},{8,76},{9,... | collective-permute-start | bytes 1572872 | tf_op jit(solution)/shard_map/ppermute | solution.py:42
  5.1 1.2 %collective-permute-start.2 = (s32[1,128]{1,0:T(1,128)S(1)}, s32[1,128]{1,0:T(1,128)S(1)}, u32[]{:S(2)}, u32[]{:S(2)}) collective-permute-start(s32[1,128]{1,0:T(1,128)S(1)} %pad_bitcast_fusion), channel_id=1, source_target_pairs={{0,1},{1,2},{2,3},{3,0},{4,5},{5,6},{6,7},{7,4},{8,9},{9,10},{10,1... | collective-permute-start | bytes 1544 | tf_op jit(solution)/shard_map/ppermute | solution.py:48
  6.3 2.5 %collective-permute-start.1 = (s32[1,128]{1,0:T(1,128)S(1)}, s32[1,128]{1,0:T(1,128)S(1)}, u32[]{:S(2)}, u32[]{:S(2)}) collective-permute-start(s32[1,128]{1,0:T(1,128)S(1)} %pad_bitcast_fusion), channel_id=1, source_target_pairs={{0,2},{1,3},{2,0},{3,1},{4,6},{5,7},{6,4},{7,5},{8,10},{9,11},{10,... | collective-permute-start | bytes 1544 | tf_op jit(solution)/shard_map/ppermute | solution.py:48
  8.8 1.2 %collective-permute-start = (s32[1,128]{1,0:T(1,128)S(1)}, s32[1,128]{1,0:T(1,128)S(1)}, u32[]{:S(2)}, u32[]{:S(2)}) collective-permute-start(s32[1,128]{1,0:T(1,128)S(1)} %pad_bitcast_fusion), channel_id=1, source_target_pairs={{0,3},{1,0},{2,1},{3,2},{4,7},{5,4},{6,5},{7,6},{8,11},{9,8},{10,9... | collective-permute-start | bytes 1544 | tf_op jit(solution)/shard_map/ppermute | solution.py:48
  11.4 3.4 %collective-permute-start.4 = (bf16[256,1024]{1,0:T(8,128)(2,1)S(1)}, bf16[256,1024]{1,0:T(8,128)(2,1)S(1)}, u32[]{:S(2)}, u32[]{:S(2)}) collective-permute-start(bf16[256,1024]{1,0:T(8,128)(2,1)S(1)} %broadcast_select_fusion), channel_id=1, source_target_pairs={{0,72},{1,73},{2,74},{3,75},{4,76},{5,77},{6,78},{7,79},{8,80},{9,... | collective-permute-start | bytes 1572872 | tf_op jit(solution)/shard_map/ppermute | solution.py:42
  15.6 1.6 %copy-done.1 = bf16[1024,1024]{1,0:T(8,128)(2,1)S(1)} copy-done((bf16[1024,1024]{1,0:T(8,128)(2,1)S(1)}, bf16[1024,1024]{1,0:T(8,128)(2,1)}, u32[]{:S(2)}) %copy-start.1) | copy-done | bytes 2097176
  17.2 1.6 %copy-done.4 = s32[1,256,2048]{2,1,0:T(8,128)S(1)} copy-done((s32[1,256,2048]{2,1,0:T(8,128)S(1)}, s32[1,256,2048]{2,1,0:T(8,128)}, u32[]{:S(2)}) %copy-start.4) | copy-done | bytes 2097176
  18.8 1.0 copy-done.5
  19.8 1.3 %shard_map.114 = (bf16[256,1024]{1,0:T(8,128)(2,1)S(1)}, bf16[1024,256]{1,0:T(8,128)(2,1)S(1)}, f32[256,1024]{1,0:T(8,128)S(1)}) custom-call(s32[1]{0:T(128)} %bitcast.1.r_0_, s32[8,2]{1,0:T(8,128)S(1)} %copy.12.r_1_.r_0_, s32[256,2048]{1,0:T(8,128)S(1)} %bitcast.19, bf16[256,1024]{1,0:T(8,128)(2,1)S(1)} %bitcast.20, bf16[1024,1024]{1,0:T(8,128)(2,1)S(1)} %copy-done.1), custom_call_target="tpu_custom_call" | custom-call | flops 536870912 | bytes 1048576 | tf_op jit(solution)/shard_map/pallas_call | solution.py:24
  21.9 3.5 %collective-permute-start.10 = (bf16[128,1024]{1,0:T(8,128)(2,1)S(1)}, bf16[128,1024]{1,0:T(8,128)(2,1)S(1)}, u32[]{:S(2)}, u32[]{:S(2)}) collective-permute-start(bf16[128,1024]{1,0:T(8,128)(2,1)S(1)} %get-tuple-element.43), channel_id=1, source_target_pairs={{0,2},{1,3},{2,0},{3,1},{4,6},{5,7},{6,4},{7,5},{8,10},{9,11},{10,... | collective-permute-start | bytes 786440 | tf_op jit(solution)/shard_map/ppermute | solution.py:48
  25.4 1.6 %collective-permute-done.4.r_5_ = bf16[256,1024]{1,0:T(8,128)(2,1)S(1)} collective-permute-done((bf16[256,1024]{1,0:T(8,128)(2,1)S(1)}, bf16[256,1024]{1,0:T(8,128)(2,1)S(1)}, u32[]{:S(2)}, u32[]{:S(2)}) %collective-permute-start.4) | collective-permute-done | bytes 524320 | tf_op jit(solution)/shard_map/ppermute | solution.py:42
  27.8 2.9 %collective-permute-start.6 = (bf16[128,1024]{1,0:T(8,128)(2,1)S(1)}, bf16[128,1024]{1,0:T(8,128)(2,1)S(1)}, u32[]{:S(2)}, u32[]{:S(2)}) collective-permute-start(bf16[128,1024]{1,0:T(8,128)(2,1)S(1)} %get-tuple-element.39), channel_id=1, source_target_pairs={{0,2},{1,3},{2,0},{3,1},{4,6},{5,7},{6,4},{7,5},{8,10},{9,11},{10,... | collective-permute-start | bytes 786440 | tf_op jit(solution)/shard_map/ppermute | solution.py:48
  30.9 1.6 %collective-permute-start.7 = (bf16[128,1024]{1,0:T(8,128)(2,1)S(1)}, bf16[128,1024]{1,0:T(8,128)(2,1)S(1)}, u32[]{:S(2)}, u32[]{:S(2)}) collective-permute-start(bf16[128,1024]{1,0:T(8,128)(2,1)S(1)} %get-tuple-element.40), channel_id=1, source_target_pairs={{0,3},{1,0},{2,1},{3,2},{4,7},{5,4},{6,5},{7,6},{8,11},{9,8},{10,9... | collective-permute-start | bytes 786440 | tf_op jit(solution)/shard_map/ppermute | solution.py:48
  32.5 5.1 %collective-permute-done.10.r_4_ = bf16[128,1024]{1,0:T(8,128)(2,1)S(1)} collective-permute-done((bf16[128,1024]{1,0:T(8,128)(2,1)S(1)}, bf16[128,1024]{1,0:T(8,128)(2,1)S(1)}, u32[]{:S(2)}, u32[]{:S(2)}) %collective-permute-start.10) | collective-permute-done | bytes 262176 | tf_op jit(solution)/shard_map/ppermute | solution.py:48
  37.6 4.6 %shard_map.116 = (bf16[640,2048]{1,0:T(8,128)(2,1)S(1)}, f32[256,2048]{1,0:T(8,128)S(1)}, f32[256,128]{1,0:T(8,128)S(1)}) custom-call(s32[8,2]{1,0:T(8,128)S(1)} %copy.12.r_1_.r_0_, bf16[256,1024]{1,0:T(8,128)(2,1)S(1)} %collective-permute-done.3.r_4_.r_1_, bf16[256,1024]{1,0:T(8,128)(2,1)S(1)} %collective-permute-done.8.r_4_.r_2_, ...), custom_call_target="tpu_custom_call" | custom-call | flops 3355443200 | bytes 1048576 | tf_op jit(solution)/shard_map/pallas_call | solution.py:24
  42.3 6.1 %collective-permute-done.6.r_1_ = bf16[128,1024]{1,0:T(8,128)(2,1)S(1)} collective-permute-done((bf16[128,1024]{1,0:T(8,128)(2,1)S(1)}, bf16[128,1024]{1,0:T(8,128)(2,1)S(1)}, u32[]{:S(2)}, u32[]{:S(2)}) %collective-permute-start.6) | collective-permute-done | bytes 262176 | tf_op jit(solution)/shard_map/ppermute | solution.py:48
  48.9 2.9 %shard_map.117 = (bf16[384,2048]{1,0:T(8,128)(2,1)S(1)}, f32[256,2048]{1,0:T(8,128)S(1)}, f32[256,128]{1,0:T(8,128)S(1)}) custom-call(bf16[128,1024]{1,0:T(8,128)(2,1)S(1)} %collective-permute-done.5.r_0_, bf16[128,1024]{1,0:T(8,128)(2,1)S(1)} %collective-permute-done.6.r_1_, bf16[128,1024]{1,0:T(8,128)(2,1)S(1)} %collective-permute-done.7.r_2_, ...), custom_call_target="tpu_custom_call" | custom-call | flops 2013265920 | bytes 1048576 | tf_op jit(solution)/shard_map/pallas_call | solution.py:24
  51.8 4.1 %shard_map.118 = (bf16[256,1024]{1,0:T(8,128)(2,1)}, f32[256,1024]{1,0:T(8,128)S(1)}, bf16[256,2048]{1,0:T(8,128)(2,1)S(1)}) custom-call(s32[1]{0:T(128)} %bitcast.16.live_ref, f32[256,2048]{1,0:T(8,128)S(1)} %get-tuple-element.47.acc_ref, f32[256,128]{1,0:T(8,128)S(1)} %get-tuple-element.48.deg_ref, f32[256,1024]{1,0:T(8,128)S(1)} %get-tuple-element.49.self_ref, ...), custom_call_target="tpu_custom_call" | custom-call | flops 2684354560 | bytes 1048576 | tf_op jit(solution)/shard_map/pallas_call | solution.py:24
  55.9 2.2 %shard_map.122 = (bf16[128,1024]{1,0:T(8,128)(2,1)S(1)}, bf16[128,1024]{1,0:T(8,128)(2,1)S(1)}, bf16[128,1024]{1,0:T(8,128)(2,1)S(1)}) custom-call(bf16[1024,256]{1,0:T(8,128)(2,1)S(1)} %get-tuple-element.52.r_0_, bf16[256,2048]{1,0:T(8,128)(2,1)S(1)} %get-tuple-element.53.r_1_, bf16[640,2048]{1,0:T(8,128)(2,1)S(1)} %get-tuple-element.54.r_2_, ...), custom_call_target="tpu_custom_call" | custom-call | flops 2013265920 | bytes 1048576 | tf_op jit(solution)/shard_map/pallas_call | solution.py:24
  58.1 2.4 %collective-permute-start.16 = (bf16[128,1024]{1,0:T(8,128)(2,1)S(1)}, bf16[128,1024]{1,0:T(8,128)(2,1)S(1)}, u32[]{:S(2)}, u32[]{:S(2)}) collective-permute-start(bf16[128,1024]{1,0:T(8,128)(2,1)S(1)} %get-tuple-element.62), channel_id=1, source_target_pairs={{0,3},{1,0},{2,1},{3,2},{4,7},{5,4},{6,5},{7,6},{8,11},{9,8},{10,9... | collective-permute-start | bytes 786440 | tf_op jit(solution)/shard_map/ppermute | solution.py:48
  60.5 2.2 %shard_map.120 = (bf16[128,1024]{1,0:T(8,128)(2,1)S(1)}, bf16[128,1024]{1,0:T(8,128)(2,1)S(1)}, bf16[128,1024]{1,0:T(8,128)(2,1)S(1)}) custom-call(bf16[1024,256]{1,0:T(8,128)(2,1)S(1)} %get-tuple-element.52.r_0_, bf16[256,2048]{1,0:T(8,128)(2,1)S(1)} %get-tuple-element.53.r_1_, bf16[384,2048]{1,0:T(8,128)(2,1)S(1)} %get-tuple-element.56.r_2_, ...), custom_call_target="tpu_custom_call" | custom-call | flops 2013265920 | bytes 1048576 | tf_op jit(solution)/shard_map/pallas_call | solution.py:24
  63.7 2.0 %collective-permute-start.12 = (bf16[128,1024]{1,0:T(8,128)(2,1)S(1)}, bf16[128,1024]{1,0:T(8,128)(2,1)S(1)}, u32[]{:S(2)}, u32[]{:S(2)}) collective-permute-start(bf16[128,1024]{1,0:T(8,128)(2,1)S(1)} %get-tuple-element.57), channel_id=1, source_target_pairs={{0,3},{1,0},{2,1},{3,2},{4,7},{5,4},{6,5},{7,6},{8,11},{9,8},{10,9... | collective-permute-start | bytes 786440 | tf_op jit(solution)/shard_map/ppermute | solution.py:48
  65.7 1.8 %collective-permute-start.13 = (bf16[128,1024]{1,0:T(8,128)(2,1)S(1)}, bf16[128,1024]{1,0:T(8,128)(2,1)S(1)}, u32[]{:S(2)}, u32[]{:S(2)}) collective-permute-start(bf16[128,1024]{1,0:T(8,128)(2,1)S(1)} %get-tuple-element.58), channel_id=1, source_target_pairs={{0,2},{1,3},{2,0},{3,1},{4,6},{5,7},{6,4},{7,5},{8,10},{9,11},{10,... | collective-permute-start | bytes 786440 | tf_op jit(solution)/shard_map/ppermute | solution.py:48
  67.5 1.6 %shard_map.119 = (bf16[128,1024]{1,0:T(8,128)(2,1)S(1)}, bf16[128,1024]{1,0:T(8,128)(2,1)S(1)}) custom-call(bf16[1024,256]{1,0:T(8,128)(2,1)S(1)} %get-tuple-element.52.r_0_, bf16[256,2048]{1,0:T(8,128)(2,1)S(1)} %get-tuple-element.53.r_1_, bf16[640,2048]{1,0:T(8,128)(2,1)S(1)} %get-tuple-element.54.r_2_, bf16[1024,2048]{1,0:T(8,128)(2,1)S(1)} %copy-done), custom_call_target="tpu_custom_call" | custom-call | flops 1342177280 | bytes 1048576 | tf_op jit(solution)/shard_map/pallas_call | solution.py:24
  69.2 7.7 %collective-permute-done.18.r_8_ = bf16[128,1024]{1,0:T(8,128)(2,1)S(1)} collective-permute-done((bf16[128,1024]{1,0:T(8,128)(2,1)S(1)}, bf16[128,1024]{1,0:T(8,128)(2,1)S(1)}, u32[]{:S(2)}, u32[]{:S(2)}) %collective-permute-start.18) | collective-permute-done | bytes 262176 | tf_op jit(solution)/shard_map/ppermute | solution.py:48
  77.8 3.6 %collective-permute-start.19 = (bf16[256,1024]{1,0:T(8,128)(2,1)S(1)}, bf16[256,1024]{1,0:T(8,128)(2,1)S(1)}, u32[]{:S(2)}, u32[]{:S(2)}) collective-permute-start(bf16[256,1024]{1,0:T(8,128)(2,1)S(1)} %shard_map.123), channel_id=1, source_target_pairs={{0,124},{1,125},{2,126},{3,127},{4,64},{5,65},{6,66},{7,67},{8,68}... | collective-permute-start | bytes 1572872 | tf_op jit(solution)/shard_map/ppermute | solution.py:42
  81.5 5.5 %collective-permute-done.14.r_8_ = bf16[128,1024]{1,0:T(8,128)(2,1)S(1)} collective-permute-done((bf16[128,1024]{1,0:T(8,128)(2,1)S(1)}, bf16[128,1024]{1,0:T(8,128)(2,1)S(1)}, u32[]{:S(2)}, u32[]{:S(2)}) %collective-permute-start.14) | collective-permute-done | bytes 262176 | tf_op jit(solution)/shard_map/ppermute | solution.py:48
  87.0 1.1 shard_map.121
  89.4 7.4 %collective-permute-done.19.b_ref = bf16[256,1024]{1,0:T(8,128)(2,1)S(1)} collective-permute-done((bf16[256,1024]{1,0:T(8,128)(2,1)S(1)}, bf16[256,1024]{1,0:T(8,128)(2,1)S(1)}, u32[]{:S(2)}, u32[]{:S(2)}) %collective-permute-start.19) | collective-permute-done | bytes 524320 | tf_op jit(solution)/shard_map/ppermute | solution.py:42
  96.8 12.0 %collective-permute-done.20.c_ref = bf16[256,1024]{1,0:T(8,128)(2,1)S(1)} collective-permute-done((bf16[256,1024]{1,0:T(8,128)(2,1)S(1)}, bf16[256,1024]{1,0:T(8,128)(2,1)S(1)}, u32[]{:S(2)}, u32[]{:S(2)}) %collective-permute-start.20) | collective-permute-done | bytes 524320 | tf_op jit(solution)/shard_map/ppermute | solution.py:42
  108.7 1.1 shard_map.124
  (45 shorter events, 8.7 us)
Async XLA Ops:
  2.5 18.7 %collective-permute-start.8 = (bf16[256,1024]{1,0:T(8,128)(2,1)S(1)}, bf16[256,1024]{1,0:T(8,128)(2,1)S(1)}, u32[]{:S(2)}, u32[]{:S(2)}) collective-permute-start(bf16[256,1024]{1,0:T(8,128)(2,1)S(1)} %broadcast_select_fusion), channel_id=1, source_target_pairs={{0,68},{1,69},{2,70},{3,71},{4,72},{5,73},{6,74},{7,75},{8,76},{9,... | collective-permute-start | bytes 1572872 | tf_op jit(solution)/shard_map/ppermute | solution.py:42
  5.1 5.5 %collective-permute-start.2 = (s32[1,128]{1,0:T(1,128)S(1)}, s32[1,128]{1,0:T(1,128)S(1)}, u32[]{:S(2)}, u32[]{:S(2)}) collective-permute-start(s32[1,128]{1,0:T(1,128)S(1)} %pad_bitcast_fusion), channel_id=1, source_target_pairs={{0,1},{1,2},{2,3},{3,0},{4,5},{5,6},{6,7},{7,4},{8,9},{9,10},{10,1... | collective-permute-start | bytes 1544 | tf_op jit(solution)/shard_map/ppermute | solution.py:48
  6.3 4.3 %collective-permute-start.1 = (s32[1,128]{1,0:T(1,128)S(1)}, s32[1,128]{1,0:T(1,128)S(1)}, u32[]{:S(2)}, u32[]{:S(2)}) collective-permute-start(s32[1,128]{1,0:T(1,128)S(1)} %pad_bitcast_fusion), channel_id=1, source_target_pairs={{0,2},{1,3},{2,0},{3,1},{4,6},{5,7},{6,4},{7,5},{8,10},{9,11},{10,... | collective-permute-start | bytes 1544 | tf_op jit(solution)/shard_map/ppermute | solution.py:48
  8.8 2.7 %collective-permute-start = (s32[1,128]{1,0:T(1,128)S(1)}, s32[1,128]{1,0:T(1,128)S(1)}, u32[]{:S(2)}, u32[]{:S(2)}) collective-permute-start(s32[1,128]{1,0:T(1,128)S(1)} %pad_bitcast_fusion), channel_id=1, source_target_pairs={{0,3},{1,0},{2,1},{3,2},{4,7},{5,4},{6,5},{7,6},{8,11},{9,8},{10,9... | collective-permute-start | bytes 1544 | tf_op jit(solution)/shard_map/ppermute | solution.py:48
  9.9 15.5 %collective-permute-start.3 = (bf16[256,1024]{1,0:T(8,128)(2,1)S(1)}, bf16[256,1024]{1,0:T(8,128)(2,1)S(1)}, u32[]{:S(2)}, u32[]{:S(2)}) collective-permute-start(bf16[256,1024]{1,0:T(8,128)(2,1)S(1)} %broadcast_select_fusion), channel_id=1, source_target_pairs={{0,64},{1,65},{2,66},{3,67},{4,68},{5,69},{6,70},{7,71},{8,72},{9,... | collective-permute-start | bytes 1572872 | tf_op jit(solution)/shard_map/ppermute | solution.py:42
  11.4 15.6 %collective-permute-start.4 = (bf16[256,1024]{1,0:T(8,128)(2,1)S(1)}, bf16[256,1024]{1,0:T(8,128)(2,1)S(1)}, u32[]{:S(2)}, u32[]{:S(2)}) collective-permute-start(bf16[256,1024]{1,0:T(8,128)(2,1)S(1)} %broadcast_select_fusion), channel_id=1, source_target_pairs={{0,72},{1,73},{2,74},{3,75},{4,76},{5,77},{6,78},{7,79},{8,80},{9,... | collective-permute-start | bytes 1572872 | tf_op jit(solution)/shard_map/ppermute | solution.py:42
  15.6 1.6 %copy-start.1 = (bf16[1024,1024]{1,0:T(8,128)(2,1)S(1)}, bf16[1024,1024]{1,0:T(8,128)(2,1)}, u32[]{:S(2)}) copy-start(bf16[1024,1024]{1,0:T(8,128)(2,1)} %sw_ref.1) | copy-start | bytes 6291460
  17.2 1.6 %copy-start.4 = (s32[1,256,2048]{2,1,0:T(8,128)S(1)}, s32[1,256,2048]{2,1,0:T(8,128)}, u32[]{:S(2)}) copy-start(s32[1,256,2048]{2,1,0:T(8,128)} %param.13) | copy-start | bytes 6291460
  18.8 1.0 copy-start.5
  19.8 17.8 %copy-start = (bf16[1024,2048]{1,0:T(8,128)(2,1)S(1)}, bf16[1024,2048]{1,0:T(8,128)(2,1)}, u32[]{:S(2)}) copy-start(bf16[1024,2048]{1,0:T(8,128)(2,1)} %r_3_.7) | copy-start | bytes 12582916
  21.2 16.5 %copy-start.7 = (f32[2048]{0:T(1024)S(1)}, f32[2048]{0:T(1024)}, u32[]{:S(2)}) copy-start(f32[2048]{0:T(1024)} %param.16) | copy-start | bytes 24580
  21.8 9.1 %collective-permute-start.9 = (bf16[128,1024]{1,0:T(8,128)(2,1)S(1)}, bf16[128,1024]{1,0:T(8,128)(2,1)S(1)}, u32[]{:S(2)}, u32[]{:S(2)}) collective-permute-start(bf16[128,1024]{1,0:T(8,128)(2,1)S(1)} %get-tuple-element.42), channel_id=1, source_target_pairs={{0,1},{1,2},{2,3},{3,0},{4,5},{5,6},{6,7},{7,4},{8,9},{9,10},{10,1... | collective-permute-start | bytes 786440 | tf_op jit(solution)/shard_map/ppermute | solution.py:48
  21.9 15.7 %collective-permute-start.10 = (bf16[128,1024]{1,0:T(8,128)(2,1)S(1)}, bf16[128,1024]{1,0:T(8,128)(2,1)S(1)}, u32[]{:S(2)}, u32[]{:S(2)}) collective-permute-start(bf16[128,1024]{1,0:T(8,128)(2,1)S(1)} %get-tuple-element.43), channel_id=1, source_target_pairs={{0,2},{1,3},{2,0},{3,1},{4,6},{5,7},{6,4},{7,5},{8,10},{9,11},{10,... | collective-permute-start | bytes 786440 | tf_op jit(solution)/shard_map/ppermute | solution.py:48
  25.4 12.2 %collective-permute-start.11 = (bf16[128,1024]{1,0:T(8,128)(2,1)S(1)}, bf16[128,1024]{1,0:T(8,128)(2,1)S(1)}, u32[]{:S(2)}, u32[]{:S(2)}) collective-permute-start(bf16[128,1024]{1,0:T(8,128)(2,1)S(1)} %get-tuple-element.44), channel_id=1, source_target_pairs={{0,3},{1,0},{2,1},{3,2},{4,7},{5,4},{6,5},{7,6},{8,11},{9,8},{10,9... | collective-permute-start | bytes 786440 | tf_op jit(solution)/shard_map/ppermute | solution.py:48
  27.7 14.6 %collective-permute-start.5 = (bf16[128,1024]{1,0:T(8,128)(2,1)S(1)}, bf16[128,1024]{1,0:T(8,128)(2,1)S(1)}, u32[]{:S(2)}, u32[]{:S(2)}) collective-permute-start(bf16[128,1024]{1,0:T(8,128)(2,1)S(1)} %get-tuple-element.38), channel_id=1, source_target_pairs={{0,1},{1,2},{2,3},{3,0},{4,5},{5,6},{6,7},{7,4},{8,9},{9,10},{10,1... | collective-permute-start | bytes 786440 | tf_op jit(solution)/shard_map/ppermute | solution.py:48
  27.8 20.6 %collective-permute-start.6 = (bf16[128,1024]{1,0:T(8,128)(2,1)S(1)}, bf16[128,1024]{1,0:T(8,128)(2,1)S(1)}, u32[]{:S(2)}, u32[]{:S(2)}) collective-permute-start(bf16[128,1024]{1,0:T(8,128)(2,1)S(1)} %get-tuple-element.39), channel_id=1, source_target_pairs={{0,2},{1,3},{2,0},{3,1},{4,6},{5,7},{6,4},{7,5},{8,10},{9,11},{10,... | collective-permute-start | bytes 786440 | tf_op jit(solution)/shard_map/ppermute | solution.py:48
  30.9 18.0 %collective-permute-start.7 = (bf16[128,1024]{1,0:T(8,128)(2,1)S(1)}, bf16[128,1024]{1,0:T(8,128)(2,1)S(1)}, u32[]{:S(2)}, u32[]{:S(2)}) collective-permute-start(bf16[128,1024]{1,0:T(8,128)(2,1)S(1)} %get-tuple-element.40), channel_id=1, source_target_pairs={{0,3},{1,0},{2,1},{3,2},{4,7},{5,4},{6,5},{7,6},{8,11},{9,8},{10,9... | collective-permute-start | bytes 786440 | tf_op jit(solution)/shard_map/ppermute | solution.py:48
  48.9 2.9 %copy-start.2 = (bf16[1024,1024]{1,0:T(8,128)(2,1)S(1)}, bf16[1024,1024]{1,0:T(8,128)(2,1)}, u32[]{:S(2)}) copy-start(bf16[1024,1024]{1,0:T(8,128)(2,1)} %sw_ref.1) | copy-start | bytes 6291460
  48.9 2.9 %copy-start.3 = (bf16[2048,1024]{1,0:T(8,128)(2,1)S(1)}, bf16[2048,1024]{1,0:T(8,128)(2,1)}, u32[]{:S(2)}) copy-start(bf16[2048,1024]{1,0:T(8,128)(2,1)} %nb_ref.1) | copy-start | bytes 12582916
  48.9 2.9 %copy-start.6 = (bf16[1,256,1024]{2,1,0:T(8,128)(2,1)S(1)}, bf16[1,256,1024]{2,1,0:T(8,128)(2,1)}, u32[]{:S(2)}) copy-start(bf16[1,256,1024]{2,1,0:T(8,128)(2,1)} %param.14) | copy-start | bytes 1572868
  48.9 2.9 %copy-start.8 = (f32[1024]{0:T(1024)S(1)}, f32[1024]{0:T(1024)}, u32[]{:S(2)}) copy-start(f32[1024]{0:T(1024)} %param.19) | copy-start | bytes 12292
  58.1 9.4 %collective-permute-start.16 = (bf16[128,1024]{1,0:T(8,128)(2,1)S(1)}, bf16[128,1024]{1,0:T(8,128)(2,1)S(1)}, u32[]{:S(2)}, u32[]{:S(2)}) collective-permute-start(bf16[128,1024]{1,0:T(8,128)(2,1)S(1)} %get-tuple-element.62), channel_id=1, source_target_pairs={{0,3},{1,0},{2,1},{3,2},{4,7},{5,4},{6,5},{7,6},{8,11},{9,8},{10,9... | collective-permute-start | bytes 786440 | tf_op jit(solution)/shard_map/ppermute | solution.py:48
  60.5 8.7 %collective-permute-start.17 = (bf16[128,1024]{1,0:T(8,128)(2,1)S(1)}, bf16[128,1024]{1,0:T(8,128)(2,1)S(1)}, u32[]{:S(2)}, u32[]{:S(2)}) collective-permute-start(bf16[128,1024]{1,0:T(8,128)(2,1)S(1)} %get-tuple-element.63), channel_id=1, source_target_pairs={{0,2},{1,3},{2,0},{3,1},{4,6},{5,7},{6,4},{7,5},{8,10},{9,11},{10,... | collective-permute-start | bytes 786440 | tf_op jit(solution)/shard_map/ppermute | solution.py:48
  62.8 14.1 %collective-permute-start.18 = (bf16[128,1024]{1,0:T(8,128)(2,1)S(1)}, bf16[128,1024]{1,0:T(8,128)(2,1)S(1)}, u32[]{:S(2)}, u32[]{:S(2)}) collective-permute-start(bf16[128,1024]{1,0:T(8,128)(2,1)S(1)} %get-tuple-element.64), channel_id=1, source_target_pairs={{0,1},{1,2},{2,3},{3,0},{4,5},{5,6},{6,7},{7,4},{8,9},{9,10},{10,1... | collective-permute-start | bytes 786440 | tf_op jit(solution)/shard_map/ppermute | solution.py:48
  63.7 17.8 %collective-permute-start.12 = (bf16[128,1024]{1,0:T(8,128)(2,1)S(1)}, bf16[128,1024]{1,0:T(8,128)(2,1)S(1)}, u32[]{:S(2)}, u32[]{:S(2)}) collective-permute-start(bf16[128,1024]{1,0:T(8,128)(2,1)S(1)} %get-tuple-element.57), channel_id=1, source_target_pairs={{0,3},{1,0},{2,1},{3,2},{4,7},{5,4},{6,5},{7,6},{8,11},{9,8},{10,9... | collective-permute-start | bytes 786440 | tf_op jit(solution)/shard_map/ppermute | solution.py:48
  65.7 15.7 %collective-permute-start.13 = (bf16[128,1024]{1,0:T(8,128)(2,1)S(1)}, bf16[128,1024]{1,0:T(8,128)(2,1)S(1)}, u32[]{:S(2)}, u32[]{:S(2)}) collective-permute-start(bf16[128,1024]{1,0:T(8,128)(2,1)S(1)} %get-tuple-element.58), channel_id=1, source_target_pairs={{0,2},{1,3},{2,0},{3,1},{4,6},{5,7},{6,4},{7,5},{8,10},{9,11},{10,... | collective-permute-start | bytes 786440 | tf_op jit(solution)/shard_map/ppermute | solution.py:48
  67.5 19.5 %collective-permute-start.14 = (bf16[128,1024]{1,0:T(8,128)(2,1)S(1)}, bf16[128,1024]{1,0:T(8,128)(2,1)S(1)}, u32[]{:S(2)}, u32[]{:S(2)}) collective-permute-start(bf16[128,1024]{1,0:T(8,128)(2,1)S(1)} %get-tuple-element.59), channel_id=1, source_target_pairs={{0,1},{1,2},{2,3},{3,0},{4,5},{5,6},{6,7},{7,4},{8,9},{9,10},{10,1... | collective-permute-start | bytes 786440 | tf_op jit(solution)/shard_map/ppermute | solution.py:48
  77.8 19.0 %collective-permute-start.19 = (bf16[256,1024]{1,0:T(8,128)(2,1)S(1)}, bf16[256,1024]{1,0:T(8,128)(2,1)S(1)}, u32[]{:S(2)}, u32[]{:S(2)}) collective-permute-start(bf16[256,1024]{1,0:T(8,128)(2,1)S(1)} %shard_map.123), channel_id=1, source_target_pairs={{0,124},{1,125},{2,126},{3,127},{4,64},{5,65},{6,66},{7,67},{8,68}... | collective-permute-start | bytes 1572872 | tf_op jit(solution)/shard_map/ppermute | solution.py:42
  88.1 8.7 %collective-permute-start.15 = (bf16[256,1024]{1,0:T(8,128)(2,1)S(1)}, bf16[256,1024]{1,0:T(8,128)(2,1)S(1)}, u32[]{:S(2)}, u32[]{:S(2)}) collective-permute-start(bf16[256,1024]{1,0:T(8,128)(2,1)S(1)} %get-tuple-element.60), channel_id=1, source_target_pairs={{0,64},{1,65},{2,66},{3,67},{4,68},{5,69},{6,70},{7,71},{8,72},{9,... | collective-permute-start | bytes 1572872 | tf_op jit(solution)/shard_map/ppermute | solution.py:42
  88.8 20.0 %collective-permute-start.20 = (bf16[256,1024]{1,0:T(8,128)(2,1)S(1)}, bf16[256,1024]{1,0:T(8,128)(2,1)S(1)}, u32[]{:S(2)}, u32[]{:S(2)}) collective-permute-start(bf16[256,1024]{1,0:T(8,128)(2,1)S(1)} %get-tuple-element.65), channel_id=1, source_target_pairs={{0,120},{1,121},{2,122},{3,123},{4,124},{5,125},{6,126},{7,127},{8... | collective-permute-start | bytes 1572872 | tf_op jit(solution)/shard_map/ppermute | solution.py:42

commit v4 on v3

--- a/solution.py
+++ b/solution.py
@@ -8,6 +8,7 @@
 EPS = 1e-06
 DEAD = 16384.0
 LIMIT = 8192.0
+MICROSECOND = 10**9
 LINE = 4
 F32 = jnp.float32
 BF16 = jnp.bfloat16
@@ -48,6 +49,17 @@
     return lax.ppermute(x, "dom", pairs)
 
 
+def straight(x, d, back=False):
+    count = lax.axis_size("dom")
+    pairs = []
+    for s in range(2):
+        for j in range(count):
+            to = j + d if j % LINE + d < LINE else j + d + LINE
+            pair = (s * count + j, (1 - s) * count + to % count)
+            pairs.append(pair[::-1] if back else pair)
+    return lax.ppermute(x, ("side", "dom"), pairs)
+
+
 def near(p, d):
     return jnp.where(p >= d, d + LINE, d)
 
@@ -60,28 +72,15 @@
     return pl.ds(pl.multiple_of(index * block, block), block)
 
 
-def pick_near_kernel(block, place_ref, m1, m2, m3, below_ref, _, *outs):
+def pick_kernel(block, offset, place_ref, m1, m2, m3, rows_ref, *refs):
+    outs = refs[-3:]
     for d, (meta, out) in enumerate(zip((m1, m2, m3), outs), 1):
         p = lax.rem(place_ref[0] + d, LINE)
-        out[...] = below_ref[at_block(meta[0, near(p, d)], block), :]
-
-
-def pick_far_kernel(block, place_ref, m1, m2, m3, same_ref, below_ref, *outs):
-    for d, (meta, out) in enumerate(zip((m1, m2, m3), outs), 1):
-        p = lax.rem(place_ref[0] + d, LINE)
-        at = at_block(meta[0, far(p, d)], block)
-
-        @pl.when(p >= d)
-        def _():
-            out[...] = same_ref[at, :]
-
-        @pl.when(p < d)
-        def _():
-            out[...] = below_ref[at, :]
+        out[...] = rows_ref[at_block(meta[0, offset(p, d)], block), :]
 
 
 def slots(p):
-    return [0, LINE] + [near(p, d) for d in range(1, LINE)] + [far(p, d) for d in range(1, LINE)]
+    return [0, LINE] + [far(p, d) for d in range(1, LINE)] + [near(p, d) for d in range(1, LINE)]
 
 
 def tiles_kernel(block, place_ref, lists_ref, counts_ref, x_ref, sw_ref, tiles_ref, tiles_t_ref, self_ref):
@@ -154,44 +153,39 @@
         gself_ref[:, cols] = dot(g, sw_ref[cols, :], 1, 1)
 
 
-def back_kernel(block, first, last, skip, *refs):
-    size = last - first
-    tt_ref, gpool_ref, msg_ref, q_ref = refs[:4]
-    outs = refs[4 : 4 + size]
-    gn_ref = refs[4 + size]
+def back_dot(block, first, last, skip, tt_ref, gpool_ref, msg_ref, q_ref, gn_ref, store):
     tt = tt_ref[first * block : last * block, :]
+    at = slice(skip * block, (skip + last - first) * block)
     step = 512
     for n in range(gpool_ref.shape[1] // step):
         cols = slice(n * step, (n + 1) * step)
-        g = dot(tt, gpool_ref[:, cols])
-        live = msg_ref[skip * block : (skip + size) * block, cols].astype(F32) > 0
-        gn_ref[:, cols] = jnp.where(live, g, 0.0).astype(BF16)
+        live = msg_ref[at, cols].astype(F32) > 0
+        gn_ref[:, cols] = jnp.where(live, dot(tt, gpool_ref[:, cols]), 0.0).astype(BF16)
     gn = gn_ref[...]
     for n in range(q_ref.shape[0] // step):
         cols = slice(n * step, (n + 1) * step)
-        part = dot(gn, q_ref[cols, :], 1, 1).astype(BF16)
+        store(cols, dot(gn, q_ref[cols, :], 1, 1))
+
+
+def back_kernel(block, first, last, skip, tt_ref, gpool_ref, msg_ref, q_ref, _, *refs):
+    outs, gn_ref = refs[:-1], refs[-1]
+
+    def store(cols, part):
         for i, out in enumerate(outs):
-            out[:, cols] = part[i * block : (i + 1) * block]
-
-
-def sum_far_kernel(block, place_ref, lists_ref, m1, m2, m3, own_ref, c1, c2, c3, same_ref, below_ref, same, below):
-    same[...] = jnp.zeros_like(same)
-    below[...] = jnp.zeros_like(below)
-    same[at_block(lists_ref[0, 1], block), :] = own_ref[...].astype(F32)
-    for d, (meta, part) in enumerate(zip((m1, m2, m3), (c1, c2, c3)), 1):
-        p = lax.rem(place_ref[0] + d, LINE)
-        at = at_block(meta[0, far(p, d)], block)
-
-        @pl.when(p >= d)
-        def _():
-            same[at, :] += part[...].astype(F32)
-
-        @pl.when(p < d)
-        def _():
-            below[at, :] += part[...].astype(F32)
-
-    same_ref[...] = same[...].astype(BF16)
-    below_ref[...] = below[...].astype(BF16)
+            out[:, cols] = part[i * block : (i + 1) * block].astype(BF16)
+
+    back_dot(block, first, last, skip, tt_ref, gpool_ref, msg_ref, q_ref, gn_ref, store)
+
+
+def back_own_kernel(block, lists_ref, tt_ref, gpool_ref, msg_ref, q_ref, _, same_ref, below_ref, gn_ref):
+    same_ref[...] = jnp.zeros_like(same_ref)
+    at = at_block(lists_ref[0, 1], block)
+
+    def store(cols, part):
+        same_ref[at, cols] = part[:block].astype(BF16)
+        below_ref[:, cols] = part[block:].astype(BF16)
+
+    back_dot(block, 0, 2, 0, tt_ref, gpool_ref, msg_ref, q_ref, gn_ref, store)
 
 
 def sum_near_kernel(block, place_ref, lists_ref, m1, m2, m3, own_ref, d1, d2, d3, out_ref, total):
@@ -203,8 +197,15 @@
     out_ref[...] = total[...].astype(BF16)
 
 
-def finish_kernel(live_ref, gself_ref, a_ref, b_ref, c_ref, out_ref):
-    total = gself_ref[...] + a_ref[...].astype(F32) + b_ref[...].astype(F32) + c_ref[...].astype(F32)
+def place_kernel(block, place_ref, m1, m2, m3, gself_ref, c1, c2, c3, total_ref):
+    total_ref[...] = gself_ref[...]
+    for d, (meta, part) in enumerate(zip((m1, m2, m3), (c1, c2, c3)), 1):
+        p = lax.rem(place_ref[0] + d, LINE)
+        total_ref[at_block(meta[0, far(p, d)], block), :] += part[...].astype(F32)
+
+
+def finish_kernel(live_ref, total_ref, same_ref, below_ref, out_ref):
+    total = total_ref[...] + same_ref[...].astype(F32) + below_ref[...].astype(F32)
     keep = lax.broadcasted_iota(jnp.int32, (total.shape[0], 1), 0) < live_ref[0]
     out_ref[...] = jnp.where(keep, total, 0.0).astype(BF16)
 
@@ -221,13 +222,23 @@
     keep = lax.broadcasted_iota(jnp.int32, (rows, 1), 0) < live[0]
     marked = jnp.where(keep, x, jnp.asarray(DEAD, BF16))
     row = jnp.pad(lists[:, 1], (0, 128 - reach))[None]
+    steps = range(1, LINE)
+    one, two = ((block, width), BF16), ((rows, width), BF16)
+
+    def pick(offset, metas, held, after):
+        return call(
+            lambda *r: pick_kernel(block, offset, *r),
+            [one] * len(steps),
+            (place, *metas, held, *after),
+            [SMEM] * (1 + len(steps)) + [VMEM] + [HELD] * len(after),
+        )
+
     below = swap_rows(marked, LINE)
+    far_metas = [straight(row, d, back=True) for d in steps]
+    near_metas = [along(row, -d) for d in steps]
     same = swap_rows(marked, 0)
-    metas = [along(row, -d) for d in range(1, LINE)]
-    later, *metas = lax.optimization_barrier((marked, *metas))
-    below2 = swap_rows(later, 2 * LINE)
-    one = ((block, width), BF16)
-    three = [SMEM] * 4
+    far_sent = pick(far, far_metas, marked, (same, *near_metas))
+    got_far = [straight(b, d) for d, b in zip(steps, far_sent)]
     tiles, tiles_t, self_pre = call(
         lambda *r: tiles_kernel(block, *r),
         [((rows, reach * block), BF16), ((reach * block, rows), BF16), ((rows, width), F32)],
@@ -235,18 +246,9 @@
         [SMEM] * 2 + [VMEM] * 3,
         flops=2 * rows * width * width,
     )
-    picked = call(
-        lambda *r: pick_near_kernel(block, *r), [one] * 3, (place, *metas, below, tiles), three + [VMEM, HELD]
-    )
-    got_near = [along(b, d) for d, b in enumerate(picked, 1)]
-    picked = call(
-        lambda *r: pick_far_kernel(block, *r),
-        [one] * 3,
-        (place, *metas, same, below2),
-        three + [VMEM] * 2,
-    )
-    got_far = [along(b, d) for d, b in enumerate(picked, 1)]
-    split = 2 + LINE - 1
+    near_sent = pick(near, near_metas, below, (tiles,))
+    got_near = [along(b, d) for d, b in zip(steps, near_sent)]
+    split = 1 + LINE
 
     def message(first, last, ins, specs):
         size = last - first
@@ -259,53 +261,59 @@
         )
 
     msg_a, acc, deg = message(
-        0, split, (lists, same, below, *got_near, q, qb, tiles), [SMEM] + [VMEM] * 8
-    )
-    msg_b, acc, deg = message(split, reach, (*got_far, q, qb, tiles, acc, deg), [VMEM] * 8)
+        0, split, (lists, same, below, *got_far, q, qb, tiles), [SMEM] + [VMEM] * 8
+    )
+    msg_b, acc, deg = message(split, reach, (*got_near, q, qb, tiles, acc, deg), [VMEM] * 8)
     emb, gself, gpool = call(
         layer_kernel,
-        [((rows, width), BF16), ((rows, width), F32), ((rows, hidden), BF16)],
+        [two, ((rows, width), F32), ((rows, hidden), BF16)],
         (live, acc, deg, self_pre, up, sw, nb, ob),
         [SMEM] + [VMEM] * 7,
         scratch=[pltpu.VMEM((rows, width), F32)],
         flops=2 * rows * width * (2 * hidden + width),
     )
 
-    def back(first, last, msg, skip):
+    def back(kernel, outs, first, last, msg, after, lead=()):
         size = last - first
         return call(
-            lambda *r: back_kernel(block, first, last, skip, *r),
-            [one] * size,
-            (tiles_t, gpool, msg, q),
+            kernel,
+            outs,
+            (*lead, tiles_t, gpool, msg, q, after),
+            [SMEM] * len(lead) + [VMEM] * 4 + [HELD],
             scratch=[pltpu.VMEM((size * block, hidden), BF16)],
             flops=2 * size * block * hidden * (width + rows),
         )
 
-    back_far = [along(b, -d) for d, b in enumerate(back(split, reach, msg_b, 0), 1)]
-    back_near = [along(b, -d) for d, b in enumerate(back(2, split, msg_a, 2), 1)]
-    own_same, own_below = back(0, 2, msg_a, 0)
-    two = ((rows, width), BF16)
+    near_back = back(
+        lambda *r: back_kernel(block, split, reach, 0, *r), [one] * 3, split, reach, msg_b, gself
+    )
+    back_near = [along(b, -d) for d, b in zip(steps, near_back)]
+    far_back = back(
+        lambda *r: back_kernel(block, 2, split, 2, *r), [one] * 3, 2, split, msg_a, near_back[0]
+    )
+    back_far = [straight(b, d, back=True) for d, b in zip(steps, far_back)]
+    own_same, own_below = back(
+        lambda *r: back_own_kernel(block, *r), [two, one], 0, 2, msg_a, far_back[0], (lists,)
+    )
+    g_same = swap_rows(own_same, 0)
     total = pltpu.VMEM((rows, width), F32)
-    sum_same, sum_below2 = call(
-        lambda *r: sum_far_kernel(block, *r),
-        [two, two],
-        (place, lists, *metas, own_same, *back_far),
-        [SMEM] * 5 + [VMEM] * 4,
-        scratch=[total, total],
-    )
-    g_below2 = swap_rows(sum_below2, -2 * LINE)
-    g_same = swap_rows(sum_same, 0)
     (sum_below,) = call(
         lambda *r: sum_near_kernel(block, *r),
         [two],
-        (place, lists, *metas, own_below, *back_near),
+        (place, lists, *near_metas, own_below, *back_near),
         [SMEM] * 5 + [VMEM] * 4,
         scratch=[total],
+        flops=20 * MICROSECOND,
     )
     g_below = swap_rows(sum_below, -LINE)
-    (grad,) = call(
-        finish_kernel, [two], (live, gself, g_same, g_below, g_below2), [SMEM] + [VMEM] * 4
-    )
+    (placed,) = call(
+        lambda *r: place_kernel(block, *r),
+        [((rows, width), F32)],
+        (place, *far_metas, gself, *back_far),
+        [SMEM] * 4 + [VMEM] * 4,
+        flops=20 * MICROSECOND,
+    )
+    (grad,) = call(finish_kernel, [two], (live, placed, g_same, g_below), [SMEM] + [VMEM] * 3)
     return emb[None], grad[None]
 
 

time: 110 us -> 110 us (level)
  the two profiles are of different devices: /device:TPU:57 before, /device:TPU:111 now
where the time goes in v4:
time: 110 us
  waiting for transfers between devices  45.1 us (41%)
  starting transfers between devices  33.3 us (30%)
  Pallas kernels  25.4 us (23%)
  local copies, waits for them, and re-layouts  3.43 us (3%)
  between operations  1.61 us (1%)
  other arithmetic  1.16 us (1%)
    pallas_call x12, Pallas kernels, call(): pl.pallas_call(kernel, out_shape=[jax.ShapeDtypeStruct(s, d) for s, d in...  25.4 us
    ppermute x9, waiting for transfers between devices, straight(): return lax.ppermute(x, ('side', 'dom'), pairs)  22.7 us
    ppermute x9, starting transfers between devices, straight(): return lax.ppermute(x, ('side', 'dom'), pairs)  19.4 us
    ppermute x9, waiting for transfers between devices, along(): return lax.ppermute(x, 'dom', pairs)  11.8 us
    ppermute x4, waiting for transfers between devices, swap_rows(): return lax.ppermute(x, ('side', 'dom'), pairs)  10.6 us
    ppermute x9, starting transfers between devices, along(): return lax.ppermute(x, 'dom', pairs)  8.55 us
    ppermute x4, starting transfers between devices, swap_rows(): return lax.ppermute(x, ('side', 'dom'), pairs)  5.33 us
    unnamed x18, local copies, waits for them, and re-layouts  2.66 us
  transfers between devices with their start and end apart: 22, of which 13 were waited for; matrix products, arithmetic and copies ran while one was open for 1% of the time, Pallas kernels for 14%

profile of v4, /device:TPU:111, one launch (start us, length us, event | category | flops | bytes accessed | tf_op | source)
XLA Modules:
  0.0 110.0 jit_solution(9358097249787972402)
XLA Ops:
  1.5 1.2 %broadcast_select_fusion.r_4_ = bf16[256,1024]{1,0:T(8,128)(2,1)S(1)} fusion(pred[256]{0:T(512)(128)(4,1)S(1)} %iota_compare_fusion, bf16[1,256,1024]{2,1,0:T(8,128)(2,1)} %param.10), kind=kLoop, calls=%fused_computation | loop fusion | flops 262144 | bytes 1048832 | tf_op jit(solution)/shard_map/jit(_where)/select_n | solution.py:223
  3.4 1.3 %collective-permute-start.3 = (bf16[256,1024]{1,0:T(8,128)(2,1)S(1)}, bf16[256,1024]{1,0:T(8,128)(2,1)}, u32[]{:S(2)}, u32[]{:S(2)}) collective-permute-start(bf16[256,1024]{1,0:T(8,128)(2,1)S(1)} %broadcast_select_fusion.r_4_), channel_id=1, source_target_pairs={{0,68},{1,69},{2,70},{3,71},{4,72},{5,73},{6,74},{7,75},{8,76},{9,... | collective-permute-start | bytes 1572872 | tf_op jit(solution)/shard_map/ppermute | solution.py:43
  5.9 3.4 %collective-permute-start.9 = (s32[1,128]{1,0:T(1,128)S(1)}, s32[1,128]{1,0:T(1,128)S(1)}, u32[]{:S(2)}, u32[]{:S(2)}) collective-permute-start(s32[1,128]{1,0:T(1,128)S(1)} %pad_bitcast_fusion), channel_id=1, source_target_pairs={{66,0},{67,1},{72,2},{73,3},{70,4},{71,5},{76,6},{77,7},{74,8},{75... | collective-permute-start | bytes 1544 | tf_op jit(solution)/shard_map/ppermute | solution.py:60
  9.2 1.5 %collective-permute-done.10.r_3_ = s32[1,128]{1,0:T(1,128)S(1)} collective-permute-done((s32[1,128]{1,0:T(1,128)S(1)}, s32[1,128]{1,0:T(1,128)S(1)}, u32[]{:S(2)}, u32[]{:S(2)}) %collective-permute-start.10) | collective-permute-done | bytes 544 | tf_op jit(solution)/shard_map/ppermute | solution.py:60
  10.7 2.5 %collective-permute-start.2 = (s32[1,128]{1,0:T(1,128)S(1)}, s32[1,128]{1,0:T(1,128)S(1)}, u32[]{:S(2)}, u32[]{:S(2)}) collective-permute-start(s32[1,128]{1,0:T(1,128)S(1)} %pad_bitcast_fusion), channel_id=1, source_target_pairs={{0,1},{1,2},{2,3},{3,0},{4,5},{5,6},{6,7},{7,4},{8,9},{9,10},{10,1... | collective-permute-start | bytes 1544 | tf_op jit(solution)/shard_map/ppermute | solution.py:49
  13.7 2.1 %collective-permute-done.8.r_1_ = s32[1,128]{1,0:T(1,128)S(1)} collective-permute-done((s32[1,128]{1,0:T(1,128)S(1)}, s32[1,128]{1,0:T(1,128)S(1)}, u32[]{:S(2)}, u32[]{:S(2)}) %collective-permute-start.8) | collective-permute-done | bytes 544 | tf_op jit(solution)/shard_map/ppermute | solution.py:60
  15.8 1.3 %collective-permute-done.1.r_2_.r_7_.r_3_ = s32[1,128]{1,0:T(1,128)S(1)} collective-permute-done((s32[1,128]{1,0:T(1,128)S(1)}, s32[1,128]{1,0:T(1,128)S(1)}, u32[]{:S(2)}, u32[]{:S(2)}) %collective-permute-start.1) | collective-permute-done | bytes 544 | tf_op jit(solution)/shard_map/ppermute | solution.py:49
  17.1 2.3 %collective-permute-done.r_1_.r_6_.r_2_ = s32[1,128]{1,0:T(1,128)S(1)} collective-permute-done((s32[1,128]{1,0:T(1,128)S(1)}, s32[1,128]{1,0:T(1,128)S(1)}, u32[]{:S(2)}, u32[]{:S(2)}) %collective-permute-start) | collective-permute-done | bytes 544 | tf_op jit(solution)/shard_map/ppermute | solution.py:49
  19.4 1.5 %shard_map.115 = (bf16[128,1024]{1,0:T(8,128)(2,1)}, bf16[128,1024]{1,0:T(8,128)(2,1)}, bf16[128,1024]{1,0:T(8,128)(2,1)}) custom-call(s32[1]{0:T(128)} %bitcast.1.r_0_, s32[1,128]{1,0:T(1,128)S(1)} %collective-permute-done.8.r_1_, s32[1,128]{1,0:T(1,128)S(1)} %collective-permute-done.9.r_2_, s32[1,128]{1,0:T(1,128)S(1)} %collective-permute-done.10.r_3_, ...), custom_call_target="tpu_custom_call" | custom-call | bytes 1048576 | tf_op jit(solution)/shard_map/pallas_call | solution.py:25
  20.9 5.3 %collective-permute-start.11 = (bf16[128,1024]{1,0:T(8,128)(2,1)}, bf16[128,1024]{1,0:T(8,128)(2,1)S(1)}, u32[]{:S(2)}, u32[]{:S(2)}) collective-permute-start(bf16[128,1024]{1,0:T(8,128)(2,1)} %get-tuple-element.32), channel_id=1, source_target_pairs={{0,65},{1,66},{2,67},{3,72},{4,69},{5,70},{6,71},{7,76},{8,73},{9,... | collective-permute-start | bytes 786440 | tf_op jit(solution)/shard_map/ppermute | solution.py:60
  26.2 1.4 %collective-permute-start.13 = (bf16[128,1024]{1,0:T(8,128)(2,1)}, bf16[128,1024]{1,0:T(8,128)(2,1)}, u32[]{:S(2)}, u32[]{:S(2)}) collective-permute-start(bf16[128,1024]{1,0:T(8,128)(2,1)} %get-tuple-element.34), channel_id=1, source_target_pairs={{0,67},{1,72},{2,73},{3,74},{4,71},{5,76},{6,77},{7,78},{8,75},{9,... | collective-permute-start | bytes 786440 | tf_op jit(solution)/shard_map/ppermute | solution.py:60
  27.6 1.6 %copy-done.3 = s32[1,256,2048]{2,1,0:T(8,128)S(1)} copy-done((s32[1,256,2048]{2,1,0:T(8,128)S(1)}, s32[1,256,2048]{2,1,0:T(8,128)}, u32[]{:S(2)}) %copy-start.3) | copy-done | bytes 2097176
  30.3 1.3 %shard_map.113 = (bf16[256,1024]{1,0:T(8,128)(2,1)S(1)}, bf16[1024,256]{1,0:T(8,128)(2,1)S(1)}, f32[256,1024]{1,0:T(8,128)S(1)}) custom-call(s32[1]{0:T(128)} %bitcast.1.r_0_, s32[8,2]{1,0:T(8,128)S(1)} %copy.12.r_1_.r_0_, s32[256,2048]{1,0:T(8,128)S(1)} %bitcast.19, bf16[256,1024]{1,0:T(8,128)(2,1)S(1)} %bitcast.20, bf16[1024,1024]{1,0:T(8,128)(2,1)S(1)} %copy-done.1), custom_call_target="tpu_custom_call" | custom-call | flops 536870912 | bytes 1048576 | tf_op jit(solution)/shard_map/pallas_call | solution.py:25
  32.7 2.3 %collective-permute-start.4 = (bf16[128,1024]{1,0:T(8,128)(2,1)S(1)}, bf16[128,1024]{1,0:T(8,128)(2,1)S(1)}, u32[]{:S(2)}, u32[]{:S(2)}) collective-permute-start(bf16[128,1024]{1,0:T(8,128)(2,1)S(1)} %get-tuple-element.29), channel_id=1, source_target_pairs={{0,1},{1,2},{2,3},{3,0},{4,5},{5,6},{6,7},{7,4},{8,9},{9,10},{10,1... | collective-permute-start | bytes 786440 | tf_op jit(solution)/shard_map/ppermute | solution.py:49
  35.0 1.6 %collective-permute-start.5 = (bf16[128,1024]{1,0:T(8,128)(2,1)S(1)}, bf16[128,1024]{1,0:T(8,128)(2,1)S(1)}, u32[]{:S(2)}, u32[]{:S(2)}) collective-permute-start(bf16[128,1024]{1,0:T(8,128)(2,1)S(1)} %get-tuple-element.30), channel_id=1, source_target_pairs={{0,2},{1,3},{2,0},{3,1},{4,6},{5,7},{6,4},{7,5},{8,10},{9,11},{10,... | collective-permute-start | bytes 786440 | tf_op jit(solution)/shard_map/ppermute | solution.py:49
  36.6 3.7 %collective-permute-done.11.r_3_ = bf16[128,1024]{1,0:T(8,128)(2,1)S(1)} collective-permute-done((bf16[128,1024]{1,0:T(8,128)(2,1)}, bf16[128,1024]{1,0:T(8,128)(2,1)S(1)}, u32[]{:S(2)}, u32[]{:S(2)}) %collective-permute-start.11) | collective-permute-done | bytes 262176 | tf_op jit(solution)/shard_map/ppermute | solution.py:60
  40.8 5.2 %shard_map.116 = (bf16[640,2048]{1,0:T(8,128)(2,1)S(1)}, f32[256,2048]{1,0:T(8,128)S(1)}, f32[256,128]{1,0:T(8,128)S(1)}) custom-call(s32[8,2]{1,0:T(8,128)S(1)} %copy.12.r_1_.r_0_, bf16[256,1024]{1,0:T(8,128)(2,1)S(1)} %collective-permute-done.7.r_5_.r_1_, bf16[256,1024]{1,0:T(8,128)(2,1)} %collective-permute-done.3.r_4_.r_2_, ...), custom_call_target="tpu_custom_call" | custom-call | flops 3355443200 | bytes 1048576 | tf_op jit(solution)/shard_map/pallas_call | solution.py:25
  46.0 4.7 %collective-permute-done.4.r_0_ = bf16[128,1024]{1,0:T(8,128)(2,1)S(1)} collective-permute-done((bf16[128,1024]{1,0:T(8,128)(2,1)S(1)}, bf16[128,1024]{1,0:T(8,128)(2,1)S(1)}, u32[]{:S(2)}, u32[]{:S(2)}) %collective-permute-start.4) | collective-permute-done | bytes 262176 | tf_op jit(solution)/shard_map/ppermute | solution.py:49
  50.7 3.0 %collective-permute-done.6.r_2_ = bf16[128,1024]{1,0:T(8,128)(2,1)S(1)} collective-permute-done((bf16[128,1024]{1,0:T(8,128)(2,1)S(1)}, bf16[128,1024]{1,0:T(8,128)(2,1)S(1)}, u32[]{:S(2)}, u32[]{:S(2)}) %collective-permute-start.6) | collective-permute-done | bytes 262176 | tf_op jit(solution)/shard_map/ppermute | solution.py:49
  53.8 2.9 %shard_map.117 = (bf16[384,2048]{1,0:T(8,128)(2,1)S(1)}, f32[256,2048]{1,0:T(8,128)S(1)}, f32[256,128]{1,0:T(8,128)S(1)}) custom-call(bf16[128,1024]{1,0:T(8,128)(2,1)S(1)} %collective-permute-done.4.r_0_, bf16[128,1024]{1,0:T(8,128)(2,1)S(1)} %collective-permute-done.5.r_1_, bf16[128,1024]{1,0:T(8,128)(2,1)S(1)} %collective-permute-done.6.r_2_, ...), custom_call_target="tpu_custom_call" | custom-call | flops 2013265920 | bytes 1048576 | tf_op jit(solution)/shard_map/pallas_call | solution.py:25
  56.7 4.1 %shard_map.118 = (bf16[256,1024]{1,0:T(8,128)(2,1)}, f32[256,1024]{1,0:T(8,128)S(1)}, bf16[256,2048]{1,0:T(8,128)(2,1)S(1)}) custom-call(s32[1]{0:T(128)} %bitcast.16.live_ref, f32[256,2048]{1,0:T(8,128)S(1)} %get-tuple-element.37.acc_ref, f32[256,128]{1,0:T(8,128)S(1)} %get-tuple-element.38.deg_ref, f32[256,1024]{1,0:T(8,128)S(1)} %get-tuple-element.39.self_ref, ...), custom_call_target="tpu_custom_call" | custom-call | flops 2684354560 | bytes 1048576 | tf_op jit(solution)/shard_map/pallas_call | solution.py:25
  60.8 2.2 %shard_map.119 = (bf16[128,1024]{1,0:T(8,128)(2,1)S(1)}, bf16[128,1024]{1,0:T(8,128)(2,1)S(1)}, bf16[128,1024]{1,0:T(8,128)(2,1)S(1)}) custom-call(bf16[1024,256]{1,0:T(8,128)(2,1)S(1)} %get-tuple-element.42.r_0_.r_1_, bf16[256,2048]{1,0:T(8,128)(2,1)S(1)} %get-tuple-element.43.r_1_.r_2_, bf16[384,2048]{1,0:T(8,128)(2,1)S(1)} %get-tuple-element.45.r_2_, ...), custom_call_target="tpu_custom_call" | custom-call | flops 2013265920 | bytes 1048576 | tf_op jit(solution)/shard_map/pallas_call | solution.py:25
  64.6 2.2 %shard_map.120 = (bf16[128,1024]{1,0:T(8,128)(2,1)S(1)}, bf16[128,1024]{1,0:T(8,128)(2,1)S(1)}, bf16[128,1024]{1,0:T(8,128)(2,1)S(1)}) custom-call(bf16[1024,256]{1,0:T(8,128)(2,1)S(1)} %get-tuple-element.42.r_0_.r_1_, bf16[256,2048]{1,0:T(8,128)(2,1)S(1)} %get-tuple-element.43.r_1_.r_2_, bf16[640,2048]{1,0:T(8,128)(2,1)S(1)} %get-tuple-element.44.r_2_.r_3_, ...), custom_call_target="tpu_custom_call" | custom-call | flops 2013265920 | bytes 1048576 | tf_op jit(solution)/shard_map/pallas_call | solution.py:25
  66.8 5.2 %collective-permute-start.15 = (bf16[128,1024]{1,0:T(8,128)(2,1)S(1)}, bf16[128,1024]{1,0:T(8,128)(2,1)S(1)}, u32[]{:S(2)}, u32[]{:S(2)}) collective-permute-start(bf16[128,1024]{1,0:T(8,128)(2,1)S(1)} %get-tuple-element.48), channel_id=1, source_target_pairs={{66,0},{67,1},{72,2},{73,3},{70,4},{71,5},{76,6},{77,7},{74,8},{75... | collective-permute-start | bytes 786440 | tf_op jit(solution)/shard_map/ppermute | solution.py:60
  72.0 2.2 %shard_map.122 = (bf16[256,1024]{1,0:T(8,128)(2,1)S(1)}, bf16[128,1024]{1,0:T(8,128)(2,1)S(1)}) custom-call(s32[8,2]{1,0:T(8,128)S(1)} %copy.12.r_1_.r_0_, bf16[1024,256]{1,0:T(8,128)(2,1)S(1)} %get-tuple-element.42.r_0_.r_1_, bf16[256,2048]{1,0:T(8,128)(2,1)S(1)} %get-tuple-element.43.r_1_.r_2_, bf16[640,2048]{1,0:T(8,128)(2,1)S(1)} %get-tuple-element.44.r_2_.r_3_, ...), custom_call_target="tpu_custom_call" | custom-call | flops 1342177280 | bytes 1048576 | tf_op jit(solution)/shard_map/pallas_call | solution.py:25
  74.3 3.6 %collective-permute-start.16 = (bf16[128,1024]{1,0:T(8,128)(2,1)S(1)}, bf16[128,1024]{1,0:T(8,128)(2,1)S(1)}, u32[]{:S(2)}, u32[]{:S(2)}) collective-permute-start(bf16[128,1024]{1,0:T(8,128)(2,1)S(1)} %get-tuple-element.49), channel_id=1, source_target_pairs={{67,0},{72,1},{73,2},{74,3},{71,4},{76,5},{77,6},{78,7},{75,8},{80... | collective-permute-start | bytes 786440 | tf_op jit(solution)/shard_map/ppermute | solution.py:60
  77.9 1.9 %collective-permute-start.17 = (bf16[256,1024]{1,0:T(8,128)(2,1)S(1)}, bf16[256,1024]{1,0:T(8,128)(2,1)S(1)}, u32[]{:S(2)}, u32[]{:S(2)}) collective-permute-start(bf16[256,1024]{1,0:T(8,128)(2,1)S(1)} %get-tuple-element.50), channel_id=1, source_target_pairs={{0,64},{1,65},{2,66},{3,67},{4,68},{5,69},{6,70},{7,71},{8,72},{9,... | collective-permute-start | bytes 1572872 | tf_op jit(solution)/shard_map/ppermute | solution.py:43
  81.2 1.4 %collective-permute-start.21 = (bf16[256,1024]{1,0:T(8,128)(2,1)S(1)}, bf16[256,1024]{1,0:T(8,128)(2,1)S(1)}, u32[]{:S(2)}, u32[]{:S(2)}) collective-permute-start(bf16[256,1024]{1,0:T(8,128)(2,1)S(1)} %shard_map.123), channel_id=1, source_target_pairs={{0,124},{1,125},{2,126},{3,127},{4,64},{5,65},{6,66},{7,67},{8,68}... | collective-permute-start | bytes 1572872 | tf_op jit(solution)/shard_map/ppermute | solution.py:43
  82.6 6.9 %collective-permute-done.15.r_6_ = bf16[128,1024]{1,0:T(8,128)(2,1)S(1)} collective-permute-done((bf16[128,1024]{1,0:T(8,128)(2,1)S(1)}, bf16[128,1024]{1,0:T(8,128)(2,1)S(1)}, u32[]{:S(2)}, u32[]{:S(2)}) %collective-permute-start.15) | collective-permute-done | bytes 262176 | tf_op jit(solution)/shard_map/ppermute | solution.py:60
  89.5 6.5 %collective-permute-done.16.r_7_ = bf16[128,1024]{1,0:T(8,128)(2,1)S(1)} collective-permute-done((bf16[128,1024]{1,0:T(8,128)(2,1)S(1)}, bf16[128,1024]{1,0:T(8,128)(2,1)S(1)}, u32[]{:S(2)}, u32[]{:S(2)}) %collective-permute-start.16) | collective-permute-done | bytes 262176 | tf_op jit(solution)/shard_map/ppermute | solution.py:60
  96.0 1.6 %collective-permute-done.14.r_5_ = bf16[128,1024]{1,0:T(8,128)(2,1)S(1)} collective-permute-done((bf16[128,1024]{1,0:T(8,128)(2,1)S(1)}, bf16[128,1024]{1,0:T(8,128)(2,1)S(1)}, u32[]{:S(2)}, u32[]{:S(2)}) %collective-permute-start.14) | collective-permute-done | bytes 262176 | tf_op jit(solution)/shard_map/ppermute | solution.py:60
  98.4 10.6 %collective-permute-done.21.below_ref = bf16[256,1024]{1,0:T(8,128)(2,1)S(1)} collective-permute-done((bf16[256,1024]{1,0:T(8,128)(2,1)S(1)}, bf16[256,1024]{1,0:T(8,128)(2,1)S(1)}, u32[]{:S(2)}, u32[]{:S(2)}) %collective-permute-start.21) | collective-permute-done | bytes 524320 | tf_op jit(solution)/shard_map/ppermute | solution.py:43
  (47 shorter events, 10.0 us)
Async XLA Ops:
  0.6 26.9 %copy-start.8 = (s32[1,1,8,2]{2,3,1,0:T(2,128)S(1)}, s32[1,1,8,2]{2,3,1,0:T(2,128)}, u32[]{:S(2)}) copy-start(s32[1,1,8,2]{2,3,1,0:T(2,128)} %param.12) | copy-start | bytes 196
  0.6 27.0 %copy-start.1 = (bf16[1024,1024]{1,0:T(8,128)(2,1)S(1)}, bf16[1024,1024]{1,0:T(8,128)(2,1)}, u32[]{:S(2)}) copy-start(bf16[1024,1024]{1,0:T(8,128)(2,1)} %sw_ref.1) | copy-start | bytes 6291460
  2.6 16.8 %collective-permute-start.7 = (bf16[256,1024]{1,0:T(8,128)(2,1)S(1)}, bf16[256,1024]{1,0:T(8,128)(2,1)S(1)}, u32[]{:S(2)}, u32[]{:S(2)}) collective-permute-start(bf16[256,1024]{1,0:T(8,128)(2,1)S(1)} %broadcast_select_fusion.r_4_), channel_id=1, source_target_pairs={{0,64},{1,65},{2,66},{3,67},{4,68},{5,69},{6,70},{7,71},{8,72},{9,... | collective-permute-start | bytes 1572872 | tf_op jit(solution)/shard_map/ppermute | solution.py:43
  3.4 28.2 %collective-permute-start.3 = (bf16[256,1024]{1,0:T(8,128)(2,1)S(1)}, bf16[256,1024]{1,0:T(8,128)(2,1)}, u32[]{:S(2)}, u32[]{:S(2)}) collective-permute-start(bf16[256,1024]{1,0:T(8,128)(2,1)S(1)} %broadcast_select_fusion.r_4_), channel_id=1, source_target_pairs={{0,68},{1,69},{2,70},{3,71},{4,72},{5,73},{6,74},{7,75},{8,76},{9,... | collective-permute-start | bytes 1572872 | tf_op jit(solution)/shard_map/ppermute | solution.py:43
  5.3 5.4 %collective-permute-start.10 = (s32[1,128]{1,0:T(1,128)S(1)}, s32[1,128]{1,0:T(1,128)S(1)}, u32[]{:S(2)}, u32[]{:S(2)}) collective-permute-start(s32[1,128]{1,0:T(1,128)S(1)} %pad_bitcast_fusion), channel_id=1, source_target_pairs={{67,0},{72,1},{73,2},{74,3},{71,4},{76,5},{77,6},{78,7},{75,8},{80... | collective-permute-start | bytes 1544 | tf_op jit(solution)/shard_map/ppermute | solution.py:60
  5.9 7.3 %collective-permute-start.9 = (s32[1,128]{1,0:T(1,128)S(1)}, s32[1,128]{1,0:T(1,128)S(1)}, u32[]{:S(2)}, u32[]{:S(2)}) collective-permute-start(s32[1,128]{1,0:T(1,128)S(1)} %pad_bitcast_fusion), channel_id=1, source_target_pairs={{66,0},{67,1},{72,2},{73,3},{70,4},{71,5},{76,6},{77,7},{74,8},{75... | collective-permute-start | bytes 1544 | tf_op jit(solution)/shard_map/ppermute | solution.py:60
  9.2 6.6 %collective-permute-start.8 = (s32[1,128]{1,0:T(1,128)S(1)}, s32[1,128]{1,0:T(1,128)S(1)}, u32[]{:S(2)}, u32[]{:S(2)}) collective-permute-start(s32[1,128]{1,0:T(1,128)S(1)} %pad_bitcast_fusion), channel_id=1, source_target_pairs={{65,0},{66,1},{67,2},{72,3},{69,4},{70,5},{71,6},{76,7},{73,8},{74... | collective-permute-start | bytes 1544 | tf_op jit(solution)/shard_map/ppermute | solution.py:60
  10.7 5.1 %collective-permute-start.2 = (s32[1,128]{1,0:T(1,128)S(1)}, s32[1,128]{1,0:T(1,128)S(1)}, u32[]{:S(2)}, u32[]{:S(2)}) collective-permute-start(s32[1,128]{1,0:T(1,128)S(1)} %pad_bitcast_fusion), channel_id=1, source_target_pairs={{0,1},{1,2},{2,3},{3,0},{4,5},{5,6},{6,7},{7,4},{8,9},{9,10},{10,1... | collective-permute-start | bytes 1544 | tf_op jit(solution)/shard_map/ppermute | solution.py:49
  13.2 3.9 %collective-permute-start.1 = (s32[1,128]{1,0:T(1,128)S(1)}, s32[1,128]{1,0:T(1,128)S(1)}, u32[]{:S(2)}, u32[]{:S(2)}) collective-permute-start(s32[1,128]{1,0:T(1,128)S(1)} %pad_bitcast_fusion), channel_id=1, source_target_pairs={{0,2},{1,3},{2,0},{3,1},{4,6},{5,7},{6,4},{7,5},{8,10},{9,11},{10,... | collective-permute-start | bytes 1544 | tf_op jit(solution)/shard_map/ppermute | solution.py:49
  15.8 3.6 %collective-permute-start = (s32[1,128]{1,0:T(1,128)S(1)}, s32[1,128]{1,0:T(1,128)S(1)}, u32[]{:S(2)}, u32[]{:S(2)}) collective-permute-start(s32[1,128]{1,0:T(1,128)S(1)} %pad_bitcast_fusion), channel_id=1, source_target_pairs={{0,3},{1,0},{2,1},{3,2},{4,7},{5,4},{6,5},{7,6},{8,11},{9,8},{10,9... | collective-permute-start | bytes 1544 | tf_op jit(solution)/shard_map/ppermute | solution.py:49
  20.9 19.5 %collective-permute-start.11 = (bf16[128,1024]{1,0:T(8,128)(2,1)}, bf16[128,1024]{1,0:T(8,128)(2,1)S(1)}, u32[]{:S(2)}, u32[]{:S(2)}) collective-permute-start(bf16[128,1024]{1,0:T(8,128)(2,1)} %get-tuple-element.32), channel_id=1, source_target_pairs={{0,65},{1,66},{2,67},{3,72},{4,69},{5,70},{6,71},{7,76},{8,73},{9,... | collective-permute-start | bytes 786440 | tf_op jit(solution)/shard_map/ppermute | solution.py:60
  26.2 14.2 %collective-permute-start.12 = (bf16[128,1024]{1,0:T(8,128)(2,1)}, bf16[128,1024]{1,0:T(8,128)(2,1)}, u32[]{:S(2)}, u32[]{:S(2)}) collective-permute-start(bf16[128,1024]{1,0:T(8,128)(2,1)} %get-tuple-element.33), channel_id=1, source_target_pairs={{0,66},{1,67},{2,72},{3,73},{4,70},{5,71},{6,76},{7,77},{8,74},{9,... | collective-permute-start | bytes 786440 | tf_op jit(solution)/shard_map/ppermute | solution.py:60
  26.2 14.6 %collective-permute-start.13 = (bf16[128,1024]{1,0:T(8,128)(2,1)}, bf16[128,1024]{1,0:T(8,128)(2,1)}, u32[]{:S(2)}, u32[]{:S(2)}) collective-permute-start(bf16[128,1024]{1,0:T(8,128)(2,1)} %get-tuple-element.34), channel_id=1, source_target_pairs={{0,67},{1,72},{2,73},{3,74},{4,71},{5,76},{6,77},{7,78},{8,75},{9,... | collective-permute-start | bytes 786440 | tf_op jit(solution)/shard_map/ppermute | solution.py:60
  27.6 1.6 %copy-start.3 = (s32[1,256,2048]{2,1,0:T(8,128)S(1)}, s32[1,256,2048]{2,1,0:T(8,128)}, u32[]{:S(2)}) copy-start(s32[1,256,2048]{2,1,0:T(8,128)} %param.13) | copy-start | bytes 6291460
  29.2 1.0 copy-start.4
  30.3 10.5 %copy-start = (bf16[1024,2048]{1,0:T(8,128)(2,1)S(1)}, bf16[1024,2048]{1,0:T(8,128)(2,1)}, u32[]{:S(2)}) copy-start(bf16[1024,2048]{1,0:T(8,128)(2,1)} %r_4_.3) | copy-start | bytes 12582916
  30.3 10.5 %copy-start.6 = (f32[2048]{0:T(1024)S(1)}, f32[2048]{0:T(1024)}, u32[]{:S(2)}) copy-start(f32[2048]{0:T(1024)} %param.16) | copy-start | bytes 24580
  32.7 18.0 %collective-permute-start.4 = (bf16[128,1024]{1,0:T(8,128)(2,1)S(1)}, bf16[128,1024]{1,0:T(8,128)(2,1)S(1)}, u32[]{:S(2)}, u32[]{:S(2)}) collective-permute-start(bf16[128,1024]{1,0:T(8,128)(2,1)S(1)} %get-tuple-element.29), channel_id=1, source_target_pairs={{0,1},{1,2},{2,3},{3,0},{4,5},{5,6},{6,7},{7,4},{8,9},{9,10},{10,1... | collective-permute-start | bytes 786440 | tf_op jit(solution)/shard_map/ppermute | solution.py:49
  35.0 15.7 %collective-permute-start.5 = (bf16[128,1024]{1,0:T(8,128)(2,1)S(1)}, bf16[128,1024]{1,0:T(8,128)(2,1)S(1)}, u32[]{:S(2)}, u32[]{:S(2)}) collective-permute-start(bf16[128,1024]{1,0:T(8,128)(2,1)S(1)} %get-tuple-element.30), channel_id=1, source_target_pairs={{0,2},{1,3},{2,0},{3,1},{4,6},{5,7},{6,4},{7,5},{8,10},{9,11},{10,... | collective-permute-start | bytes 786440 | tf_op jit(solution)/shard_map/ppermute | solution.py:49
  40.4 13.4 %collective-permute-start.6 = (bf16[128,1024]{1,0:T(8,128)(2,1)S(1)}, bf16[128,1024]{1,0:T(8,128)(2,1)S(1)}, u32[]{:S(2)}, u32[]{:S(2)}) collective-permute-start(bf16[128,1024]{1,0:T(8,128)(2,1)S(1)} %get-tuple-element.31), channel_id=1, source_target_pairs={{0,3},{1,0},{2,1},{3,2},{4,7},{5,4},{6,5},{7,6},{8,11},{9,8},{10,9... | collective-permute-start | bytes 786440 | tf_op jit(solution)/shard_map/ppermute | solution.py:49
  53.8 2.9 %copy-start.2 = (bf16[2048,1024]{1,0:T(8,128)(2,1)S(1)}, bf16[2048,1024]{1,0:T(8,128)(2,1)}, u32[]{:S(2)}) copy-start(bf16[2048,1024]{1,0:T(8,128)(2,1)} %nb_ref.1) | copy-start | bytes 12582916
  53.8 2.9 %copy-start.5 = (bf16[1,256,1024]{2,1,0:T(8,128)(2,1)S(1)}, bf16[1,256,1024]{2,1,0:T(8,128)(2,1)}, u32[]{:S(2)}) copy-start(bf16[1,256,1024]{2,1,0:T(8,128)(2,1)} %param.14) | copy-start | bytes 1572868
  53.8 2.9 %copy-start.7 = (f32[1024]{0:T(1024)S(1)}, f32[1024]{0:T(1024)}, u32[]{:S(2)}) copy-start(f32[1024]{0:T(1024)} %param.19) | copy-start | bytes 12292
  63.0 11.3 %collective-permute-start.19 = (bf16[128,1024]{1,0:T(8,128)(2,1)S(1)}, bf16[128,1024]{1,0:T(8,128)(2,1)S(1)}, u32[]{:S(2)}, u32[]{:S(2)}) collective-permute-start(bf16[128,1024]{1,0:T(8,128)(2,1)S(1)} %get-tuple-element.52), channel_id=1, source_target_pairs={{0,2},{1,3},{2,0},{3,1},{4,6},{5,7},{6,4},{7,5},{8,10},{9,11},{10,... | collective-permute-start | bytes 786440 | tf_op jit(solution)/shard_map/ppermute | solution.py:49
  63.1 14.8 %collective-permute-start.20 = (bf16[128,1024]{1,0:T(8,128)(2,1)S(1)}, bf16[128,1024]{1,0:T(8,128)(2,1)S(1)}, u32[]{:S(2)}, u32[]{:S(2)}) collective-permute-start(bf16[128,1024]{1,0:T(8,128)(2,1)S(1)} %get-tuple-element.53), channel_id=1, source_target_pairs={{0,1},{1,2},{2,3},{3,0},{4,5},{5,6},{6,7},{7,4},{8,9},{9,10},{10,1... | collective-permute-start | bytes 786440 | tf_op jit(solution)/shard_map/ppermute | solution.py:49
  63.8 16.5 %collective-permute-start.18 = (bf16[128,1024]{1,0:T(8,128)(2,1)S(1)}, bf16[128,1024]{1,0:T(8,128)(2,1)S(1)}, u32[]{:S(2)}, u32[]{:S(2)}) collective-permute-start(bf16[128,1024]{1,0:T(8,128)(2,1)S(1)} %get-tuple-element.46.r_4_), channel_id=1, source_target_pairs={{0,3},{1,0},{2,1},{3,2},{4,7},{5,4},{6,5},{7,6},{8,11},{9,8},{10,9... | collective-permute-start | bytes 786440 | tf_op jit(solution)/shard_map/ppermute | solution.py:49
  66.8 22.7 %collective-permute-start.15 = (bf16[128,1024]{1,0:T(8,128)(2,1)S(1)}, bf16[128,1024]{1,0:T(8,128)(2,1)S(1)}, u32[]{:S(2)}, u32[]{:S(2)}) collective-permute-start(bf16[128,1024]{1,0:T(8,128)(2,1)S(1)} %get-tuple-element.48), channel_id=1, source_target_pairs={{66,0},{67,1},{72,2},{73,3},{70,4},{71,5},{76,6},{77,7},{74,8},{75... | collective-permute-start | bytes 786440 | tf_op jit(solution)/shard_map/ppermute | solution.py:60
  72.0 25.6 %collective-permute-start.14 = (bf16[128,1024]{1,0:T(8,128)(2,1)S(1)}, bf16[128,1024]{1,0:T(8,128)(2,1)S(1)}, u32[]{:S(2)}, u32[]{:S(2)}) collective-permute-start(bf16[128,1024]{1,0:T(8,128)(2,1)S(1)} %get-tuple-element.47.r_5_), channel_id=1, source_target_pairs={{65,0},{66,1},{67,2},{72,3},{69,4},{70,5},{71,6},{76,7},{73,8},{74... | collective-permute-start | bytes 786440 | tf_op jit(solution)/shard_map/ppermute | solution.py:60
  74.3 21.8 %collective-permute-start.16 = (bf16[128,1024]{1,0:T(8,128)(2,1)S(1)}, bf16[128,1024]{1,0:T(8,128)(2,1)S(1)}, u32[]{:S(2)}, u32[]{:S(2)}) collective-permute-start(bf16[128,1024]{1,0:T(8,128)(2,1)S(1)} %get-tuple-element.49), channel_id=1, source_target_pairs={{67,0},{72,1},{73,2},{74,3},{71,4},{76,5},{77,6},{78,7},{75,8},{80... | collective-permute-start | bytes 786440 | tf_op jit(solution)/shard_map/ppermute | solution.py:60
  77.9 20.5 %collective-permute-start.17 = (bf16[256,1024]{1,0:T(8,128)(2,1)S(1)}, bf16[256,1024]{1,0:T(8,128)(2,1)S(1)}, u32[]{:S(2)}, u32[]{:S(2)}) collective-permute-start(bf16[256,1024]{1,0:T(8,128)(2,1)S(1)} %get-tuple-element.50), channel_id=1, source_target_pairs={{0,64},{1,65},{2,66},{3,67},{4,68},{5,69},{6,70},{7,71},{8,72},{9,... | collective-permute-start | bytes 1572872 | tf_op jit(solution)/shard_map/ppermute | solution.py:43
  81.2 27.7 %collective-permute-start.21 = (bf16[256,1024]{1,0:T(8,128)(2,1)S(1)}, bf16[256,1024]{1,0:T(8,128)(2,1)S(1)}, u32[]{:S(2)}, u32[]{:S(2)}) collective-permute-start(bf16[256,1024]{1,0:T(8,128)(2,1)S(1)} %shard_map.123), channel_id=1, source_target_pairs={{0,124},{1,125},{2,126},{3,127},{4,64},{5,65},{6,66},{7,67},{8,68}... | collective-permute-start | bytes 1572872 | tf_op jit(solution)/shard_map/ppermute | solution.py:43

commit v5 on v4

--- a/solution.py
+++ b/solution.py
@@ -49,14 +49,13 @@
     return lax.ppermute(x, "dom", pairs)
 
 
-def straight(x, d, back=False):
+def straight_back(x, d):
     count = lax.axis_size("dom")
     pairs = []
     for s in range(2):
         for j in range(count):
             to = j + d if j % LINE + d < LINE else j + d + LINE
-            pair = (s * count + j, (1 - s) * count + to % count)
-            pairs.append(pair[::-1] if back else pair)
+            pairs.append(((1 - s) * count + to % count, s * count + j))
     return lax.ppermute(x, ("side", "dom"), pairs)
 
 
@@ -72,15 +71,28 @@
     return pl.ds(pl.multiple_of(index * block, block), block)
 
 
-def pick_kernel(block, offset, place_ref, m1, m2, m3, rows_ref, *refs):
-    outs = refs[-3:]
+def pick_near_kernel(block, place_ref, m1, m2, m3, rows_ref, _, *outs):
     for d, (meta, out) in enumerate(zip((m1, m2, m3), outs), 1):
         p = lax.rem(place_ref[0] + d, LINE)
-        out[...] = rows_ref[at_block(meta[0, offset(p, d)], block), :]
+        out[...] = rows_ref[at_block(meta[0, near(p, d)], block), :]
+
+
+def pick_far_kernel(block, place_ref, m1, m2, m3, same_ref, below_ref, *outs):
+    for d, (meta, out) in enumerate(zip((m1, m2, m3), outs), 1):
+        p = lax.rem(place_ref[0] + d, LINE)
+        at = at_block(meta[0, far(p, d)], block)
+
+        @pl.when(p >= d)
+        def _():
+            out[...] = same_ref[at, :]
+
+        @pl.when(p < d)
+        def _():
+            out[...] = below_ref[at, :]
 
 
 def slots(p):
-    return [0, LINE] + [far(p, d) for d in range(1, LINE)] + [near(p, d) for d in range(1, LINE)]
+    return [0, LINE] + [near(p, d) for d in range(1, LINE)] + [far(p, d) for d in range(1, LINE)]
 
 
 def tiles_kernel(block, place_ref, lists_ref, counts_ref, x_ref, sw_ref, tiles_ref, tiles_t_ref, self_ref):
@@ -126,13 +138,25 @@
 
 
 def layer_kernel(
-    live_ref, acc_ref, deg_ref, self_ref, up_ref, sw_ref, nb_ref, ob_ref,
-    emb_ref, gself_ref, gpool_ref, pre_ref,
+    block, live_ref, got_ref, q_ref, qb_ref, tiles_ref, acc_ref, deg_ref, self_ref, up_ref, nb_ref, ob_ref, tt_ref,
+    msg_ref, g_ref, gpool_ref, pre_ref, last_ref, near1, near2, near3, pooled_ref, gn_ref,
 ):
     rows, width = self_ref.shape
-    inv_deg = 1.0 / (1.0 + deg_ref[:, :1])
-    pooled = (acc_ref[...] * inv_deg).astype(BF16)
+    hidden = nb_ref.shape[0]
     step = 512
+    x = got_ref[...]
+    keep = x[:, :128].astype(F32) < LIMIT
+    tiles = tiles_ref[:, -block:]
+    deg = deg_ref[...] + dot(tiles, jnp.where(keep, 1.0, 0.0).astype(BF16))
+    inv_deg = 1.0 / (1.0 + deg[:, :1])
+    keep = keep[:, :1]
+    for n in range(hidden // step):
+        cols = slice(n * step, (n + 1) * step)
+        pre = dot(x, q_ref[:, cols]) + qb_ref[:, cols]
+        msg = jnp.where(keep, jnp.maximum(pre, 0.0), 0.0).astype(BF16)
+        last_ref[:, cols] = msg
+        pooled_ref[:, cols] = ((acc_ref[:, cols] + dot(tiles, msg)) * inv_deg).astype(BF16)
+    pooled = pooled_ref[...]
     for n in range(width // step):
         cols = slice(n * step, (n + 1) * step)
         pre_ref[:, cols] = self_ref[:, cols] + dot(pooled, nb_ref[:, cols]) + ob_ref[:, cols]
@@ -140,26 +164,29 @@
     act = jnp.maximum(pre, 0.0)
     inv = lax.rsqrt(jnp.mean(act * act, axis=1, keepdims=True) + EPS)
     keep = lax.broadcasted_iota(jnp.int32, (rows, 1), 0) < live_ref[0]
-    emb_ref[...] = jnp.where(keep, act * inv, 0.0).astype(BF16)
     up = jnp.where(keep, up_ref[...].astype(F32), 0.0)
     inner = jnp.sum(up * act, axis=1, keepdims=True) / width
     g = inv * up - act * (inv * inv * inv * inner)
     g = jnp.where(pre > 0, g, 0.0).astype(BF16)
-    for n in range(nb_ref.shape[0] // step):
+    g_ref[...] = g
+    for n in range(hidden // step):
         cols = slice(n * step, (n + 1) * step)
         gpool_ref[:, cols] = (dot(g, nb_ref[cols, :], 1, 1) * inv_deg).astype(BF16)
-    for n in range(width // step):
-        cols = slice(n * step, (n + 1) * step)
-        gself_ref[:, cols] = dot(g, sw_ref[cols, :], 1, 1)
-
-
-def back_dot(block, first, last, skip, tt_ref, gpool_ref, msg_ref, q_ref, gn_ref, store):
-    tt = tt_ref[first * block : last * block, :]
-    at = slice(skip * block, (skip + last - first) * block)
+
+    def store(cols, part):
+        for i, out in enumerate((near1, near2, near3)):
+            out[:, cols] = part[i * block : (i + 1) * block].astype(BF16)
+
+    back_dot(2 * block, tt_ref, gpool_ref, [msg_ref[2 * block :, :]], q_ref, gn_ref, store)
+
+
+def back_dot(first, tt_ref, gpool_ref, messages, q_ref, gn_ref, store):
+    rows = gn_ref.shape[0]
+    tt = tt_ref[first : first + rows, :]
     step = 512
     for n in range(gpool_ref.shape[1] // step):
         cols = slice(n * step, (n + 1) * step)
-        live = msg_ref[at, cols].astype(F32) > 0
+        live = jnp.concatenate([m[:, cols] for m in messages], axis=0).astype(F32) > 0
         gn_ref[:, cols] = jnp.where(live, dot(tt, gpool_ref[:, cols]), 0.0).astype(BF16)
     gn = gn_ref[...]
     for n in range(q_ref.shape[0] // step):
@@ -167,17 +194,25 @@
         store(cols, dot(gn, q_ref[cols, :], 1, 1))
 
 
-def back_kernel(block, first, last, skip, tt_ref, gpool_ref, msg_ref, q_ref, _, *refs):
+def back_far_kernel(block, place_ref, lists_ref, tt_ref, gpool_ref, early_ref, last_ref, q_ref, _, *refs):
     outs, gn_ref = refs[:-1], refs[-1]
+    width = q_ref.shape[0]
 
     def store(cols, part):
         for i, out in enumerate(outs):
             out[:, cols] = part[i * block : (i + 1) * block].astype(BF16)
 
-    back_dot(block, first, last, skip, tt_ref, gpool_ref, msg_ref, q_ref, gn_ref, store)
-
-
-def back_own_kernel(block, lists_ref, tt_ref, gpool_ref, msg_ref, q_ref, _, same_ref, below_ref, gn_ref):
+    for d, out in enumerate(outs, 1):
+        which = lists_ref[far(place_ref[0], d), 1].astype(F32)
+        out[:, width:] = jnp.full((block, 128), which, F32).astype(BF16)
+    messages = [early_ref[...], last_ref[...]]
+    back_dot((1 + LINE) * block, tt_ref, gpool_ref, messages, q_ref, gn_ref, store)
+
+
+def back_own_kernel(
+    block, lists_ref, live_ref, tt_ref, gpool_ref, msg_ref, q_ref, g_ref, sw_ref, pre_ref, _,
+    same_ref, below_ref, gself_ref, emb_ref, gn_ref,
+):
     same_ref[...] = jnp.zeros_like(same_ref)
     at = at_block(lists_ref[0, 1], block)
 
@@ -185,7 +220,16 @@
         same_ref[at, cols] = part[:block].astype(BF16)
         below_ref[:, cols] = part[block:].astype(BF16)
 
-    back_dot(block, 0, 2, 0, tt_ref, gpool_ref, msg_ref, q_ref, gn_ref, store)
+    back_dot(0, tt_ref, gpool_ref, [msg_ref[: 2 * block, :]], q_ref, gn_ref, store)
+    rows, width = pre_ref.shape
+    step = 512
+    for n in range(width // step):
+        cols = slice(n * step, (n + 1) * step)
+        gself_ref[:, cols] = dot(g_ref[...], sw_ref[cols, :], 1, 1)
+    act = jnp.maximum(pre_ref[...], 0.0)
+    inv = lax.rsqrt(jnp.mean(act * act, axis=1, keepdims=True) + EPS)
+    keep = lax.broadcasted_iota(jnp.int32, (rows, 1), 0) < live_ref[0]
+    emb_ref[...] = jnp.where(keep, act * inv, 0.0).astype(BF16)
 
 
 def sum_near_kernel(block, place_ref, lists_ref, m1, m2, m3, own_ref, d1, d2, d3, out_ref, total):
@@ -197,11 +241,16 @@
     out_ref[...] = total[...].astype(BF16)
 
 
-def place_kernel(block, place_ref, m1, m2, m3, gself_ref, c1, c2, c3, total_ref):
-    total_ref[...] = gself_ref[...]
-    for d, (meta, part) in enumerate(zip((m1, m2, m3), (c1, c2, c3)), 1):
-        p = lax.rem(place_ref[0] + d, LINE)
-        total_ref[at_block(meta[0, far(p, d)], block), :] += part[...].astype(F32)
+def place_kernel(gself_ref, c1, c2, c3, total_ref):
+    block, width = c1.shape[0], gself_ref.shape[1]
+    first, second = gself_ref[:block, :], gself_ref[block:, :]
+    for part in (c1, c2, c3):
+        grad = part[:, :width].astype(F32)
+        late = part[:, width : width + 1].astype(F32) > 0.5
+        first += jnp.where(late, 0.0, grad)
+        second += jnp.where(late, grad, 0.0)
+    total_ref[:block, :] = first
+    total_ref[block:, :] = second
 
 
 def finish_kernel(live_ref, total_ref, same_ref, below_ref, out_ref):
@@ -225,20 +274,12 @@
     steps = range(1, LINE)
     one, two = ((block, width), BF16), ((rows, width), BF16)
 
-    def pick(offset, metas, held, after):
-        return call(
-            lambda *r: pick_kernel(block, offset, *r),
-            [one] * len(steps),
-            (place, *metas, held, *after),
-            [SMEM] * (1 + len(steps)) + [VMEM] + [HELD] * len(after),
-        )
-
     below = swap_rows(marked, LINE)
-    far_metas = [straight(row, d, back=True) for d in steps]
-    near_metas = [along(row, -d) for d in steps]
     same = swap_rows(marked, 0)
-    far_sent = pick(far, far_metas, marked, (same, *near_metas))
-    got_far = [straight(b, d) for d, b in zip(steps, far_sent)]
+    metas = [along(row, -d) for d in steps]
+    later, *metas = lax.optimization_barrier((marked, *metas))
+    below2 = swap_rows(later, 2 * LINE)
+    scalars = [SMEM] * (1 + len(steps))
     tiles, tiles_t, self_pre = call(
         lambda *r: tiles_kernel(block, *r),
         [((rows, reach * block), BF16), ((reach * block, rows), BF16), ((rows, width), F32)],
@@ -246,8 +287,20 @@
         [SMEM] * 2 + [VMEM] * 3,
         flops=2 * rows * width * width,
     )
-    near_sent = pick(near, near_metas, below, (tiles,))
-    got_near = [along(b, d) for d, b in zip(steps, near_sent)]
+    sent = call(
+        lambda *r: pick_near_kernel(block, *r),
+        [one] * len(steps),
+        (place, *metas, below, tiles),
+        scalars + [VMEM, HELD],
+    )
+    got_near = [along(b, d) for d, b in zip(steps, sent)]
+    sent = call(
+        lambda *r: pick_far_kernel(block, *r),
+        [one] * len(steps),
+        (place, *metas, same, below2),
+        scalars + [VMEM] * 2,
+    )
+    got_far = [along(b, d) for d, b in zip(steps, sent)]
     split = 1 + LINE
 
     def message(first, last, ins, specs):
@@ -261,56 +314,54 @@
         )
 
     msg_a, acc, deg = message(
-        0, split, (lists, same, below, *got_far, q, qb, tiles), [SMEM] + [VMEM] * 8
-    )
-    msg_b, acc, deg = message(split, reach, (*got_near, q, qb, tiles, acc, deg), [VMEM] * 8)
-    emb, gself, gpool = call(
-        layer_kernel,
-        [two, ((rows, width), F32), ((rows, hidden), BF16)],
-        (live, acc, deg, self_pre, up, sw, nb, ob),
-        [SMEM] + [VMEM] * 7,
-        scratch=[pltpu.VMEM((rows, width), F32)],
-        flops=2 * rows * width * (2 * hidden + width),
-    )
-
-    def back(kernel, outs, first, last, msg, after, lead=()):
-        size = last - first
-        return call(
-            kernel,
-            outs,
-            (*lead, tiles_t, gpool, msg, q, after),
-            [SMEM] * len(lead) + [VMEM] * 4 + [HELD],
-            scratch=[pltpu.VMEM((size * block, hidden), BF16)],
-            flops=2 * size * block * hidden * (width + rows),
-        )
-
-    near_back = back(
-        lambda *r: back_kernel(block, split, reach, 0, *r), [one] * 3, split, reach, msg_b, gself
+        0, split, (lists, same, below, *got_near, q, qb, tiles), [SMEM] + [VMEM] * 8
+    )
+    msg_b, acc, deg = message(
+        split, reach - 1, (*got_far[:-1], q, qb, tiles, acc, deg), [VMEM] * (5 + len(steps) - 1)
+    )
+    gn = pltpu.VMEM((3 * block, hidden), BF16)
+    g, gpool, pre, msg_c, *near_back = call(
+        lambda *r: layer_kernel(block, *r),
+        [two, ((rows, hidden), BF16), ((rows, width), F32), ((block, hidden), BF16)] + [one] * 3,
+        (live, got_far[-1], q, qb, tiles, acc, deg, self_pre, up, nb, ob, tiles_t, msg_a),
+        [SMEM] + [VMEM] * 12,
+        scratch=[pltpu.VMEM((rows, hidden), BF16), gn],
+        flops=8 * MICROSECOND,
     )
     back_near = [along(b, -d) for d, b in zip(steps, near_back)]
-    far_back = back(
-        lambda *r: back_kernel(block, 2, split, 2, *r), [one] * 3, 2, split, msg_a, near_back[0]
-    )
-    back_far = [straight(b, d, back=True) for d, b in zip(steps, far_back)]
-    own_same, own_below = back(
-        lambda *r: back_own_kernel(block, *r), [two, one], 0, 2, msg_a, far_back[0], (lists,)
+    far_back = call(
+        lambda *r: back_far_kernel(block, *r),
+        [((block, width + 128), BF16)] * 3,
+        (place, lists, tiles_t, gpool, msg_b, msg_c, q, near_back[0]),
+        [SMEM] * 2 + [VMEM] * 5 + [HELD],
+        scratch=[gn],
+        flops=2 * MICROSECOND,
+    )
+    back_far = [straight_back(b, d) for d, b in zip(steps, far_back)]
+    own_same, own_below, gself, emb = call(
+        lambda *r: back_own_kernel(block, *r),
+        [two, one, ((rows, width), F32), two],
+        (lists, live, tiles_t, gpool, msg_a, q, g, sw, pre, far_back[0]),
+        [SMEM] * 2 + [VMEM] * 7 + [HELD],
+        scratch=[pltpu.VMEM((2 * block, hidden), BF16)],
+        flops=3 * MICROSECOND,
     )
     g_same = swap_rows(own_same, 0)
     total = pltpu.VMEM((rows, width), F32)
     (sum_below,) = call(
         lambda *r: sum_near_kernel(block, *r),
         [two],
-        (place, lists, *near_metas, own_below, *back_near),
+        (place, lists, *metas, own_below, *back_near),
         [SMEM] * 5 + [VMEM] * 4,
         scratch=[total],
         flops=20 * MICROSECOND,
     )
     g_below = swap_rows(sum_below, -LINE)
     (placed,) = call(
-        lambda *r: place_kernel(block, *r),
+        place_kernel,
         [((rows, width), F32)],
-        (place, *far_metas, gself, *back_far),
-        [SMEM] * 4 + [VMEM] * 4,
+        (gself, *back_far),
+        [VMEM] * 4,
         flops=20 * MICROSECOND,
     )
     (grad,) = call(finish_kernel, [two], (live, placed, g_same, g_below), [SMEM] + [VMEM] * 3)

time: 110 us -> 106 us (0.964)
  the two profiles are of different devices: /device:TPU:111 before, /device:TPU:7 now
where the time goes in v5:
time: 106 us; the launch traced here: 105 us
  waiting for transfers between devices  44.3 us (42%)
  starting transfers between devices  27.7 us (26%)
  Pallas kernels  24.4 us (23%)
  local copies, waits for them, and re-layouts  5.77 us (5%)
  between operations  1.44 us (1%)
  other arithmetic  1.16 us (1%)
    ppermute x5, waiting for transfers between devices, swap_rows(): return lax.ppermute(x, ('side', 'dom'), pairs)  25.8 us
    pallas_call x11, Pallas kernels, call(): pl.pallas_call(kernel, out_shape=[jax.ShapeDtypeStruct(s, d) for s, d in...  24.4 us
    ppermute x12, starting transfers between devices, along(): return lax.ppermute(x, 'dom', pairs)  10.7 us
    ppermute x12, waiting for transfers between devices, along(): return lax.ppermute(x, 'dom', pairs)  9.93 us
    ppermute x3, starting transfers between devices, straight_back(): return lax.ppermute(x, ('side', 'dom'), pairs)  9.62 us
    ppermute x3, waiting for transfers between devices, straight_back(): return lax.ppermute(x, ('side', 'dom'), pairs)  8.49 us
    ppermute x5, starting transfers between devices, swap_rows(): return lax.ppermute(x, ('side', 'dom'), pairs)  7.39 us
    unnamed x18, local copies, waits for them, and re-layouts  4.33 us
  transfers between devices with their start and end apart: 20, of which 9 were waited for; matrix products, arithmetic and copies ran while one was open for 1% of the time, Pallas kernels for 16%

profile of v5, /device:TPU:7, one launch (start us, length us, event | category | flops | bytes accessed | tf_op | source)
XLA Modules:
  0.0 104.7 jit_solution(6599161455414650251)
XLA Ops:
  1.3 1.2 %broadcast_select_fusion = bf16[256,1024]{1,0:T(8,128)(2,1)S(1)} fusion(pred[256]{0:T(512)(128)(4,1)S(1)} %iota_compare_fusion, bf16[1,256,1024]{2,1,0:T(8,128)(2,1)} %param.10), kind=kLoop, calls=%fused_computation | loop fusion | flops 262144 | bytes 1048832 | tf_op jit(solution)/shard_map/jit(_where)/select_n | solution.py:272
  2.5 1.9 %collective-permute-start.8 = (bf16[256,1024]{1,0:T(8,128)(2,1)S(1)}, bf16[256,1024]{1,0:T(8,128)(2,1)S(1)}, u32[]{:S(2)}, u32[]{:S(2)}) collective-permute-start(bf16[256,1024]{1,0:T(8,128)(2,1)S(1)} %broadcast_select_fusion), channel_id=1, source_target_pairs={{0,68},{1,69},{2,70},{3,71},{4,72},{5,73},{6,74},{7,75},{8,76},{9,... | collective-permute-start | bytes 1572872 | tf_op jit(solution)/shard_map/ppermute | solution.py:43
  4.4 0.7 slice_bitcast_fusion
  5.3 2.2 %collective-permute-start.1 = (s32[1,128]{1,0:T(1,128)S(1)}, s32[1,128]{1,0:T(1,128)S(1)}, u32[]{:S(2)}, u32[]{:S(2)}) collective-permute-start(s32[1,128]{1,0:T(1,128)S(1)} %pad_bitcast_fusion), channel_id=1, source_target_pairs={{0,2},{1,3},{2,0},{3,1},{4,6},{5,7},{6,4},{7,5},{8,10},{9,11},{10,... | collective-permute-start | bytes 1544 | tf_op jit(solution)/shard_map/ppermute | solution.py:49
  7.8 1.4 %collective-permute-done.1.r_2_.r_3_ = s32[1,128]{1,0:T(1,128)S(1)} collective-permute-done((s32[1,128]{1,0:T(1,128)S(1)}, s32[1,128]{1,0:T(1,128)S(1)}, u32[]{:S(2)}, u32[]{:S(2)}) %collective-permute-start.1) | collective-permute-done | bytes 544 | tf_op jit(solution)/shard_map/ppermute | solution.py:49
  9.2 2.1 %collective-permute-done.r_1_.r_2_ = s32[1,128]{1,0:T(1,128)S(1)} collective-permute-done((s32[1,128]{1,0:T(1,128)S(1)}, s32[1,128]{1,0:T(1,128)S(1)}, u32[]{:S(2)}, u32[]{:S(2)}) %collective-permute-start) | collective-permute-done | bytes 544 | tf_op jit(solution)/shard_map/ppermute | solution.py:49
  11.3 3.7 %collective-permute-start.4 = (bf16[256,1024]{1,0:T(8,128)(2,1)S(1)}, bf16[256,1024]{1,0:T(8,128)(2,1)S(1)}, u32[]{:S(2)}, u32[]{:S(2)}) collective-permute-start(bf16[256,1024]{1,0:T(8,128)(2,1)S(1)} %broadcast_select_fusion), channel_id=1, source_target_pairs={{0,72},{1,73},{2,74},{3,75},{4,76},{5,77},{6,78},{7,79},{8,80},{9,... | collective-permute-start | bytes 1572872 | tf_op jit(solution)/shard_map/ppermute | solution.py:43
  15.1 0.8 copy.15.r_1_.r_0_
  15.8 1.6 %copy-done.1 = bf16[1024,1024]{1,0:T(8,128)(2,1)S(1)} copy-done((bf16[1024,1024]{1,0:T(8,128)(2,1)S(1)}, bf16[1024,1024]{1,0:T(8,128)(2,1)}, u32[]{:S(2)}) %copy-start.1) | copy-done | bytes 2097176
  17.4 1.6 %copy-done.3 = s32[1,256,2048]{2,1,0:T(8,128)S(1)} copy-done((s32[1,256,2048]{2,1,0:T(8,128)S(1)}, s32[1,256,2048]{2,1,0:T(8,128)}, u32[]{:S(2)}) %copy-start.3) | copy-done | bytes 2097176
  19.0 1.0 copy-done.4
  20.0 1.3 %shard_map.113 = (bf16[256,1024]{1,0:T(8,128)(2,1)S(1)}, bf16[1024,256]{1,0:T(8,128)(2,1)S(1)}, f32[256,1024]{1,0:T(8,128)S(1)}) custom-call(s32[1]{0:T(128)} %bitcast.2.r_0_, s32[8,2]{1,0:T(8,128)S(1)} %copy.15.r_1_.r_0_, s32[256,2048]{1,0:T(8,128)S(1)} %bitcast.20, bf16[256,1024]{1,0:T(8,128)(2,1)S(1)} %bitcast.21, bf16[1024,1024]{1,0:T(8,128)(2,1)S(1)} %copy-done.1), custom_call_target="tpu_custom_call" | custom-call | flops 536870912 | bytes 1048576 | tf_op jit(solution)/shard_map/pallas_call | solution.py:25
  22.4 1.6 %collective-permute-start.10 = (bf16[128,1024]{1,0:T(8,128)(2,1)S(1)}, bf16[128,1024]{1,0:T(8,128)(2,1)S(1)}, u32[]{:S(2)}, u32[]{:S(2)}) collective-permute-start(bf16[128,1024]{1,0:T(8,128)(2,1)S(1)} %get-tuple-element.45), channel_id=1, source_target_pairs={{0,2},{1,3},{2,0},{3,1},{4,6},{5,7},{6,4},{7,5},{8,10},{9,11},{10,... | collective-permute-start | bytes 786440 | tf_op jit(solution)/shard_map/ppermute | solution.py:49
  24.0 10.2 %collective-permute-done.4.r_5_ = bf16[256,1024]{1,0:T(8,128)(2,1)S(1)} collective-permute-done((bf16[256,1024]{1,0:T(8,128)(2,1)S(1)}, bf16[256,1024]{1,0:T(8,128)(2,1)S(1)}, u32[]{:S(2)}, u32[]{:S(2)}) %collective-permute-start.4) | collective-permute-done | bytes 524320 | tf_op jit(solution)/shard_map/ppermute | solution.py:43
  34.2 0.6 shard_map.114
  34.8 0.6 collective-permute-start.5
  35.4 2.1 %collective-permute-start.6 = (bf16[128,1024]{1,0:T(8,128)(2,1)S(1)}, bf16[128,1024]{1,0:T(8,128)(2,1)S(1)}, u32[]{:S(2)}, u32[]{:S(2)}) collective-permute-start(bf16[128,1024]{1,0:T(8,128)(2,1)S(1)} %get-tuple-element.42), channel_id=1, source_target_pairs={{0,1},{1,2},{2,3},{3,0},{4,5},{5,6},{6,7},{7,4},{8,9},{9,10},{10,1... | collective-permute-start | bytes 786440 | tf_op jit(solution)/shard_map/ppermute | solution.py:49
  37.8 4.6 %shard_map.116 = (bf16[640,2048]{1,0:T(8,128)(2,1)S(1)}, f32[256,2048]{1,0:T(8,128)S(1)}, f32[256,128]{1,0:T(8,128)S(1)}) custom-call(s32[8,2]{1,0:T(8,128)S(1)} %copy.15.r_1_.r_0_, bf16[256,1024]{1,0:T(8,128)(2,1)S(1)} %collective-permute-done.3.r_4_.r_1_, bf16[256,1024]{1,0:T(8,128)(2,1)S(1)} %collective-permute-done.8.r_4_.r_2_, ...), custom_call_target="tpu_custom_call" | custom-call | flops 3355443200 | bytes 1048576 | tf_op jit(solution)/shard_map/pallas_call | solution.py:25
  43.0 5.6 %collective-permute-done.7.r_1_ = bf16[128,1024]{1,0:T(8,128)(2,1)S(1)} collective-permute-done((bf16[128,1024]{1,0:T(8,128)(2,1)S(1)}, bf16[128,1024]{1,0:T(8,128)(2,1)S(1)}, u32[]{:S(2)}, u32[]{:S(2)}) %collective-permute-start.7) | collective-permute-done | bytes 262176 | tf_op jit(solution)/shard_map/ppermute | solution.py:49
  48.6 2.2 %shard_map.117 = (bf16[256,2048]{1,0:T(8,128)(2,1)S(1)}, f32[256,2048]{1,0:T(8,128)S(1)}, f32[256,128]{1,0:T(8,128)S(1)}) custom-call(bf16[128,1024]{1,0:T(8,128)(2,1)S(1)} %collective-permute-done.6.r_0_, bf16[128,1024]{1,0:T(8,128)(2,1)S(1)} %collective-permute-done.7.r_1_, bf16[1024,2048]{1,0:T(8,128)(2,1)S(1)} %copy-done, f32[1,2048]{1,0:T(1,128)S(1)} %bitcast.23, ...), custom_call_target="tpu_custom_call" | custom-call | flops 1342177280 | bytes 1048576 | tf_op jit(solution)/shard_map/pallas_call | solution.py:25
  50.9 6.3 %shard_map.118 = (bf16[256,1024]{1,0:T(8,128)(2,1)S(1)}, bf16[256,2048]{1,0:T(8,128)(2,1)S(1)}, f32[256,1024]{1,0:T(8,128)S(1)}, bf16[128,2048]{1,0:T(8,128)(2,1...) custom-call(s32[1]{0:T(128)} %bitcast.16.r_0_, ...), custom_call_target="tpu_custom_call" | custom-call | flops 8000000000 | bytes 1048576 | tf_op jit(solution)/shard_map/pallas_call | solution.py:25
  57.2 1.5 %collective-permute-start.17 = (bf16[128,1024]{1,0:T(8,128)(2,1)S(1)}, bf16[128,1024]{1,0:T(8,128)(2,1)S(1)}, u32[]{:S(2)}, u32[]{:S(2)}) collective-permute-start(bf16[128,1024]{1,0:T(8,128)(2,1)S(1)} %get-tuple-element.66), channel_id=1, source_target_pairs={{0,2},{1,3},{2,0},{3,1},{4,6},{5,7},{6,4},{7,5},{8,10},{9,11},{10,... | collective-permute-start | bytes 786440 | tf_op jit(solution)/shard_map/ppermute | solution.py:49
  58.7 2.1 %collective-permute-start.18 = (bf16[128,1024]{1,0:T(8,128)(2,1)S(1)}, bf16[128,1024]{1,0:T(8,128)(2,1)S(1)}, u32[]{:S(2)}, u32[]{:S(2)}) collective-permute-start(bf16[128,1024]{1,0:T(8,128)(2,1)S(1)} %get-tuple-element.67), channel_id=1, source_target_pairs={{0,1},{1,2},{2,3},{3,0},{4,5},{5,6},{6,7},{7,4},{8,9},{9,10},{10,1... | collective-permute-start | bytes 786440 | tf_op jit(solution)/shard_map/ppermute | solution.py:49
  60.9 2.8 %shard_map.119 = (bf16[128,1152]{1,0:T(8,128)(2,1)S(1)}, bf16[128,1152]{1,0:T(8,128)(2,1)S(1)}, bf16[128,1152]{1,0:T(8,128)(2,1)S(1)}) custom-call(s32[1]{0:T(128)} %bitcast.2.r_0_, s32[8,2]{1,0:T(8,128)S(1)} %copy.15.r_1_.r_0_, bf16[1024,256]{1,0:T(8,128)(2,1)S(1)} %get-tuple-element.35.r_11_.r_2_, bf16[256,2048]{1,0:T(8,128)(2,1)S(1)} %get-tuple-element.53.r_3_, ...), custom_call_target="tpu_custom_call" | custom-call | flops 2000000000 | bytes 1048576 | tf_op jit(solution)/shard_map/pallas_call | solution.py:25
  63.7 3.8 %collective-permute-start.13 = (bf16[128,1152]{1,0:T(8,128)(2,1)S(1)}, bf16[128,1152]{1,0:T(8,128)(2,1)S(1)}, u32[]{:S(2)}, u32[]{:S(2)}) collective-permute-start(bf16[128,1152]{1,0:T(8,128)(2,1)S(1)} %get-tuple-element.62), channel_id=1, source_target_pairs={{66,0},{67,1},{72,2},{73,3},{70,4},{71,5},{76,6},{77,7},{74,8},{75... | collective-permute-start | bytes 884744 | tf_op jit(solution)/shard_map/ppermute | solution.py:59
  67.5 3.6 %shard_map.120 = (bf16[256,1024]{1,0:T(8,128)(2,1)S(1)}, bf16[128,1024]{1,0:T(8,128)(2,1)S(1)}, f32[256,1024]{1,0:T(8,128)S(1)}, bf16[256,1024]{1,0:T(8,128)(2,1)}) custom-call(s32[8,2]{1,0:T(8,128)S(1)} %copy.15.r_1_.r_0_, s32[1]{0:T(128)} %bitcast.17.r_1_, bf16[1024,256]{1,0:T(8,128)(2,1)S(1)} %get-tuple-element.35.r_11_.r_2_, ...), custom_call_target="tpu_custom_call" | custom-call | flops 3000000000 | bytes 1048576 | tf_op jit(solution)/shard_map/pallas_call | solution.py:25
  71.1 5.8 %collective-permute-start.14 = (bf16[128,1152]{1,0:T(8,128)(2,1)S(1)}, bf16[128,1152]{1,0:T(8,128)(2,1)S(1)}, u32[]{:S(2)}, u32[]{:S(2)}) collective-permute-start(bf16[128,1152]{1,0:T(8,128)(2,1)S(1)} %get-tuple-element.63), channel_id=1, source_target_pairs={{67,0},{72,1},{73,2},{74,3},{71,4},{76,5},{77,6},{78,7},{75,8},{80... | collective-permute-start | bytes 884744 | tf_op jit(solution)/shard_map/ppermute | solution.py:59
  76.9 1.3 %collective-permute-start.15 = (bf16[256,1024]{1,0:T(8,128)(2,1)S(1)}, bf16[256,1024]{1,0:T(8,128)(2,1)S(1)}, u32[]{:S(2)}, u32[]{:S(2)}) collective-permute-start(bf16[256,1024]{1,0:T(8,128)(2,1)S(1)} %get-tuple-element.64), channel_id=1, source_target_pairs={{0,64},{1,65},{2,66},{3,67},{4,68},{5,69},{6,70},{7,71},{8,72},{9,... | collective-permute-start | bytes 1572872 | tf_op jit(solution)/shard_map/ppermute | solution.py:43
  78.2 0.9 shard_map.122
  79.2 8.3 %collective-permute-done.14.c3 = bf16[128,1152]{1,0:T(8,128)(2,1)S(1)} collective-permute-done((bf16[128,1152]{1,0:T(8,128)(2,1)S(1)}, bf16[128,1152]{1,0:T(8,128)(2,1)S(1)}, u32[]{:S(2)}, u32[]{:S(2)}) %collective-permute-start.14) | collective-permute-done | bytes 294944 | tf_op jit(solution)/shard_map/ppermute | solution.py:59
  88.1 15.6 %collective-permute-done.19.below_ref = bf16[256,1024]{1,0:T(8,128)(2,1)S(1)} collective-permute-done((bf16[256,1024]{1,0:T(8,128)(2,1)S(1)}, bf16[256,1024]{1,0:T(8,128)(2,1)S(1)}, u32[]{:S(2)}, u32[]{:S(2)}) %collective-permute-start.19) | collective-permute-done | bytes 524320 | tf_op jit(solution)/shard_map/ppermute | solution.py:43
  103.7 1.0 shard_map.123
  (42 shorter events, 3.1 us)
Async XLA Ops:
  2.5 18.9 %collective-permute-start.8 = (bf16[256,1024]{1,0:T(8,128)(2,1)S(1)}, bf16[256,1024]{1,0:T(8,128)(2,1)S(1)}, u32[]{:S(2)}, u32[]{:S(2)}) collective-permute-start(bf16[256,1024]{1,0:T(8,128)(2,1)S(1)} %broadcast_select_fusion), channel_id=1, source_target_pairs={{0,68},{1,69},{2,70},{3,71},{4,72},{5,73},{6,74},{7,75},{8,76},{9,... | collective-permute-start | bytes 1572872 | tf_op jit(solution)/shard_map/ppermute | solution.py:43
  5.1 2.7 %collective-permute-start.2 = (s32[1,128]{1,0:T(1,128)S(1)}, s32[1,128]{1,0:T(1,128)S(1)}, u32[]{:S(2)}, u32[]{:S(2)}) collective-permute-start(s32[1,128]{1,0:T(1,128)S(1)} %pad_bitcast_fusion), channel_id=1, source_target_pairs={{0,1},{1,2},{2,3},{3,0},{4,5},{5,6},{6,7},{7,4},{8,9},{9,10},{10,1... | collective-permute-start | bytes 1544 | tf_op jit(solution)/shard_map/ppermute | solution.py:49
  5.3 3.9 %collective-permute-start.1 = (s32[1,128]{1,0:T(1,128)S(1)}, s32[1,128]{1,0:T(1,128)S(1)}, u32[]{:S(2)}, u32[]{:S(2)}) collective-permute-start(s32[1,128]{1,0:T(1,128)S(1)} %pad_bitcast_fusion), channel_id=1, source_target_pairs={{0,2},{1,3},{2,0},{3,1},{4,6},{5,7},{6,4},{7,5},{8,10},{9,11},{10,... | collective-permute-start | bytes 1544 | tf_op jit(solution)/shard_map/ppermute | solution.py:49
  7.4 3.9 %collective-permute-start = (s32[1,128]{1,0:T(1,128)S(1)}, s32[1,128]{1,0:T(1,128)S(1)}, u32[]{:S(2)}, u32[]{:S(2)}) collective-permute-start(s32[1,128]{1,0:T(1,128)S(1)} %pad_bitcast_fusion), channel_id=1, source_target_pairs={{0,3},{1,0},{2,1},{3,2},{4,7},{5,4},{6,5},{7,6},{8,11},{9,8},{10,9... | collective-permute-start | bytes 1544 | tf_op jit(solution)/shard_map/ppermute | solution.py:49
  7.4 16.5 %collective-permute-start.3 = (bf16[256,1024]{1,0:T(8,128)(2,1)S(1)}, bf16[256,1024]{1,0:T(8,128)(2,1)S(1)}, u32[]{:S(2)}, u32[]{:S(2)}) collective-permute-start(bf16[256,1024]{1,0:T(8,128)(2,1)S(1)} %broadcast_select_fusion), channel_id=1, source_target_pairs={{0,64},{1,65},{2,66},{3,67},{4,68},{5,69},{6,70},{7,71},{8,72},{9,... | collective-permute-start | bytes 1572872 | tf_op jit(solution)/shard_map/ppermute | solution.py:43
  11.3 22.8 %collective-permute-start.4 = (bf16[256,1024]{1,0:T(8,128)(2,1)S(1)}, bf16[256,1024]{1,0:T(8,128)(2,1)S(1)}, u32[]{:S(2)}, u32[]{:S(2)}) collective-permute-start(bf16[256,1024]{1,0:T(8,128)(2,1)S(1)} %broadcast_select_fusion), channel_id=1, source_target_pairs={{0,72},{1,73},{2,74},{3,75},{4,76},{5,77},{6,78},{7,79},{8,80},{9,... | collective-permute-start | bytes 1572872 | tf_op jit(solution)/shard_map/ppermute | solution.py:43
  15.8 1.6 %copy-start.1 = (bf16[1024,1024]{1,0:T(8,128)(2,1)S(1)}, bf16[1024,1024]{1,0:T(8,128)(2,1)}, u32[]{:S(2)}) copy-start(bf16[1024,1024]{1,0:T(8,128)(2,1)} %r_7_.1) | copy-start | bytes 6291460
  17.4 1.6 %copy-start.3 = (s32[1,256,2048]{2,1,0:T(8,128)S(1)}, s32[1,256,2048]{2,1,0:T(8,128)}, u32[]{:S(2)}) copy-start(s32[1,256,2048]{2,1,0:T(8,128)} %param.13) | copy-start | bytes 6291460
  19.0 1.0 copy-start.4
  20.0 17.7 %copy-start = (bf16[1024,2048]{1,0:T(8,128)(2,1)S(1)}, bf16[1024,2048]{1,0:T(8,128)(2,1)}, u32[]{:S(2)}) copy-start(bf16[1024,2048]{1,0:T(8,128)(2,1)} %r_5_.1) | copy-start | bytes 12582916
  21.4 16.4 %copy-start.5 = (f32[2048]{0:T(1024)S(1)}, f32[2048]{0:T(1024)}, u32[]{:S(2)}) copy-start(f32[2048]{0:T(1024)} %param.16) | copy-start | bytes 24580
  22.0 15.6 %collective-permute-start.9 = (bf16[128,1024]{1,0:T(8,128)(2,1)S(1)}, bf16[128,1024]{1,0:T(8,128)(2,1)S(1)}, u32[]{:S(2)}, u32[]{:S(2)}) collective-permute-start(bf16[128,1024]{1,0:T(8,128)(2,1)S(1)} %get-tuple-element.44), channel_id=1, source_target_pairs={{0,1},{1,2},{2,3},{3,0},{4,5},{5,6},{6,7},{7,4},{8,9},{9,10},{10,1... | collective-permute-start | bytes 786440 | tf_op jit(solution)/shard_map/ppermute | solution.py:49
  22.4 15.2 %collective-permute-start.10 = (bf16[128,1024]{1,0:T(8,128)(2,1)S(1)}, bf16[128,1024]{1,0:T(8,128)(2,1)S(1)}, u32[]{:S(2)}, u32[]{:S(2)}) collective-permute-start(bf16[128,1024]{1,0:T(8,128)(2,1)S(1)} %get-tuple-element.45), channel_id=1, source_target_pairs={{0,2},{1,3},{2,0},{3,1},{4,6},{5,7},{6,4},{7,5},{8,10},{9,11},{10,... | collective-permute-start | bytes 786440 | tf_op jit(solution)/shard_map/ppermute | solution.py:49
  23.9 13.8 %collective-permute-start.11 = (bf16[128,1024]{1,0:T(8,128)(2,1)S(1)}, bf16[128,1024]{1,0:T(8,128)(2,1)S(1)}, u32[]{:S(2)}, u32[]{:S(2)}) collective-permute-start(bf16[128,1024]{1,0:T(8,128)(2,1)S(1)} %get-tuple-element.46), channel_id=1, source_target_pairs={{0,3},{1,0},{2,1},{3,2},{4,7},{5,4},{6,5},{7,6},{8,11},{9,8},{10,9... | collective-permute-start | bytes 786440 | tf_op jit(solution)/shard_map/ppermute | solution.py:49
  34.8 16.0 %collective-permute-start.5 = (bf16[128,1024]{1,0:T(8,128)(2,1)S(1)}, bf16[128,1024]{1,0:T(8,128)(2,1)S(1)}, u32[]{:S(2)}, u32[]{:S(2)}) collective-permute-start(bf16[128,1024]{1,0:T(8,128)(2,1)S(1)} %get-tuple-element.40), channel_id=1, source_target_pairs={{0,3},{1,0},{2,1},{3,2},{4,7},{5,4},{6,5},{7,6},{8,11},{9,8},{10,9... | collective-permute-start | bytes 786440 | tf_op jit(solution)/shard_map/ppermute | solution.py:49
  35.4 7.5 %collective-permute-start.6 = (bf16[128,1024]{1,0:T(8,128)(2,1)S(1)}, bf16[128,1024]{1,0:T(8,128)(2,1)S(1)}, u32[]{:S(2)}, u32[]{:S(2)}) collective-permute-start(bf16[128,1024]{1,0:T(8,128)(2,1)S(1)} %get-tuple-element.42), channel_id=1, source_target_pairs={{0,1},{1,2},{2,3},{3,0},{4,5},{5,6},{6,7},{7,4},{8,9},{9,10},{10,1... | collective-permute-start | bytes 786440 | tf_op jit(solution)/shard_map/ppermute | solution.py:49
  37.6 11.0 %collective-permute-start.7 = (bf16[128,1024]{1,0:T(8,128)(2,1)S(1)}, bf16[128,1024]{1,0:T(8,128)(2,1)S(1)}, u32[]{:S(2)}, u32[]{:S(2)}) collective-permute-start(bf16[128,1024]{1,0:T(8,128)(2,1)S(1)} %get-tuple-element.43), channel_id=1, source_target_pairs={{0,2},{1,3},{2,0},{3,1},{4,6},{5,7},{6,4},{7,5},{8,10},{9,11},{10,... | collective-permute-start | bytes 786440 | tf_op jit(solution)/shard_map/ppermute | solution.py:49
  48.6 2.2 %copy-start.6 = (bf16[2048,1024]{1,0:T(8,128)(2,1)S(1)}, bf16[2048,1024]{1,0:T(8,128)(2,1)}, u32[]{:S(2)}) copy-start(bf16[2048,1024]{1,0:T(8,128)(2,1)} %r_9_.1) | copy-start | bytes 12582916
  48.6 2.3 %copy-start.7 = (bf16[1,256,1024]{2,1,0:T(8,128)(2,1)S(1)}, bf16[1,256,1024]{2,1,0:T(8,128)(2,1)}, u32[]{:S(2)}) copy-start(bf16[1,256,1024]{2,1,0:T(8,128)(2,1)} %param.14) | copy-start | bytes 1572868
  48.6 2.3 %copy-start.8 = (f32[1024]{0:T(1024)S(1)}, f32[1024]{0:T(1024)}, u32[]{:S(2)}) copy-start(f32[1024]{0:T(1024)} %param.19) | copy-start | bytes 12292
  57.2 13.9 %collective-permute-start.17 = (bf16[128,1024]{1,0:T(8,128)(2,1)S(1)}, bf16[128,1024]{1,0:T(8,128)(2,1)S(1)}, u32[]{:S(2)}, u32[]{:S(2)}) collective-permute-start(bf16[128,1024]{1,0:T(8,128)(2,1)S(1)} %get-tuple-element.66), channel_id=1, source_target_pairs={{0,2},{1,3},{2,0},{3,1},{4,6},{5,7},{6,4},{7,5},{8,10},{9,11},{10,... | collective-permute-start | bytes 786440 | tf_op jit(solution)/shard_map/ppermute | solution.py:49
  58.7 18.2 %collective-permute-start.18 = (bf16[128,1024]{1,0:T(8,128)(2,1)S(1)}, bf16[128,1024]{1,0:T(8,128)(2,1)S(1)}, u32[]{:S(2)}, u32[]{:S(2)}) collective-permute-start(bf16[128,1024]{1,0:T(8,128)(2,1)S(1)} %get-tuple-element.67), channel_id=1, source_target_pairs={{0,1},{1,2},{2,3},{3,0},{4,5},{5,6},{6,7},{7,4},{8,9},{9,10},{10,1... | collective-permute-start | bytes 786440 | tf_op jit(solution)/shard_map/ppermute | solution.py:49
  60.9 17.4 %collective-permute-start.16 = (bf16[128,1024]{1,0:T(8,128)(2,1)S(1)}, bf16[128,1024]{1,0:T(8,128)(2,1)S(1)}, u32[]{:S(2)}, u32[]{:S(2)}) collective-permute-start(bf16[128,1024]{1,0:T(8,128)(2,1)S(1)} %get-tuple-element.58.r_7_), channel_id=1, source_target_pairs={{0,3},{1,0},{2,1},{3,2},{4,7},{5,4},{6,5},{7,6},{8,11},{9,8},{10,9... | collective-permute-start | bytes 786440 | tf_op jit(solution)/shard_map/ppermute | solution.py:49
  60.9 6.7 %copy-start.2 = (bf16[1024,1024]{1,0:T(8,128)(2,1)S(1)}, bf16[1024,1024]{1,0:T(8,128)(2,1)}, u32[]{:S(2)}) copy-start(bf16[1024,1024]{1,0:T(8,128)(2,1)} %r_7_.1) | copy-start | bytes 6291460
  63.7 15.6 %collective-permute-start.13 = (bf16[128,1152]{1,0:T(8,128)(2,1)S(1)}, bf16[128,1152]{1,0:T(8,128)(2,1)S(1)}, u32[]{:S(2)}, u32[]{:S(2)}) collective-permute-start(bf16[128,1152]{1,0:T(8,128)(2,1)S(1)} %get-tuple-element.62), channel_id=1, source_target_pairs={{66,0},{67,1},{72,2},{73,3},{70,4},{71,5},{76,6},{77,7},{74,8},{75... | collective-permute-start | bytes 884744 | tf_op jit(solution)/shard_map/ppermute | solution.py:59
  67.5 20.2 %collective-permute-start.12 = (bf16[128,1152]{1,0:T(8,128)(2,1)S(1)}, bf16[128,1152]{1,0:T(8,128)(2,1)S(1)}, u32[]{:S(2)}, u32[]{:S(2)}) collective-permute-start(bf16[128,1152]{1,0:T(8,128)(2,1)S(1)} %get-tuple-element.59.r_9_), channel_id=1, source_target_pairs={{65,0},{66,1},{67,2},{72,3},{69,4},{70,5},{71,6},{76,7},{73,8},{74... | collective-permute-start | bytes 884744 | tf_op jit(solution)/shard_map/ppermute | solution.py:59
  71.1 16.4 %collective-permute-start.14 = (bf16[128,1152]{1,0:T(8,128)(2,1)S(1)}, bf16[128,1152]{1,0:T(8,128)(2,1)S(1)}, u32[]{:S(2)}, u32[]{:S(2)}) collective-permute-start(bf16[128,1152]{1,0:T(8,128)(2,1)S(1)} %get-tuple-element.63), channel_id=1, source_target_pairs={{67,0},{72,1},{73,2},{74,3},{71,4},{76,5},{77,6},{78,7},{75,8},{80... | collective-permute-start | bytes 884744 | tf_op jit(solution)/shard_map/ppermute | solution.py:59
  76.9 11.2 %collective-permute-start.15 = (bf16[256,1024]{1,0:T(8,128)(2,1)S(1)}, bf16[256,1024]{1,0:T(8,128)(2,1)S(1)}, u32[]{:S(2)}, u32[]{:S(2)}) collective-permute-start(bf16[256,1024]{1,0:T(8,128)(2,1)S(1)} %get-tuple-element.64), channel_id=1, source_target_pairs={{0,64},{1,65},{2,66},{3,67},{4,68},{5,69},{6,70},{7,71},{8,72},{9,... | collective-permute-start | bytes 1572872 | tf_op jit(solution)/shard_map/ppermute | solution.py:43
  79.2 24.6 %collective-permute-start.19 = (bf16[256,1024]{1,0:T(8,128)(2,1)S(1)}, bf16[256,1024]{1,0:T(8,128)(2,1)S(1)}, u32[]{:S(2)}, u32[]{:S(2)}) collective-permute-start(bf16[256,1024]{1,0:T(8,128)(2,1)S(1)} %shard_map.122), channel_id=1, source_target_pairs={{0,124},{1,125},{2,126},{3,127},{4,64},{5,65},{6,66},{7,67},{8,68}... | collective-permute-start | bytes 1572872 | tf_op jit(solution)/shard_map/ppermute | solution.py:43

commit v6 on v5

--- a/solution.py
+++ b/solution.py
@@ -9,6 +9,7 @@
 DEAD = 16384.0
 LIMIT = 8192.0
 MICROSECOND = 10**9
+FAR_ORDER = (1, 3, 2)
 LINE = 4
 F32 = jnp.float32
 BF16 = jnp.bfloat16
@@ -92,7 +93,7 @@
 
 
 def slots(p):
-    return [0, LINE] + [near(p, d) for d in range(1, LINE)] + [far(p, d) for d in range(1, LINE)]
+    return [0, LINE] + [near(p, d) for d in range(1, LINE)] + [far(p, d) for d in FAR_ORDER]
 
 
 def tiles_kernel(block, place_ref, lists_ref, counts_ref, x_ref, sw_ref, tiles_ref, tiles_t_ref, self_ref):
@@ -138,8 +139,8 @@
 
 
 def layer_kernel(
-    block, live_ref, got_ref, q_ref, qb_ref, tiles_ref, acc_ref, deg_ref, self_ref, up_ref, nb_ref, ob_ref, tt_ref,
-    msg_ref, g_ref, gpool_ref, pre_ref, last_ref, near1, near2, near3, pooled_ref, gn_ref,
+    block, live_ref, place_ref, lists_ref, got_ref, q_ref, qb_ref, tiles_ref, acc_ref, deg_ref, self_ref, up_ref, nb_ref, ob_ref, tt_ref,
+    early_ref, g_ref, gpool_ref, pre_ref, out1, out2, out3, pooled_ref, gn_ref, last_ref,
 ):
     rows, width = self_ref.shape
     hidden = nb_ref.shape[0]
@@ -173,11 +174,17 @@
         cols = slice(n * step, (n + 1) * step)
         gpool_ref[:, cols] = (dot(g, nb_ref[cols, :], 1, 1) * inv_deg).astype(BF16)
 
+    outs = (out1, out2, out3)
+
     def store(cols, part):
-        for i, out in enumerate((near1, near2, near3)):
+        for i, out in enumerate(outs):
             out[:, cols] = part[i * block : (i + 1) * block].astype(BF16)
 
-    back_dot(2 * block, tt_ref, gpool_ref, [msg_ref[2 * block :, :]], q_ref, gn_ref, store)
+    for d, out in zip(FAR_ORDER, outs):
+        which = lists_ref[far(place_ref[0], d), 1].astype(F32)
+        out[:, width:] = jnp.full((block, 128), which, F32).astype(BF16)
+    first = (1 + LINE) * block
+    back_dot(first, tt_ref, gpool_ref, [early_ref[...], last_ref[...]], q_ref, gn_ref, store)
 
 
 def back_dot(first, tt_ref, gpool_ref, messages, q_ref, gn_ref, store):
@@ -194,19 +201,14 @@
         store(cols, dot(gn, q_ref[cols, :], 1, 1))
 
 
-def back_far_kernel(block, place_ref, lists_ref, tt_ref, gpool_ref, early_ref, last_ref, q_ref, _, *refs):
+def back_near_kernel(block, tt_ref, gpool_ref, msg_ref, q_ref, _, *refs):
     outs, gn_ref = refs[:-1], refs[-1]
-    width = q_ref.shape[0]
 
     def store(cols, part):
         for i, out in enumerate(outs):
             out[:, cols] = part[i * block : (i + 1) * block].astype(BF16)
 
-    for d, out in enumerate(outs, 1):
-        which = lists_ref[far(place_ref[0], d), 1].astype(F32)
-        out[:, width:] = jnp.full((block, 128), which, F32).astype(BF16)
-    messages = [early_ref[...], last_ref[...]]
-    back_dot((1 + LINE) * block, tt_ref, gpool_ref, messages, q_ref, gn_ref, store)
+    back_dot(2 * block, tt_ref, gpool_ref, [msg_ref[2 * block :, :]], q_ref, gn_ref, store)
 
 
 def back_own_kernel(
@@ -300,7 +302,7 @@
         (place, *metas, same, below2),
         scalars + [VMEM] * 2,
     )
-    got_far = [along(b, d) for d, b in zip(steps, sent)]
+    got_far = [along(sent[d - 1], d) for d in FAR_ORDER]
     split = 1 + LINE
 
     def message(first, last, ins, specs):
@@ -320,28 +322,31 @@
         split, reach - 1, (*got_far[:-1], q, qb, tiles, acc, deg), [VMEM] * (5 + len(steps) - 1)
     )
     gn = pltpu.VMEM((3 * block, hidden), BF16)
-    g, gpool, pre, msg_c, *near_back = call(
+    g, gpool, pre, *far_back = call(
         lambda *r: layer_kernel(block, *r),
-        [two, ((rows, hidden), BF16), ((rows, width), F32), ((block, hidden), BF16)] + [one] * 3,
-        (live, got_far[-1], q, qb, tiles, acc, deg, self_pre, up, nb, ob, tiles_t, msg_a),
-        [SMEM] + [VMEM] * 12,
-        scratch=[pltpu.VMEM((rows, hidden), BF16), gn],
+        [two, ((rows, hidden), BF16), ((rows, width), F32)] + [((block, width + 128), BF16)] * 3,
+        (
+            live, place, lists, got_far[-1], q, qb, tiles, acc, deg, self_pre, up, nb, ob, tiles_t,
+            msg_b,
+        ),
+        [SMEM] * 3 + [VMEM] * 12,
+        scratch=[pltpu.VMEM((rows, hidden), BF16), gn, pltpu.VMEM((block, hidden), BF16)],
         flops=8 * MICROSECOND,
     )
-    back_near = [along(b, -d) for d, b in zip(steps, near_back)]
-    far_back = call(
-        lambda *r: back_far_kernel(block, *r),
-        [((block, width + 128), BF16)] * 3,
-        (place, lists, tiles_t, gpool, msg_b, msg_c, q, near_back[0]),
-        [SMEM] * 2 + [VMEM] * 5 + [HELD],
+    back_far = [straight_back(b, d) for d, b in zip(FAR_ORDER, far_back)]
+    near_back = call(
+        lambda *r: back_near_kernel(block, *r),
+        [one] * 3,
+        (tiles_t, gpool, msg_a, q, far_back[0]),
+        [VMEM] * 4 + [HELD],
         scratch=[gn],
         flops=2 * MICROSECOND,
     )
-    back_far = [straight_back(b, d) for d, b in zip(steps, far_back)]
+    back_near = [along(b, -d) for d, b in zip(steps, near_back)]
     own_same, own_below, gself, emb = call(
         lambda *r: back_own_kernel(block, *r),
         [two, one, ((rows, width), F32), two],
-        (lists, live, tiles_t, gpool, msg_a, q, g, sw, pre, far_back[0]),
+        (lists, live, tiles_t, gpool, msg_a, q, g, sw, pre, near_back[0]),
         [SMEM] * 2 + [VMEM] * 7 + [HELD],
         scratch=[pltpu.VMEM((2 * block, hidden), BF16)],
         flops=3 * MICROSECOND,

time: 106 us -> 111 us (1.047); the launches traced: 105 us -> 111 us
  waiting for transfers between devices: 44.3 us -> 53.1 us
  starting transfers between devices: 27.7 us -> 25.2 us
    ppermute x12, waiting for transfers between devices: 9.93 us -> 29.3 us  [along(): return lax.ppermute(x, 'dom', pairs)]
    ppermute x3, waiting for transfers between devices: 8.49 us -> 0.01 us  [straight_back(): return lax.ppermute(x, ('side', 'dom'), pairs)]
    ppermute x5, waiting for transfers between devices: 25.8 us -> 23.7 us  [swap_rows(): return lax.ppermute(x, ('side', 'dom'), pairs)]
    ppermute x3, starting transfers between devices: 9.62 us -> 7.59 us  [straight_back(): return lax.ppermute(x, ('side', 'dom'), pairs)]
  transfers between devices with their start and end apart: 20 -> 20, of which waited for: 9 -> 9; matrix products, arithmetic and copies ran while one was open for 1% -> 1% of each run, Pallas kernels for 16% -> 15%
where the time goes in v6:
time: 111 us
  waiting for transfers between devices  53.1 us (48%)
  starting transfers between devices  25.2 us (23%)
  Pallas kernels  24.5 us (22%)
  local copies, waits for them, and re-layouts  5.79 us (5%)
  between operations  1.48 us (1%)
  other arithmetic  1.16 us (1%)
    ppermute x12, waiting for transfers between devices, along(): return lax.ppermute(x, 'dom', pairs)  29.3 us
    pallas_call x11, Pallas kernels, call(): pl.pallas_call(kernel, out_shape=[jax.ShapeDtypeStruct(s, d) for s, d in...  24.5 us
    ppermute x5, waiting for transfers between devices, swap_rows(): return lax.ppermute(x, ('side', 'dom'), pairs)  23.7 us
    ppermute x12, starting transfers between devices, along(): return lax.ppermute(x, 'dom', pairs)  10.6 us
    ppermute x3, starting transfers between devices, straight_back(): return lax.ppermute(x, ('side', 'dom'), pairs)  7.59 us
    ppermute x5, starting transfers between devices, swap_rows(): return lax.ppermute(x, ('side', 'dom'), pairs)  7.04 us
    unnamed x18, local copies, waits for them, and re-layouts  4.35 us
  transfers between devices with their start and end apart: 20, of which 9 were waited for; matrix products, arithmetic and copies ran while one was open for 1% of the time, Pallas kernels for 15%

profile of v6, /device:TPU:7, one launch (start us, length us, event | category | flops | bytes accessed | tf_op | source)
XLA Modules:
  0.0 111.1 jit_solution(7670890258304104407)
XLA Ops:
  1.3 1.2 %broadcast_select_fusion = bf16[256,1024]{1,0:T(8,128)(2,1)S(1)} fusion(pred[256]{0:T(512)(128)(4,1)S(1)} %iota_compare_fusion, bf16[1,256,1024]{2,1,0:T(8,128)(2,1)} %param.10), kind=kLoop, calls=%fused_computation | loop fusion | flops 262144 | bytes 1048832 | tf_op jit(solution)/shard_map/jit(_where)/select_n | solution.py:274
  2.5 1.9 %collective-permute-start.8 = (bf16[256,1024]{1,0:T(8,128)(2,1)S(1)}, bf16[256,1024]{1,0:T(8,128)(2,1)S(1)}, u32[]{:S(2)}, u32[]{:S(2)}) collective-permute-start(bf16[256,1024]{1,0:T(8,128)(2,1)S(1)} %broadcast_select_fusion), channel_id=1, source_target_pairs={{0,68},{1,69},{2,70},{3,71},{4,72},{5,73},{6,74},{7,75},{8,76},{9,... | collective-permute-start | bytes 1572872 | tf_op jit(solution)/shard_map/ppermute | solution.py:44
  5.3 2.2 %collective-permute-start.1 = (s32[1,128]{1,0:T(1,128)S(1)}, s32[1,128]{1,0:T(1,128)S(1)}, u32[]{:S(2)}, u32[]{:S(2)}) collective-permute-start(s32[1,128]{1,0:T(1,128)S(1)} %pad_bitcast_fusion), channel_id=1, source_target_pairs={{0,2},{1,3},{2,0},{3,1},{4,6},{5,7},{6,4},{7,5},{8,10},{9,11},{10,... | collective-permute-start | bytes 1544 | tf_op jit(solution)/shard_map/ppermute | solution.py:50
  7.8 1.4 %collective-permute-done.1.r_2_.r_3_ = s32[1,128]{1,0:T(1,128)S(1)} collective-permute-done((s32[1,128]{1,0:T(1,128)S(1)}, s32[1,128]{1,0:T(1,128)S(1)}, u32[]{:S(2)}, u32[]{:S(2)}) %collective-permute-start.1) | collective-permute-done | bytes 544 | tf_op jit(solution)/shard_map/ppermute | solution.py:50
  9.2 2.1 %collective-permute-done.r_1_.r_2_ = s32[1,128]{1,0:T(1,128)S(1)} collective-permute-done((s32[1,128]{1,0:T(1,128)S(1)}, s32[1,128]{1,0:T(1,128)S(1)}, u32[]{:S(2)}, u32[]{:S(2)}) %collective-permute-start) | collective-permute-done | bytes 544 | tf_op jit(solution)/shard_map/ppermute | solution.py:50
  11.3 3.7 %collective-permute-start.4 = (bf16[256,1024]{1,0:T(8,128)(2,1)S(1)}, bf16[256,1024]{1,0:T(8,128)(2,1)S(1)}, u32[]{:S(2)}, u32[]{:S(2)}) collective-permute-start(bf16[256,1024]{1,0:T(8,128)(2,1)S(1)} %broadcast_select_fusion), channel_id=1, source_target_pairs={{0,72},{1,73},{2,74},{3,75},{4,76},{5,77},{6,78},{7,79},{8,80},{9,... | collective-permute-start | bytes 1572872 | tf_op jit(solution)/shard_map/ppermute | solution.py:44
  15.8 1.6 %copy-done.1 = bf16[1024,1024]{1,0:T(8,128)(2,1)S(1)} copy-done((bf16[1024,1024]{1,0:T(8,128)(2,1)S(1)}, bf16[1024,1024]{1,0:T(8,128)(2,1)}, u32[]{:S(2)}) %copy-start.1) | copy-done | bytes 2097176
  17.4 1.6 %copy-done.3 = s32[1,256,2048]{2,1,0:T(8,128)S(1)} copy-done((s32[1,256,2048]{2,1,0:T(8,128)S(1)}, s32[1,256,2048]{2,1,0:T(8,128)}, u32[]{:S(2)}) %copy-start.3) | copy-done | bytes 2097176
  19.0 1.0 copy-done.4
  20.0 1.3 %shard_map.113 = (bf16[256,1024]{1,0:T(8,128)(2,1)S(1)}, bf16[1024,256]{1,0:T(8,128)(2,1)S(1)}, f32[256,1024]{1,0:T(8,128)S(1)}) custom-call(s32[1]{0:T(128)} %bitcast.2.r_0_.r_1_, s32[8,2]{1,0:T(8,128)S(1)} %copy.15.r_1_.r_0_.r_2_, s32[256,2048]{1,0:T(8,128)S(1)} %bitcast.20, bf16[256,1024]{1,0:T(8,128)(2,1)S(1)} %bitcast.21, bf16[1024,1024]{1,0:T(8,128)(2,1)S(1)} %copy-done.1), custom_call_target="tpu_custom_call" | custom-call | flops 536870912 | bytes 1048576 | tf_op jit(solution)/shard_map/pallas_call | solution.py:26
  22.4 1.6 %collective-permute-start.10 = (bf16[128,1024]{1,0:T(8,128)(2,1)S(1)}, bf16[128,1024]{1,0:T(8,128)(2,1)S(1)}, u32[]{:S(2)}, u32[]{:S(2)}) collective-permute-start(bf16[128,1024]{1,0:T(8,128)(2,1)S(1)} %get-tuple-element.44), channel_id=1, source_target_pairs={{0,2},{1,3},{2,0},{3,1},{4,6},{5,7},{6,4},{7,5},{8,10},{9,11},{10,... | collective-permute-start | bytes 786440 | tf_op jit(solution)/shard_map/ppermute | solution.py:50
  24.0 10.2 %collective-permute-done.4.r_5_ = bf16[256,1024]{1,0:T(8,128)(2,1)S(1)} collective-permute-done((bf16[256,1024]{1,0:T(8,128)(2,1)S(1)}, bf16[256,1024]{1,0:T(8,128)(2,1)S(1)}, u32[]{:S(2)}, u32[]{:S(2)}) %collective-permute-start.4) | collective-permute-done | bytes 524320 | tf_op jit(solution)/shard_map/ppermute | solution.py:44
  34.8 1.2 %collective-permute-start.5 = (bf16[128,1024]{1,0:T(8,128)(2,1)S(1)}, bf16[128,1024]{1,0:T(8,128)(2,1)S(1)}, u32[]{:S(2)}, u32[]{:S(2)}) collective-permute-start(bf16[128,1024]{1,0:T(8,128)(2,1)S(1)} %get-tuple-element.39), channel_id=1, source_target_pairs={{0,2},{1,3},{2,0},{3,1},{4,6},{5,7},{6,4},{7,5},{8,10},{9,11},{10,... | collective-permute-start | bytes 786440 | tf_op jit(solution)/shard_map/ppermute | solution.py:50
  36.0 1.8 %collective-permute-start.6 = (bf16[128,1024]{1,0:T(8,128)(2,1)S(1)}, bf16[128,1024]{1,0:T(8,128)(2,1)S(1)}, u32[]{:S(2)}, u32[]{:S(2)}) collective-permute-start(bf16[128,1024]{1,0:T(8,128)(2,1)S(1)} %get-tuple-element.41), channel_id=1, source_target_pairs={{0,1},{1,2},{2,3},{3,0},{4,5},{5,6},{6,7},{7,4},{8,9},{9,10},{10,1... | collective-permute-start | bytes 786440 | tf_op jit(solution)/shard_map/ppermute | solution.py:50
  37.9 4.6 %shard_map.116 = (bf16[640,2048]{1,0:T(8,128)(2,1)S(1)}, f32[256,2048]{1,0:T(8,128)S(1)}, f32[256,128]{1,0:T(8,128)S(1)}) custom-call(s32[8,2]{1,0:T(8,128)S(1)} %copy.15.r_1_.r_0_.r_2_, bf16[256,1024]{1,0:T(8,128)(2,1)S(1)} %collective-permute-done.3.r_4_.r_1_, bf16[256,1024]{1,0:T(8,128)(2,1)S(1)} %collective-permute-done.8.r_4_.r_2_, ...), custom_call_target="tpu_custom_call" | custom-call | flops 3355443200 | bytes 1048576 | tf_op jit(solution)/shard_map/pallas_call | solution.py:26
  42.5 4.9 %collective-permute-done.6.r_0_ = bf16[128,1024]{1,0:T(8,128)(2,1)S(1)} collective-permute-done((bf16[128,1024]{1,0:T(8,128)(2,1)S(1)}, bf16[128,1024]{1,0:T(8,128)(2,1)S(1)}, u32[]{:S(2)}, u32[]{:S(2)}) %collective-permute-start.6) | collective-permute-done | bytes 262176 | tf_op jit(solution)/shard_map/ppermute | solution.py:50
  47.4 2.9 %collective-permute-done.7.r_1_ = bf16[128,1024]{1,0:T(8,128)(2,1)S(1)} collective-permute-done((bf16[128,1024]{1,0:T(8,128)(2,1)S(1)}, bf16[128,1024]{1,0:T(8,128)(2,1)S(1)}, u32[]{:S(2)}, u32[]{:S(2)}) %collective-permute-start.7) | collective-permute-done | bytes 262176 | tf_op jit(solution)/shard_map/ppermute | solution.py:50
  50.3 2.2 %shard_map.117 = (bf16[256,2048]{1,0:T(8,128)(2,1)S(1)}, f32[256,2048]{1,0:T(8,128)S(1)}, f32[256,128]{1,0:T(8,128)S(1)}) custom-call(bf16[128,1024]{1,0:T(8,128)(2,1)S(1)} %collective-permute-done.6.r_0_, bf16[128,1024]{1,0:T(8,128)(2,1)S(1)} %collective-permute-done.7.r_1_, bf16[1024,2048]{1,0:T(8,128)(2,1)S(1)} %copy-done, f32[1,2048]{1,0:T(1,128)S(1)} %bitcast.23, ...), custom_call_target="tpu_custom_call" | custom-call | flops 1342177280 | bytes 1048576 | tf_op jit(solution)/shard_map/pallas_call | solution.py:26
  52.6 7.0 %shard_map.118 = (bf16[256,1024]{1,0:T(8,128)(2,1)S(1)}, bf16[256,2048]{1,0:T(8,128)(2,1)S(1)}, f32[256,1024]{1,0:T(8,128)S(1)}, bf16[128,1152]{1,0:T(8,128)(2,1...) custom-call(s32[1]{0:T(128)} %bitcast.16.r_0_, s32[1]{0:T(128)} %bitcast.2.r_0_.r_1_, ...), custom_call_target="tpu_custom_call" | custom-call | flops 8000000000 | bytes 1048576 | tf_op jit(solution)/shard_map/pallas_call | solution.py:26
  59.6 0.8 collective-permute-start.13
  60.3 6.8 %collective-permute-start.12 = (bf16[128,1152]{1,0:T(8,128)(2,1)S(1)}, bf16[128,1152]{1,0:T(8,128)(2,1)S(1)}, u32[]{:S(2)}, u32[]{:S(2)}) collective-permute-start(bf16[128,1152]{1,0:T(8,128)(2,1)S(1)} %get-tuple-element.56.r_4_), channel_id=1, source_target_pairs={{65,0},{66,1},{67,2},{72,3},{69,4},{70,5},{71,6},{76,7},{73,8},{74... | collective-permute-start | bytes 884744 | tf_op jit(solution)/shard_map/ppermute | solution.py:60
  67.1 2.2 %shard_map.119 = (bf16[128,1024]{1,0:T(8,128)(2,1)S(1)}, bf16[128,1024]{1,0:T(8,128)(2,1)S(1)}, bf16[128,1024]{1,0:T(8,128)(2,1)S(1)}) custom-call(bf16[1024,256]{1,0:T(8,128)(2,1)S(1)} %get-tuple-element.34.r_13_.r_0_.r_2_, bf16[256,2048]{1,0:T(8,128)(2,1)S(1)} %get-tuple-element.52.r_1_.r_3_, bf16[640,2048]{1,0:T(8,128)(2,1)S(1)} %get-tuple-element.53.r_2_.r_4_, ...), custom_call_target="tpu_custom_call" | custom-call | flops 2000000000 | bytes 1048576 | tf_op jit(solution)/shard_map/pallas_call | solution.py:26
  69.4 1.8 %collective-permute-start.17 = (bf16[128,1024]{1,0:T(8,128)(2,1)S(1)}, bf16[128,1024]{1,0:T(8,128)(2,1)S(1)}, u32[]{:S(2)}, u32[]{:S(2)}) collective-permute-start(bf16[128,1024]{1,0:T(8,128)(2,1)S(1)} %get-tuple-element.64), channel_id=1, source_target_pairs={{0,2},{1,3},{2,0},{3,1},{4,6},{5,7},{6,4},{7,5},{8,10},{9,11},{10,... | collective-permute-start | bytes 786440 | tf_op jit(solution)/shard_map/ppermute | solution.py:50
  71.1 1.3 %collective-permute-start.18 = (bf16[128,1024]{1,0:T(8,128)(2,1)S(1)}, bf16[128,1024]{1,0:T(8,128)(2,1)S(1)}, u32[]{:S(2)}, u32[]{:S(2)}) collective-permute-start(bf16[128,1024]{1,0:T(8,128)(2,1)S(1)} %get-tuple-element.65), channel_id=1, source_target_pairs={{0,1},{1,2},{2,3},{3,0},{4,5},{5,6},{6,7},{7,4},{8,9},{9,10},{10,1... | collective-permute-start | bytes 786440 | tf_op jit(solution)/shard_map/ppermute | solution.py:50
  72.6 3.6 %shard_map.120 = (bf16[256,1024]{1,0:T(8,128)(2,1)S(1)}, bf16[128,1024]{1,0:T(8,128)(2,1)S(1)}, f32[256,1024]{1,0:T(8,128)S(1)}, bf16[256,1024]{1,0:T(8,128)(2,1)}) custom-call(s32[8,2]{1,0:T(8,128)S(1)} %copy.15.r_1_.r_0_.r_2_, s32[1]{0:T(128)} %bitcast.17.r_1_, bf16[1024,256]{1,0:T(8,128)(2,1)S(1)} %get-tuple-element.34.r_13_.r_0_.r_2_, ...), custom_call_target="tpu_custom_call" | custom-call | flops 3000000000 | bytes 1048576 | tf_op jit(solution)/shard_map/pallas_call | solution.py:26
  76.2 5.3 %collective-permute-done.17.r_7_ = bf16[128,1024]{1,0:T(8,128)(2,1)S(1)} collective-permute-done((bf16[128,1024]{1,0:T(8,128)(2,1)S(1)}, bf16[128,1024]{1,0:T(8,128)(2,1)S(1)}, u32[]{:S(2)}, u32[]{:S(2)}) %collective-permute-start.17) | collective-permute-done | bytes 262176 | tf_op jit(solution)/shard_map/ppermute | solution.py:50
  81.5 2.6 %collective-permute-done.18.r_8_ = bf16[128,1024]{1,0:T(8,128)(2,1)S(1)} collective-permute-done((bf16[128,1024]{1,0:T(8,128)(2,1)S(1)}, bf16[128,1024]{1,0:T(8,128)(2,1)S(1)}, u32[]{:S(2)}, u32[]{:S(2)}) %collective-permute-start.18) | collective-permute-done | bytes 262176 | tf_op jit(solution)/shard_map/ppermute | solution.py:50
  84.1 1.0 collective-permute-start.15
  85.0 10.2 %collective-permute-done.16.r_6_ = bf16[128,1024]{1,0:T(8,128)(2,1)S(1)} collective-permute-done((bf16[128,1024]{1,0:T(8,128)(2,1)S(1)}, bf16[128,1024]{1,0:T(8,128)(2,1)S(1)}, u32[]{:S(2)}, u32[]{:S(2)}) %collective-permute-start.16) | collective-permute-done | bytes 262176 | tf_op jit(solution)/shard_map/ppermute | solution.py:50
  95.2 0.9 shard_map.122
  96.7 13.5 %collective-permute-done.19.below_ref = bf16[256,1024]{1,0:T(8,128)(2,1)S(1)} collective-permute-done((bf16[256,1024]{1,0:T(8,128)(2,1)S(1)}, bf16[256,1024]{1,0:T(8,128)(2,1)S(1)}, u32[]{:S(2)}, u32[]{:S(2)}) %collective-permute-start.19) | collective-permute-done | bytes 524320 | tf_op jit(solution)/shard_map/ppermute | solution.py:44
  110.1 1.0 shard_map.123
  (42 shorter events, 4.4 us)
Async XLA Ops:
  2.5 18.9 %collective-permute-start.8 = (bf16[256,1024]{1,0:T(8,128)(2,1)S(1)}, bf16[256,1024]{1,0:T(8,128)(2,1)S(1)}, u32[]{:S(2)}, u32[]{:S(2)}) collective-permute-start(bf16[256,1024]{1,0:T(8,128)(2,1)S(1)} %broadcast_select_fusion), channel_id=1, source_target_pairs={{0,68},{1,69},{2,70},{3,71},{4,72},{5,73},{6,74},{7,75},{8,76},{9,... | collective-permute-start | bytes 1572872 | tf_op jit(solution)/shard_map/ppermute | solution.py:44
  5.1 2.7 %collective-permute-start.2 = (s32[1,128]{1,0:T(1,128)S(1)}, s32[1,128]{1,0:T(1,128)S(1)}, u32[]{:S(2)}, u32[]{:S(2)}) collective-permute-start(s32[1,128]{1,0:T(1,128)S(1)} %pad_bitcast_fusion), channel_id=1, source_target_pairs={{0,1},{1,2},{2,3},{3,0},{4,5},{5,6},{6,7},{7,4},{8,9},{9,10},{10,1... | collective-permute-start | bytes 1544 | tf_op jit(solution)/shard_map/ppermute | solution.py:50
  5.3 3.9 %collective-permute-start.1 = (s32[1,128]{1,0:T(1,128)S(1)}, s32[1,128]{1,0:T(1,128)S(1)}, u32[]{:S(2)}, u32[]{:S(2)}) collective-permute-start(s32[1,128]{1,0:T(1,128)S(1)} %pad_bitcast_fusion), channel_id=1, source_target_pairs={{0,2},{1,3},{2,0},{3,1},{4,6},{5,7},{6,4},{7,5},{8,10},{9,11},{10,... | collective-permute-start | bytes 1544 | tf_op jit(solution)/shard_map/ppermute | solution.py:50
  7.4 3.9 %collective-permute-start = (s32[1,128]{1,0:T(1,128)S(1)}, s32[1,128]{1,0:T(1,128)S(1)}, u32[]{:S(2)}, u32[]{:S(2)}) collective-permute-start(s32[1,128]{1,0:T(1,128)S(1)} %pad_bitcast_fusion), channel_id=1, source_target_pairs={{0,3},{1,0},{2,1},{3,2},{4,7},{5,4},{6,5},{7,6},{8,11},{9,8},{10,9... | collective-permute-start | bytes 1544 | tf_op jit(solution)/shard_map/ppermute | solution.py:50
  7.4 16.5 %collective-permute-start.3 = (bf16[256,1024]{1,0:T(8,128)(2,1)S(1)}, bf16[256,1024]{1,0:T(8,128)(2,1)S(1)}, u32[]{:S(2)}, u32[]{:S(2)}) collective-permute-start(bf16[256,1024]{1,0:T(8,128)(2,1)S(1)} %broadcast_select_fusion), channel_id=1, source_target_pairs={{0,64},{1,65},{2,66},{3,67},{4,68},{5,69},{6,70},{7,71},{8,72},{9,... | collective-permute-start | bytes 1572872 | tf_op jit(solution)/shard_map/ppermute | solution.py:44
  11.3 22.8 %collective-permute-start.4 = (bf16[256,1024]{1,0:T(8,128)(2,1)S(1)}, bf16[256,1024]{1,0:T(8,128)(2,1)S(1)}, u32[]{:S(2)}, u32[]{:S(2)}) collective-permute-start(bf16[256,1024]{1,0:T(8,128)(2,1)S(1)} %broadcast_select_fusion), channel_id=1, source_target_pairs={{0,72},{1,73},{2,74},{3,75},{4,76},{5,77},{6,78},{7,79},{8,80},{9,... | collective-permute-start | bytes 1572872 | tf_op jit(solution)/shard_map/ppermute | solution.py:44
  15.8 1.6 %copy-start.1 = (bf16[1024,1024]{1,0:T(8,128)(2,1)S(1)}, bf16[1024,1024]{1,0:T(8,128)(2,1)}, u32[]{:S(2)}) copy-start(bf16[1024,1024]{1,0:T(8,128)(2,1)} %r_7_.1) | copy-start | bytes 6291460
  17.4 1.6 %copy-start.3 = (s32[1,256,2048]{2,1,0:T(8,128)S(1)}, s32[1,256,2048]{2,1,0:T(8,128)}, u32[]{:S(2)}) copy-start(s32[1,256,2048]{2,1,0:T(8,128)} %param.13) | copy-start | bytes 6291460
  19.0 1.0 copy-start.4
  20.0 17.8 %copy-start = (bf16[1024,2048]{1,0:T(8,128)(2,1)S(1)}, bf16[1024,2048]{1,0:T(8,128)(2,1)}, u32[]{:S(2)}) copy-start(bf16[1024,2048]{1,0:T(8,128)(2,1)} %r_5_.1) | copy-start | bytes 12582916
  21.4 16.5 %copy-start.5 = (f32[2048]{0:T(1024)S(1)}, f32[2048]{0:T(1024)}, u32[]{:S(2)}) copy-start(f32[2048]{0:T(1024)} %param.16) | copy-start | bytes 24580
  22.0 15.8 %collective-permute-start.9 = (bf16[128,1024]{1,0:T(8,128)(2,1)S(1)}, bf16[128,1024]{1,0:T(8,128)(2,1)S(1)}, u32[]{:S(2)}, u32[]{:S(2)}) collective-permute-start(bf16[128,1024]{1,0:T(8,128)(2,1)S(1)} %get-tuple-element.43), channel_id=1, source_target_pairs={{0,1},{1,2},{2,3},{3,0},{4,5},{5,6},{6,7},{7,4},{8,9},{9,10},{10,1... | collective-permute-start | bytes 786440 | tf_op jit(solution)/shard_map/ppermute | solution.py:50
  22.4 15.5 %collective-permute-start.10 = (bf16[128,1024]{1,0:T(8,128)(2,1)S(1)}, bf16[128,1024]{1,0:T(8,128)(2,1)S(1)}, u32[]{:S(2)}, u32[]{:S(2)}) collective-permute-start(bf16[128,1024]{1,0:T(8,128)(2,1)S(1)} %get-tuple-element.44), channel_id=1, source_target_pairs={{0,2},{1,3},{2,0},{3,1},{4,6},{5,7},{6,4},{7,5},{8,10},{9,11},{10,... | collective-permute-start | bytes 786440 | tf_op jit(solution)/shard_map/ppermute | solution.py:50
  23.9 13.9 %collective-permute-start.11 = (bf16[128,1024]{1,0:T(8,128)(2,1)S(1)}, bf16[128,1024]{1,0:T(8,128)(2,1)S(1)}, u32[]{:S(2)}, u32[]{:S(2)}) collective-permute-start(bf16[128,1024]{1,0:T(8,128)(2,1)S(1)} %get-tuple-element.45), channel_id=1, source_target_pairs={{0,3},{1,0},{2,1},{3,2},{4,7},{5,4},{6,5},{7,6},{8,11},{9,8},{10,9... | collective-permute-start | bytes 786440 | tf_op jit(solution)/shard_map/ppermute | solution.py:50
  34.8 17.6 %collective-permute-start.5 = (bf16[128,1024]{1,0:T(8,128)(2,1)S(1)}, bf16[128,1024]{1,0:T(8,128)(2,1)S(1)}, u32[]{:S(2)}, u32[]{:S(2)}) collective-permute-start(bf16[128,1024]{1,0:T(8,128)(2,1)S(1)} %get-tuple-element.39), channel_id=1, source_target_pairs={{0,2},{1,3},{2,0},{3,1},{4,6},{5,7},{6,4},{7,5},{8,10},{9,11},{10,... | collective-permute-start | bytes 786440 | tf_op jit(solution)/shard_map/ppermute | solution.py:50
  36.0 11.3 %collective-permute-start.6 = (bf16[128,1024]{1,0:T(8,128)(2,1)S(1)}, bf16[128,1024]{1,0:T(8,128)(2,1)S(1)}, u32[]{:S(2)}, u32[]{:S(2)}) collective-permute-start(bf16[128,1024]{1,0:T(8,128)(2,1)S(1)} %get-tuple-element.41), channel_id=1, source_target_pairs={{0,1},{1,2},{2,3},{3,0},{4,5},{5,6},{6,7},{7,4},{8,9},{9,10},{10,1... | collective-permute-start | bytes 786440 | tf_op jit(solution)/shard_map/ppermute | solution.py:50
  37.8 12.4 %collective-permute-start.7 = (bf16[128,1024]{1,0:T(8,128)(2,1)S(1)}, bf16[128,1024]{1,0:T(8,128)(2,1)S(1)}, u32[]{:S(2)}, u32[]{:S(2)}) collective-permute-start(bf16[128,1024]{1,0:T(8,128)(2,1)S(1)} %get-tuple-element.42), channel_id=1, source_target_pairs={{0,3},{1,0},{2,1},{3,2},{4,7},{5,4},{6,5},{7,6},{8,11},{9,8},{10,9... | collective-permute-start | bytes 786440 | tf_op jit(solution)/shard_map/ppermute | solution.py:50
  50.2 2.2 %copy-start.6 = (bf16[2048,1024]{1,0:T(8,128)(2,1)S(1)}, bf16[2048,1024]{1,0:T(8,128)(2,1)}, u32[]{:S(2)}) copy-start(bf16[2048,1024]{1,0:T(8,128)(2,1)} %r_11_.1) | copy-start | bytes 12582916
  50.3 2.3 %copy-start.7 = (bf16[1,256,1024]{2,1,0:T(8,128)(2,1)S(1)}, bf16[1,256,1024]{2,1,0:T(8,128)(2,1)}, u32[]{:S(2)}) copy-start(bf16[1,256,1024]{2,1,0:T(8,128)(2,1)} %param.14) | copy-start | bytes 1572868
  50.3 2.3 %copy-start.8 = (f32[1024]{0:T(1024)S(1)}, f32[1024]{0:T(1024)}, u32[]{:S(2)}) copy-start(f32[1024]{0:T(1024)} %param.19) | copy-start | bytes 12292
  59.6 36.7 %collective-permute-start.13 = (bf16[128,1152]{1,0:T(8,128)(2,1)S(1)}, bf16[128,1152]{1,0:T(8,128)(2,1)S(1)}, u32[]{:S(2)}, u32[]{:S(2)}) collective-permute-start(bf16[128,1152]{1,0:T(8,128)(2,1)S(1)} %get-tuple-element.60), channel_id=1, source_target_pairs={{67,0},{72,1},{73,2},{74,3},{71,4},{76,5},{77,6},{78,7},{75,8},{80... | collective-permute-start | bytes 884744 | tf_op jit(solution)/shard_map/ppermute | solution.py:60
  60.3 35.9 %collective-permute-start.12 = (bf16[128,1152]{1,0:T(8,128)(2,1)S(1)}, bf16[128,1152]{1,0:T(8,128)(2,1)S(1)}, u32[]{:S(2)}, u32[]{:S(2)}) collective-permute-start(bf16[128,1152]{1,0:T(8,128)(2,1)S(1)} %get-tuple-element.56.r_4_), channel_id=1, source_target_pairs={{65,0},{66,1},{67,2},{72,3},{69,4},{70,5},{71,6},{76,7},{73,8},{74... | collective-permute-start | bytes 884744 | tf_op jit(solution)/shard_map/ppermute | solution.py:60
  67.1 5.5 %copy-start.2 = (bf16[1024,1024]{1,0:T(8,128)(2,1)S(1)}, bf16[1024,1024]{1,0:T(8,128)(2,1)}, u32[]{:S(2)}) copy-start(bf16[1024,1024]{1,0:T(8,128)(2,1)} %r_7_.1) | copy-start | bytes 6291460
  69.4 12.1 %collective-permute-start.17 = (bf16[128,1024]{1,0:T(8,128)(2,1)S(1)}, bf16[128,1024]{1,0:T(8,128)(2,1)S(1)}, u32[]{:S(2)}, u32[]{:S(2)}) collective-permute-start(bf16[128,1024]{1,0:T(8,128)(2,1)S(1)} %get-tuple-element.64), channel_id=1, source_target_pairs={{0,2},{1,3},{2,0},{3,1},{4,6},{5,7},{6,4},{7,5},{8,10},{9,11},{10,... | collective-permute-start | bytes 786440 | tf_op jit(solution)/shard_map/ppermute | solution.py:50
  71.1 12.9 %collective-permute-start.18 = (bf16[128,1024]{1,0:T(8,128)(2,1)S(1)}, bf16[128,1024]{1,0:T(8,128)(2,1)S(1)}, u32[]{:S(2)}, u32[]{:S(2)}) collective-permute-start(bf16[128,1024]{1,0:T(8,128)(2,1)S(1)} %get-tuple-element.65), channel_id=1, source_target_pairs={{0,1},{1,2},{2,3},{3,0},{4,5},{5,6},{6,7},{7,4},{8,9},{9,10},{10,1... | collective-permute-start | bytes 786440 | tf_op jit(solution)/shard_map/ppermute | solution.py:50
  72.5 22.8 %collective-permute-start.16 = (bf16[128,1024]{1,0:T(8,128)(2,1)S(1)}, bf16[128,1024]{1,0:T(8,128)(2,1)S(1)}, u32[]{:S(2)}, u32[]{:S(2)}) collective-permute-start(bf16[128,1024]{1,0:T(8,128)(2,1)S(1)} %get-tuple-element.57.r_9_), channel_id=1, source_target_pairs={{0,3},{1,0},{2,1},{3,2},{4,7},{5,4},{6,5},{7,6},{8,11},{9,8},{10,9... | collective-permute-start | bytes 786440 | tf_op jit(solution)/shard_map/ppermute | solution.py:50
  81.5 14.8 %collective-permute-start.14 = (bf16[128,1152]{1,0:T(8,128)(2,1)S(1)}, bf16[128,1152]{1,0:T(8,128)(2,1)S(1)}, u32[]{:S(2)}, u32[]{:S(2)}) collective-permute-start(bf16[128,1152]{1,0:T(8,128)(2,1)S(1)} %get-tuple-element.61), channel_id=1, source_target_pairs={{66,0},{67,1},{72,2},{73,3},{70,4},{71,5},{76,6},{77,7},{74,8},{75... | collective-permute-start | bytes 884744 | tf_op jit(solution)/shard_map/ppermute | solution.py:60
  84.1 12.6 %collective-permute-start.15 = (bf16[256,1024]{1,0:T(8,128)(2,1)S(1)}, bf16[256,1024]{1,0:T(8,128)(2,1)S(1)}, u32[]{:S(2)}, u32[]{:S(2)}) collective-permute-start(bf16[256,1024]{1,0:T(8,128)(2,1)S(1)} %get-tuple-element.62), channel_id=1, source_target_pairs={{0,64},{1,65},{2,66},{3,67},{4,68},{5,69},{6,70},{7,71},{8,72},{9,... | collective-permute-start | bytes 1572872 | tf_op jit(solution)/shard_map/ppermute | solution.py:44
  96.1 14.0 %collective-permute-start.19 = (bf16[256,1024]{1,0:T(8,128)(2,1)S(1)}, bf16[256,1024]{1,0:T(8,128)(2,1)S(1)}, u32[]{:S(2)}, u32[]{:S(2)}) collective-permute-start(bf16[256,1024]{1,0:T(8,128)(2,1)S(1)} %shard_map.122), channel_id=1, source_target_pairs={{0,124},{1,125},{2,126},{3,127},{4,64},{5,65},{6,66},{7,67},{8,68}... | collective-permute-start | bytes 1572872 | tf_op jit(solution)/shard_map/ppermute | solution.py:44

commit v7 on v5

--- a/solution.py
+++ b/solution.py
@@ -49,13 +49,15 @@
     return lax.ppermute(x, "dom", pairs)
 
 
-def straight_back(x, d):
+def far_route(x, d):
     count = lax.axis_size("dom")
     pairs = []
     for s in range(2):
         for j in range(count):
-            to = j + d if j % LINE + d < LINE else j + d + LINE
-            pairs.append(((1 - s) * count + to % count, s * count + j))
+            wraps = j % LINE < d
+            to = j - d - LINE if wraps and d > 1 else j - d
+            group = s if wraps and d == 1 else 1 - s
+            pairs.append((s * count + j, group * count + to % count))
     return lax.ppermute(x, ("side", "dom"), pairs)
 
 
@@ -95,7 +97,8 @@
     return [0, LINE] + [near(p, d) for d in range(1, LINE)] + [far(p, d) for d in range(1, LINE)]
 
 
-def tiles_kernel(block, place_ref, lists_ref, counts_ref, x_ref, sw_ref, tiles_ref, tiles_t_ref, self_ref):
+def tiles_kernel(block, place_ref, lists_ref, counts_ref, x_ref, sw_ref, *refs):
+    tiles_ref, tiles_t_ref, self_ref = refs[-3:]
     for i, o in enumerate(slots(place_ref[0])):
         first, second = lists_ref[o, 0], lists_ref[o, 1]
         at = pl.ds(pl.multiple_of((o * 2 + second) * block, block), block)
@@ -138,15 +141,15 @@
 
 
 def layer_kernel(
-    block, live_ref, got_ref, q_ref, qb_ref, tiles_ref, acc_ref, deg_ref, self_ref, up_ref, nb_ref, ob_ref, tt_ref,
+    block, live_ref, got_a, got_b, q_ref, qb_ref, tiles_ref, acc_ref, deg_ref, self_ref, up_ref, nb_ref, ob_ref, tt_ref,
     msg_ref, g_ref, gpool_ref, pre_ref, last_ref, near1, near2, near3, pooled_ref, gn_ref,
 ):
     rows, width = self_ref.shape
     hidden = nb_ref.shape[0]
     step = 512
-    x = got_ref[...]
+    x = jnp.concatenate([got_a[...], got_b[...]], axis=0)
     keep = x[:, :128].astype(F32) < LIMIT
-    tiles = tiles_ref[:, -block:]
+    tiles = tiles_ref[:, -2 * block :]
     deg = deg_ref[...] + dot(tiles, jnp.where(keep, 1.0, 0.0).astype(BF16))
     inv_deg = 1.0 / (1.0 + deg[:, :1])
     keep = keep[:, :1]
@@ -194,17 +197,13 @@
         store(cols, dot(gn, q_ref[cols, :], 1, 1))
 
 
-def back_far_kernel(block, place_ref, lists_ref, tt_ref, gpool_ref, early_ref, last_ref, q_ref, _, *refs):
+def back_far_kernel(block, tt_ref, gpool_ref, early_ref, last_ref, q_ref, _, *refs):
     outs, gn_ref = refs[:-1], refs[-1]
-    width = q_ref.shape[0]
 
     def store(cols, part):
         for i, out in enumerate(outs):
             out[:, cols] = part[i * block : (i + 1) * block].astype(BF16)
 
-    for d, out in enumerate(outs, 1):
-        which = lists_ref[far(place_ref[0], d), 1].astype(F32)
-        out[:, width:] = jnp.full((block, 128), which, F32).astype(BF16)
     messages = [early_ref[...], last_ref[...]]
     back_dot((1 + LINE) * block, tt_ref, gpool_ref, messages, q_ref, gn_ref, store)
 
@@ -232,25 +231,28 @@
     emb_ref[...] = jnp.where(keep, act * inv, 0.0).astype(BF16)
 
 
-def sum_near_kernel(block, place_ref, lists_ref, m1, m2, m3, own_ref, d1, d2, d3, out_ref, total):
+def sum_near_kernel(block, place_ref, lists_ref, f1, m1, m2, m3, own_ref, c1, d1, d2, d3, out_ref, total):
     total[...] = jnp.zeros_like(total)
     total[at_block(lists_ref[LINE, 1], block), :] = own_ref[...].astype(F32)
     for d, (meta, part) in enumerate(zip((m1, m2, m3), (d1, d2, d3)), 1):
         p = lax.rem(place_ref[0] + d, LINE)
         total[at_block(meta[0, near(p, d)], block), :] += part[...].astype(F32)
+
+    @pl.when(place_ref[0] == LINE - 1)
+    def _():
+        total[at_block(f1[0, far(0, 1)], block), :] += c1[...].astype(F32)
+
     out_ref[...] = total[...].astype(BF16)
 
 
-def place_kernel(gself_ref, c1, c2, c3, total_ref):
-    block, width = c1.shape[0], gself_ref.shape[1]
-    first, second = gself_ref[:block, :], gself_ref[block:, :]
-    for part in (c1, c2, c3):
-        grad = part[:, :width].astype(F32)
-        late = part[:, width : width + 1].astype(F32) > 0.5
-        first += jnp.where(late, 0.0, grad)
-        second += jnp.where(late, grad, 0.0)
-    total_ref[:block, :] = first
-    total_ref[block:, :] = second
+def place_kernel(block, place_ref, f1, f2, f3, gself_ref, c1, c2, c3, total_ref):
+    total_ref[...] = gself_ref[...]
+    for d, (meta, part) in enumerate(zip((f1, f2, f3), (c1, c2, c3)), 1):
+        p = lax.rem(place_ref[0] + d, LINE)
+
+        @pl.when((d > 1) | (p >= d))
+        def _():
+            total_ref[at_block(meta[0, far(p, d)], block), :] += part[...].astype(F32)
 
 
 def finish_kernel(live_ref, total_ref, same_ref, below_ref, out_ref):
@@ -277,14 +279,15 @@
     below = swap_rows(marked, LINE)
     same = swap_rows(marked, 0)
     metas = [along(row, -d) for d in steps]
-    later, *metas = lax.optimization_barrier((marked, *metas))
+    later, row, *metas = lax.optimization_barrier((marked, row, *metas))
     below2 = swap_rows(later, 2 * LINE)
+    far_metas = [far_route(row, d) for d in steps]
     scalars = [SMEM] * (1 + len(steps))
     tiles, tiles_t, self_pre = call(
         lambda *r: tiles_kernel(block, *r),
         [((rows, reach * block), BF16), ((reach * block, rows), BF16), ((rows, width), F32)],
-        (place, lists, counts, x, sw),
-        [SMEM] * 2 + [VMEM] * 3,
+        (place, lists, counts, x, sw, same, *far_metas),
+        [SMEM] * 2 + [VMEM] * 3 + [HELD] * (1 + len(steps)),
         flops=2 * rows * width * width,
     )
     sent = call(
@@ -317,27 +320,28 @@
         0, split, (lists, same, below, *got_near, q, qb, tiles), [SMEM] + [VMEM] * 8
     )
     msg_b, acc, deg = message(
-        split, reach - 1, (*got_far[:-1], q, qb, tiles, acc, deg), [VMEM] * (5 + len(steps) - 1)
+        split, split + 1, (got_far[0], q, qb, tiles, acc, deg), [VMEM] * 6
     )
     gn = pltpu.VMEM((3 * block, hidden), BF16)
     g, gpool, pre, msg_c, *near_back = call(
         lambda *r: layer_kernel(block, *r),
-        [two, ((rows, hidden), BF16), ((rows, width), F32), ((block, hidden), BF16)] + [one] * 3,
-        (live, got_far[-1], q, qb, tiles, acc, deg, self_pre, up, nb, ob, tiles_t, msg_a),
-        [SMEM] + [VMEM] * 12,
+        [two, ((rows, hidden), BF16), ((rows, width), F32), ((2 * block, hidden), BF16)] + [one] * 3,
+        (live, *got_far[1:], q, qb, tiles, acc, deg, self_pre, up, nb, ob, tiles_t, msg_a),
+        [SMEM] + [VMEM] * 13,
         scratch=[pltpu.VMEM((rows, hidden), BF16), gn],
         flops=8 * MICROSECOND,
     )
     back_near = [along(b, -d) for d, b in zip(steps, near_back)]
+    gate = swap_rows(lax.optimization_barrier((row, near_back[0]))[0], 0)
     far_back = call(
         lambda *r: back_far_kernel(block, *r),
-        [((block, width + 128), BF16)] * 3,
-        (place, lists, tiles_t, gpool, msg_b, msg_c, q, near_back[0]),
-        [SMEM] * 2 + [VMEM] * 5 + [HELD],
+        [one] * 3,
+        (tiles_t, gpool, msg_b, msg_c, q, gate),
+        [VMEM] * 5 + [HELD],
         scratch=[gn],
         flops=2 * MICROSECOND,
     )
-    back_far = [straight_back(b, d) for d, b in zip(steps, far_back)]
+    back_far = [far_route(b, d) for d, b in zip(steps, far_back)]
     own_same, own_below, gself, emb = call(
         lambda *r: back_own_kernel(block, *r),
         [two, one, ((rows, width), F32), two],
@@ -351,17 +355,17 @@
     (sum_below,) = call(
         lambda *r: sum_near_kernel(block, *r),
         [two],
-        (place, lists, *metas, own_below, *back_near),
-        [SMEM] * 5 + [VMEM] * 4,
+        (place, lists, far_metas[0], *metas, own_below, back_far[0], *back_near),
+        [SMEM] * 6 + [VMEM] * 5,
         scratch=[total],
         flops=20 * MICROSECOND,
     )
     g_below = swap_rows(sum_below, -LINE)
     (placed,) = call(
-        place_kernel,
+        lambda *r: place_kernel(block, *r),
         [((rows, width), F32)],
-        (gself, *back_far),
-        [VMEM] * 4,
+        (place, *far_metas, gself, *back_far),
+        [SMEM] * 4 + [VMEM] * 4,
         flops=20 * MICROSECOND,
     )
     (grad,) = call(finish_kernel, [two], (live, placed, g_same, g_below), [SMEM] + [VMEM] * 3)

time: 106 us -> 123 us (1.16)
  starting transfers between devices: 27.7 us -> 42.2 us
  waiting for transfers between devices: 44.3 us -> 47.2 us
    ppermute x5 -> x6, waiting for transfers between devices: 25.8 us -> 11 us  [swap_rows(): return lax.ppermute(x, ('side', 'dom'), pairs)]
    ppermute x12, waiting for transfers between devices: 9.93 us -> 21.2 us  [along(): return lax.ppermute(x, 'dom', pairs)]
    ppermute x5 -> x6, starting transfers between devices: 7.39 us -> 18.5 us  [swap_rows(): return lax.ppermute(x, ('side', 'dom'), pairs)]
    ppermute x12, starting transfers between devices: 10.7 us -> 17.4 us  [along(): return lax.ppermute(x, 'dom', pairs)]
    ppermute x3 -> x6, waiting for transfers between devices: 8.49 us -> 15 us  [far_route(): return lax.ppermute(x, ('side', 'dom'), pairs)]
    ppermute x3 -> x6, starting transfers between devices: 9.62 us -> 6.3 us  [far_route(): return lax.ppermute(x, ('side', 'dom'), pairs)]
  transfers between devices with their start and end apart: 20 -> 24, of which waited for: 9 -> 11; matrix products, arithmetic and copies ran while one was open for 1% -> 1% of each run, Pallas kernels for 16% -> 13%
where the time goes in v7:
time: 123 us
  waiting for transfers between devices  47.2 us (38%)
  starting transfers between devices  42.2 us (34%)
  Pallas kernels  24.3 us (20%)
  local copies, waits for them, and re-layouts  6.39 us (5%)
  between operations  1.44 us (1%)
    pallas_call x11, Pallas kernels, call(): pl.pallas_call(kernel, out_shape=[jax.ShapeDtypeStruct(s, d) for s, d in...  24.3 us
    ppermute x12, waiting for transfers between devices, along(): return lax.ppermute(x, 'dom', pairs)  21.2 us
    ppermute x6, starting transfers between devices, swap_rows(): return lax.ppermute(x, ('side', 'dom'), pairs)  18.5 us
    ppermute x12, starting transfers between devices, along(): return lax.ppermute(x, 'dom', pairs)  17.4 us
    ppermute x6, waiting for transfers between devices, far_route(): return lax.ppermute(x, ('side', 'dom'), pairs)  15 us
    ppermute x6, waiting for transfers between devices, swap_rows(): return lax.ppermute(x, ('side', 'dom'), pairs)  11 us
    ppermute x6, starting transfers between devices, far_route(): return lax.ppermute(x, ('side', 'dom'), pairs)  6.3 us
    unnamed x18, local copies, waits for them, and re-layouts  4.95 us
  transfers between devices with their start and end apart: 24, of which 11 were waited for; matrix products, arithmetic and copies ran while one was open for 1% of the time, Pallas kernels for 13%

profile of v7, /device:TPU:7, one launch (start us, length us, event | category | flops | bytes accessed | tf_op | source)
XLA Modules:
  0.0 122.7 jit_solution(9078752515905275069)
XLA Ops:
  1.3 1.2 broadcast_select_fusion
  2.5 1.9 %collective-permute-start.11 = (bf16[256,1024]{1,0:T(8,128)(2,1)S(1)}, bf16[256,1024]{1,0:T(8,128)(2,1)S(1)}, u32[]{:S(2)}, u32[]{:S(2)}) collective-permute-start(bf16[256,1024]{1,0:T(8,128)(2,1)S(1)} %broadcast_select_fusion), channel_id=1, source_target_pairs={{0,68},{1,69},{2,70},{3,71},{4,72},{5,73},{6,74},{7,75},{8,76},{9,... | collective-permute-start | bytes 1572872 | tf_op jit(solution)/shard_map/ppermute | solution.py:43
  5.3 2.1 %collective-permute-start.2 = (s32[1,128]{1,0:T(1,128)S(1)}, s32[1,128]{1,0:T(1,128)S(1)}, u32[]{:S(2)}, u32[]{:S(2)}) collective-permute-start(s32[1,128]{1,0:T(1,128)S(1)} %pad_bitcast_fusion), channel_id=1, source_target_pairs={{0,2},{1,3},{2,0},{3,1},{4,6},{5,7},{6,4},{7,5},{8,10},{9,11},{10,... | collective-permute-start | bytes 1544 | tf_op jit(solution)/shard_map/ppermute | solution.py:49
  7.5 1.7 %collective-permute-done.2.r_2_.r_4_ = s32[1,128]{1,0:T(1,128)S(1)} collective-permute-done((s32[1,128]{1,0:T(1,128)S(1)}, s32[1,128]{1,0:T(1,128)S(1)}, u32[]{:S(2)}, u32[]{:S(2)}) %collective-permute-start.2) | collective-permute-done | bytes 544 | tf_op jit(solution)/shard_map/ppermute | solution.py:49
  9.2 2.1 %collective-permute-done.1.r_1_.r_3_ = s32[1,128]{1,0:T(1,128)S(1)} collective-permute-done((s32[1,128]{1,0:T(1,128)S(1)}, s32[1,128]{1,0:T(1,128)S(1)}, u32[]{:S(2)}, u32[]{:S(2)}) %collective-permute-start.1) | collective-permute-done | bytes 544 | tf_op jit(solution)/shard_map/ppermute | solution.py:49
  11.3 4.4 %collective-permute-start.7 = (bf16[256,1024]{1,0:T(8,128)(2,1)S(1)}, bf16[256,1024]{1,0:T(8,128)(2,1)S(1)}, u32[]{:S(2)}, u32[]{:S(2)}) collective-permute-start(bf16[256,1024]{1,0:T(8,128)(2,1)S(1)} %broadcast_select_fusion), channel_id=1, source_target_pairs={{0,72},{1,73},{2,74},{3,75},{4,76},{5,77},{6,78},{7,79},{8,80},{9,... | collective-permute-start | bytes 1572872 | tf_op jit(solution)/shard_map/ppermute | solution.py:43
  15.7 3.4 %collective-permute-start.5 = (s32[1,128]{1,0:T(1,128)S(1)}, s32[1,128]{1,0:T(1,128)S(1)}, u32[]{:S(2)}, u32[]{:S(2)}) collective-permute-start(s32[1,128]{1,0:T(1,128)S(1)} %pad_bitcast_fusion), channel_id=1, source_target_pairs={{0,122},{1,123},{2,64},{3,65},{4,126},{5,127},{6,68},{7,69},{8,66}... | collective-permute-start | bytes 1544 | tf_op jit(solution)/shard_map/ppermute | solution.py:61
  19.1 2.0 %collective-permute-done.6.r_8_.r_3_ = s32[1,128]{1,0:T(1,128)S(1)} collective-permute-done((s32[1,128]{1,0:T(1,128)S(1)}, s32[1,128]{1,0:T(1,128)S(1)}, u32[]{:S(2)}, u32[]{:S(2)}) %collective-permute-start.6) | collective-permute-done | bytes 544 | tf_op jit(solution)/shard_map/ppermute | solution.py:61
  22.7 3.3 %collective-permute-done.4.r_6_.r_1_.r_2_ = s32[1,128]{1,0:T(1,128)S(1)} collective-permute-done((s32[1,128]{1,0:T(1,128)S(1)}, s32[1,128]{1,0:T(1,128)S(1)}, u32[]{:S(2)}, u32[]{:S(2)}) %collective-permute-start.4) | collective-permute-done | bytes 544 | tf_op jit(solution)/shard_map/ppermute | solution.py:61
  26.0 1.6 %copy-done.1 = bf16[1024,1024]{1,0:T(8,128)(2,1)S(1)} copy-done((bf16[1024,1024]{1,0:T(8,128)(2,1)S(1)}, bf16[1024,1024]{1,0:T(8,128)(2,1)}, u32[]{:S(2)}) %copy-start.1) | copy-done | bytes 2097176
  27.6 1.6 %copy-done.3 = s32[1,256,2048]{2,1,0:T(8,128)S(1)} copy-done((s32[1,256,2048]{2,1,0:T(8,128)S(1)}, s32[1,256,2048]{2,1,0:T(8,128)}, u32[]{:S(2)}) %copy-start.3) | copy-done | bytes 2097176
  29.1 1.0 copy-done.4
  30.2 1.3 %shard_map.113 = (bf16[256,1024]{1,0:T(8,128)(2,1)S(1)}, bf16[1024,256]{1,0:T(8,128)(2,1)S(1)}, f32[256,1024]{1,0:T(8,128)S(1)}) custom-call(s32[1]{0:T(128)} %bitcast.2.r_0_, s32[8,2]{1,0:T(8,128)S(1)} %copy.14.r_1_.r_0_, s32[256,2048]{1,0:T(8,128)S(1)} %bitcast.20, bf16[256,1024]{1,0:T(8,128)(2,1)S(1)} %bitcast.21, bf16[1024,1024]{1,0:T(8,128)(2,1)S(1)} %copy-done.1, ...), custom_call_target="tpu_custom_call" | custom-call | flops 536870912 | bytes 1048576 | tf_op jit(solution)/shard_map/pallas_call | solution.py:25
  32.2 3.7 %collective-permute-start.12 = (bf16[128,1024]{1,0:T(8,128)(2,1)S(1)}, bf16[128,1024]{1,0:T(8,128)(2,1)S(1)}, u32[]{:S(2)}, u32[]{:S(2)}) collective-permute-start(bf16[128,1024]{1,0:T(8,128)(2,1)S(1)} %get-tuple-element.47), channel_id=1, source_target_pairs={{0,1},{1,2},{2,3},{3,0},{4,5},{5,6},{6,7},{7,4},{8,9},{9,10},{10,1... | collective-permute-start | bytes 786440 | tf_op jit(solution)/shard_map/ppermute | solution.py:49
  37.1 2.4 %collective-permute-start.8 = (bf16[128,1024]{1,0:T(8,128)(2,1)S(1)}, bf16[128,1024]{1,0:T(8,128)(2,1)S(1)}, u32[]{:S(2)}, u32[]{:S(2)}) collective-permute-start(bf16[128,1024]{1,0:T(8,128)(2,1)S(1)} %get-tuple-element.43), channel_id=1, source_target_pairs={{0,2},{1,3},{2,0},{3,1},{4,6},{5,7},{6,4},{7,5},{8,10},{9,11},{10,... | collective-permute-start | bytes 786440 | tf_op jit(solution)/shard_map/ppermute | solution.py:49
  39.8 13.1 %collective-permute-done.12.r_3_ = bf16[128,1024]{1,0:T(8,128)(2,1)S(1)} collective-permute-done((bf16[128,1024]{1,0:T(8,128)(2,1)S(1)}, bf16[128,1024]{1,0:T(8,128)(2,1)S(1)}, u32[]{:S(2)}, u32[]{:S(2)}) %collective-permute-start.12) | collective-permute-done | bytes 262176 | tf_op jit(solution)/shard_map/ppermute | solution.py:49
  53.0 3.4 %collective-permute-start.10 = (bf16[128,1024]{1,0:T(8,128)(2,1)S(1)}, bf16[128,1024]{1,0:T(8,128)(2,1)S(1)}, u32[]{:S(2)}, u32[]{:S(2)}) collective-permute-start(bf16[128,1024]{1,0:T(8,128)(2,1)S(1)} %get-tuple-element.46), channel_id=1, source_target_pairs={{0,1},{1,2},{2,3},{3,0},{4,5},{5,6},{6,7},{7,4},{8,9},{9,10},{10,1... | collective-permute-start | bytes 786440 | tf_op jit(solution)/shard_map/ppermute | solution.py:49
  56.4 4.6 %shard_map.116 = (bf16[640,2048]{1,0:T(8,128)(2,1)S(1)}, f32[256,2048]{1,0:T(8,128)S(1)}, f32[256,128]{1,0:T(8,128)S(1)}) custom-call(s32[8,2]{1,0:T(8,128)S(1)} %copy.14.r_1_.r_0_, bf16[256,1024]{1,0:T(8,128)(2,1)S(1)} %collective-permute-done.r_5_.r_4_.r_1_, bf16[256,1024]{1,0:T(8,128)(2,1)S(1)} %collective-permute-done.11.r_4_.r_2_, ...), custom_call_target="tpu_custom_call" | custom-call | flops 3355443200 | bytes 1048576 | tf_op jit(solution)/shard_map/pallas_call | solution.py:25
  61.4 1.6 %shard_map.117 = (bf16[128,2048]{1,0:T(8,128)(2,1)S(1)}, f32[256,2048]{1,0:T(8,128)S(1)}, f32[256,128]{1,0:T(8,128)S(1)}) custom-call(bf16[128,1024]{1,0:T(8,128)(2,1)S(1)} %collective-permute-done.10.r_0_, bf16[1024,2048]{1,0:T(8,128)(2,1)S(1)} %copy-done, f32[1,2048]{1,0:T(1,128)S(1)} %bitcast.23, bf16[256,1024]{1,0:T(8,128)(2,1)S(1)} %get-tuple-element.45.r_5_.r_8_.r_3_, ...), custom_call_target="tpu_custom_call" | custom-call | flops 671088640 | bytes 1048576 | tf_op jit(solution)/shard_map/pallas_call | solution.py:25
  63.7 7.0 %shard_map.118 = (bf16[256,1024]{1,0:T(8,128)(2,1)S(1)}, bf16[256,2048]{1,0:T(8,128)(2,1)S(1)}, f32[256,1024]{1,0:T(8,128)S(1)}, bf16[256,2048]{1,0:T(8,128)(2,1...) custom-call(s32[1]{0:T(128)} %bitcast.16.r_0_, ...), custom_call_target="tpu_custom_call" | custom-call | flops 8000000000 | bytes 1048576 | tf_op jit(solution)/shard_map/pallas_call | solution.py:25
  70.7 1.6 %collective-permute-start.15 = (s32[1,128]{1,0:T(1,128)S(1)}, s32[1,128]{1,0:T(1,128)S(1)}, u32[]{:S(2)}, u32[]{:S(2)}) collective-permute-start(s32[1,128]{1,0:T(1,128)S(1)} %pad_bitcast_fusion), channel_id=1, source_target_pairs={{0,64},{1,65},{2,66},{3,67},{4,68},{5,69},{6,70},{7,71},{8,72},{9,... | collective-permute-start | bytes 1544 | tf_op jit(solution)/shard_map/ppermute | solution.py:43
  72.3 4.6 %collective-permute-start.21 = (bf16[128,1024]{1,0:T(8,128)(2,1)S(1)}, bf16[128,1024]{1,0:T(8,128)(2,1)S(1)}, u32[]{:S(2)}, u32[]{:S(2)}) collective-permute-start(bf16[128,1024]{1,0:T(8,128)(2,1)S(1)} %get-tuple-element.70), channel_id=1, source_target_pairs={{0,2},{1,3},{2,0},{3,1},{4,6},{5,7},{6,4},{7,5},{8,10},{9,11},{10,... | collective-permute-start | bytes 786440 | tf_op jit(solution)/shard_map/ppermute | solution.py:49
  76.9 2.2 %shard_map.119 = (bf16[128,1024]{1,0:T(8,128)(2,1)S(1)}, bf16[128,1024]{1,0:T(8,128)(2,1)S(1)}, bf16[128,1024]{1,0:T(8,128)(2,1)S(1)}) custom-call(bf16[1024,256]{1,0:T(8,128)(2,1)S(1)} %get-tuple-element.38.r_12_.r_0_.r_2_, bf16[256,2048]{1,0:T(8,128)(2,1)S(1)} %get-tuple-element.56.r_1_.r_3_, bf16[128,2048]{1,0:T(8,128)(2,1)S(1)} %get-tuple-element.59.r_2_, ...), custom_call_target="tpu_custom_call" | custom-call | flops 2000000000 | bytes 1048576 | tf_op jit(solution)/shard_map/pallas_call | solution.py:25
  79.2 1.8 %collective-permute-start.17 = (bf16[128,1024]{1,0:T(8,128)(2,1)S(1)}, bf16[128,1024]{1,0:T(8,128)(2,1)S(1)}, u32[]{:S(2)}, u32[]{:S(2)}) collective-permute-start(bf16[128,1024]{1,0:T(8,128)(2,1)S(1)} %get-tuple-element.66), channel_id=1, source_target_pairs={{0,122},{1,123},{2,64},{3,65},{4,126},{5,127},{6,68},{7,69},{8,66}... | collective-permute-start | bytes 786440 | tf_op jit(solution)/shard_map/ppermute | solution.py:61
  81.6 3.6 %shard_map.120 = (bf16[256,1024]{1,0:T(8,128)(2,1)S(1)}, bf16[128,1024]{1,0:T(8,128)(2,1)S(1)}, f32[256,1024]{1,0:T(8,128)S(1)}, bf16[256,1024]{1,0:T(8,128)(2,1)}) custom-call(s32[8,2]{1,0:T(8,128)S(1)} %copy.14.r_1_.r_0_, s32[1]{0:T(128)} %bitcast.17.r_1_, bf16[1024,256]{1,0:T(8,128)(2,1)S(1)} %get-tuple-element.38.r_12_.r_0_.r_2_, ...), custom_call_target="tpu_custom_call" | custom-call | flops 3000000000 | bytes 1048576 | tf_op jit(solution)/shard_map/pallas_call | solution.py:25
  85.2 3.8 %collective-permute-done.21.r_9_ = bf16[128,1024]{1,0:T(8,128)(2,1)S(1)} collective-permute-done((bf16[128,1024]{1,0:T(8,128)(2,1)S(1)}, bf16[128,1024]{1,0:T(8,128)(2,1)S(1)}, u32[]{:S(2)}, u32[]{:S(2)}) %collective-permute-start.21) | collective-permute-done | bytes 262176 | tf_op jit(solution)/shard_map/ppermute | solution.py:49
  89.4 0.9 collective-permute-start.19
  90.4 8.9 %collective-permute-done.16.r_5_.r_7_ = bf16[128,1024]{1,0:T(8,128)(2,1)S(1)} collective-permute-done((bf16[128,1024]{1,0:T(8,128)(2,1)S(1)}, bf16[128,1024]{1,0:T(8,128)(2,1)S(1)}, u32[]{:S(2)}, u32[]{:S(2)}) %collective-permute-start.16) | collective-permute-done | bytes 262176 | tf_op jit(solution)/shard_map/ppermute | solution.py:61
  99.3 1.0 shard_map.122
  100.3 9.7 %collective-permute-start.23 = (bf16[256,1024]{1,0:T(8,128)(2,1)S(1)}, bf16[256,1024]{1,0:T(8,128)(2,1)S(1)}, u32[]{:S(2)}, u32[]{:S(2)}) collective-permute-start(bf16[256,1024]{1,0:T(8,128)(2,1)S(1)} %shard_map.122), channel_id=1, source_target_pairs={{0,124},{1,125},{2,126},{3,127},{4,64},{5,65},{6,66},{7,67},{8,68}... | collective-permute-start | bytes 1572872 | tf_op jit(solution)/shard_map/ppermute | solution.py:43
  110.7 11.0 %collective-permute-done.23.below_ref = bf16[256,1024]{1,0:T(8,128)(2,1)S(1)} collective-permute-done((bf16[256,1024]{1,0:T(8,128)(2,1)S(1)}, bf16[256,1024]{1,0:T(8,128)(2,1)S(1)}, u32[]{:S(2)}, u32[]{:S(2)}) %collective-permute-start.23) | collective-permute-done | bytes 524320 | tf_op jit(solution)/shard_map/ppermute | solution.py:43
  121.7 1.0 shard_map.123
  (50 shorter events, 7.6 us)
Async XLA Ops:
  2.5 29.1 %collective-permute-start.11 = (bf16[256,1024]{1,0:T(8,128)(2,1)S(1)}, bf16[256,1024]{1,0:T(8,128)(2,1)S(1)}, u32[]{:S(2)}, u32[]{:S(2)}) collective-permute-start(bf16[256,1024]{1,0:T(8,128)(2,1)S(1)} %broadcast_select_fusion), channel_id=1, source_target_pairs={{0,68},{1,69},{2,70},{3,71},{4,72},{5,73},{6,74},{7,75},{8,76},{9,... | collective-permute-start | bytes 1572872 | tf_op jit(solution)/shard_map/ppermute | solution.py:43
  4.4 21.6 %collective-permute-start = (bf16[256,1024]{1,0:T(8,128)(2,1)S(1)}, bf16[256,1024]{1,0:T(8,128)(2,1)S(1)}, u32[]{:S(2)}, u32[]{:S(2)}) collective-permute-start(bf16[256,1024]{1,0:T(8,128)(2,1)S(1)} %broadcast_select_fusion), channel_id=1, source_target_pairs={{0,64},{1,65},{2,66},{3,67},{4,68},{5,69},{6,70},{7,71},{8,72},{9,... | collective-permute-start | bytes 1572872 | tf_op jit(solution)/shard_map/ppermute | solution.py:43
  5.1 2.4 %collective-permute-start.3 = (s32[1,128]{1,0:T(1,128)S(1)}, s32[1,128]{1,0:T(1,128)S(1)}, u32[]{:S(2)}, u32[]{:S(2)}) collective-permute-start(s32[1,128]{1,0:T(1,128)S(1)} %pad_bitcast_fusion), channel_id=1, source_target_pairs={{0,1},{1,2},{2,3},{3,0},{4,5},{5,6},{6,7},{7,4},{8,9},{9,10},{10,1... | collective-permute-start | bytes 1544 | tf_op jit(solution)/shard_map/ppermute | solution.py:49
  5.3 3.9 %collective-permute-start.2 = (s32[1,128]{1,0:T(1,128)S(1)}, s32[1,128]{1,0:T(1,128)S(1)}, u32[]{:S(2)}, u32[]{:S(2)}) collective-permute-start(s32[1,128]{1,0:T(1,128)S(1)} %pad_bitcast_fusion), channel_id=1, source_target_pairs={{0,2},{1,3},{2,0},{3,1},{4,6},{5,7},{6,4},{7,5},{8,10},{9,11},{10,... | collective-permute-start | bytes 1544 | tf_op jit(solution)/shard_map/ppermute | solution.py:49
  7.4 3.9 %collective-permute-start.1 = (s32[1,128]{1,0:T(1,128)S(1)}, s32[1,128]{1,0:T(1,128)S(1)}, u32[]{:S(2)}, u32[]{:S(2)}) collective-permute-start(s32[1,128]{1,0:T(1,128)S(1)} %pad_bitcast_fusion), channel_id=1, source_target_pairs={{0,3},{1,0},{2,1},{3,2},{4,7},{5,4},{6,5},{7,6},{8,11},{9,8},{10,9... | collective-permute-start | bytes 1544 | tf_op jit(solution)/shard_map/ppermute | solution.py:49
  11.3 25.2 %collective-permute-start.7 = (bf16[256,1024]{1,0:T(8,128)(2,1)S(1)}, bf16[256,1024]{1,0:T(8,128)(2,1)S(1)}, u32[]{:S(2)}, u32[]{:S(2)}) collective-permute-start(bf16[256,1024]{1,0:T(8,128)(2,1)S(1)} %broadcast_select_fusion), channel_id=1, source_target_pairs={{0,72},{1,73},{2,74},{3,75},{4,76},{5,77},{6,78},{7,79},{8,80},{9,... | collective-permute-start | bytes 1572872 | tf_op jit(solution)/shard_map/ppermute | solution.py:43
  15.7 5.4 %collective-permute-start.6 = (s32[1,128]{1,0:T(1,128)S(1)}, s32[1,128]{1,0:T(1,128)S(1)}, u32[]{:S(2)}, u32[]{:S(2)}) collective-permute-start(s32[1,128]{1,0:T(1,128)S(1)} %pad_bitcast_fusion), channel_id=1, source_target_pairs={{0,121},{1,122},{2,123},{3,64},{4,125},{5,126},{6,127},{7,68},{8,6... | collective-permute-start | bytes 1544 | tf_op jit(solution)/shard_map/ppermute | solution.py:61
  15.7 6.9 %collective-permute-start.5 = (s32[1,128]{1,0:T(1,128)S(1)}, s32[1,128]{1,0:T(1,128)S(1)}, u32[]{:S(2)}, u32[]{:S(2)}) collective-permute-start(s32[1,128]{1,0:T(1,128)S(1)} %pad_bitcast_fusion), channel_id=1, source_target_pairs={{0,122},{1,123},{2,64},{3,65},{4,126},{5,127},{6,68},{7,69},{8,66}... | collective-permute-start | bytes 1544 | tf_op jit(solution)/shard_map/ppermute | solution.py:61
  21.2 4.8 %collective-permute-start.4 = (s32[1,128]{1,0:T(1,128)S(1)}, s32[1,128]{1,0:T(1,128)S(1)}, u32[]{:S(2)}, u32[]{:S(2)}) collective-permute-start(s32[1,128]{1,0:T(1,128)S(1)} %pad_bitcast_fusion), channel_id=1, source_target_pairs={{0,63},{1,64},{2,65},{3,66},{4,3},{5,68},{6,69},{7,70},{8,7},{9,72... | collective-permute-start | bytes 1544 | tf_op jit(solution)/shard_map/ppermute | solution.py:61
  26.0 1.6 %copy-start.1 = (bf16[1024,1024]{1,0:T(8,128)(2,1)S(1)}, bf16[1024,1024]{1,0:T(8,128)(2,1)}, u32[]{:S(2)}) copy-start(bf16[1024,1024]{1,0:T(8,128)(2,1)} %r_7_.1) | copy-start | bytes 6291460
  27.6 1.6 %copy-start.3 = (s32[1,256,2048]{2,1,0:T(8,128)S(1)}, s32[1,256,2048]{2,1,0:T(8,128)}, u32[]{:S(2)}) copy-start(s32[1,256,2048]{2,1,0:T(8,128)} %param.13) | copy-start | bytes 6291460
  30.2 26.2 %copy-start = (bf16[1024,2048]{1,0:T(8,128)(2,1)S(1)}, bf16[1024,2048]{1,0:T(8,128)(2,1)}, u32[]{:S(2)}) copy-start(bf16[1024,2048]{1,0:T(8,128)(2,1)} %r_5_.1) | copy-start | bytes 12582916
  31.5 24.9 %copy-start.5 = (f32[2048]{0:T(1024)S(1)}, f32[2048]{0:T(1024)}, u32[]{:S(2)}) copy-start(f32[2048]{0:T(1024)} %param.16) | copy-start | bytes 24580
  32.2 20.8 %collective-permute-start.12 = (bf16[128,1024]{1,0:T(8,128)(2,1)S(1)}, bf16[128,1024]{1,0:T(8,128)(2,1)S(1)}, u32[]{:S(2)}, u32[]{:S(2)}) collective-permute-start(bf16[128,1024]{1,0:T(8,128)(2,1)S(1)} %get-tuple-element.47), channel_id=1, source_target_pairs={{0,1},{1,2},{2,3},{3,0},{4,5},{5,6},{6,7},{7,4},{8,9},{9,10},{10,1... | collective-permute-start | bytes 786440 | tf_op jit(solution)/shard_map/ppermute | solution.py:49
  35.8 20.6 %collective-permute-start.13 = (bf16[128,1024]{1,0:T(8,128)(2,1)S(1)}, bf16[128,1024]{1,0:T(8,128)(2,1)S(1)}, u32[]{:S(2)}, u32[]{:S(2)}) collective-permute-start(bf16[128,1024]{1,0:T(8,128)(2,1)S(1)} %get-tuple-element.48), channel_id=1, source_target_pairs={{0,2},{1,3},{2,0},{3,1},{4,6},{5,7},{6,4},{7,5},{8,10},{9,11},{10,... | collective-permute-start | bytes 786440 | tf_op jit(solution)/shard_map/ppermute | solution.py:49
  35.8 20.6 %collective-permute-start.14 = (bf16[128,1024]{1,0:T(8,128)(2,1)S(1)}, bf16[128,1024]{1,0:T(8,128)(2,1)S(1)}, u32[]{:S(2)}, u32[]{:S(2)}) collective-permute-start(bf16[128,1024]{1,0:T(8,128)(2,1)S(1)} %get-tuple-element.49), channel_id=1, source_target_pairs={{0,3},{1,0},{2,1},{3,2},{4,7},{5,4},{6,5},{7,6},{8,11},{9,8},{10,9... | collective-permute-start | bytes 786440 | tf_op jit(solution)/shard_map/ppermute | solution.py:49
  37.1 25.8 %collective-permute-start.8 = (bf16[128,1024]{1,0:T(8,128)(2,1)S(1)}, bf16[128,1024]{1,0:T(8,128)(2,1)S(1)}, u32[]{:S(2)}, u32[]{:S(2)}) collective-permute-start(bf16[128,1024]{1,0:T(8,128)(2,1)S(1)} %get-tuple-element.43), channel_id=1, source_target_pairs={{0,2},{1,3},{2,0},{3,1},{4,6},{5,7},{6,4},{7,5},{8,10},{9,11},{10,... | collective-permute-start | bytes 786440 | tf_op jit(solution)/shard_map/ppermute | solution.py:49
  39.5 23.5 %collective-permute-start.9 = (bf16[128,1024]{1,0:T(8,128)(2,1)S(1)}, bf16[128,1024]{1,0:T(8,128)(2,1)S(1)}, u32[]{:S(2)}, u32[]{:S(2)}) collective-permute-start(bf16[128,1024]{1,0:T(8,128)(2,1)S(1)} %get-tuple-element.44), channel_id=1, source_target_pairs={{0,3},{1,0},{2,1},{3,2},{4,7},{5,4},{6,5},{7,6},{8,11},{9,8},{10,9... | collective-permute-start | bytes 786440 | tf_op jit(solution)/shard_map/ppermute | solution.py:49
  53.0 8.4 %collective-permute-start.10 = (bf16[128,1024]{1,0:T(8,128)(2,1)S(1)}, bf16[128,1024]{1,0:T(8,128)(2,1)S(1)}, u32[]{:S(2)}, u32[]{:S(2)}) collective-permute-start(bf16[128,1024]{1,0:T(8,128)(2,1)S(1)} %get-tuple-element.46), channel_id=1, source_target_pairs={{0,1},{1,2},{2,3},{3,0},{4,5},{5,6},{6,7},{7,4},{8,9},{9,10},{10,1... | collective-permute-start | bytes 786440 | tf_op jit(solution)/shard_map/ppermute | solution.py:49
  61.4 2.2 %copy-start.6 = (bf16[2048,1024]{1,0:T(8,128)(2,1)S(1)}, bf16[2048,1024]{1,0:T(8,128)(2,1)}, u32[]{:S(2)}) copy-start(bf16[2048,1024]{1,0:T(8,128)(2,1)} %r_10_.1) | copy-start | bytes 12582916
  61.4 2.3 %copy-start.7 = (bf16[1,256,1024]{2,1,0:T(8,128)(2,1)S(1)}, bf16[1,256,1024]{2,1,0:T(8,128)(2,1)}, u32[]{:S(2)}) copy-start(bf16[1,256,1024]{2,1,0:T(8,128)(2,1)} %param.14) | copy-start | bytes 1572868
  61.4 2.3 %copy-start.8 = (f32[1024]{0:T(1024)S(1)}, f32[1024]{0:T(1024)}, u32[]{:S(2)}) copy-start(f32[1024]{0:T(1024)} %param.19) | copy-start | bytes 12292
  70.7 6.2 %collective-permute-start.15 = (s32[1,128]{1,0:T(1,128)S(1)}, s32[1,128]{1,0:T(1,128)S(1)}, u32[]{:S(2)}, u32[]{:S(2)}) collective-permute-start(s32[1,128]{1,0:T(1,128)S(1)} %pad_bitcast_fusion), channel_id=1, source_target_pairs={{0,64},{1,65},{2,66},{3,67},{4,68},{5,69},{6,70},{7,71},{8,72},{9,... | collective-permute-start | bytes 1544 | tf_op jit(solution)/shard_map/ppermute | solution.py:43
  72.3 18.0 %collective-permute-start.20 = (bf16[128,1024]{1,0:T(8,128)(2,1)S(1)}, bf16[128,1024]{1,0:T(8,128)(2,1)S(1)}, u32[]{:S(2)}, u32[]{:S(2)}) collective-permute-start(bf16[128,1024]{1,0:T(8,128)(2,1)S(1)} %get-tuple-element.61), channel_id=1, source_target_pairs={{0,3},{1,0},{2,1},{3,2},{4,7},{5,4},{6,5},{7,6},{8,11},{9,8},{10,9... | collective-permute-start | bytes 786440 | tf_op jit(solution)/shard_map/ppermute | solution.py:49
  72.3 16.6 %collective-permute-start.21 = (bf16[128,1024]{1,0:T(8,128)(2,1)S(1)}, bf16[128,1024]{1,0:T(8,128)(2,1)S(1)}, u32[]{:S(2)}, u32[]{:S(2)}) collective-permute-start(bf16[128,1024]{1,0:T(8,128)(2,1)S(1)} %get-tuple-element.70), channel_id=1, source_target_pairs={{0,2},{1,3},{2,0},{3,1},{4,6},{5,7},{6,4},{7,5},{8,10},{9,11},{10,... | collective-permute-start | bytes 786440 | tf_op jit(solution)/shard_map/ppermute | solution.py:49
  76.9 12.5 %collective-permute-start.22 = (bf16[128,1024]{1,0:T(8,128)(2,1)S(1)}, bf16[128,1024]{1,0:T(8,128)(2,1)S(1)}, u32[]{:S(2)}, u32[]{:S(2)}) collective-permute-start(bf16[128,1024]{1,0:T(8,128)(2,1)S(1)} %get-tuple-element.71), channel_id=1, source_target_pairs={{0,1},{1,2},{2,3},{3,0},{4,5},{5,6},{6,7},{7,4},{8,9},{9,10},{10,1... | collective-permute-start | bytes 786440 | tf_op jit(solution)/shard_map/ppermute | solution.py:49
  76.9 4.7 %copy-start.2 = (bf16[1024,1024]{1,0:T(8,128)(2,1)S(1)}, bf16[1024,1024]{1,0:T(8,128)(2,1)}, u32[]{:S(2)}) copy-start(bf16[1024,1024]{1,0:T(8,128)(2,1)} %r_7_.1) | copy-start | bytes 6291460
  79.2 30.8 %collective-permute-start.17 = (bf16[128,1024]{1,0:T(8,128)(2,1)S(1)}, bf16[128,1024]{1,0:T(8,128)(2,1)S(1)}, u32[]{:S(2)}, u32[]{:S(2)}) collective-permute-start(bf16[128,1024]{1,0:T(8,128)(2,1)S(1)} %get-tuple-element.66), channel_id=1, source_target_pairs={{0,122},{1,123},{2,64},{3,65},{4,126},{5,127},{6,68},{7,69},{8,66}... | collective-permute-start | bytes 786440 | tf_op jit(solution)/shard_map/ppermute | solution.py:61
  81.0 18.3 %collective-permute-start.16 = (bf16[128,1024]{1,0:T(8,128)(2,1)S(1)}, bf16[128,1024]{1,0:T(8,128)(2,1)S(1)}, u32[]{:S(2)}, u32[]{:S(2)}) collective-permute-start(bf16[128,1024]{1,0:T(8,128)(2,1)S(1)} %get-tuple-element.63.r_9_), channel_id=1, source_target_pairs={{0,63},{1,64},{2,65},{3,66},{4,3},{5,68},{6,69},{7,70},{8,7},{9,72... | collective-permute-start | bytes 786440 | tf_op jit(solution)/shard_map/ppermute | solution.py:61
  88.9 21.0 %collective-permute-start.18 = (bf16[128,1024]{1,0:T(8,128)(2,1)S(1)}, bf16[128,1024]{1,0:T(8,128)(2,1)S(1)}, u32[]{:S(2)}, u32[]{:S(2)}) collective-permute-start(bf16[128,1024]{1,0:T(8,128)(2,1)S(1)} %get-tuple-element.67), channel_id=1, source_target_pairs={{0,121},{1,122},{2,123},{3,64},{4,125},{5,126},{6,127},{7,68},{8,6... | collective-permute-start | bytes 786440 | tf_op jit(solution)/shard_map/ppermute | solution.py:61
  89.4 21.3 %collective-permute-start.19 = (bf16[256,1024]{1,0:T(8,128)(2,1)S(1)}, bf16[256,1024]{1,0:T(8,128)(2,1)S(1)}, u32[]{:S(2)}, u32[]{:S(2)}) collective-permute-start(bf16[256,1024]{1,0:T(8,128)(2,1)S(1)} %get-tuple-element.68), channel_id=1, source_target_pairs={{0,64},{1,65},{2,66},{3,67},{4,68},{5,69},{6,70},{7,71},{8,72},{9,... | collective-permute-start | bytes 1572872 | tf_op jit(solution)/shard_map/ppermute | solution.py:43
  100.3 21.4 %collective-permute-start.23 = (bf16[256,1024]{1,0:T(8,128)(2,1)S(1)}, bf16[256,1024]{1,0:T(8,128)(2,1)S(1)}, u32[]{:S(2)}, u32[]{:S(2)}) collective-permute-start(bf16[256,1024]{1,0:T(8,128)(2,1)S(1)} %shard_map.122), channel_id=1, source_target_pairs={{0,124},{1,125},{2,126},{3,127},{4,64},{5,65},{6,66},{7,67},{8,68}... | collective-permute-start | bytes 1572872 | tf_op jit(solution)/shard_map/ppermute | solution.py:43
  (1 other events, 1.0 us)

commit v8 on v5

--- a/solution.py
+++ b/solution.py
@@ -71,7 +71,7 @@
     return pl.ds(pl.multiple_of(index * block, block), block)
 
 
-def pick_near_kernel(block, place_ref, m1, m2, m3, rows_ref, _, *outs):
+def pick_near_kernel(block, place_ref, m1, m2, m3, rows_ref, *outs):
     for d, (meta, out) in enumerate(zip((m1, m2, m3), outs), 1):
         p = lax.rem(place_ref[0] + d, LINE)
         out[...] = rows_ref[at_block(meta[0, near(p, d)], block), :]
@@ -95,7 +95,7 @@
     return [0, LINE] + [near(p, d) for d in range(1, LINE)] + [far(p, d) for d in range(1, LINE)]
 
 
-def tiles_kernel(block, place_ref, lists_ref, counts_ref, x_ref, sw_ref, tiles_ref, tiles_t_ref, self_ref):
+def tiles_kernel(block, place_ref, lists_ref, counts_ref, x_ref, sw_ref, _, tiles_ref, tiles_t_ref, self_ref):
     for i, o in enumerate(slots(place_ref[0])):
         first, second = lists_ref[o, 0], lists_ref[o, 1]
         at = pl.ds(pl.multiple_of((o * 2 + second) * block, block), block)
@@ -138,15 +138,15 @@
 
 
 def layer_kernel(
-    block, live_ref, got_ref, q_ref, qb_ref, tiles_ref, acc_ref, deg_ref, self_ref, up_ref, nb_ref, ob_ref, tt_ref,
+    block, live_ref, got_a, got_b, q_ref, qb_ref, tiles_ref, acc_ref, deg_ref, self_ref, up_ref, nb_ref, ob_ref, tt_ref,
     msg_ref, g_ref, gpool_ref, pre_ref, last_ref, near1, near2, near3, pooled_ref, gn_ref,
 ):
     rows, width = self_ref.shape
     hidden = nb_ref.shape[0]
     step = 512
-    x = got_ref[...]
+    x = jnp.concatenate([got_a[...], got_b[...]], axis=0)
     keep = x[:, :128].astype(F32) < LIMIT
-    tiles = tiles_ref[:, -block:]
+    tiles = tiles_ref[:, -2 * block :]
     deg = deg_ref[...] + dot(tiles, jnp.where(keep, 1.0, 0.0).astype(BF16))
     inv_deg = 1.0 / (1.0 + deg[:, :1])
     keep = keep[:, :1]
@@ -280,18 +280,11 @@
     later, *metas = lax.optimization_barrier((marked, *metas))
     below2 = swap_rows(later, 2 * LINE)
     scalars = [SMEM] * (1 + len(steps))
-    tiles, tiles_t, self_pre = call(
-        lambda *r: tiles_kernel(block, *r),
-        [((rows, reach * block), BF16), ((reach * block, rows), BF16), ((rows, width), F32)],
-        (place, lists, counts, x, sw),
-        [SMEM] * 2 + [VMEM] * 3,
-        flops=2 * rows * width * width,
-    )
     sent = call(
         lambda *r: pick_near_kernel(block, *r),
         [one] * len(steps),
-        (place, *metas, below, tiles),
-        scalars + [VMEM, HELD],
+        (place, *metas, below),
+        scalars + [VMEM],
     )
     got_near = [along(b, d) for d, b in zip(steps, sent)]
     sent = call(
@@ -301,6 +294,13 @@
         scalars + [VMEM] * 2,
     )
     got_far = [along(b, d) for d, b in zip(steps, sent)]
+    tiles, tiles_t, self_pre = call(
+        lambda *r: tiles_kernel(block, *r),
+        [((rows, reach * block), BF16), ((reach * block, rows), BF16), ((rows, width), F32)],
+        (place, lists, counts, x, sw, sent[0]),
+        [SMEM] * 2 + [VMEM] * 3 + [HELD],
+        flops=2 * rows * width * width,
+    )
     split = 1 + LINE
 
     def message(first, last, ins, specs):
@@ -317,14 +317,14 @@
         0, split, (lists, same, below, *got_near, q, qb, tiles), [SMEM] + [VMEM] * 8
     )
     msg_b, acc, deg = message(
-        split, reach - 1, (*got_far[:-1], q, qb, tiles, acc, deg), [VMEM] * (5 + len(steps) - 1)
+        split, split + 1, (got_far[0], q, qb, tiles, acc, deg), [VMEM] * 6
     )
     gn = pltpu.VMEM((3 * block, hidden), BF16)
     g, gpool, pre, msg_c, *near_back = call(
         lambda *r: layer_kernel(block, *r),
-        [two, ((rows, hidden), BF16), ((rows, width), F32), ((block, hidden), BF16)] + [one] * 3,
-        (live, got_far[-1], q, qb, tiles, acc, deg, self_pre, up, nb, ob, tiles_t, msg_a),
-        [SMEM] + [VMEM] * 12,
+        [two, ((rows, hidden), BF16), ((rows, width), F32), ((2 * block, hidden), BF16)] + [one] * 3,
+        (live, *got_far[1:], q, qb, tiles, acc, deg, self_pre, up, nb, ob, tiles_t, msg_a),
+        [SMEM] + [VMEM] * 13,
         scratch=[pltpu.VMEM((rows, hidden), BF16), gn],
         flops=8 * MICROSECOND,
     )

time: 106 us -> 103 us (0.972)
  waiting for transfers between devices: 44.3 us -> 38.6 us
  starting transfers between devices: 27.7 us -> 30.1 us
  local copies, waits for them, and re-layouts: 5.77 us -> 3.62 us
  Pallas kernels: 24.4 us -> 26.5 us
    ppermute x12, waiting for transfers between devices: 9.93 us -> 4.86 us  [along(): return lax.ppermute(x, 'dom', pairs)]
    ppermute x5, waiting for transfers between devices: 25.8 us -> 20.8 us  [swap_rows(): return lax.ppermute(x, ('side', 'dom'), pairs)]
    ppermute x3, waiting for transfers between devices: 8.49 us -> 12.9 us  [straight_back(): return lax.ppermute(x, ('side', 'dom'), pairs)]
    unnamed x18 -> x16, local copies, waits for them, and re-layouts: 4.33 us -> 2.18 us
    pallas_call x11, Pallas kernels: 24.4 us -> 26.5 us  [call(): pl.pallas_call(kernel, out_shape=[jax.ShapeDtypeStruct(s, d) for s, d in...]
    ppermute x12, starting transfers between devices: 10.7 us -> 12.8 us  [along(): return lax.ppermute(x, 'dom', pairs)]
  transfers between devices with their start and end apart: 20 -> 20, of which waited for: 9 -> 8; matrix products, arithmetic and copies ran while one was open for 1% -> 1% of each run, Pallas kernels for 16% -> 18%
where the time goes in v8:
time: 103 us; the launch traced here: 102 us
  waiting for transfers between devices  38.6 us (37%)
  starting transfers between devices  30.1 us (29%)
  Pallas kernels  26.5 us (26%)
  local copies, waits for them, and re-layouts  3.62 us (4%)
  other arithmetic  1.96 us (2%)
  between operations  1.58 us (2%)
    pallas_call x11, Pallas kernels, call(): pl.pallas_call(kernel, out_shape=[jax.ShapeDtypeStruct(s, d) for s, d in...  26.5 us
    ppermute x5, waiting for transfers between devices, swap_rows(): return lax.ppermute(x, ('side', 'dom'), pairs)  20.8 us
    ppermute x3, waiting for transfers between devices, straight_back(): return lax.ppermute(x, ('side', 'dom'), pairs)  12.9 us
    ppermute x12, starting transfers between devices, along(): return lax.ppermute(x, 'dom', pairs)  12.8 us
    ppermute x3, starting transfers between devices, straight_back(): return lax.ppermute(x, ('side', 'dom'), pairs)  10 us
    ppermute x5, starting transfers between devices, swap_rows(): return lax.ppermute(x, ('side', 'dom'), pairs)  7.26 us
    ppermute x12, waiting for transfers between devices, along(): return lax.ppermute(x, 'dom', pairs)  4.86 us
    unnamed x16, local copies, waits for them, and re-layouts  2.18 us
  transfers between devices with their start and end apart: 20, of which 8 were waited for; matrix products, arithmetic and copies ran while one was open for 1% of the time, Pallas kernels for 18%

profile of v8, /device:TPU:7, one launch (start us, length us, event | category | flops | bytes accessed | tf_op | source)
XLA Modules:
  0.0 102.4 jit_solution(4035339874177166008)
XLA Ops:
  1.5 2.0 %broadcast_select_fusion = bf16[256,1024]{1,0:T(8,128)(2,1)} fusion(pred[256]{0:T(512)(128)(4,1)S(1)} %iota_compare_fusion, bf16[1,256,1024]{2,1,0:T(8,128)(2,1)} %param.10), kind=kLoop, calls=%fused_computation | loop fusion | flops 262144 | bytes 1048832 | tf_op jit(solution)/shard_map/jit(_where)/select_n | solution.py:272
  3.4 1.9 %collective-permute-start.8 = (bf16[256,1024]{1,0:T(8,128)(2,1)}, bf16[256,1024]{1,0:T(8,128)(2,1)S(1)}, u32[]{:S(2)}, u32[]{:S(2)}) collective-permute-start(bf16[256,1024]{1,0:T(8,128)(2,1)} %broadcast_select_fusion), channel_id=1, source_target_pairs={{0,68},{1,69},{2,70},{3,71},{4,72},{5,73},{6,74},{7,75},{8,76},{9,... | collective-permute-start | bytes 1572872 | tf_op jit(solution)/shard_map/ppermute | solution.py:43
  5.3 0.7 slice_bitcast_fusion
  6.2 2.2 %collective-permute-start.1 = (s32[1,128]{1,0:T(1,128)S(1)}, s32[1,128]{1,0:T(1,128)S(1)}, u32[]{:S(2)}, u32[]{:S(2)}) collective-permute-start(s32[1,128]{1,0:T(1,128)S(1)} %pad_bitcast_fusion), channel_id=1, source_target_pairs={{0,2},{1,3},{2,0},{3,1},{4,6},{5,7},{6,4},{7,5},{8,10},{9,11},{10,... | collective-permute-start | bytes 1544 | tf_op jit(solution)/shard_map/ppermute | solution.py:49
  8.7 1.4 %collective-permute-done.1.r_2_.r_3_ = s32[1,128]{1,0:T(1,128)S(1)} collective-permute-done((s32[1,128]{1,0:T(1,128)S(1)}, s32[1,128]{1,0:T(1,128)S(1)}, u32[]{:S(2)}, u32[]{:S(2)}) %collective-permute-start.1) | collective-permute-done | bytes 544 | tf_op jit(solution)/shard_map/ppermute | solution.py:49
  10.1 2.1 %collective-permute-done.r_1_.r_2_ = s32[1,128]{1,0:T(1,128)S(1)} collective-permute-done((s32[1,128]{1,0:T(1,128)S(1)}, s32[1,128]{1,0:T(1,128)S(1)}, u32[]{:S(2)}, u32[]{:S(2)}) %collective-permute-start) | collective-permute-done | bytes 544 | tf_op jit(solution)/shard_map/ppermute | solution.py:49
  12.2 3.7 %collective-permute-start.4 = (bf16[256,1024]{1,0:T(8,128)(2,1)}, bf16[256,1024]{1,0:T(8,128)(2,1)}, u32[]{:S(2)}, u32[]{:S(2)}) collective-permute-start(bf16[256,1024]{1,0:T(8,128)(2,1)} %broadcast_select_fusion), channel_id=1, source_target_pairs={{0,72},{1,73},{2,74},{3,75},{4,76},{5,77},{6,78},{7,79},{8,80},{9,... | collective-permute-start | bytes 1572872 | tf_op jit(solution)/shard_map/ppermute | solution.py:43
  15.9 6.1 %collective-permute-done.8.r_4_.r_2_ = bf16[256,1024]{1,0:T(8,128)(2,1)S(1)} collective-permute-done((bf16[256,1024]{1,0:T(8,128)(2,1)}, bf16[256,1024]{1,0:T(8,128)(2,1)S(1)}, u32[]{:S(2)}, u32[]{:S(2)}) %collective-permute-start.8) | collective-permute-done | bytes 524320 | tf_op jit(solution)/shard_map/ppermute | solution.py:43
  22.0 1.5 %shard_map.115 = (bf16[128,1024]{1,0:T(8,128)(2,1)}, bf16[128,1024]{1,0:T(8,128)(2,1)}, bf16[128,1024]{1,0:T(8,128)(2,1)}) custom-call(s32[1]{0:T(128)} %bitcast.2.r_0_, s32[1,128]{1,0:T(1,128)S(1)} %collective-permute-done.r_1_.r_2_, s32[1,128]{1,0:T(1,128)S(1)} %collective-permute-done.1.r_2_.r_3_, s32[1,128]{1,0:T(1,128)S(1)} %collective-permute-done.2.r_3_.r_4_, ...), custom_call_target="tpu_custom_call" | custom-call | bytes 1048576 | tf_op jit(solution)/shard_map/pallas_call | solution.py:25
  23.7 2.1 %collective-permute-start.10 = (bf16[128,1024]{1,0:T(8,128)(2,1)}, bf16[128,1024]{1,0:T(8,128)(2,1)}, u32[]{:S(2)}, u32[]{:S(2)}) collective-permute-start(bf16[128,1024]{1,0:T(8,128)(2,1)} %get-tuple-element.45), channel_id=1, source_target_pairs={{0,2},{1,3},{2,0},{3,1},{4,6},{5,7},{6,4},{7,5},{8,10},{9,11},{10,... | collective-permute-start | bytes 786440 | tf_op jit(solution)/shard_map/ppermute | solution.py:49
  25.8 0.8 copy.15.r_1_.r_0_
  26.6 8.8 %collective-permute-done.4.r_5_ = bf16[256,1024]{1,0:T(8,128)(2,1)} collective-permute-done((bf16[256,1024]{1,0:T(8,128)(2,1)}, bf16[256,1024]{1,0:T(8,128)(2,1)}, u32[]{:S(2)}, u32[]{:S(2)}) %collective-permute-start.4) | collective-permute-done | bytes 524320 | tf_op jit(solution)/shard_map/ppermute | solution.py:43
  35.4 1.3 %shard_map.113 = (bf16[128,1024]{1,0:T(8,128)(2,1)S(1)}, bf16[128,1024]{1,0:T(8,128)(2,1)S(1)}, bf16[128,1024]{1,0:T(8,128)(2,1)S(1)}) custom-call(s32[1]{0:T(128)} %bitcast.2.r_0_, s32[1,128]{1,0:T(1,128)S(1)} %collective-permute-done.r_1_.r_2_, s32[1,128]{1,0:T(1,128)S(1)} %collective-permute-done.1.r_2_.r_3_, ...), custom_call_target="tpu_custom_call" | custom-call | bytes 1048576 | tf_op jit(solution)/shard_map/pallas_call | solution.py:25
  36.7 1.2 %collective-permute-start.5 = (bf16[128,1024]{1,0:T(8,128)(2,1)S(1)}, bf16[128,1024]{1,0:T(8,128)(2,1)S(1)}, u32[]{:S(2)}, u32[]{:S(2)}) collective-permute-start(bf16[128,1024]{1,0:T(8,128)(2,1)S(1)} %get-tuple-element.41), channel_id=1, source_target_pairs={{0,2},{1,3},{2,0},{3,1},{4,6},{5,7},{6,4},{7,5},{8,10},{9,11},{10,... | collective-permute-start | bytes 786440 | tf_op jit(solution)/shard_map/ppermute | solution.py:49
  37.9 1.8 %collective-permute-start.7 = (bf16[128,1024]{1,0:T(8,128)(2,1)S(1)}, bf16[128,1024]{1,0:T(8,128)(2,1)S(1)}, u32[]{:S(2)}, u32[]{:S(2)}) collective-permute-start(bf16[128,1024]{1,0:T(8,128)(2,1)S(1)} %get-tuple-element.39.r_5_), channel_id=1, source_target_pairs={{0,1},{1,2},{2,3},{3,0},{4,5},{5,6},{6,7},{7,4},{8,9},{9,10},{10,1... | collective-permute-start | bytes 786440 | tf_op jit(solution)/shard_map/ppermute | solution.py:49
  39.7 1.6 %copy-done.3 = s32[1,256,2048]{2,1,0:T(8,128)S(1)} copy-done((s32[1,256,2048]{2,1,0:T(8,128)S(1)}, s32[1,256,2048]{2,1,0:T(8,128)}, u32[]{:S(2)}) %copy-start.3) | copy-done | bytes 2097176
  41.3 1.3 %shard_map.114 = (bf16[256,1024]{1,0:T(8,128)(2,1)S(1)}, bf16[1024,256]{1,0:T(8,128)(2,1)S(1)}, f32[256,1024]{1,0:T(8,128)S(1)}) custom-call(s32[1]{0:T(128)} %bitcast.2.r_0_, s32[8,2]{1,0:T(8,128)S(1)} %copy.15.r_1_.r_0_, s32[256,2048]{1,0:T(8,128)S(1)} %bitcast.21, bf16[256,1024]{1,0:T(8,128)(2,1)S(1)} %bitcast.20, bf16[1024,1024]{1,0:T(8,128)(2,1)S(1)} %copy-done.1, ...), custom_call_target="tpu_custom_call" | custom-call | flops 536870912 | bytes 1048576 | tf_op jit(solution)/shard_map/pallas_call | solution.py:25
  43.5 5.2 %shard_map.116 = (bf16[640,2048]{1,0:T(8,128)(2,1)S(1)}, f32[256,2048]{1,0:T(8,128)S(1)}, f32[256,128]{1,0:T(8,128)S(1)}) custom-call(s32[8,2]{1,0:T(8,128)S(1)} %copy.15.r_1_.r_0_, bf16[256,1024]{1,0:T(8,128)(2,1)} %collective-permute-done.3.r_4_.r_1_, bf16[256,1024]{1,0:T(8,128)(2,1)S(1)} %collective-permute-done.8.r_4_.r_2_, ...), custom_call_target="tpu_custom_call" | custom-call | flops 3355443200 | bytes 1048576 | tf_op jit(solution)/shard_map/pallas_call | solution.py:25
  49.2 1.5 %shard_map.117 = (bf16[128,2048]{1,0:T(8,128)(2,1)S(1)}, f32[256,2048]{1,0:T(8,128)S(1)}, f32[256,128]{1,0:T(8,128)S(1)}) custom-call(bf16[128,1024]{1,0:T(8,128)(2,1)S(1)} %collective-permute-done.7.r_0_, bf16[1024,2048]{1,0:T(8,128)(2,1)S(1)} %copy-done, f32[1,2048]{1,0:T(1,128)S(1)} %bitcast.23, bf16[256,1024]{1,0:T(8,128)(2,1)S(1)} %get-tuple-element.43.r_8_.r_3_.r_5_, ...), custom_call_target="tpu_custom_call" | custom-call | flops 671088640 | bytes 1048576 | tf_op jit(solution)/shard_map/pallas_call | solution.py:25
  50.8 0.8 collective-permute-done.6.r_2_
  51.6 7.0 %shard_map.118 = (bf16[256,1024]{1,0:T(8,128)(2,1)S(1)}, bf16[256,2048]{1,0:T(8,128)(2,1)S(1)}, f32[256,1024]{1,0:T(8,128)S(1)}, bf16[256,2048]{1,0:T(8,128)(2,1...) custom-call(s32[1]{0:T(128)} %bitcast.16.r_0_, ...), custom_call_target="tpu_custom_call" | custom-call | flops 8000000000 | bytes 1048576 | tf_op jit(solution)/shard_map/pallas_call | solution.py:25
  58.6 3.4 %collective-permute-start.17 = (bf16[128,1024]{1,0:T(8,128)(2,1)S(1)}, bf16[128,1024]{1,0:T(8,128)(2,1)S(1)}, u32[]{:S(2)}, u32[]{:S(2)}) collective-permute-start(bf16[128,1024]{1,0:T(8,128)(2,1)S(1)} %get-tuple-element.66), channel_id=1, source_target_pairs={{0,2},{1,3},{2,0},{3,1},{4,6},{5,7},{6,4},{7,5},{8,10},{9,11},{10,... | collective-permute-start | bytes 786440 | tf_op jit(solution)/shard_map/ppermute | solution.py:49
  62.0 0.9 collective-permute-start.18
  63.4 2.8 %shard_map.119 = (bf16[128,1152]{1,0:T(8,128)(2,1)S(1)}, bf16[128,1152]{1,0:T(8,128)(2,1)S(1)}, bf16[128,1152]{1,0:T(8,128)(2,1)S(1)}) custom-call(s32[1]{0:T(128)} %bitcast.2.r_0_, s32[8,2]{1,0:T(8,128)S(1)} %copy.15.r_1_.r_0_, bf16[1024,256]{1,0:T(8,128)(2,1)S(1)} %get-tuple-element.40.r_12_.r_2_, bf16[256,2048]{1,0:T(8,128)(2,1)S(1)} %get-tuple-element.53.r_3_, ...), custom_call_target="tpu_custom_call" | custom-call | flops 2000000000 | bytes 1048576 | tf_op jit(solution)/shard_map/pallas_call | solution.py:25
  66.3 2.3 %collective-permute-start.13 = (bf16[128,1152]{1,0:T(8,128)(2,1)S(1)}, bf16[128,1152]{1,0:T(8,128)(2,1)S(1)}, u32[]{:S(2)}, u32[]{:S(2)}) collective-permute-start(bf16[128,1152]{1,0:T(8,128)(2,1)S(1)} %get-tuple-element.62), channel_id=1, source_target_pairs={{66,0},{67,1},{72,2},{73,3},{70,4},{71,5},{76,6},{77,7},{74,8},{75... | collective-permute-start | bytes 884744 | tf_op jit(solution)/shard_map/ppermute | solution.py:59
  69.3 3.6 %shard_map.120 = (bf16[256,1024]{1,0:T(8,128)(2,1)S(1)}, bf16[128,1024]{1,0:T(8,128)(2,1)S(1)}, f32[256,1024]{1,0:T(8,128)S(1)}, bf16[256,1024]{1,0:T(8,128)(2,1)}) custom-call(s32[8,2]{1,0:T(8,128)S(1)} %copy.15.r_1_.r_0_, s32[1]{0:T(128)} %bitcast.17.r_1_, bf16[1024,256]{1,0:T(8,128)(2,1)S(1)} %get-tuple-element.40.r_12_.r_2_, ...), custom_call_target="tpu_custom_call" | custom-call | flops 3000000000 | bytes 1048576 | tf_op jit(solution)/shard_map/pallas_call | solution.py:25
  72.8 7.0 %collective-permute-start.14 = (bf16[128,1152]{1,0:T(8,128)(2,1)S(1)}, bf16[128,1152]{1,0:T(8,128)(2,1)S(1)}, u32[]{:S(2)}, u32[]{:S(2)}) collective-permute-start(bf16[128,1152]{1,0:T(8,128)(2,1)S(1)} %get-tuple-element.63), channel_id=1, source_target_pairs={{67,0},{72,1},{73,2},{74,3},{71,4},{76,5},{77,6},{78,7},{75,8},{80... | collective-permute-start | bytes 884744 | tf_op jit(solution)/shard_map/ppermute | solution.py:59
  79.9 1.1 %collective-permute-start.15 = (bf16[256,1024]{1,0:T(8,128)(2,1)S(1)}, bf16[256,1024]{1,0:T(8,128)(2,1)S(1)}, u32[]{:S(2)}, u32[]{:S(2)}) collective-permute-start(bf16[256,1024]{1,0:T(8,128)(2,1)S(1)} %get-tuple-element.64), channel_id=1, source_target_pairs={{0,64},{1,65},{2,66},{3,67},{4,68},{5,69},{6,70},{7,71},{8,72},{9,... | collective-permute-start | bytes 1572872 | tf_op jit(solution)/shard_map/ppermute | solution.py:43
  80.9 0.9 shard_map.122
  82.1 12.9 %collective-permute-done.14.c3 = bf16[128,1152]{1,0:T(8,128)(2,1)S(1)} collective-permute-done((bf16[128,1152]{1,0:T(8,128)(2,1)S(1)}, bf16[128,1152]{1,0:T(8,128)(2,1)S(1)}, u32[]{:S(2)}, u32[]{:S(2)}) %collective-permute-start.14) | collective-permute-done | bytes 294944 | tf_op jit(solution)/shard_map/ppermute | solution.py:59
  95.4 6.0 %collective-permute-done.19.below_ref = bf16[256,1024]{1,0:T(8,128)(2,1)S(1)} collective-permute-done((bf16[256,1024]{1,0:T(8,128)(2,1)S(1)}, bf16[256,1024]{1,0:T(8,128)(2,1)S(1)}, u32[]{:S(2)}, u32[]{:S(2)}) %collective-permute-start.19) | collective-permute-done | bytes 524320 | tf_op jit(solution)/shard_map/ppermute | solution.py:43
  101.4 1.0 shard_map.123
  (40 shorter events, 4.1 us)
Async XLA Ops:
  0.6 39.1 %copy-start.2 = (bf16[1,256,1024]{2,1,0:T(8,128)(2,1)S(1)}, bf16[1,256,1024]{2,1,0:T(8,128)(2,1)}, u32[]{:S(2)}) copy-start(bf16[1,256,1024]{2,1,0:T(8,128)(2,1)} %param.10) | copy-start | bytes 1572868
  0.6 39.1 %copy-start.1 = (bf16[1024,1024]{1,0:T(8,128)(2,1)S(1)}, bf16[1024,1024]{1,0:T(8,128)(2,1)}, u32[]{:S(2)}) copy-start(bf16[1024,1024]{1,0:T(8,128)(2,1)} %r_7_.1) | copy-start | bytes 6291460
  3.4 18.6 %collective-permute-start.8 = (bf16[256,1024]{1,0:T(8,128)(2,1)}, bf16[256,1024]{1,0:T(8,128)(2,1)S(1)}, u32[]{:S(2)}, u32[]{:S(2)}) collective-permute-start(bf16[256,1024]{1,0:T(8,128)(2,1)} %broadcast_select_fusion), channel_id=1, source_target_pairs={{0,68},{1,69},{2,70},{3,71},{4,72},{5,73},{6,74},{7,75},{8,76},{9,... | collective-permute-start | bytes 1572872 | tf_op jit(solution)/shard_map/ppermute | solution.py:43
  6.0 2.7 %collective-permute-start.2 = (s32[1,128]{1,0:T(1,128)S(1)}, s32[1,128]{1,0:T(1,128)S(1)}, u32[]{:S(2)}, u32[]{:S(2)}) collective-permute-start(s32[1,128]{1,0:T(1,128)S(1)} %pad_bitcast_fusion), channel_id=1, source_target_pairs={{0,1},{1,2},{2,3},{3,0},{4,5},{5,6},{6,7},{7,4},{8,9},{9,10},{10,1... | collective-permute-start | bytes 1544 | tf_op jit(solution)/shard_map/ppermute | solution.py:49
  6.2 3.9 %collective-permute-start.1 = (s32[1,128]{1,0:T(1,128)S(1)}, s32[1,128]{1,0:T(1,128)S(1)}, u32[]{:S(2)}, u32[]{:S(2)}) collective-permute-start(s32[1,128]{1,0:T(1,128)S(1)} %pad_bitcast_fusion), channel_id=1, source_target_pairs={{0,2},{1,3},{2,0},{3,1},{4,6},{5,7},{6,4},{7,5},{8,10},{9,11},{10,... | collective-permute-start | bytes 1544 | tf_op jit(solution)/shard_map/ppermute | solution.py:49
  8.3 3.9 %collective-permute-start = (s32[1,128]{1,0:T(1,128)S(1)}, s32[1,128]{1,0:T(1,128)S(1)}, u32[]{:S(2)}, u32[]{:S(2)}) collective-permute-start(s32[1,128]{1,0:T(1,128)S(1)} %pad_bitcast_fusion), channel_id=1, source_target_pairs={{0,3},{1,0},{2,1},{3,2},{4,7},{5,4},{6,5},{7,6},{8,11},{9,8},{10,9... | collective-permute-start | bytes 1544 | tf_op jit(solution)/shard_map/ppermute | solution.py:49
  8.3 18.3 %collective-permute-start.3 = (bf16[256,1024]{1,0:T(8,128)(2,1)}, bf16[256,1024]{1,0:T(8,128)(2,1)}, u32[]{:S(2)}, u32[]{:S(2)}) collective-permute-start(bf16[256,1024]{1,0:T(8,128)(2,1)} %broadcast_select_fusion), channel_id=1, source_target_pairs={{0,64},{1,65},{2,66},{3,67},{4,68},{5,69},{6,70},{7,71},{8,72},{9,... | collective-permute-start | bytes 1572872 | tf_op jit(solution)/shard_map/ppermute | solution.py:43
  12.2 23.2 %collective-permute-start.4 = (bf16[256,1024]{1,0:T(8,128)(2,1)}, bf16[256,1024]{1,0:T(8,128)(2,1)}, u32[]{:S(2)}, u32[]{:S(2)}) collective-permute-start(bf16[256,1024]{1,0:T(8,128)(2,1)} %broadcast_select_fusion), channel_id=1, source_target_pairs={{0,72},{1,73},{2,74},{3,75},{4,76},{5,77},{6,78},{7,79},{8,80},{9,... | collective-permute-start | bytes 1572872 | tf_op jit(solution)/shard_map/ppermute | solution.py:43
  23.5 19.1 %collective-permute-start.9 = (bf16[128,1024]{1,0:T(8,128)(2,1)}, bf16[128,1024]{1,0:T(8,128)(2,1)S(1)}, u32[]{:S(2)}, u32[]{:S(2)}) collective-permute-start(bf16[128,1024]{1,0:T(8,128)(2,1)} %get-tuple-element.44), channel_id=1, source_target_pairs={{0,1},{1,2},{2,3},{3,0},{4,5},{5,6},{6,7},{7,4},{8,9},{9,10},{10,1... | collective-permute-start | bytes 786440 | tf_op jit(solution)/shard_map/ppermute | solution.py:49
  23.7 19.2 %collective-permute-start.10 = (bf16[128,1024]{1,0:T(8,128)(2,1)}, bf16[128,1024]{1,0:T(8,128)(2,1)}, u32[]{:S(2)}, u32[]{:S(2)}) collective-permute-start(bf16[128,1024]{1,0:T(8,128)(2,1)} %get-tuple-element.45), channel_id=1, source_target_pairs={{0,2},{1,3},{2,0},{3,1},{4,6},{5,7},{6,4},{7,5},{8,10},{9,11},{10,... | collective-permute-start | bytes 786440 | tf_op jit(solution)/shard_map/ppermute | solution.py:49
  25.8 17.1 %collective-permute-start.11 = (bf16[128,1024]{1,0:T(8,128)(2,1)}, bf16[128,1024]{1,0:T(8,128)(2,1)}, u32[]{:S(2)}, u32[]{:S(2)}) collective-permute-start(bf16[128,1024]{1,0:T(8,128)(2,1)} %get-tuple-element.46), channel_id=1, source_target_pairs={{0,3},{1,0},{2,1},{3,2},{4,7},{5,4},{6,5},{7,6},{8,11},{9,8},{10,9... | collective-permute-start | bytes 786440 | tf_op jit(solution)/shard_map/ppermute | solution.py:49
  36.7 14.1 %collective-permute-start.5 = (bf16[128,1024]{1,0:T(8,128)(2,1)S(1)}, bf16[128,1024]{1,0:T(8,128)(2,1)S(1)}, u32[]{:S(2)}, u32[]{:S(2)}) collective-permute-start(bf16[128,1024]{1,0:T(8,128)(2,1)S(1)} %get-tuple-element.41), channel_id=1, source_target_pairs={{0,2},{1,3},{2,0},{3,1},{4,6},{5,7},{6,4},{7,5},{8,10},{9,11},{10,... | collective-permute-start | bytes 786440 | tf_op jit(solution)/shard_map/ppermute | solution.py:49
  37.9 11.3 %collective-permute-start.7 = (bf16[128,1024]{1,0:T(8,128)(2,1)S(1)}, bf16[128,1024]{1,0:T(8,128)(2,1)S(1)}, u32[]{:S(2)}, u32[]{:S(2)}) collective-permute-start(bf16[128,1024]{1,0:T(8,128)(2,1)S(1)} %get-tuple-element.39.r_5_), channel_id=1, source_target_pairs={{0,1},{1,2},{2,3},{3,0},{4,5},{5,6},{6,7},{7,4},{8,9},{9,10},{10,1... | collective-permute-start | bytes 786440 | tf_op jit(solution)/shard_map/ppermute | solution.py:49
  39.7 1.6 %copy-start.3 = (s32[1,256,2048]{2,1,0:T(8,128)S(1)}, s32[1,256,2048]{2,1,0:T(8,128)}, u32[]{:S(2)}) copy-start(s32[1,256,2048]{2,1,0:T(8,128)} %param.13) | copy-start | bytes 6291460
  41.3 2.2 %copy-start = (bf16[1024,2048]{1,0:T(8,128)(2,1)S(1)}, bf16[1024,2048]{1,0:T(8,128)(2,1)}, u32[]{:S(2)}) copy-start(bf16[1024,2048]{1,0:T(8,128)(2,1)} %r_5_.1) | copy-start | bytes 12582916
  41.3 2.2 %copy-start.4 = (f32[2048]{0:T(1024)S(1)}, f32[2048]{0:T(1024)}, u32[]{:S(2)}) copy-start(f32[2048]{0:T(1024)} %param.16) | copy-start | bytes 24580
  42.7 8.9 %collective-permute-start.6 = (bf16[128,1024]{1,0:T(8,128)(2,1)S(1)}, bf16[128,1024]{1,0:T(8,128)(2,1)S(1)}, u32[]{:S(2)}, u32[]{:S(2)}) collective-permute-start(bf16[128,1024]{1,0:T(8,128)(2,1)S(1)} %get-tuple-element.42), channel_id=1, source_target_pairs={{0,3},{1,0},{2,1},{3,2},{4,7},{5,4},{6,5},{7,6},{8,11},{9,8},{10,9... | collective-permute-start | bytes 786440 | tf_op jit(solution)/shard_map/ppermute | solution.py:49
  49.2 2.3 %copy-start.5 = (bf16[2048,1024]{1,0:T(8,128)(2,1)S(1)}, bf16[2048,1024]{1,0:T(8,128)(2,1)}, u32[]{:S(2)}) copy-start(bf16[2048,1024]{1,0:T(8,128)(2,1)} %r_10_.1) | copy-start | bytes 12582916
  49.2 2.3 %copy-start.6 = (bf16[1,256,1024]{2,1,0:T(8,128)(2,1)S(1)}, bf16[1,256,1024]{2,1,0:T(8,128)(2,1)}, u32[]{:S(2)}) copy-start(bf16[1,256,1024]{2,1,0:T(8,128)(2,1)} %param.14) | copy-start | bytes 1572868
  49.2 2.3 %copy-start.7 = (f32[1024]{0:T(1024)S(1)}, f32[1024]{0:T(1024)}, u32[]{:S(2)}) copy-start(f32[1024]{0:T(1024)} %param.19) | copy-start | bytes 12292
  58.6 14.3 %collective-permute-start.17 = (bf16[128,1024]{1,0:T(8,128)(2,1)S(1)}, bf16[128,1024]{1,0:T(8,128)(2,1)S(1)}, u32[]{:S(2)}, u32[]{:S(2)}) collective-permute-start(bf16[128,1024]{1,0:T(8,128)(2,1)S(1)} %get-tuple-element.66), channel_id=1, source_target_pairs={{0,2},{1,3},{2,0},{3,1},{4,6},{5,7},{6,4},{7,5},{8,10},{9,11},{10,... | collective-permute-start | bytes 786440 | tf_op jit(solution)/shard_map/ppermute | solution.py:49
  62.0 17.9 %collective-permute-start.18 = (bf16[128,1024]{1,0:T(8,128)(2,1)S(1)}, bf16[128,1024]{1,0:T(8,128)(2,1)S(1)}, u32[]{:S(2)}, u32[]{:S(2)}) collective-permute-start(bf16[128,1024]{1,0:T(8,128)(2,1)S(1)} %get-tuple-element.67), channel_id=1, source_target_pairs={{0,1},{1,2},{2,3},{3,0},{4,5},{5,6},{6,7},{7,4},{8,9},{9,10},{10,1... | collective-permute-start | bytes 786440 | tf_op jit(solution)/shard_map/ppermute | solution.py:49
  62.8 18.1 %collective-permute-start.16 = (bf16[128,1024]{1,0:T(8,128)(2,1)S(1)}, bf16[128,1024]{1,0:T(8,128)(2,1)S(1)}, u32[]{:S(2)}, u32[]{:S(2)}) collective-permute-start(bf16[128,1024]{1,0:T(8,128)(2,1)S(1)} %get-tuple-element.58.r_7_), channel_id=1, source_target_pairs={{0,3},{1,0},{2,1},{3,2},{4,7},{5,4},{6,5},{7,6},{8,11},{9,8},{10,9... | collective-permute-start | bytes 786440 | tf_op jit(solution)/shard_map/ppermute | solution.py:49
  66.3 15.9 %collective-permute-start.13 = (bf16[128,1152]{1,0:T(8,128)(2,1)S(1)}, bf16[128,1152]{1,0:T(8,128)(2,1)S(1)}, u32[]{:S(2)}, u32[]{:S(2)}) collective-permute-start(bf16[128,1152]{1,0:T(8,128)(2,1)S(1)} %get-tuple-element.62), channel_id=1, source_target_pairs={{66,0},{67,1},{72,2},{73,3},{70,4},{71,5},{76,6},{77,7},{74,8},{75... | collective-permute-start | bytes 884744 | tf_op jit(solution)/shard_map/ppermute | solution.py:59
  68.6 26.5 %collective-permute-start.12 = (bf16[128,1152]{1,0:T(8,128)(2,1)S(1)}, bf16[128,1152]{1,0:T(8,128)(2,1)S(1)}, u32[]{:S(2)}, u32[]{:S(2)}) collective-permute-start(bf16[128,1152]{1,0:T(8,128)(2,1)S(1)} %get-tuple-element.59.r_9_), channel_id=1, source_target_pairs={{65,0},{66,1},{67,2},{72,3},{69,4},{70,5},{71,6},{76,7},{73,8},{74... | collective-permute-start | bytes 884744 | tf_op jit(solution)/shard_map/ppermute | solution.py:59
  72.8 22.2 %collective-permute-start.14 = (bf16[128,1152]{1,0:T(8,128)(2,1)S(1)}, bf16[128,1152]{1,0:T(8,128)(2,1)S(1)}, u32[]{:S(2)}, u32[]{:S(2)}) collective-permute-start(bf16[128,1152]{1,0:T(8,128)(2,1)S(1)} %get-tuple-element.63), channel_id=1, source_target_pairs={{67,0},{72,1},{73,2},{74,3},{71,4},{76,5},{77,6},{78,7},{75,8},{80... | collective-permute-start | bytes 884744 | tf_op jit(solution)/shard_map/ppermute | solution.py:59
  79.9 15.6 %collective-permute-start.15 = (bf16[256,1024]{1,0:T(8,128)(2,1)S(1)}, bf16[256,1024]{1,0:T(8,128)(2,1)S(1)}, u32[]{:S(2)}, u32[]{:S(2)}) collective-permute-start(bf16[256,1024]{1,0:T(8,128)(2,1)S(1)} %get-tuple-element.64), channel_id=1, source_target_pairs={{0,64},{1,65},{2,66},{3,67},{4,68},{5,69},{6,70},{7,71},{8,72},{9,... | collective-permute-start | bytes 1572872 | tf_op jit(solution)/shard_map/ppermute | solution.py:43
  81.9 19.5 %collective-permute-start.19 = (bf16[256,1024]{1,0:T(8,128)(2,1)S(1)}, bf16[256,1024]{1,0:T(8,128)(2,1)S(1)}, u32[]{:S(2)}, u32[]{:S(2)}) collective-permute-start(bf16[256,1024]{1,0:T(8,128)(2,1)S(1)} %shard_map.122), channel_id=1, source_target_pairs={{0,124},{1,125},{2,126},{3,127},{4,64},{5,65},{6,66},{7,67},{8,68}... | collective-permute-start | bytes 1572872 | tf_op jit(solution)/shard_map/ppermute | solution.py:43

commit v9 on v8

--- a/solution.py
+++ b/solution.py
@@ -71,7 +71,8 @@
     return pl.ds(pl.multiple_of(index * block, block), block)
 
 
-def pick_near_kernel(block, place_ref, m1, m2, m3, rows_ref, *outs):
+def pick_near_kernel(block, place_ref, m1, m2, m3, rows_ref, *refs):
+    outs = refs[-3:]
     for d, (meta, out) in enumerate(zip((m1, m2, m3), outs), 1):
         p = lax.rem(place_ref[0] + d, LINE)
         out[...] = rows_ref[at_block(meta[0, near(p, d)], block), :]
@@ -194,17 +195,13 @@
         store(cols, dot(gn, q_ref[cols, :], 1, 1))
 
 
-def back_far_kernel(block, place_ref, lists_ref, tt_ref, gpool_ref, early_ref, last_ref, q_ref, _, *refs):
+def back_far_kernel(block, tt_ref, gpool_ref, early_ref, last_ref, q_ref, _, *refs):
     outs, gn_ref = refs[:-1], refs[-1]
-    width = q_ref.shape[0]
 
     def store(cols, part):
         for i, out in enumerate(outs):
             out[:, cols] = part[i * block : (i + 1) * block].astype(BF16)
 
-    for d, out in enumerate(outs, 1):
-        which = lists_ref[far(place_ref[0], d), 1].astype(F32)
-        out[:, width:] = jnp.full((block, 128), which, F32).astype(BF16)
     messages = [early_ref[...], last_ref[...]]
     back_dot((1 + LINE) * block, tt_ref, gpool_ref, messages, q_ref, gn_ref, store)
 
@@ -241,16 +238,13 @@
     out_ref[...] = total[...].astype(BF16)
 
 
-def place_kernel(gself_ref, c1, c2, c3, total_ref):
-    block, width = c1.shape[0], gself_ref.shape[1]
-    first, second = gself_ref[:block, :], gself_ref[block:, :]
-    for part in (c1, c2, c3):
-        grad = part[:, :width].astype(F32)
-        late = part[:, width : width + 1].astype(F32) > 0.5
-        first += jnp.where(late, 0.0, grad)
-        second += jnp.where(late, grad, 0.0)
-    total_ref[:block, :] = first
-    total_ref[block:, :] = second
+def place_kernel(block, place_ref, same_ref, two_ref, gself_ref, c1, c2, c3, total_ref):
+    total_ref[...] = gself_ref[...]
+    for d, part in enumerate((c1, c2, c3), 1):
+        p = lax.rem(place_ref[0] + d, LINE)
+        o = far(p, d)
+        which = jnp.where(p >= d, same_ref[d - 1, o], two_ref[d - 1, o])
+        total_ref[at_block(which, block), :] += part[...].astype(F32)
 
 
 def finish_kernel(live_ref, total_ref, same_ref, below_ref, out_ref):
@@ -279,12 +273,15 @@
     metas = [along(row, -d) for d in steps]
     later, *metas = lax.optimization_barrier((marked, *metas))
     below2 = swap_rows(later, 2 * LINE)
+    gathered = jnp.concatenate(metas, axis=0)
+    lists_same = swap_rows(gathered, 0)
+    lists_two = swap_rows(gathered, -2 * LINE)
     scalars = [SMEM] * (1 + len(steps))
     sent = call(
         lambda *r: pick_near_kernel(block, *r),
         [one] * len(steps),
-        (place, *metas, below),
-        scalars + [VMEM],
+        (place, *metas, below, lists_same, lists_two),
+        scalars + [VMEM, HELD, HELD],
     )
     got_near = [along(b, d) for d, b in zip(steps, sent)]
     sent = call(
@@ -329,11 +326,12 @@
         flops=8 * MICROSECOND,
     )
     back_near = [along(b, -d) for d, b in zip(steps, near_back)]
+    gate = swap_rows(lax.optimization_barrier((row, near_back[0]))[0], 0)
     far_back = call(
         lambda *r: back_far_kernel(block, *r),
-        [((block, width + 128), BF16)] * 3,
-        (place, lists, tiles_t, gpool, msg_b, msg_c, q, near_back[0]),
-        [SMEM] * 2 + [VMEM] * 5 + [HELD],
+        [one] * 3,
+        (tiles_t, gpool, msg_b, msg_c, q, gate),
+        [VMEM] * 5 + [HELD],
         scratch=[gn],
         flops=2 * MICROSECOND,
     )
@@ -358,10 +356,10 @@
     )
     g_below = swap_rows(sum_below, -LINE)
     (placed,) = call(
-        place_kernel,
+        lambda *r: place_kernel(block, *r),
         [((rows, width), F32)],
-        (gself, *back_far),
-        [VMEM] * 4,
+        (place, lists_same, lists_two, gself, *back_far),
+        [SMEM] * 3 + [VMEM] * 4,
         flops=20 * MICROSECOND,
     )
     (grad,) = call(finish_kernel, [two], (live, placed, g_same, g_below), [SMEM] + [VMEM] * 3)

time: 103 us -> 113 us (1.097)
  waiting for transfers between devices: 38.6 us -> 49.9 us
  starting transfers between devices: 30.1 us -> 28.5 us
    ppermute x12, waiting for transfers between devices: 4.86 us -> 15.5 us  [along(): return lax.ppermute(x, 'dom', pairs)]
    ppermute x3, starting transfers between devices: 10 us -> 5.15 us  [straight_back(): return lax.ppermute(x, ('side', 'dom'), pairs)]
    ppermute x5 -> x8, starting transfers between devices: 7.26 us -> 10.8 us  [swap_rows(): return lax.ppermute(x, ('side', 'dom'), pairs)]
    ppermute x3, waiting for transfers between devices: 12.9 us -> 14.6 us  [straight_back(): return lax.ppermute(x, ('side', 'dom'), pairs)]
    ppermute x5 -> x8, waiting for transfers between devices: 20.8 us -> 19.7 us  [swap_rows(): return lax.ppermute(x, ('side', 'dom'), pairs)]
  transfers between devices with their start and end apart: 20 -> 23, of which waited for: 8 -> 10; matrix products, arithmetic and copies ran while one was open for 1% -> 1% of each run, Pallas kernels for 18% -> 17%
where the time goes in v9:
time: 113 us; the launch traced here: 111 us
  waiting for transfers between devices  49.9 us (44%)
  starting transfers between devices  28.5 us (25%)
  Pallas kernels  26.4 us (23%)
  local copies, waits for them, and re-layouts  3.06 us (3%)
  other arithmetic  1.97 us (2%)
  between operations  1.57 us (1%)
    pallas_call x11, Pallas kernels, call(): pl.pallas_call(kernel, out_shape=[jax.ShapeDtypeStruct(s, d) for s, d in...  26.4 us
    ppermute x8, waiting for transfers between devices, swap_rows(): return lax.ppermute(x, ('side', 'dom'), pairs)  19.7 us
    ppermute x12, waiting for transfers between devices, along(): return lax.ppermute(x, 'dom', pairs)  15.5 us
    ppermute x3, waiting for transfers between devices, straight_back(): return lax.ppermute(x, ('side', 'dom'), pairs)  14.6 us
    ppermute x12, starting transfers between devices, along(): return lax.ppermute(x, 'dom', pairs)  12.6 us
    ppermute x8, starting transfers between devices, swap_rows(): return lax.ppermute(x, ('side', 'dom'), pairs)  10.8 us
    ppermute x3, starting transfers between devices, straight_back(): return lax.ppermute(x, ('side', 'dom'), pairs)  5.15 us
  transfers between devices with their start and end apart: 23, of which 10 were waited for; matrix products, arithmetic and copies ran while one was open for 1% of the time, Pallas kernels for 17%

profile of v9, /device:TPU:7, one launch (start us, length us, event | category | flops | bytes accessed | tf_op | source)
XLA Modules:
  0.0 111.4 jit_solution(10265318878408096203)
XLA Ops:
  1.5 2.0 %broadcast_select_fusion = bf16[256,1024]{1,0:T(8,128)(2,1)} fusion(pred[256]{0:T(512)(128)(4,1)S(1)} %iota_compare_fusion, bf16[1,256,1024]{2,1,0:T(8,128)(2,1)} %param.10), kind=kLoop, calls=%fused_computation | loop fusion | flops 262144 | bytes 1048832 | tf_op jit(solution)/shard_map/jit(_where)/select_n | solution.py:266
  3.4 1.9 %collective-permute-start.8 = (bf16[256,1024]{1,0:T(8,128)(2,1)}, bf16[256,1024]{1,0:T(8,128)(2,1)S(1)}, u32[]{:S(2)}, u32[]{:S(2)}) collective-permute-start(bf16[256,1024]{1,0:T(8,128)(2,1)} %broadcast_select_fusion), channel_id=1, source_target_pairs={{0,68},{1,69},{2,70},{3,71},{4,72},{5,73},{6,74},{7,75},{8,76},{9,... | collective-permute-start | bytes 1572872 | tf_op jit(solution)/shard_map/ppermute | solution.py:43
  6.2 2.2 %collective-permute-start.1 = (s32[1,128]{1,0:T(1,128)S(1)}, s32[1,128]{1,0:T(1,128)S(1)}, u32[]{:S(2)}, u32[]{:S(2)}) collective-permute-start(s32[1,128]{1,0:T(1,128)S(1)} %pad_bitcast_fusion), channel_id=1, source_target_pairs={{0,2},{1,3},{2,0},{3,1},{4,6},{5,7},{6,4},{7,5},{8,10},{9,11},{10,... | collective-permute-start | bytes 1544 | tf_op jit(solution)/shard_map/ppermute | solution.py:49
  8.7 1.4 %collective-permute-done.1.r_2_.r_3_ = s32[1,128]{1,0:T(1,128)S(1)} collective-permute-done((s32[1,128]{1,0:T(1,128)S(1)}, s32[1,128]{1,0:T(1,128)S(1)}, u32[]{:S(2)}, u32[]{:S(2)}) %collective-permute-start.1) | collective-permute-done | bytes 544 | tf_op jit(solution)/shard_map/ppermute | solution.py:49
  10.1 2.1 %collective-permute-done.r_1_.r_2_ = s32[1,128]{1,0:T(1,128)S(1)} collective-permute-done((s32[1,128]{1,0:T(1,128)S(1)}, s32[1,128]{1,0:T(1,128)S(1)}, u32[]{:S(2)}, u32[]{:S(2)}) %collective-permute-start) | collective-permute-done | bytes 544 | tf_op jit(solution)/shard_map/ppermute | solution.py:49
  12.2 3.7 %collective-permute-start.4 = (bf16[256,1024]{1,0:T(8,128)(2,1)}, bf16[256,1024]{1,0:T(8,128)(2,1)}, u32[]{:S(2)}, u32[]{:S(2)}) collective-permute-start(bf16[256,1024]{1,0:T(8,128)(2,1)} %broadcast_select_fusion), channel_id=1, source_target_pairs={{0,72},{1,73},{2,74},{3,75},{4,76},{5,77},{6,78},{7,79},{8,80},{9,... | collective-permute-start | bytes 1572872 | tf_op jit(solution)/shard_map/ppermute | solution.py:43
  16.0 3.5 %collective-permute-start.10 = (s32[3,128]{1,0:T(4,128)S(1)}, s32[3,128]{1,0:T(4,128)S(1)}, u32[]{:S(2)}, u32[]{:S(2)}) collective-permute-start(s32[3,128]{1,0:T(4,128)S(1)} %pad_add_fusion), channel_id=1, source_target_pairs={{0,120},{1,121},{2,122},{3,123},{4,124},{5,125},{6,126},{7,127},{8... | collective-permute-start | bytes 4616 | tf_op jit(solution)/shard_map/ppermute | solution.py:43
  19.5 12.5 %collective-permute-done.10.r_6_.r_2_ = s32[3,128]{1,0:T(4,128)S(1)} collective-permute-done((s32[3,128]{1,0:T(4,128)S(1)}, s32[3,128]{1,0:T(4,128)S(1)}, u32[]{:S(2)}, u32[]{:S(2)}) %collective-permute-start.10) | collective-permute-done | bytes 1568 | tf_op jit(solution)/shard_map/ppermute | solution.py:43
  32.0 1.5 %shard_map.115 = (bf16[128,1024]{1,0:T(8,128)(2,1)}, bf16[128,1024]{1,0:T(8,128)(2,1)}, bf16[128,1024]{1,0:T(8,128)(2,1)}) custom-call(s32[1]{0:T(128)} %bitcast.2.r_0_, s32[1,128]{1,0:T(1,128)S(1)} %collective-permute-done.r_1_.r_2_, s32[1,128]{1,0:T(1,128)S(1)} %collective-permute-done.1.r_2_.r_3_, s32[1,128]{1,0:T(1,128)S(1)} %collective-permute-done.2.r_3_.r_4_, ...), custom_call_target="tpu_custom_call" | custom-call | bytes 1048576 | tf_op jit(solution)/shard_map/pallas_call | solution.py:25
  33.7 2.1 %collective-permute-start.12 = (bf16[128,1024]{1,0:T(8,128)(2,1)}, bf16[128,1024]{1,0:T(8,128)(2,1)}, u32[]{:S(2)}, u32[]{:S(2)}) collective-permute-start(bf16[128,1024]{1,0:T(8,128)(2,1)} %get-tuple-element.46), channel_id=1, source_target_pairs={{0,2},{1,3},{2,0},{3,1},{4,6},{5,7},{6,4},{7,5},{8,10},{9,11},{10,... | collective-permute-start | bytes 786440 | tf_op jit(solution)/shard_map/ppermute | solution.py:49
  36.6 1.3 %shard_map.113 = (bf16[128,1024]{1,0:T(8,128)(2,1)S(1)}, bf16[128,1024]{1,0:T(8,128)(2,1)S(1)}, bf16[128,1024]{1,0:T(8,128)(2,1)S(1)}) custom-call(s32[1]{0:T(128)} %bitcast.2.r_0_, s32[1,128]{1,0:T(1,128)S(1)} %collective-permute-done.r_1_.r_2_, s32[1,128]{1,0:T(1,128)S(1)} %collective-permute-done.1.r_2_.r_3_, ...), custom_call_target="tpu_custom_call" | custom-call | bytes 1048576 | tf_op jit(solution)/shard_map/pallas_call | solution.py:25
  37.9 2.8 %collective-permute-start.5 = (bf16[128,1024]{1,0:T(8,128)(2,1)S(1)}, bf16[128,1024]{1,0:T(8,128)(2,1)S(1)}, u32[]{:S(2)}, u32[]{:S(2)}) collective-permute-start(bf16[128,1024]{1,0:T(8,128)(2,1)S(1)} %get-tuple-element.42), channel_id=1, source_target_pairs={{0,2},{1,3},{2,0},{3,1},{4,6},{5,7},{6,4},{7,5},{8,10},{9,11},{10,... | collective-permute-start | bytes 786440 | tf_op jit(solution)/shard_map/ppermute | solution.py:49
  40.9 1.6 %copy-done.3 = s32[1,256,2048]{2,1,0:T(8,128)S(1)} copy-done((s32[1,256,2048]{2,1,0:T(8,128)S(1)}, s32[1,256,2048]{2,1,0:T(8,128)}, u32[]{:S(2)}) %copy-start.3) | copy-done | bytes 2097176
  42.5 1.3 %shard_map.114 = (bf16[256,1024]{1,0:T(8,128)(2,1)S(1)}, bf16[1024,256]{1,0:T(8,128)(2,1)S(1)}, f32[256,1024]{1,0:T(8,128)S(1)}) custom-call(s32[1]{0:T(128)} %bitcast.2.r_0_, s32[8,2]{1,0:T(8,128)S(1)} %copy.14.r_1_.r_0_, s32[256,2048]{1,0:T(8,128)S(1)} %bitcast.21, bf16[256,1024]{1,0:T(8,128)(2,1)S(1)} %bitcast.20, bf16[1024,1024]{1,0:T(8,128)(2,1)S(1)} %copy-done.1, ...), custom_call_target="tpu_custom_call" | custom-call | flops 536870912 | bytes 1048576 | tf_op jit(solution)/shard_map/pallas_call | solution.py:25
  43.9 1.5 %collective-permute-start.6 = (bf16[128,1024]{1,0:T(8,128)(2,1)S(1)}, bf16[128,1024]{1,0:T(8,128)(2,1)S(1)}, u32[]{:S(2)}, u32[]{:S(2)}) collective-permute-start(bf16[128,1024]{1,0:T(8,128)(2,1)S(1)} %get-tuple-element.43), channel_id=1, source_target_pairs={{0,3},{1,0},{2,1},{3,2},{4,7},{5,4},{6,5},{7,6},{8,11},{9,8},{10,9... | collective-permute-start | bytes 786440 | tf_op jit(solution)/shard_map/ppermute | solution.py:49
  45.4 4.9 %collective-permute-done.13.r_5_ = bf16[128,1024]{1,0:T(8,128)(2,1)} collective-permute-done((bf16[128,1024]{1,0:T(8,128)(2,1)}, bf16[128,1024]{1,0:T(8,128)(2,1)}, u32[]{:S(2)}, u32[]{:S(2)}) %collective-permute-start.13) | collective-permute-done | bytes 262176 | tf_op jit(solution)/shard_map/ppermute | solution.py:49
  50.3 5.2 %shard_map.116 = (bf16[640,2048]{1,0:T(8,128)(2,1)S(1)}, f32[256,2048]{1,0:T(8,128)S(1)}, f32[256,128]{1,0:T(8,128)S(1)}) custom-call(s32[8,2]{1,0:T(8,128)S(1)} %copy.14.r_1_.r_0_, bf16[256,1024]{1,0:T(8,128)(2,1)} %collective-permute-done.3.r_4_.r_1_, bf16[256,1024]{1,0:T(8,128)(2,1)S(1)} %collective-permute-done.8.r_4_.r_2_, ...), custom_call_target="tpu_custom_call" | custom-call | flops 3355443200 | bytes 1048576 | tf_op jit(solution)/shard_map/pallas_call | solution.py:25
  55.5 2.7 %collective-permute-done.7.r_0_ = bf16[128,1024]{1,0:T(8,128)(2,1)S(1)} collective-permute-done((bf16[128,1024]{1,0:T(8,128)(2,1)S(1)}, bf16[128,1024]{1,0:T(8,128)(2,1)S(1)}, u32[]{:S(2)}, u32[]{:S(2)}) %collective-permute-start.7) | collective-permute-done | bytes 262176 | tf_op jit(solution)/shard_map/ppermute | solution.py:49
  58.2 1.6 %shard_map.117 = (bf16[128,2048]{1,0:T(8,128)(2,1)S(1)}, f32[256,2048]{1,0:T(8,128)S(1)}, f32[256,128]{1,0:T(8,128)S(1)}) custom-call(bf16[128,1024]{1,0:T(8,128)(2,1)S(1)} %collective-permute-done.7.r_0_, bf16[1024,2048]{1,0:T(8,128)(2,1)S(1)} %copy-done, f32[1,2048]{1,0:T(1,128)S(1)} %bitcast.23, bf16[256,1024]{1,0:T(8,128)(2,1)S(1)} %get-tuple-element.44.r_8_.r_3_.r_5_, ...), custom_call_target="tpu_custom_call" | custom-call | flops 671088640 | bytes 1048576 | tf_op jit(solution)/shard_map/pallas_call | solution.py:25
  60.5 7.0 %shard_map.118 = (bf16[256,1024]{1,0:T(8,128)(2,1)S(1)}, bf16[256,2048]{1,0:T(8,128)(2,1)S(1)}, f32[256,1024]{1,0:T(8,128)S(1)}, bf16[256,2048]{1,0:T(8,128)(2,1...) custom-call(s32[1]{0:T(128)} %bitcast.16.r_0_, ...), custom_call_target="tpu_custom_call" | custom-call | flops 8000000000 | bytes 1048576 | tf_op jit(solution)/shard_map/pallas_call | solution.py:25
  67.5 1.2 %collective-permute-start.14 = (s32[1,128]{1,0:T(1,128)S(1)}, s32[1,128]{1,0:T(1,128)S(1)}, u32[]{:S(2)}, u32[]{:S(2)}) collective-permute-start(s32[1,128]{1,0:T(1,128)S(1)} %pad_bitcast_fusion), channel_id=1, source_target_pairs={{0,64},{1,65},{2,66},{3,67},{4,68},{5,69},{6,70},{7,71},{8,72},{9,... | collective-permute-start | bytes 1544 | tf_op jit(solution)/shard_map/ppermute | solution.py:43
  69.2 2.8 %collective-permute-start.20 = (bf16[128,1024]{1,0:T(8,128)(2,1)S(1)}, bf16[128,1024]{1,0:T(8,128)(2,1)S(1)}, u32[]{:S(2)}, u32[]{:S(2)}) collective-permute-start(bf16[128,1024]{1,0:T(8,128)(2,1)S(1)} %get-tuple-element.68), channel_id=1, source_target_pairs={{0,2},{1,3},{2,0},{3,1},{4,6},{5,7},{6,4},{7,5},{8,10},{9,11},{10,... | collective-permute-start | bytes 786440 | tf_op jit(solution)/shard_map/ppermute | solution.py:49
  72.1 2.2 %shard_map.119 = (bf16[128,1024]{1,0:T(8,128)(2,1)S(1)}, bf16[128,1024]{1,0:T(8,128)(2,1)S(1)}, bf16[128,1024]{1,0:T(8,128)(2,1)S(1)}) custom-call(bf16[1024,256]{1,0:T(8,128)(2,1)S(1)} %get-tuple-element.41.r_12_.r_0_.r_2_, bf16[256,2048]{1,0:T(8,128)(2,1)S(1)} %get-tuple-element.54.r_1_.r_3_, bf16[128,2048]{1,0:T(8,128)(2,1)S(1)} %get-tuple-element.57.r_2_, ...), custom_call_target="tpu_custom_call" | custom-call | flops 2000000000 | bytes 1048576 | tf_op jit(solution)/shard_map/pallas_call | solution.py:25
  74.3 2.5 %collective-permute-start.16 = (bf16[128,1024]{1,0:T(8,128)(2,1)S(1)}, bf16[128,1024]{1,0:T(8,128)(2,1)S(1)}, u32[]{:S(2)}, u32[]{:S(2)}) collective-permute-start(bf16[128,1024]{1,0:T(8,128)(2,1)S(1)} %get-tuple-element.64), channel_id=1, source_target_pairs={{66,0},{67,1},{72,2},{73,3},{70,4},{71,5},{76,6},{77,7},{74,8},{75... | collective-permute-start | bytes 786440 | tf_op jit(solution)/shard_map/ppermute | solution.py:59
  76.9 3.6 %shard_map.120 = (bf16[256,1024]{1,0:T(8,128)(2,1)S(1)}, bf16[128,1024]{1,0:T(8,128)(2,1)S(1)}, f32[256,1024]{1,0:T(8,128)S(1)}, bf16[256,1024]{1,0:T(8,128)(2,1)}) custom-call(s32[8,2]{1,0:T(8,128)S(1)} %copy.14.r_1_.r_0_, s32[1]{0:T(128)} %bitcast.17.r_1_, bf16[1024,256]{1,0:T(8,128)(2,1)S(1)} %get-tuple-element.41.r_12_.r_0_.r_2_, ...), custom_call_target="tpu_custom_call" | custom-call | flops 3000000000 | bytes 1048576 | tf_op jit(solution)/shard_map/pallas_call | solution.py:25
  80.5 3.6 %collective-permute-done.20.r_7_ = bf16[128,1024]{1,0:T(8,128)(2,1)S(1)} collective-permute-done((bf16[128,1024]{1,0:T(8,128)(2,1)S(1)}, bf16[128,1024]{1,0:T(8,128)(2,1)S(1)}, u32[]{:S(2)}, u32[]{:S(2)}) %collective-permute-start.20) | collective-permute-done | bytes 262176 | tf_op jit(solution)/shard_map/ppermute | solution.py:49
  84.1 2.6 %collective-permute-start.17 = (bf16[128,1024]{1,0:T(8,128)(2,1)S(1)}, bf16[128,1024]{1,0:T(8,128)(2,1)S(1)}, u32[]{:S(2)}, u32[]{:S(2)}) collective-permute-start(bf16[128,1024]{1,0:T(8,128)(2,1)S(1)} %get-tuple-element.65), channel_id=1, source_target_pairs={{67,0},{72,1},{73,2},{74,3},{71,4},{76,5},{77,6},{78,7},{75,8},{80... | collective-permute-start | bytes 786440 | tf_op jit(solution)/shard_map/ppermute | solution.py:59
  86.7 0.9 shard_map.122
  87.7 4.5 %collective-permute-done.16.r_5_ = bf16[128,1024]{1,0:T(8,128)(2,1)S(1)} collective-permute-done((bf16[128,1024]{1,0:T(8,128)(2,1)S(1)}, bf16[128,1024]{1,0:T(8,128)(2,1)S(1)}, u32[]{:S(2)}, u32[]{:S(2)}) %collective-permute-start.16) | collective-permute-done | bytes 262176 | tf_op jit(solution)/shard_map/ppermute | solution.py:59
  92.2 10.1 %collective-permute-done.17.r_6_ = bf16[128,1024]{1,0:T(8,128)(2,1)S(1)} collective-permute-done((bf16[128,1024]{1,0:T(8,128)(2,1)S(1)}, bf16[128,1024]{1,0:T(8,128)(2,1)S(1)}, u32[]{:S(2)}, u32[]{:S(2)}) %collective-permute-start.17) | collective-permute-done | bytes 262176 | tf_op jit(solution)/shard_map/ppermute | solution.py:59
  103.2 7.2 %collective-permute-done.22.below_ref = bf16[256,1024]{1,0:T(8,128)(2,1)S(1)} collective-permute-done((bf16[256,1024]{1,0:T(8,128)(2,1)S(1)}, bf16[256,1024]{1,0:T(8,128)(2,1)S(1)}, u32[]{:S(2)}, u32[]{:S(2)}) %collective-permute-start.22) | collective-permute-done | bytes 524320 | tf_op jit(solution)/shard_map/ppermute | solution.py:43
  110.4 1.0 shard_map.123
  (47 shorter events, 4.6 us)
Async XLA Ops:
  0.6 40.3 %copy-start.2 = (bf16[1,256,1024]{2,1,0:T(8,128)(2,1)S(1)}, bf16[1,256,1024]{2,1,0:T(8,128)(2,1)}, u32[]{:S(2)}) copy-start(bf16[1,256,1024]{2,1,0:T(8,128)(2,1)} %param.10) | copy-start | bytes 1572868
  0.6 40.3 %copy-start.1 = (bf16[1024,1024]{1,0:T(8,128)(2,1)S(1)}, bf16[1024,1024]{1,0:T(8,128)(2,1)}, u32[]{:S(2)}) copy-start(bf16[1024,1024]{1,0:T(8,128)(2,1)} %r_7_.1) | copy-start | bytes 6291460
  3.4 28.6 %collective-permute-start.8 = (bf16[256,1024]{1,0:T(8,128)(2,1)}, bf16[256,1024]{1,0:T(8,128)(2,1)S(1)}, u32[]{:S(2)}, u32[]{:S(2)}) collective-permute-start(bf16[256,1024]{1,0:T(8,128)(2,1)} %broadcast_select_fusion), channel_id=1, source_target_pairs={{0,68},{1,69},{2,70},{3,71},{4,72},{5,73},{6,74},{7,75},{8,76},{9,... | collective-permute-start | bytes 1572872 | tf_op jit(solution)/shard_map/ppermute | solution.py:43
  6.0 2.7 %collective-permute-start.2 = (s32[1,128]{1,0:T(1,128)S(1)}, s32[1,128]{1,0:T(1,128)S(1)}, u32[]{:S(2)}, u32[]{:S(2)}) collective-permute-start(s32[1,128]{1,0:T(1,128)S(1)} %pad_bitcast_fusion), channel_id=1, source_target_pairs={{0,1},{1,2},{2,3},{3,0},{4,5},{5,6},{6,7},{7,4},{8,9},{9,10},{10,1... | collective-permute-start | bytes 1544 | tf_op jit(solution)/shard_map/ppermute | solution.py:49
  6.2 3.9 %collective-permute-start.1 = (s32[1,128]{1,0:T(1,128)S(1)}, s32[1,128]{1,0:T(1,128)S(1)}, u32[]{:S(2)}, u32[]{:S(2)}) collective-permute-start(s32[1,128]{1,0:T(1,128)S(1)} %pad_bitcast_fusion), channel_id=1, source_target_pairs={{0,2},{1,3},{2,0},{3,1},{4,6},{5,7},{6,4},{7,5},{8,10},{9,11},{10,... | collective-permute-start | bytes 1544 | tf_op jit(solution)/shard_map/ppermute | solution.py:49
  8.3 3.9 %collective-permute-start = (s32[1,128]{1,0:T(1,128)S(1)}, s32[1,128]{1,0:T(1,128)S(1)}, u32[]{:S(2)}, u32[]{:S(2)}) collective-permute-start(s32[1,128]{1,0:T(1,128)S(1)} %pad_bitcast_fusion), channel_id=1, source_target_pairs={{0,3},{1,0},{2,1},{3,2},{4,7},{5,4},{6,5},{7,6},{8,11},{9,8},{10,9... | collective-permute-start | bytes 1544 | tf_op jit(solution)/shard_map/ppermute | solution.py:49
  8.3 28.3 %collective-permute-start.3 = (bf16[256,1024]{1,0:T(8,128)(2,1)}, bf16[256,1024]{1,0:T(8,128)(2,1)}, u32[]{:S(2)}, u32[]{:S(2)}) collective-permute-start(bf16[256,1024]{1,0:T(8,128)(2,1)} %broadcast_select_fusion), channel_id=1, source_target_pairs={{0,64},{1,65},{2,66},{3,67},{4,68},{5,69},{6,70},{7,71},{8,72},{9,... | collective-permute-start | bytes 1572872 | tf_op jit(solution)/shard_map/ppermute | solution.py:43
  12.2 24.4 %collective-permute-start.4 = (bf16[256,1024]{1,0:T(8,128)(2,1)}, bf16[256,1024]{1,0:T(8,128)(2,1)}, u32[]{:S(2)}, u32[]{:S(2)}) collective-permute-start(bf16[256,1024]{1,0:T(8,128)(2,1)} %broadcast_select_fusion), channel_id=1, source_target_pairs={{0,72},{1,73},{2,74},{3,75},{4,76},{5,77},{6,78},{7,79},{8,80},{9,... | collective-permute-start | bytes 1572872 | tf_op jit(solution)/shard_map/ppermute | solution.py:43
  16.0 16.1 %collective-permute-start.10 = (s32[3,128]{1,0:T(4,128)S(1)}, s32[3,128]{1,0:T(4,128)S(1)}, u32[]{:S(2)}, u32[]{:S(2)}) collective-permute-start(s32[3,128]{1,0:T(4,128)S(1)} %pad_add_fusion), channel_id=1, source_target_pairs={{0,120},{1,121},{2,122},{3,123},{4,124},{5,125},{6,126},{7,127},{8... | collective-permute-start | bytes 4616 | tf_op jit(solution)/shard_map/ppermute | solution.py:43
  19.5 12.5 %collective-permute-start.9 = (s32[3,128]{1,0:T(4,128)S(1)}, s32[3,128]{1,0:T(4,128)S(1)}, u32[]{:S(2)}, u32[]{:S(2)}) collective-permute-start(s32[3,128]{1,0:T(4,128)S(1)} %pad_add_fusion), channel_id=1, source_target_pairs={{0,64},{1,65},{2,66},{3,67},{4,68},{5,69},{6,70},{7,71},{8,72},{9,... | collective-permute-start | bytes 4616 | tf_op jit(solution)/shard_map/ppermute | solution.py:43
  33.5 10.3 %collective-permute-start.11 = (bf16[128,1024]{1,0:T(8,128)(2,1)}, bf16[128,1024]{1,0:T(8,128)(2,1)S(1)}, u32[]{:S(2)}, u32[]{:S(2)}) collective-permute-start(bf16[128,1024]{1,0:T(8,128)(2,1)} %get-tuple-element.45), channel_id=1, source_target_pairs={{0,1},{1,2},{2,3},{3,0},{4,5},{5,6},{6,7},{7,4},{8,9},{9,10},{10,1... | collective-permute-start | bytes 786440 | tf_op jit(solution)/shard_map/ppermute | solution.py:49
  33.7 11.7 %collective-permute-start.12 = (bf16[128,1024]{1,0:T(8,128)(2,1)}, bf16[128,1024]{1,0:T(8,128)(2,1)}, u32[]{:S(2)}, u32[]{:S(2)}) collective-permute-start(bf16[128,1024]{1,0:T(8,128)(2,1)} %get-tuple-element.46), channel_id=1, source_target_pairs={{0,2},{1,3},{2,0},{3,1},{4,6},{5,7},{6,4},{7,5},{8,10},{9,11},{10,... | collective-permute-start | bytes 786440 | tf_op jit(solution)/shard_map/ppermute | solution.py:49
  35.9 14.5 %collective-permute-start.13 = (bf16[128,1024]{1,0:T(8,128)(2,1)}, bf16[128,1024]{1,0:T(8,128)(2,1)}, u32[]{:S(2)}, u32[]{:S(2)}) collective-permute-start(bf16[128,1024]{1,0:T(8,128)(2,1)} %get-tuple-element.47), channel_id=1, source_target_pairs={{0,3},{1,0},{2,1},{3,2},{4,7},{5,4},{6,5},{7,6},{8,11},{9,8},{10,9... | collective-permute-start | bytes 786440 | tf_op jit(solution)/shard_map/ppermute | solution.py:49
  37.9 21.8 %collective-permute-start.5 = (bf16[128,1024]{1,0:T(8,128)(2,1)S(1)}, bf16[128,1024]{1,0:T(8,128)(2,1)S(1)}, u32[]{:S(2)}, u32[]{:S(2)}) collective-permute-start(bf16[128,1024]{1,0:T(8,128)(2,1)S(1)} %get-tuple-element.42), channel_id=1, source_target_pairs={{0,2},{1,3},{2,0},{3,1},{4,6},{5,7},{6,4},{7,5},{8,10},{9,11},{10,... | collective-permute-start | bytes 786440 | tf_op jit(solution)/shard_map/ppermute | solution.py:49
  40.7 17.5 %collective-permute-start.7 = (bf16[128,1024]{1,0:T(8,128)(2,1)S(1)}, bf16[128,1024]{1,0:T(8,128)(2,1)S(1)}, u32[]{:S(2)}, u32[]{:S(2)}) collective-permute-start(bf16[128,1024]{1,0:T(8,128)(2,1)S(1)} %get-tuple-element.40.r_5_), channel_id=1, source_target_pairs={{0,1},{1,2},{2,3},{3,0},{4,5},{5,6},{6,7},{7,4},{8,9},{9,10},{10,1... | collective-permute-start | bytes 786440 | tf_op jit(solution)/shard_map/ppermute | solution.py:49
  40.9 1.6 %copy-start.3 = (s32[1,256,2048]{2,1,0:T(8,128)S(1)}, s32[1,256,2048]{2,1,0:T(8,128)}, u32[]{:S(2)}) copy-start(s32[1,256,2048]{2,1,0:T(8,128)} %param.13) | copy-start | bytes 6291460
  42.5 7.8 %copy-start = (bf16[1024,2048]{1,0:T(8,128)(2,1)S(1)}, bf16[1024,2048]{1,0:T(8,128)(2,1)}, u32[]{:S(2)}) copy-start(bf16[1024,2048]{1,0:T(8,128)(2,1)} %r_5_.1) | copy-start | bytes 12582916
  42.5 7.8 %copy-start.4 = (f32[2048]{0:T(1024)S(1)}, f32[2048]{0:T(1024)}, u32[]{:S(2)}) copy-start(f32[2048]{0:T(1024)} %param.16) | copy-start | bytes 24580
  43.9 16.7 %collective-permute-start.6 = (bf16[128,1024]{1,0:T(8,128)(2,1)S(1)}, bf16[128,1024]{1,0:T(8,128)(2,1)S(1)}, u32[]{:S(2)}, u32[]{:S(2)}) collective-permute-start(bf16[128,1024]{1,0:T(8,128)(2,1)S(1)} %get-tuple-element.43), channel_id=1, source_target_pairs={{0,3},{1,0},{2,1},{3,2},{4,7},{5,4},{6,5},{7,6},{8,11},{9,8},{10,9... | collective-permute-start | bytes 786440 | tf_op jit(solution)/shard_map/ppermute | solution.py:49
  58.2 2.3 %copy-start.5 = (bf16[2048,1024]{1,0:T(8,128)(2,1)S(1)}, bf16[2048,1024]{1,0:T(8,128)(2,1)}, u32[]{:S(2)}) copy-start(bf16[2048,1024]{1,0:T(8,128)(2,1)} %r_10_.1) | copy-start | bytes 12582916
  58.2 2.3 %copy-start.6 = (bf16[1,256,1024]{2,1,0:T(8,128)(2,1)S(1)}, bf16[1,256,1024]{2,1,0:T(8,128)(2,1)}, u32[]{:S(2)}) copy-start(bf16[1,256,1024]{2,1,0:T(8,128)(2,1)} %param.14) | copy-start | bytes 1572868
  58.2 2.3 %copy-start.7 = (f32[1024]{0:T(1024)S(1)}, f32[1024]{0:T(1024)}, u32[]{:S(2)}) copy-start(f32[1024]{0:T(1024)} %param.19) | copy-start | bytes 12292
  67.5 4.6 %collective-permute-start.14 = (s32[1,128]{1,0:T(1,128)S(1)}, s32[1,128]{1,0:T(1,128)S(1)}, u32[]{:S(2)}, u32[]{:S(2)}) collective-permute-start(s32[1,128]{1,0:T(1,128)S(1)} %pad_bitcast_fusion), channel_id=1, source_target_pairs={{0,64},{1,65},{2,66},{3,67},{4,68},{5,69},{6,70},{7,71},{8,72},{9,... | collective-permute-start | bytes 1544 | tf_op jit(solution)/shard_map/ppermute | solution.py:43
  68.7 18.0 %collective-permute-start.19 = (bf16[128,1024]{1,0:T(8,128)(2,1)S(1)}, bf16[128,1024]{1,0:T(8,128)(2,1)S(1)}, u32[]{:S(2)}, u32[]{:S(2)}) collective-permute-start(bf16[128,1024]{1,0:T(8,128)(2,1)S(1)} %get-tuple-element.59), channel_id=1, source_target_pairs={{0,3},{1,0},{2,1},{3,2},{4,7},{5,4},{6,5},{7,6},{8,11},{9,8},{10,9... | collective-permute-start | bytes 786440 | tf_op jit(solution)/shard_map/ppermute | solution.py:49
  69.2 14.9 %collective-permute-start.20 = (bf16[128,1024]{1,0:T(8,128)(2,1)S(1)}, bf16[128,1024]{1,0:T(8,128)(2,1)S(1)}, u32[]{:S(2)}, u32[]{:S(2)}) collective-permute-start(bf16[128,1024]{1,0:T(8,128)(2,1)S(1)} %get-tuple-element.68), channel_id=1, source_target_pairs={{0,2},{1,3},{2,0},{3,1},{4,6},{5,7},{6,4},{7,5},{8,10},{9,11},{10,... | collective-permute-start | bytes 786440 | tf_op jit(solution)/shard_map/ppermute | solution.py:49
  72.1 14.6 %collective-permute-start.21 = (bf16[128,1024]{1,0:T(8,128)(2,1)S(1)}, bf16[128,1024]{1,0:T(8,128)(2,1)S(1)}, u32[]{:S(2)}, u32[]{:S(2)}) collective-permute-start(bf16[128,1024]{1,0:T(8,128)(2,1)S(1)} %get-tuple-element.69), channel_id=1, source_target_pairs={{0,1},{1,2},{2,3},{3,0},{4,5},{5,6},{6,7},{7,4},{8,9},{9,10},{10,1... | collective-permute-start | bytes 786440 | tf_op jit(solution)/shard_map/ppermute | solution.py:49
  74.3 17.9 %collective-permute-start.16 = (bf16[128,1024]{1,0:T(8,128)(2,1)S(1)}, bf16[128,1024]{1,0:T(8,128)(2,1)S(1)}, u32[]{:S(2)}, u32[]{:S(2)}) collective-permute-start(bf16[128,1024]{1,0:T(8,128)(2,1)S(1)} %get-tuple-element.64), channel_id=1, source_target_pairs={{66,0},{67,1},{72,2},{73,3},{70,4},{71,5},{76,6},{77,7},{74,8},{75... | collective-permute-start | bytes 786440 | tf_op jit(solution)/shard_map/ppermute | solution.py:59
  76.9 25.5 %collective-permute-start.15 = (bf16[128,1024]{1,0:T(8,128)(2,1)S(1)}, bf16[128,1024]{1,0:T(8,128)(2,1)S(1)}, u32[]{:S(2)}, u32[]{:S(2)}) collective-permute-start(bf16[128,1024]{1,0:T(8,128)(2,1)S(1)} %get-tuple-element.61.r_9_), channel_id=1, source_target_pairs={{65,0},{66,1},{67,2},{72,3},{69,4},{70,5},{71,6},{76,7},{73,8},{74... | collective-permute-start | bytes 786440 | tf_op jit(solution)/shard_map/ppermute | solution.py:59
  84.1 18.3 %collective-permute-start.17 = (bf16[128,1024]{1,0:T(8,128)(2,1)S(1)}, bf16[128,1024]{1,0:T(8,128)(2,1)S(1)}, u32[]{:S(2)}, u32[]{:S(2)}) collective-permute-start(bf16[128,1024]{1,0:T(8,128)(2,1)S(1)} %get-tuple-element.65), channel_id=1, source_target_pairs={{67,0},{72,1},{73,2},{74,3},{71,4},{76,5},{77,6},{78,7},{75,8},{80... | collective-permute-start | bytes 786440 | tf_op jit(solution)/shard_map/ppermute | solution.py:59
  86.7 16.5 %collective-permute-start.18 = (bf16[256,1024]{1,0:T(8,128)(2,1)S(1)}, bf16[256,1024]{1,0:T(8,128)(2,1)S(1)}, u32[]{:S(2)}, u32[]{:S(2)}) collective-permute-start(bf16[256,1024]{1,0:T(8,128)(2,1)S(1)} %get-tuple-element.66), channel_id=1, source_target_pairs={{0,64},{1,65},{2,66},{3,67},{4,68},{5,69},{6,70},{7,71},{8,72},{9,... | collective-permute-start | bytes 1572872 | tf_op jit(solution)/shard_map/ppermute | solution.py:43
  87.6 22.7 %collective-permute-start.22 = (bf16[256,1024]{1,0:T(8,128)(2,1)S(1)}, bf16[256,1024]{1,0:T(8,128)(2,1)S(1)}, u32[]{:S(2)}, u32[]{:S(2)}) collective-permute-start(bf16[256,1024]{1,0:T(8,128)(2,1)S(1)} %shard_map.122), channel_id=1, source_target_pairs={{0,124},{1,125},{2,126},{3,127},{4,64},{5,65},{6,66},{7,67},{8,68}... | collective-permute-start | bytes 1572872 | tf_op jit(solution)/shard_map/ppermute | solution.py:43

commit v10 on v5

--- a/solution.py
+++ b/solution.py
@@ -138,15 +138,15 @@
 
 
 def layer_kernel(
-    block, live_ref, got_ref, q_ref, qb_ref, tiles_ref, acc_ref, deg_ref, self_ref, up_ref, nb_ref, ob_ref, tt_ref,
+    block, live_ref, got_a, got_b, q_ref, qb_ref, tiles_ref, acc_ref, deg_ref, self_ref, up_ref, nb_ref, ob_ref, tt_ref,
     msg_ref, g_ref, gpool_ref, pre_ref, last_ref, near1, near2, near3, pooled_ref, gn_ref,
 ):
     rows, width = self_ref.shape
     hidden = nb_ref.shape[0]
     step = 512
-    x = got_ref[...]
+    x = jnp.concatenate([got_a[...], got_b[...]], axis=0)
     keep = x[:, :128].astype(F32) < LIMIT
-    tiles = tiles_ref[:, -block:]
+    tiles = tiles_ref[:, -2 * block :]
     deg = deg_ref[...] + dot(tiles, jnp.where(keep, 1.0, 0.0).astype(BF16))
     inv_deg = 1.0 / (1.0 + deg[:, :1])
     keep = keep[:, :1]
@@ -317,14 +317,14 @@
         0, split, (lists, same, below, *got_near, q, qb, tiles), [SMEM] + [VMEM] * 8
     )
     msg_b, acc, deg = message(
-        split, reach - 1, (*got_far[:-1], q, qb, tiles, acc, deg), [VMEM] * (5 + len(steps) - 1)
+        split, split + 1, (got_far[0], q, qb, tiles, acc, deg), [VMEM] * 6
     )
     gn = pltpu.VMEM((3 * block, hidden), BF16)
     g, gpool, pre, msg_c, *near_back = call(
         lambda *r: layer_kernel(block, *r),
-        [two, ((rows, hidden), BF16), ((rows, width), F32), ((block, hidden), BF16)] + [one] * 3,
-        (live, got_far[-1], q, qb, tiles, acc, deg, self_pre, up, nb, ob, tiles_t, msg_a),
-        [SMEM] + [VMEM] * 12,
+        [two, ((rows, hidden), BF16), ((rows, width), F32), ((2 * block, hidden), BF16)] + [one] * 3,
+        (live, *got_far[1:], q, qb, tiles, acc, deg, self_pre, up, nb, ob, tiles_t, msg_a),
+        [SMEM] + [VMEM] * 13,
         scratch=[pltpu.VMEM((rows, hidden), BF16), gn],
         flops=8 * MICROSECOND,
     )

time: 106 us -> 104 us (0.981)
  waiting for transfers between devices: 44.3 us -> 40.3 us
  starting transfers between devices: 27.7 us -> 30.2 us
    ppermute x5, waiting for transfers between devices: 25.8 us -> 18.4 us  [swap_rows(): return lax.ppermute(x, ('side', 'dom'), pairs)]
    ppermute x3, waiting for transfers between devices: 8.49 us -> 13 us  [straight_back(): return lax.ppermute(x, ('side', 'dom'), pairs)]
    ppermute x12, starting transfers between devices: 10.7 us -> 13.5 us  [along(): return lax.ppermute(x, 'dom', pairs)]
    ppermute x12, waiting for transfers between devices: 9.93 us -> 8.85 us  [along(): return lax.ppermute(x, 'dom', pairs)]
  transfers between devices with their start and end apart: 20 -> 20, of which waited for: 9 -> 7; matrix products, arithmetic and copies ran while one was open for 1% -> 1% of each run, Pallas kernels for 16% -> 16%
where the time goes in v10:
time: 104 us; the launch traced here: 103 us
  waiting for transfers between devices  40.3 us (39%)
  starting transfers between devices  30.2 us (29%)
  Pallas kernels  24.4 us (23%)
  local copies, waits for them, and re-layouts  5.69 us (5%)
  between operations  1.45 us (1%)
  other arithmetic  1.16 us (1%)
    pallas_call x11, Pallas kernels, call(): pl.pallas_call(kernel, out_shape=[jax.ShapeDtypeStruct(s, d) for s, d in...  24.4 us
    ppermute x5, waiting for transfers between devices, swap_rows(): return lax.ppermute(x, ('side', 'dom'), pairs)  18.4 us
    ppermute x12, starting transfers between devices, along(): return lax.ppermute(x, 'dom', pairs)  13.5 us
    ppermute x3, waiting for transfers between devices, straight_back(): return lax.ppermute(x, ('side', 'dom'), pairs)  13 us
    ppermute x3, starting transfers between devices, straight_back(): return lax.ppermute(x, ('side', 'dom'), pairs)  9.34 us
    ppermute x12, waiting for transfers between devices, along(): return lax.ppermute(x, 'dom', pairs)  8.85 us
    ppermute x5, starting transfers between devices, swap_rows(): return lax.ppermute(x, ('side', 'dom'), pairs)  7.31 us
    unnamed x18, local copies, waits for them, and re-layouts  4.25 us
  transfers between devices with their start and end apart: 20, of which 7 were waited for; matrix products, arithmetic and copies ran while one was open for 1% of the time, Pallas kernels for 16%

profile of v10, /device:TPU:7, one launch (start us, length us, event | category | flops | bytes accessed | tf_op | source)
XLA Modules:
  0.0 103.2 jit_solution(14395809350188026197)
XLA Ops:
  1.3 1.2 %broadcast_select_fusion = bf16[256,1024]{1,0:T(8,128)(2,1)S(1)} fusion(pred[256]{0:T(512)(128)(4,1)S(1)} %iota_compare_fusion, bf16[1,256,1024]{2,1,0:T(8,128)(2,1)} %param.10), kind=kLoop, calls=%fused_computation | loop fusion | flops 262144 | bytes 1048832 | tf_op jit(solution)/shard_map/jit(_where)/select_n | solution.py:272
  2.5 1.9 %collective-permute-start.8 = (bf16[256,1024]{1,0:T(8,128)(2,1)S(1)}, bf16[256,1024]{1,0:T(8,128)(2,1)S(1)}, u32[]{:S(2)}, u32[]{:S(2)}) collective-permute-start(bf16[256,1024]{1,0:T(8,128)(2,1)S(1)} %broadcast_select_fusion), channel_id=1, source_target_pairs={{0,68},{1,69},{2,70},{3,71},{4,72},{5,73},{6,74},{7,75},{8,76},{9,... | collective-permute-start | bytes 1572872 | tf_op jit(solution)/shard_map/ppermute | solution.py:43
  5.3 2.2 %collective-permute-start.1 = (s32[1,128]{1,0:T(1,128)S(1)}, s32[1,128]{1,0:T(1,128)S(1)}, u32[]{:S(2)}, u32[]{:S(2)}) collective-permute-start(s32[1,128]{1,0:T(1,128)S(1)} %pad_bitcast_fusion), channel_id=1, source_target_pairs={{0,2},{1,3},{2,0},{3,1},{4,6},{5,7},{6,4},{7,5},{8,10},{9,11},{10,... | collective-permute-start | bytes 1544 | tf_op jit(solution)/shard_map/ppermute | solution.py:49
  7.8 1.4 %collective-permute-done.1.r_2_.r_3_ = s32[1,128]{1,0:T(1,128)S(1)} collective-permute-done((s32[1,128]{1,0:T(1,128)S(1)}, s32[1,128]{1,0:T(1,128)S(1)}, u32[]{:S(2)}, u32[]{:S(2)}) %collective-permute-start.1) | collective-permute-done | bytes 544 | tf_op jit(solution)/shard_map/ppermute | solution.py:49
  9.2 2.1 %collective-permute-done.r_1_.r_2_ = s32[1,128]{1,0:T(1,128)S(1)} collective-permute-done((s32[1,128]{1,0:T(1,128)S(1)}, s32[1,128]{1,0:T(1,128)S(1)}, u32[]{:S(2)}, u32[]{:S(2)}) %collective-permute-start) | collective-permute-done | bytes 544 | tf_op jit(solution)/shard_map/ppermute | solution.py:49
  11.3 3.7 %collective-permute-start.4 = (bf16[256,1024]{1,0:T(8,128)(2,1)S(1)}, bf16[256,1024]{1,0:T(8,128)(2,1)S(1)}, u32[]{:S(2)}, u32[]{:S(2)}) collective-permute-start(bf16[256,1024]{1,0:T(8,128)(2,1)S(1)} %broadcast_select_fusion), channel_id=1, source_target_pairs={{0,72},{1,73},{2,74},{3,75},{4,76},{5,77},{6,78},{7,79},{8,80},{9,... | collective-permute-start | bytes 1572872 | tf_op jit(solution)/shard_map/ppermute | solution.py:43
  15.1 0.8 copy.15.r_1_.r_0_
  15.8 1.6 %copy-done.1 = bf16[1024,1024]{1,0:T(8,128)(2,1)S(1)} copy-done((bf16[1024,1024]{1,0:T(8,128)(2,1)S(1)}, bf16[1024,1024]{1,0:T(8,128)(2,1)}, u32[]{:S(2)}) %copy-start.1) | copy-done | bytes 2097176
  17.4 1.6 %copy-done.3 = s32[1,256,2048]{2,1,0:T(8,128)S(1)} copy-done((s32[1,256,2048]{2,1,0:T(8,128)S(1)}, s32[1,256,2048]{2,1,0:T(8,128)}, u32[]{:S(2)}) %copy-start.3) | copy-done | bytes 2097176
  19.0 1.0 %copy-done.4 = bf16[1,256,1024]{2,1,0:T(8,128)(2,1)S(1)} copy-done((bf16[1,256,1024]{2,1,0:T(8,128)(2,1)S(1)}, bf16[1,256,1024]{2,1,0:T(8,128)(2,1)}, u32[]{:S(2)}) %copy-start.4) | copy-done | bytes 524312
  20.0 1.3 %shard_map.113 = (bf16[256,1024]{1,0:T(8,128)(2,1)S(1)}, bf16[1024,256]{1,0:T(8,128)(2,1)S(1)}, f32[256,1024]{1,0:T(8,128)S(1)}) custom-call(s32[1]{0:T(128)} %bitcast.2.r_0_, s32[8,2]{1,0:T(8,128)S(1)} %copy.15.r_1_.r_0_, s32[256,2048]{1,0:T(8,128)S(1)} %bitcast.20, bf16[256,1024]{1,0:T(8,128)(2,1)S(1)} %bitcast.21, bf16[1024,1024]{1,0:T(8,128)(2,1)S(1)} %copy-done.1), custom_call_target="tpu_custom_call" | custom-call | flops 536870912 | bytes 1048576 | tf_op jit(solution)/shard_map/pallas_call | solution.py:25
  22.4 1.6 %collective-permute-start.10 = (bf16[128,1024]{1,0:T(8,128)(2,1)S(1)}, bf16[128,1024]{1,0:T(8,128)(2,1)S(1)}, u32[]{:S(2)}, u32[]{:S(2)}) collective-permute-start(bf16[128,1024]{1,0:T(8,128)(2,1)S(1)} %get-tuple-element.45), channel_id=1, source_target_pairs={{0,2},{1,3},{2,0},{3,1},{4,6},{5,7},{6,4},{7,5},{8,10},{9,11},{10,... | collective-permute-start | bytes 786440 | tf_op jit(solution)/shard_map/ppermute | solution.py:49
  24.0 10.2 %collective-permute-done.4.r_5_ = bf16[256,1024]{1,0:T(8,128)(2,1)S(1)} collective-permute-done((bf16[256,1024]{1,0:T(8,128)(2,1)S(1)}, bf16[256,1024]{1,0:T(8,128)(2,1)S(1)}, u32[]{:S(2)}, u32[]{:S(2)}) %collective-permute-start.4) | collective-permute-done | bytes 524320 | tf_op jit(solution)/shard_map/ppermute | solution.py:43
  34.8 1.2 %collective-permute-start.5 = (bf16[128,1024]{1,0:T(8,128)(2,1)S(1)}, bf16[128,1024]{1,0:T(8,128)(2,1)S(1)}, u32[]{:S(2)}, u32[]{:S(2)}) collective-permute-start(bf16[128,1024]{1,0:T(8,128)(2,1)S(1)} %get-tuple-element.40), channel_id=1, source_target_pairs={{0,2},{1,3},{2,0},{3,1},{4,6},{5,7},{6,4},{7,5},{8,10},{9,11},{10,... | collective-permute-start | bytes 786440 | tf_op jit(solution)/shard_map/ppermute | solution.py:49
  36.0 2.7 %collective-permute-start.7 = (bf16[128,1024]{1,0:T(8,128)(2,1)S(1)}, bf16[128,1024]{1,0:T(8,128)(2,1)S(1)}, u32[]{:S(2)}, u32[]{:S(2)}) collective-permute-start(bf16[128,1024]{1,0:T(8,128)(2,1)S(1)} %get-tuple-element.43), channel_id=1, source_target_pairs={{0,1},{1,2},{2,3},{3,0},{4,5},{5,6},{6,7},{7,4},{8,9},{9,10},{10,1... | collective-permute-start | bytes 786440 | tf_op jit(solution)/shard_map/ppermute | solution.py:49
  38.7 4.6 %shard_map.116 = (bf16[640,2048]{1,0:T(8,128)(2,1)S(1)}, f32[256,2048]{1,0:T(8,128)S(1)}, f32[256,128]{1,0:T(8,128)S(1)}) custom-call(s32[8,2]{1,0:T(8,128)S(1)} %copy.15.r_1_.r_0_, bf16[256,1024]{1,0:T(8,128)(2,1)S(1)} %collective-permute-done.3.r_4_.r_1_, bf16[256,1024]{1,0:T(8,128)(2,1)S(1)} %collective-permute-done.8.r_4_.r_2_, ...), custom_call_target="tpu_custom_call" | custom-call | flops 3355443200 | bytes 1048576 | tf_op jit(solution)/shard_map/pallas_call | solution.py:25
  43.4 4.0 %collective-permute-done.7.r_0_ = bf16[128,1024]{1,0:T(8,128)(2,1)S(1)} collective-permute-done((bf16[128,1024]{1,0:T(8,128)(2,1)S(1)}, bf16[128,1024]{1,0:T(8,128)(2,1)S(1)}, u32[]{:S(2)}, u32[]{:S(2)}) %collective-permute-start.7) | collective-permute-done | bytes 262176 | tf_op jit(solution)/shard_map/ppermute | solution.py:49
  47.3 1.6 %shard_map.117 = (bf16[128,2048]{1,0:T(8,128)(2,1)S(1)}, f32[256,2048]{1,0:T(8,128)S(1)}, f32[256,128]{1,0:T(8,128)S(1)}) custom-call(bf16[128,1024]{1,0:T(8,128)(2,1)S(1)} %collective-permute-done.7.r_0_, bf16[1024,2048]{1,0:T(8,128)(2,1)S(1)} %copy-done, f32[1,2048]{1,0:T(1,128)S(1)} %bitcast.23, bf16[256,1024]{1,0:T(8,128)(2,1)S(1)} %get-tuple-element.42.r_5_.r_8_.r_3_, ...), custom_call_target="tpu_custom_call" | custom-call | flops 671088640 | bytes 1048576 | tf_op jit(solution)/shard_map/pallas_call | solution.py:25
  48.9 1.3 %collective-permute-done.6.r_2_ = bf16[128,1024]{1,0:T(8,128)(2,1)S(1)} collective-permute-done((bf16[128,1024]{1,0:T(8,128)(2,1)S(1)}, bf16[128,1024]{1,0:T(8,128)(2,1)S(1)}, u32[]{:S(2)}, u32[]{:S(2)}) %collective-permute-start.6) | collective-permute-done | bytes 262176 | tf_op jit(solution)/shard_map/ppermute | solution.py:49
  50.3 7.0 %shard_map.118 = (bf16[256,1024]{1,0:T(8,128)(2,1)S(1)}, bf16[256,2048]{1,0:T(8,128)(2,1)S(1)}, f32[256,1024]{1,0:T(8,128)S(1)}, bf16[256,2048]{1,0:T(8,128)(2,1...) custom-call(s32[1]{0:T(128)} %bitcast.16.r_0_, ...), custom_call_target="tpu_custom_call" | custom-call | flops 8000000000 | bytes 1048576 | tf_op jit(solution)/shard_map/pallas_call | solution.py:25
  57.3 2.8 %collective-permute-start.17 = (bf16[128,1024]{1,0:T(8,128)(2,1)S(1)}, bf16[128,1024]{1,0:T(8,128)(2,1)S(1)}, u32[]{:S(2)}, u32[]{:S(2)}) collective-permute-start(bf16[128,1024]{1,0:T(8,128)(2,1)S(1)} %get-tuple-element.66), channel_id=1, source_target_pairs={{0,2},{1,3},{2,0},{3,1},{4,6},{5,7},{6,4},{7,5},{8,10},{9,11},{10,... | collective-permute-start | bytes 786440 | tf_op jit(solution)/shard_map/ppermute | solution.py:49
  60.1 2.5 %collective-permute-start.18 = (bf16[128,1024]{1,0:T(8,128)(2,1)S(1)}, bf16[128,1024]{1,0:T(8,128)(2,1)S(1)}, u32[]{:S(2)}, u32[]{:S(2)}) collective-permute-start(bf16[128,1024]{1,0:T(8,128)(2,1)S(1)} %get-tuple-element.67), channel_id=1, source_target_pairs={{0,1},{1,2},{2,3},{3,0},{4,5},{5,6},{6,7},{7,4},{8,9},{9,10},{10,1... | collective-permute-start | bytes 786440 | tf_op jit(solution)/shard_map/ppermute | solution.py:49
  62.6 2.8 %shard_map.119 = (bf16[128,1152]{1,0:T(8,128)(2,1)S(1)}, bf16[128,1152]{1,0:T(8,128)(2,1)S(1)}, bf16[128,1152]{1,0:T(8,128)(2,1)S(1)}) custom-call(s32[1]{0:T(128)} %bitcast.2.r_0_, s32[8,2]{1,0:T(8,128)S(1)} %copy.15.r_1_.r_0_, bf16[1024,256]{1,0:T(8,128)(2,1)S(1)} %get-tuple-element.35.r_12_.r_2_, bf16[256,2048]{1,0:T(8,128)(2,1)S(1)} %get-tuple-element.53.r_3_, ...), custom_call_target="tpu_custom_call" | custom-call | flops 2000000000 | bytes 1048576 | tf_op jit(solution)/shard_map/pallas_call | solution.py:25
  65.4 2.2 %collective-permute-start.13 = (bf16[128,1152]{1,0:T(8,128)(2,1)S(1)}, bf16[128,1152]{1,0:T(8,128)(2,1)S(1)}, u32[]{:S(2)}, u32[]{:S(2)}) collective-permute-start(bf16[128,1152]{1,0:T(8,128)(2,1)S(1)} %get-tuple-element.62), channel_id=1, source_target_pairs={{66,0},{67,1},{72,2},{73,3},{70,4},{71,5},{76,6},{77,7},{74,8},{75... | collective-permute-start | bytes 884744 | tf_op jit(solution)/shard_map/ppermute | solution.py:59
  67.6 1.4 %collective-permute-start.12 = (bf16[128,1152]{1,0:T(8,128)(2,1)S(1)}, bf16[128,1152]{1,0:T(8,128)(2,1)S(1)}, u32[]{:S(2)}, u32[]{:S(2)}) collective-permute-start(bf16[128,1152]{1,0:T(8,128)(2,1)S(1)} %get-tuple-element.59.r_9_), channel_id=1, source_target_pairs={{65,0},{66,1},{67,2},{72,3},{69,4},{70,5},{71,6},{76,7},{73,8},{74... | collective-permute-start | bytes 884744 | tf_op jit(solution)/shard_map/ppermute | solution.py:59
  69.0 3.6 %shard_map.120 = (bf16[256,1024]{1,0:T(8,128)(2,1)S(1)}, bf16[128,1024]{1,0:T(8,128)(2,1)S(1)}, f32[256,1024]{1,0:T(8,128)S(1)}, bf16[256,1024]{1,0:T(8,128)(2,1)}) custom-call(s32[8,2]{1,0:T(8,128)S(1)} %copy.15.r_1_.r_0_, s32[1]{0:T(128)} %bitcast.17.r_1_, bf16[1024,256]{1,0:T(8,128)(2,1)S(1)} %get-tuple-element.35.r_12_.r_2_, ...), custom_call_target="tpu_custom_call" | custom-call | flops 3000000000 | bytes 1048576 | tf_op jit(solution)/shard_map/pallas_call | solution.py:25
  72.6 5.7 %collective-permute-start.14 = (bf16[128,1152]{1,0:T(8,128)(2,1)S(1)}, bf16[128,1152]{1,0:T(8,128)(2,1)S(1)}, u32[]{:S(2)}, u32[]{:S(2)}) collective-permute-start(bf16[128,1152]{1,0:T(8,128)(2,1)S(1)} %get-tuple-element.63), channel_id=1, source_target_pairs={{67,0},{72,1},{73,2},{74,3},{71,4},{76,5},{77,6},{78,7},{75,8},{80... | collective-permute-start | bytes 884744 | tf_op jit(solution)/shard_map/ppermute | solution.py:59
  78.3 1.2 %collective-permute-start.15 = (bf16[256,1024]{1,0:T(8,128)(2,1)S(1)}, bf16[256,1024]{1,0:T(8,128)(2,1)S(1)}, u32[]{:S(2)}, u32[]{:S(2)}) collective-permute-start(bf16[256,1024]{1,0:T(8,128)(2,1)S(1)} %get-tuple-element.64), channel_id=1, source_target_pairs={{0,64},{1,65},{2,66},{3,67},{4,68},{5,69},{6,70},{7,71},{8,72},{9,... | collective-permute-start | bytes 1572872 | tf_op jit(solution)/shard_map/ppermute | solution.py:43
  79.6 0.9 shard_map.122
  80.6 13.0 %collective-permute-done.14.c3 = bf16[128,1152]{1,0:T(8,128)(2,1)S(1)} collective-permute-done((bf16[128,1152]{1,0:T(8,128)(2,1)S(1)}, bf16[128,1152]{1,0:T(8,128)(2,1)S(1)}, u32[]{:S(2)}, u32[]{:S(2)}) %collective-permute-start.14) | collective-permute-done | bytes 294944 | tf_op jit(solution)/shard_map/ppermute | solution.py:59
  94.0 8.2 %collective-permute-done.19.below_ref = bf16[256,1024]{1,0:T(8,128)(2,1)S(1)} collective-permute-done((bf16[256,1024]{1,0:T(8,128)(2,1)S(1)}, bf16[256,1024]{1,0:T(8,128)(2,1)S(1)}, u32[]{:S(2)}, u32[]{:S(2)}) %collective-permute-start.19) | collective-permute-done | bytes 524320 | tf_op jit(solution)/shard_map/ppermute | solution.py:43
  102.2 1.0 shard_map.123
  (42 shorter events, 3.4 us)
Async XLA Ops:
  2.5 18.9 %collective-permute-start.8 = (bf16[256,1024]{1,0:T(8,128)(2,1)S(1)}, bf16[256,1024]{1,0:T(8,128)(2,1)S(1)}, u32[]{:S(2)}, u32[]{:S(2)}) collective-permute-start(bf16[256,1024]{1,0:T(8,128)(2,1)S(1)} %broadcast_select_fusion), channel_id=1, source_target_pairs={{0,68},{1,69},{2,70},{3,71},{4,72},{5,73},{6,74},{7,75},{8,76},{9,... | collective-permute-start | bytes 1572872 | tf_op jit(solution)/shard_map/ppermute | solution.py:43
  5.1 2.7 %collective-permute-start.2 = (s32[1,128]{1,0:T(1,128)S(1)}, s32[1,128]{1,0:T(1,128)S(1)}, u32[]{:S(2)}, u32[]{:S(2)}) collective-permute-start(s32[1,128]{1,0:T(1,128)S(1)} %pad_bitcast_fusion), channel_id=1, source_target_pairs={{0,1},{1,2},{2,3},{3,0},{4,5},{5,6},{6,7},{7,4},{8,9},{9,10},{10,1... | collective-permute-start | bytes 1544 | tf_op jit(solution)/shard_map/ppermute | solution.py:49
  5.3 3.9 %collective-permute-start.1 = (s32[1,128]{1,0:T(1,128)S(1)}, s32[1,128]{1,0:T(1,128)S(1)}, u32[]{:S(2)}, u32[]{:S(2)}) collective-permute-start(s32[1,128]{1,0:T(1,128)S(1)} %pad_bitcast_fusion), channel_id=1, source_target_pairs={{0,2},{1,3},{2,0},{3,1},{4,6},{5,7},{6,4},{7,5},{8,10},{9,11},{10,... | collective-permute-start | bytes 1544 | tf_op jit(solution)/shard_map/ppermute | solution.py:49
  7.4 3.9 %collective-permute-start = (s32[1,128]{1,0:T(1,128)S(1)}, s32[1,128]{1,0:T(1,128)S(1)}, u32[]{:S(2)}, u32[]{:S(2)}) collective-permute-start(s32[1,128]{1,0:T(1,128)S(1)} %pad_bitcast_fusion), channel_id=1, source_target_pairs={{0,3},{1,0},{2,1},{3,2},{4,7},{5,4},{6,5},{7,6},{8,11},{9,8},{10,9... | collective-permute-start | bytes 1544 | tf_op jit(solution)/shard_map/ppermute | solution.py:49
  7.4 16.5 %collective-permute-start.3 = (bf16[256,1024]{1,0:T(8,128)(2,1)S(1)}, bf16[256,1024]{1,0:T(8,128)(2,1)S(1)}, u32[]{:S(2)}, u32[]{:S(2)}) collective-permute-start(bf16[256,1024]{1,0:T(8,128)(2,1)S(1)} %broadcast_select_fusion), channel_id=1, source_target_pairs={{0,64},{1,65},{2,66},{3,67},{4,68},{5,69},{6,70},{7,71},{8,72},{9,... | collective-permute-start | bytes 1572872 | tf_op jit(solution)/shard_map/ppermute | solution.py:43
  11.3 22.8 %collective-permute-start.4 = (bf16[256,1024]{1,0:T(8,128)(2,1)S(1)}, bf16[256,1024]{1,0:T(8,128)(2,1)S(1)}, u32[]{:S(2)}, u32[]{:S(2)}) collective-permute-start(bf16[256,1024]{1,0:T(8,128)(2,1)S(1)} %broadcast_select_fusion), channel_id=1, source_target_pairs={{0,72},{1,73},{2,74},{3,75},{4,76},{5,77},{6,78},{7,79},{8,80},{9,... | collective-permute-start | bytes 1572872 | tf_op jit(solution)/shard_map/ppermute | solution.py:43
  15.8 1.6 %copy-start.1 = (bf16[1024,1024]{1,0:T(8,128)(2,1)S(1)}, bf16[1024,1024]{1,0:T(8,128)(2,1)}, u32[]{:S(2)}) copy-start(bf16[1024,1024]{1,0:T(8,128)(2,1)} %r_7_.1) | copy-start | bytes 6291460
  17.4 1.6 %copy-start.3 = (s32[1,256,2048]{2,1,0:T(8,128)S(1)}, s32[1,256,2048]{2,1,0:T(8,128)}, u32[]{:S(2)}) copy-start(s32[1,256,2048]{2,1,0:T(8,128)} %param.13) | copy-start | bytes 6291460
  19.0 1.0 %copy-start.4 = (bf16[1,256,1024]{2,1,0:T(8,128)(2,1)S(1)}, bf16[1,256,1024]{2,1,0:T(8,128)(2,1)}, u32[]{:S(2)}) copy-start(bf16[1,256,1024]{2,1,0:T(8,128)(2,1)} %param.10) | copy-start | bytes 1572868
  20.0 18.7 %copy-start = (bf16[1024,2048]{1,0:T(8,128)(2,1)S(1)}, bf16[1024,2048]{1,0:T(8,128)(2,1)}, u32[]{:S(2)}) copy-start(bf16[1024,2048]{1,0:T(8,128)(2,1)} %r_5_.1) | copy-start | bytes 12582916
  21.4 17.4 %copy-start.5 = (f32[2048]{0:T(1024)S(1)}, f32[2048]{0:T(1024)}, u32[]{:S(2)}) copy-start(f32[2048]{0:T(1024)} %param.16) | copy-start | bytes 24580
  22.0 14.0 %collective-permute-start.9 = (bf16[128,1024]{1,0:T(8,128)(2,1)S(1)}, bf16[128,1024]{1,0:T(8,128)(2,1)S(1)}, u32[]{:S(2)}, u32[]{:S(2)}) collective-permute-start(bf16[128,1024]{1,0:T(8,128)(2,1)S(1)} %get-tuple-element.44), channel_id=1, source_target_pairs={{0,1},{1,2},{2,3},{3,0},{4,5},{5,6},{6,7},{7,4},{8,9},{9,10},{10,1... | collective-permute-start | bytes 786440 | tf_op jit(solution)/shard_map/ppermute | solution.py:49
  22.4 16.3 %collective-permute-start.10 = (bf16[128,1024]{1,0:T(8,128)(2,1)S(1)}, bf16[128,1024]{1,0:T(8,128)(2,1)S(1)}, u32[]{:S(2)}, u32[]{:S(2)}) collective-permute-start(bf16[128,1024]{1,0:T(8,128)(2,1)S(1)} %get-tuple-element.45), channel_id=1, source_target_pairs={{0,2},{1,3},{2,0},{3,1},{4,6},{5,7},{6,4},{7,5},{8,10},{9,11},{10,... | collective-permute-start | bytes 786440 | tf_op jit(solution)/shard_map/ppermute | solution.py:49
  23.9 14.8 %collective-permute-start.11 = (bf16[128,1024]{1,0:T(8,128)(2,1)S(1)}, bf16[128,1024]{1,0:T(8,128)(2,1)S(1)}, u32[]{:S(2)}, u32[]{:S(2)}) collective-permute-start(bf16[128,1024]{1,0:T(8,128)(2,1)S(1)} %get-tuple-element.46), channel_id=1, source_target_pairs={{0,3},{1,0},{2,1},{3,2},{4,7},{5,4},{6,5},{7,6},{8,11},{9,8},{10,9... | collective-permute-start | bytes 786440 | tf_op jit(solution)/shard_map/ppermute | solution.py:49
  34.8 14.1 %collective-permute-start.5 = (bf16[128,1024]{1,0:T(8,128)(2,1)S(1)}, bf16[128,1024]{1,0:T(8,128)(2,1)S(1)}, u32[]{:S(2)}, u32[]{:S(2)}) collective-permute-start(bf16[128,1024]{1,0:T(8,128)(2,1)S(1)} %get-tuple-element.40), channel_id=1, source_target_pairs={{0,2},{1,3},{2,0},{3,1},{4,6},{5,7},{6,4},{7,5},{8,10},{9,11},{10,... | collective-permute-start | bytes 786440 | tf_op jit(solution)/shard_map/ppermute | solution.py:49
  36.0 14.2 %collective-permute-start.6 = (bf16[128,1024]{1,0:T(8,128)(2,1)S(1)}, bf16[128,1024]{1,0:T(8,128)(2,1)S(1)}, u32[]{:S(2)}, u32[]{:S(2)}) collective-permute-start(bf16[128,1024]{1,0:T(8,128)(2,1)S(1)} %get-tuple-element.41), channel_id=1, source_target_pairs={{0,3},{1,0},{2,1},{3,2},{4,7},{5,4},{6,5},{7,6},{8,11},{9,8},{10,9... | collective-permute-start | bytes 786440 | tf_op jit(solution)/shard_map/ppermute | solution.py:49
  36.0 11.3 %collective-permute-start.7 = (bf16[128,1024]{1,0:T(8,128)(2,1)S(1)}, bf16[128,1024]{1,0:T(8,128)(2,1)S(1)}, u32[]{:S(2)}, u32[]{:S(2)}) collective-permute-start(bf16[128,1024]{1,0:T(8,128)(2,1)S(1)} %get-tuple-element.43), channel_id=1, source_target_pairs={{0,1},{1,2},{2,3},{3,0},{4,5},{5,6},{6,7},{7,4},{8,9},{9,10},{10,1... | collective-permute-start | bytes 786440 | tf_op jit(solution)/shard_map/ppermute | solution.py:49
  47.3 2.9 %copy-start.6 = (bf16[2048,1024]{1,0:T(8,128)(2,1)S(1)}, bf16[2048,1024]{1,0:T(8,128)(2,1)}, u32[]{:S(2)}) copy-start(bf16[2048,1024]{1,0:T(8,128)(2,1)} %r_10_.1) | copy-start | bytes 12582916
  47.3 2.9 %copy-start.7 = (bf16[1,256,1024]{2,1,0:T(8,128)(2,1)S(1)}, bf16[1,256,1024]{2,1,0:T(8,128)(2,1)}, u32[]{:S(2)}) copy-start(bf16[1,256,1024]{2,1,0:T(8,128)(2,1)} %param.14) | copy-start | bytes 1572868
  47.3 2.9 %copy-start.8 = (f32[1024]{0:T(1024)S(1)}, f32[1024]{0:T(1024)}, u32[]{:S(2)}) copy-start(f32[1024]{0:T(1024)} %param.19) | copy-start | bytes 12292
  57.3 15.3 %collective-permute-start.17 = (bf16[128,1024]{1,0:T(8,128)(2,1)S(1)}, bf16[128,1024]{1,0:T(8,128)(2,1)S(1)}, u32[]{:S(2)}, u32[]{:S(2)}) collective-permute-start(bf16[128,1024]{1,0:T(8,128)(2,1)S(1)} %get-tuple-element.66), channel_id=1, source_target_pairs={{0,2},{1,3},{2,0},{3,1},{4,6},{5,7},{6,4},{7,5},{8,10},{9,11},{10,... | collective-permute-start | bytes 786440 | tf_op jit(solution)/shard_map/ppermute | solution.py:49
  60.1 18.2 %collective-permute-start.18 = (bf16[128,1024]{1,0:T(8,128)(2,1)S(1)}, bf16[128,1024]{1,0:T(8,128)(2,1)S(1)}, u32[]{:S(2)}, u32[]{:S(2)}) collective-permute-start(bf16[128,1024]{1,0:T(8,128)(2,1)S(1)} %get-tuple-element.67), channel_id=1, source_target_pairs={{0,1},{1,2},{2,3},{3,0},{4,5},{5,6},{6,7},{7,4},{8,9},{9,10},{10,1... | collective-permute-start | bytes 786440 | tf_op jit(solution)/shard_map/ppermute | solution.py:49
  62.6 17.0 %collective-permute-start.16 = (bf16[128,1024]{1,0:T(8,128)(2,1)S(1)}, bf16[128,1024]{1,0:T(8,128)(2,1)S(1)}, u32[]{:S(2)}, u32[]{:S(2)}) collective-permute-start(bf16[128,1024]{1,0:T(8,128)(2,1)S(1)} %get-tuple-element.58.r_7_), channel_id=1, source_target_pairs={{0,3},{1,0},{2,1},{3,2},{4,7},{5,4},{6,5},{7,6},{8,11},{9,8},{10,9... | collective-permute-start | bytes 786440 | tf_op jit(solution)/shard_map/ppermute | solution.py:49
  62.6 6.4 %copy-start.2 = (bf16[1024,1024]{1,0:T(8,128)(2,1)S(1)}, bf16[1024,1024]{1,0:T(8,128)(2,1)}, u32[]{:S(2)}) copy-start(bf16[1024,1024]{1,0:T(8,128)(2,1)} %r_7_.1) | copy-start | bytes 6291460
  65.4 15.2 %collective-permute-start.13 = (bf16[128,1152]{1,0:T(8,128)(2,1)S(1)}, bf16[128,1152]{1,0:T(8,128)(2,1)S(1)}, u32[]{:S(2)}, u32[]{:S(2)}) collective-permute-start(bf16[128,1152]{1,0:T(8,128)(2,1)S(1)} %get-tuple-element.62), channel_id=1, source_target_pairs={{66,0},{67,1},{72,2},{73,3},{70,4},{71,5},{76,6},{77,7},{74,8},{75... | collective-permute-start | bytes 884744 | tf_op jit(solution)/shard_map/ppermute | solution.py:59
  67.6 26.0 %collective-permute-start.12 = (bf16[128,1152]{1,0:T(8,128)(2,1)S(1)}, bf16[128,1152]{1,0:T(8,128)(2,1)S(1)}, u32[]{:S(2)}, u32[]{:S(2)}) collective-permute-start(bf16[128,1152]{1,0:T(8,128)(2,1)S(1)} %get-tuple-element.59.r_9_), channel_id=1, source_target_pairs={{65,0},{66,1},{67,2},{72,3},{69,4},{70,5},{71,6},{76,7},{73,8},{74... | collective-permute-start | bytes 884744 | tf_op jit(solution)/shard_map/ppermute | solution.py:59
  72.6 21.0 %collective-permute-start.14 = (bf16[128,1152]{1,0:T(8,128)(2,1)S(1)}, bf16[128,1152]{1,0:T(8,128)(2,1)S(1)}, u32[]{:S(2)}, u32[]{:S(2)}) collective-permute-start(bf16[128,1152]{1,0:T(8,128)(2,1)S(1)} %get-tuple-element.63), channel_id=1, source_target_pairs={{67,0},{72,1},{73,2},{74,3},{71,4},{76,5},{77,6},{78,7},{75,8},{80... | collective-permute-start | bytes 884744 | tf_op jit(solution)/shard_map/ppermute | solution.py:59
  78.3 15.6 %collective-permute-start.15 = (bf16[256,1024]{1,0:T(8,128)(2,1)S(1)}, bf16[256,1024]{1,0:T(8,128)(2,1)S(1)}, u32[]{:S(2)}, u32[]{:S(2)}) collective-permute-start(bf16[256,1024]{1,0:T(8,128)(2,1)S(1)} %get-tuple-element.64), channel_id=1, source_target_pairs={{0,64},{1,65},{2,66},{3,67},{4,68},{5,69},{6,70},{7,71},{8,72},{9,... | collective-permute-start | bytes 1572872 | tf_op jit(solution)/shard_map/ppermute | solution.py:43
  80.5 21.7 %collective-permute-start.19 = (bf16[256,1024]{1,0:T(8,128)(2,1)S(1)}, bf16[256,1024]{1,0:T(8,128)(2,1)S(1)}, u32[]{:S(2)}, u32[]{:S(2)}) collective-permute-start(bf16[256,1024]{1,0:T(8,128)(2,1)S(1)} %shard_map.122), channel_id=1, source_target_pairs={{0,124},{1,125},{2,126},{3,127},{4,64},{5,65},{6,66},{7,67},{8,68}... | collective-permute-start | bytes 1572872 | tf_op jit(solution)/shard_map/ppermute | solution.py:43

commit v11 on v10

--- a/solution.py
+++ b/solution.py
@@ -138,15 +138,15 @@
 
 
 def layer_kernel(
-    block, live_ref, got_a, got_b, q_ref, qb_ref, tiles_ref, acc_ref, deg_ref, self_ref, up_ref, nb_ref, ob_ref, tt_ref,
+    block, live_ref, got_a, got_b, got_c, q_ref, qb_ref, tiles_ref, acc_ref, deg_ref, self_ref, up_ref, nb_ref, ob_ref, tt_ref,
     msg_ref, g_ref, gpool_ref, pre_ref, last_ref, near1, near2, near3, pooled_ref, gn_ref,
 ):
     rows, width = self_ref.shape
     hidden = nb_ref.shape[0]
     step = 512
-    x = jnp.concatenate([got_a[...], got_b[...]], axis=0)
+    x = jnp.concatenate([got_a[...], got_b[...], got_c[...]], axis=0)
     keep = x[:, :128].astype(F32) < LIMIT
-    tiles = tiles_ref[:, -2 * block :]
+    tiles = tiles_ref[:, -3 * block :]
     deg = deg_ref[...] + dot(tiles, jnp.where(keep, 1.0, 0.0).astype(BF16))
     inv_deg = 1.0 / (1.0 + deg[:, :1])
     keep = keep[:, :1]
@@ -194,7 +194,7 @@
         store(cols, dot(gn, q_ref[cols, :], 1, 1))
 
 
-def back_far_kernel(block, place_ref, lists_ref, tt_ref, gpool_ref, early_ref, last_ref, q_ref, _, *refs):
+def back_far_kernel(block, place_ref, lists_ref, tt_ref, gpool_ref, msg_ref, q_ref, _, *refs):
     outs, gn_ref = refs[:-1], refs[-1]
     width = q_ref.shape[0]
 
@@ -205,14 +205,10 @@
     for d, out in enumerate(outs, 1):
         which = lists_ref[far(place_ref[0], d), 1].astype(F32)
         out[:, width:] = jnp.full((block, 128), which, F32).astype(BF16)
-    messages = [early_ref[...], last_ref[...]]
-    back_dot((1 + LINE) * block, tt_ref, gpool_ref, messages, q_ref, gn_ref, store)
-
-
-def back_own_kernel(
-    block, lists_ref, live_ref, tt_ref, gpool_ref, msg_ref, q_ref, g_ref, sw_ref, pre_ref, _,
-    same_ref, below_ref, gself_ref, emb_ref, gn_ref,
-):
+    back_dot((1 + LINE) * block, tt_ref, gpool_ref, [msg_ref[...]], q_ref, gn_ref, store)
+
+
+def back_own_kernel(block, lists_ref, tt_ref, gpool_ref, msg_ref, q_ref, _, same_ref, below_ref, gn_ref):
     same_ref[...] = jnp.zeros_like(same_ref)
     at = at_block(lists_ref[0, 1], block)
 
@@ -221,6 +217,9 @@
         below_ref[:, cols] = part[block:].astype(BF16)
 
     back_dot(0, tt_ref, gpool_ref, [msg_ref[: 2 * block, :]], q_ref, gn_ref, store)
+
+
+def own_rows_kernel(live_ref, g_ref, sw_ref, pre_ref, _, gself_ref, emb_ref):
     rows, width = pre_ref.shape
     step = 512
     for n in range(width // step):
@@ -316,15 +315,12 @@
     msg_a, acc, deg = message(
         0, split, (lists, same, below, *got_near, q, qb, tiles), [SMEM] + [VMEM] * 8
     )
-    msg_b, acc, deg = message(
-        split, split + 1, (got_far[0], q, qb, tiles, acc, deg), [VMEM] * 6
-    )
     gn = pltpu.VMEM((3 * block, hidden), BF16)
-    g, gpool, pre, msg_c, *near_back = call(
+    g, gpool, pre, msg_b, *near_back = call(
         lambda *r: layer_kernel(block, *r),
-        [two, ((rows, hidden), BF16), ((rows, width), F32), ((2 * block, hidden), BF16)] + [one] * 3,
-        (live, *got_far[1:], q, qb, tiles, acc, deg, self_pre, up, nb, ob, tiles_t, msg_a),
-        [SMEM] + [VMEM] * 13,
+        [two, ((rows, hidden), BF16), ((rows, width), F32), ((3 * block, hidden), BF16)] + [one] * 3,
+        (live, *got_far, q, qb, tiles, acc, deg, self_pre, up, nb, ob, tiles_t, msg_a),
+        [SMEM] + [VMEM] * 14,
         scratch=[pltpu.VMEM((rows, hidden), BF16), gn],
         flops=8 * MICROSECOND,
     )
@@ -332,19 +328,19 @@
     far_back = call(
         lambda *r: back_far_kernel(block, *r),
         [((block, width + 128), BF16)] * 3,
-        (place, lists, tiles_t, gpool, msg_b, msg_c, q, near_back[0]),
-        [SMEM] * 2 + [VMEM] * 5 + [HELD],
+        (place, lists, tiles_t, gpool, msg_b, q, near_back[0]),
+        [SMEM] * 2 + [VMEM] * 4 + [HELD],
         scratch=[gn],
         flops=2 * MICROSECOND,
     )
     back_far = [straight_back(b, d) for d, b in zip(steps, far_back)]
-    own_same, own_below, gself, emb = call(
+    own_same, own_below = call(
         lambda *r: back_own_kernel(block, *r),
-        [two, one, ((rows, width), F32), two],
-        (lists, live, tiles_t, gpool, msg_a, q, g, sw, pre, far_back[0]),
-        [SMEM] * 2 + [VMEM] * 7 + [HELD],
+        [two, one],
+        (lists, tiles_t, gpool, msg_a, q, far_back[0]),
+        [SMEM] + [VMEM] * 4 + [HELD],
         scratch=[pltpu.VMEM((2 * block, hidden), BF16)],
-        flops=3 * MICROSECOND,
+        flops=2 * MICROSECOND,
     )
     g_same = swap_rows(own_same, 0)
     total = pltpu.VMEM((rows, width), F32)
@@ -357,6 +353,13 @@
         flops=20 * MICROSECOND,
     )
     g_below = swap_rows(sum_below, -LINE)
+    gself, emb = call(
+        own_rows_kernel,
+        [((rows, width), F32), two],
+        (live, g, sw, pre, sum_below),
+        [SMEM] + [VMEM] * 3 + [HELD],
+        flops=2 * MICROSECOND,
+    )
     (placed,) = call(
         place_kernel,
         [((rows, width), F32)],

time: 104 us -> 105 us (level)
  waiting for transfers between devices: 40.3 us -> 44.5 us
  starting transfers between devices: 30.2 us -> 26.7 us
    ppermute x12, starting transfers between devices: 13.5 us -> 9.02 us  [along(): return lax.ppermute(x, 'dom', pairs)]
    ppermute x12, waiting for transfers between devices: 8.85 us -> 12.1 us  [along(): return lax.ppermute(x, 'dom', pairs)]
    ppermute x5, waiting for transfers between devices: 18.4 us -> 21.1 us  [swap_rows(): return lax.ppermute(x, ('side', 'dom'), pairs)]
    ppermute x3, waiting for transfers between devices: 13 us -> 11.4 us  [straight_back(): return lax.ppermute(x, ('side', 'dom'), pairs)]
  transfers between devices with their start and end apart: 20 -> 20, of which waited for: 7 -> 8; matrix products, arithmetic and copies ran while one was open for 1% -> 1% of each run, Pallas kernels for 16% -> 15%
where the time goes in v11:
time: 105 us; the launch traced here: 104 us
  waiting for transfers between devices  44.5 us (42%)
  starting transfers between devices  26.7 us (25%)
  Pallas kernels  23.7 us (23%)
  local copies, waits for them, and re-layouts  6.26 us (6%)
  between operations  1.45 us (1%)
  other arithmetic  1.16 us (1%)
    pallas_call x11, Pallas kernels, call(): pl.pallas_call(kernel, out_shape=[jax.ShapeDtypeStruct(s, d) for s, d in...  23.7 us
    ppermute x5, waiting for transfers between devices, swap_rows(): return lax.ppermute(x, ('side', 'dom'), pairs)  21.1 us
    ppermute x12, waiting for transfers between devices, along(): return lax.ppermute(x, 'dom', pairs)  12.1 us
    ppermute x3, waiting for transfers between devices, straight_back(): return lax.ppermute(x, ('side', 'dom'), pairs)  11.4 us
    ppermute x3, starting transfers between devices, straight_back(): return lax.ppermute(x, ('side', 'dom'), pairs)  9.84 us
    ppermute x12, starting transfers between devices, along(): return lax.ppermute(x, 'dom', pairs)  9.02 us
    ppermute x5, starting transfers between devices, swap_rows(): return lax.ppermute(x, ('side', 'dom'), pairs)  7.8 us
    unnamed x18, local copies, waits for them, and re-layouts  4.82 us
  transfers between devices with their start and end apart: 20, of which 8 were waited for; matrix products, arithmetic and copies ran while one was open for 1% of the time, Pallas kernels for 15%

profile of v11, /device:TPU:7, one launch (start us, length us, event | category | flops | bytes accessed | tf_op | source)
XLA Modules:
  0.0 103.8 jit_solution(11313667358949815375)
XLA Ops:
  1.3 1.2 %broadcast_select_fusion = bf16[256,1024]{1,0:T(8,128)(2,1)S(1)} fusion(pred[256]{0:T(512)(128)(4,1)S(1)} %iota_compare_fusion, bf16[1,256,1024]{2,1,0:T(8,128)(2,1)} %param.10), kind=kLoop, calls=%fused_computation | loop fusion | flops 262144 | bytes 1048832 | tf_op jit(solution)/shard_map/jit(_where)/select_n | solution.py:271
  2.5 1.9 %collective-permute-start.8 = (bf16[256,1024]{1,0:T(8,128)(2,1)S(1)}, bf16[256,1024]{1,0:T(8,128)(2,1)S(1)}, u32[]{:S(2)}, u32[]{:S(2)}) collective-permute-start(bf16[256,1024]{1,0:T(8,128)(2,1)S(1)} %broadcast_select_fusion), channel_id=1, source_target_pairs={{0,68},{1,69},{2,70},{3,71},{4,72},{5,73},{6,74},{7,75},{8,76},{9,... | collective-permute-start | bytes 1572872 | tf_op jit(solution)/shard_map/ppermute | solution.py:43
  4.4 0.7 slice_bitcast_fusion
  5.3 2.2 %collective-permute-start.1 = (s32[1,128]{1,0:T(1,128)S(1)}, s32[1,128]{1,0:T(1,128)S(1)}, u32[]{:S(2)}, u32[]{:S(2)}) collective-permute-start(s32[1,128]{1,0:T(1,128)S(1)} %pad_bitcast_fusion), channel_id=1, source_target_pairs={{0,2},{1,3},{2,0},{3,1},{4,6},{5,7},{6,4},{7,5},{8,10},{9,11},{10,... | collective-permute-start | bytes 1544 | tf_op jit(solution)/shard_map/ppermute | solution.py:49
  7.8 1.4 %collective-permute-done.1.r_2_.r_3_ = s32[1,128]{1,0:T(1,128)S(1)} collective-permute-done((s32[1,128]{1,0:T(1,128)S(1)}, s32[1,128]{1,0:T(1,128)S(1)}, u32[]{:S(2)}, u32[]{:S(2)}) %collective-permute-start.1) | collective-permute-done | bytes 544 | tf_op jit(solution)/shard_map/ppermute | solution.py:49
  9.2 2.1 %collective-permute-done.r_1_.r_2_ = s32[1,128]{1,0:T(1,128)S(1)} collective-permute-done((s32[1,128]{1,0:T(1,128)S(1)}, s32[1,128]{1,0:T(1,128)S(1)}, u32[]{:S(2)}, u32[]{:S(2)}) %collective-permute-start) | collective-permute-done | bytes 544 | tf_op jit(solution)/shard_map/ppermute | solution.py:49
  11.3 3.7 %collective-permute-start.4 = (bf16[256,1024]{1,0:T(8,128)(2,1)S(1)}, bf16[256,1024]{1,0:T(8,128)(2,1)S(1)}, u32[]{:S(2)}, u32[]{:S(2)}) collective-permute-start(bf16[256,1024]{1,0:T(8,128)(2,1)S(1)} %broadcast_select_fusion), channel_id=1, source_target_pairs={{0,72},{1,73},{2,74},{3,75},{4,76},{5,77},{6,78},{7,79},{8,80},{9,... | collective-permute-start | bytes 1572872 | tf_op jit(solution)/shard_map/ppermute | solution.py:43
  15.1 0.8 copy.12.r_1_.r_0_
  15.8 1.6 %copy-done.1 = s32[1,256,2048]{2,1,0:T(8,128)S(1)} copy-done((s32[1,256,2048]{2,1,0:T(8,128)S(1)}, s32[1,256,2048]{2,1,0:T(8,128)}, u32[]{:S(2)}) %copy-start.1) | copy-done | bytes 2097176
  17.4 1.6 %copy-done.2 = bf16[1024,1024]{1,0:T(8,128)(2,1)S(1)} copy-done((bf16[1024,1024]{1,0:T(8,128)(2,1)S(1)}, bf16[1024,1024]{1,0:T(8,128)(2,1)}, u32[]{:S(2)}) %copy-start.2) | copy-done | bytes 2097176
  19.0 1.0 %copy-done.4 = bf16[1,256,1024]{2,1,0:T(8,128)(2,1)S(1)} copy-done((bf16[1,256,1024]{2,1,0:T(8,128)(2,1)S(1)}, bf16[1,256,1024]{2,1,0:T(8,128)(2,1)}, u32[]{:S(2)}) %copy-start.4) | copy-done | bytes 524312
  20.0 1.3 %shard_map.114 = (bf16[256,1024]{1,0:T(8,128)(2,1)S(1)}, bf16[1024,256]{1,0:T(8,128)(2,1)S(1)}, f32[256,1024]{1,0:T(8,128)S(1)}) custom-call(s32[1]{0:T(128)} %bitcast.1.r_0_, s32[8,2]{1,0:T(8,128)S(1)} %copy.12.r_1_.r_0_, s32[256,2048]{1,0:T(8,128)S(1)} %bitcast.20, bf16[256,1024]{1,0:T(8,128)(2,1)S(1)} %bitcast.21, bf16[1024,1024]{1,0:T(8,128)(2,1)S(1)} %copy-done.2), custom_call_target="tpu_custom_call" | custom-call | flops 536870912 | bytes 1048576 | tf_op jit(solution)/shard_map/pallas_call | solution.py:25
  22.4 1.6 %collective-permute-start.10 = (bf16[128,1024]{1,0:T(8,128)(2,1)S(1)}, bf16[128,1024]{1,0:T(8,128)(2,1)S(1)}, u32[]{:S(2)}, u32[]{:S(2)}) collective-permute-start(bf16[128,1024]{1,0:T(8,128)(2,1)S(1)} %get-tuple-element.41), channel_id=1, source_target_pairs={{0,2},{1,3},{2,0},{3,1},{4,6},{5,7},{6,4},{7,5},{8,10},{9,11},{10,... | collective-permute-start | bytes 786440 | tf_op jit(solution)/shard_map/ppermute | solution.py:49
  24.0 10.2 %collective-permute-done.4.r_5_ = bf16[256,1024]{1,0:T(8,128)(2,1)S(1)} collective-permute-done((bf16[256,1024]{1,0:T(8,128)(2,1)S(1)}, bf16[256,1024]{1,0:T(8,128)(2,1)S(1)}, u32[]{:S(2)}, u32[]{:S(2)}) %collective-permute-start.4) | collective-permute-done | bytes 524320 | tf_op jit(solution)/shard_map/ppermute | solution.py:43
  34.2 0.6 shard_map.113
  35.1 2.1 %collective-permute-start.6 = (bf16[128,1024]{1,0:T(8,128)(2,1)S(1)}, bf16[128,1024]{1,0:T(8,128)(2,1)S(1)}, u32[]{:S(2)}, u32[]{:S(2)}) collective-permute-start(bf16[128,1024]{1,0:T(8,128)(2,1)S(1)} %get-tuple-element.37), channel_id=1, source_target_pairs={{0,2},{1,3},{2,0},{3,1},{4,6},{5,7},{6,4},{7,5},{8,10},{9,11},{10,... | collective-permute-start | bytes 786440 | tf_op jit(solution)/shard_map/ppermute | solution.py:49
  37.8 4.6 %shard_map.116 = (bf16[640,2048]{1,0:T(8,128)(2,1)S(1)}, f32[256,2048]{1,0:T(8,128)S(1)}, f32[256,128]{1,0:T(8,128)S(1)}) custom-call(s32[8,2]{1,0:T(8,128)S(1)} %copy.12.r_1_.r_0_, bf16[256,1024]{1,0:T(8,128)(2,1)S(1)} %collective-permute-done.3.r_4_.r_1_, bf16[256,1024]{1,0:T(8,128)(2,1)S(1)} %collective-permute-done.8.r_4_.r_2_, ...), custom_call_target="tpu_custom_call" | custom-call | flops 3355443200 | bytes 1048576 | tf_op jit(solution)/shard_map/pallas_call | solution.py:25
  42.4 1.4 %collective-permute-done.6.r_2_ = bf16[128,1024]{1,0:T(8,128)(2,1)S(1)} collective-permute-done((bf16[128,1024]{1,0:T(8,128)(2,1)S(1)}, bf16[128,1024]{1,0:T(8,128)(2,1)S(1)}, u32[]{:S(2)}, u32[]{:S(2)}) %collective-permute-start.6) | collective-permute-done | bytes 262176 | tf_op jit(solution)/shard_map/ppermute | solution.py:49
  43.8 6.6 %collective-permute-done.7.r_3_ = bf16[128,1024]{1,0:T(8,128)(2,1)S(1)} collective-permute-done((bf16[128,1024]{1,0:T(8,128)(2,1)S(1)}, bf16[128,1024]{1,0:T(8,128)(2,1)S(1)}, u32[]{:S(2)}, u32[]{:S(2)}) %collective-permute-start.7) | collective-permute-done | bytes 262176 | tf_op jit(solution)/shard_map/ppermute | solution.py:49
  50.5 7.6 %shard_map.117 = (bf16[256,1024]{1,0:T(8,128)(2,1)S(1)}, bf16[256,2048]{1,0:T(8,128)(2,1)S(1)}, f32[256,1024]{1,0:T(8,128)S(1)}, bf16[384,2048]{1,0:T(8,128)(2,1...) custom-call(s32[1]{0:T(128)} %bitcast.16.r_0_, ...), custom_call_target="tpu_custom_call" | custom-call | flops 8000000000 | bytes 1048576 | tf_op jit(solution)/shard_map/pallas_call | solution.py:25
  58.1 0.8 collective-permute-start.13
  58.9 1.3 %collective-permute-start.14 = (bf16[128,1024]{1,0:T(8,128)(2,1)S(1)}, bf16[128,1024]{1,0:T(8,128)(2,1)S(1)}, u32[]{:S(2)}, u32[]{:S(2)}) collective-permute-start(bf16[128,1024]{1,0:T(8,128)(2,1)S(1)} %get-tuple-element.56), channel_id=1, source_target_pairs={{0,1},{1,2},{2,3},{3,0},{4,5},{5,6},{6,7},{7,4},{8,9},{9,10},{10,1... | collective-permute-start | bytes 786440 | tf_op jit(solution)/shard_map/ppermute | solution.py:49
  60.4 2.8 %shard_map.118 = (bf16[128,1152]{1,0:T(8,128)(2,1)S(1)}, bf16[128,1152]{1,0:T(8,128)(2,1)S(1)}, bf16[128,1152]{1,0:T(8,128)(2,1)S(1)}) custom-call(s32[1]{0:T(128)} %bitcast.1.r_0_, s32[8,2]{1,0:T(8,128)S(1)} %copy.12.r_1_.r_0_, bf16[1024,256]{1,0:T(8,128)(2,1)S(1)} %get-tuple-element.46.r_13_.r_2_.r_1_, bf16[256,2048]{1,0:T(8,128)(2,1)S(1)} %get-tuple-element.50.r_3_.r_2_, ...), custom_call_target="tpu_custom_call" | custom-call | flops 2000000000 | bytes 1048576 | tf_op jit(solution)/shard_map/pallas_call | solution.py:25
  63.2 3.5 %collective-permute-start.16 = (bf16[128,1152]{1,0:T(8,128)(2,1)S(1)}, bf16[128,1152]{1,0:T(8,128)(2,1)S(1)}, u32[]{:S(2)}, u32[]{:S(2)}) collective-permute-start(bf16[128,1152]{1,0:T(8,128)(2,1)S(1)} %get-tuple-element.59), channel_id=1, source_target_pairs={{66,0},{67,1},{72,2},{73,3},{70,4},{71,5},{76,6},{77,7},{74,8},{75... | collective-permute-start | bytes 884744 | tf_op jit(solution)/shard_map/ppermute | solution.py:59
  66.7 2.2 %shard_map.119 = (bf16[256,1024]{1,0:T(8,128)(2,1)S(1)}, bf16[128,1024]{1,0:T(8,128)(2,1)S(1)}) custom-call(s32[8,2]{1,0:T(8,128)S(1)} %copy.12.r_1_.r_0_, bf16[1024,256]{1,0:T(8,128)(2,1)S(1)} %get-tuple-element.46.r_13_.r_2_.r_1_, bf16[256,2048]{1,0:T(8,128)(2,1)S(1)} %get-tuple-element.50.r_3_.r_2_, bf16[640,2048]{1,0:T(8,128)(2,1)S(1)} %get-tuple-element.47.r_14_.r_3_, ...), custom_call_target="tpu_custom_call" | custom-call | flops 2000000000 | bytes 1048576 | tf_op jit(solution)/shard_map/pallas_call | solution.py:25
  69.0 6.3 %collective-permute-start.17 = (bf16[128,1152]{1,0:T(8,128)(2,1)S(1)}, bf16[128,1152]{1,0:T(8,128)(2,1)S(1)}, u32[]{:S(2)}, u32[]{:S(2)}) collective-permute-start(bf16[128,1152]{1,0:T(8,128)(2,1)S(1)} %get-tuple-element.60), channel_id=1, source_target_pairs={{67,0},{72,1},{73,2},{74,3},{71,4},{76,5},{77,6},{78,7},{75,8},{80... | collective-permute-start | bytes 884744 | tf_op jit(solution)/shard_map/ppermute | solution.py:59
  75.3 1.7 %collective-permute-start.18 = (bf16[256,1024]{1,0:T(8,128)(2,1)S(1)}, bf16[256,1024]{1,0:T(8,128)(2,1)S(1)}, u32[]{:S(2)}, u32[]{:S(2)}) collective-permute-start(bf16[256,1024]{1,0:T(8,128)(2,1)S(1)} %get-tuple-element.61), channel_id=1, source_target_pairs={{0,64},{1,65},{2,66},{3,67},{4,68},{5,69},{6,70},{7,71},{8,72},{9,... | collective-permute-start | bytes 1572872 | tf_op jit(solution)/shard_map/ppermute | solution.py:43
  77.0 0.9 shard_map.120._
  78.6 1.6 %shard_map.121 = (f32[256,1024]{1,0:T(8,128)S(1)}, bf16[256,1024]{1,0:T(8,128)(2,1)}) custom-call(s32[1]{0:T(128)} %bitcast.17.live_ref, bf16[256,1024]{1,0:T(8,128)(2,1)S(1)} %get-tuple-element.48.g_ref, bf16[1024,1024]{1,0:T(8,128)(2,1)S(1)} %copy-done.3, f32[256,1024]{1,0:T(8,128)S(1)} %get-tuple-element.49.pre_ref, bf16[256,1024]{1,0:T(8,128)(2,1)S(1)} %shard_map.120._), custom_call_target="tpu_custom_call" | custom-call | flops 2000000000 | bytes 1048576 | tf_op jit(solution)/shard_map/pallas_call | solution.py:25
  80.2 11.3 %collective-permute-done.17.c3 = bf16[128,1152]{1,0:T(8,128)(2,1)S(1)} collective-permute-done((bf16[128,1152]{1,0:T(8,128)(2,1)S(1)}, bf16[128,1152]{1,0:T(8,128)(2,1)S(1)}, u32[]{:S(2)}, u32[]{:S(2)}) %collective-permute-start.17) | collective-permute-done | bytes 294944 | tf_op jit(solution)/shard_map/ppermute | solution.py:59
  91.9 10.9 %collective-permute-done.19.below_ref = bf16[256,1024]{1,0:T(8,128)(2,1)S(1)} collective-permute-done((bf16[256,1024]{1,0:T(8,128)(2,1)S(1)}, bf16[256,1024]{1,0:T(8,128)(2,1)S(1)}, u32[]{:S(2)}, u32[]{:S(2)}) %collective-permute-start.19) | collective-permute-done | bytes 524320 | tf_op jit(solution)/shard_map/ppermute | solution.py:43
  102.8 1.0 shard_map.123
  (42 shorter events, 3.6 us)
Async XLA Ops:
  2.5 18.9 %collective-permute-start.8 = (bf16[256,1024]{1,0:T(8,128)(2,1)S(1)}, bf16[256,1024]{1,0:T(8,128)(2,1)S(1)}, u32[]{:S(2)}, u32[]{:S(2)}) collective-permute-start(bf16[256,1024]{1,0:T(8,128)(2,1)S(1)} %broadcast_select_fusion), channel_id=1, source_target_pairs={{0,68},{1,69},{2,70},{3,71},{4,72},{5,73},{6,74},{7,75},{8,76},{9,... | collective-permute-start | bytes 1572872 | tf_op jit(solution)/shard_map/ppermute | solution.py:43
  5.1 2.7 %collective-permute-start.2 = (s32[1,128]{1,0:T(1,128)S(1)}, s32[1,128]{1,0:T(1,128)S(1)}, u32[]{:S(2)}, u32[]{:S(2)}) collective-permute-start(s32[1,128]{1,0:T(1,128)S(1)} %pad_bitcast_fusion), channel_id=1, source_target_pairs={{0,1},{1,2},{2,3},{3,0},{4,5},{5,6},{6,7},{7,4},{8,9},{9,10},{10,1... | collective-permute-start | bytes 1544 | tf_op jit(solution)/shard_map/ppermute | solution.py:49
  5.3 3.9 %collective-permute-start.1 = (s32[1,128]{1,0:T(1,128)S(1)}, s32[1,128]{1,0:T(1,128)S(1)}, u32[]{:S(2)}, u32[]{:S(2)}) collective-permute-start(s32[1,128]{1,0:T(1,128)S(1)} %pad_bitcast_fusion), channel_id=1, source_target_pairs={{0,2},{1,3},{2,0},{3,1},{4,6},{5,7},{6,4},{7,5},{8,10},{9,11},{10,... | collective-permute-start | bytes 1544 | tf_op jit(solution)/shard_map/ppermute | solution.py:49
  7.4 3.9 %collective-permute-start = (s32[1,128]{1,0:T(1,128)S(1)}, s32[1,128]{1,0:T(1,128)S(1)}, u32[]{:S(2)}, u32[]{:S(2)}) collective-permute-start(s32[1,128]{1,0:T(1,128)S(1)} %pad_bitcast_fusion), channel_id=1, source_target_pairs={{0,3},{1,0},{2,1},{3,2},{4,7},{5,4},{6,5},{7,6},{8,11},{9,8},{10,9... | collective-permute-start | bytes 1544 | tf_op jit(solution)/shard_map/ppermute | solution.py:49
  7.4 16.5 %collective-permute-start.3 = (bf16[256,1024]{1,0:T(8,128)(2,1)S(1)}, bf16[256,1024]{1,0:T(8,128)(2,1)S(1)}, u32[]{:S(2)}, u32[]{:S(2)}) collective-permute-start(bf16[256,1024]{1,0:T(8,128)(2,1)S(1)} %broadcast_select_fusion), channel_id=1, source_target_pairs={{0,64},{1,65},{2,66},{3,67},{4,68},{5,69},{6,70},{7,71},{8,72},{9,... | collective-permute-start | bytes 1572872 | tf_op jit(solution)/shard_map/ppermute | solution.py:43
  11.3 22.8 %collective-permute-start.4 = (bf16[256,1024]{1,0:T(8,128)(2,1)S(1)}, bf16[256,1024]{1,0:T(8,128)(2,1)S(1)}, u32[]{:S(2)}, u32[]{:S(2)}) collective-permute-start(bf16[256,1024]{1,0:T(8,128)(2,1)S(1)} %broadcast_select_fusion), channel_id=1, source_target_pairs={{0,72},{1,73},{2,74},{3,75},{4,76},{5,77},{6,78},{7,79},{8,80},{9,... | collective-permute-start | bytes 1572872 | tf_op jit(solution)/shard_map/ppermute | solution.py:43
  15.8 1.6 %copy-start.1 = (s32[1,256,2048]{2,1,0:T(8,128)S(1)}, s32[1,256,2048]{2,1,0:T(8,128)}, u32[]{:S(2)}) copy-start(s32[1,256,2048]{2,1,0:T(8,128)} %param.13) | copy-start | bytes 6291460
  17.4 1.6 %copy-start.2 = (bf16[1024,1024]{1,0:T(8,128)(2,1)S(1)}, bf16[1024,1024]{1,0:T(8,128)(2,1)}, u32[]{:S(2)}) copy-start(bf16[1024,1024]{1,0:T(8,128)(2,1)} %sw_ref.1) | copy-start | bytes 6291460
  19.0 1.0 %copy-start.4 = (bf16[1,256,1024]{2,1,0:T(8,128)(2,1)S(1)}, bf16[1,256,1024]{2,1,0:T(8,128)(2,1)}, u32[]{:S(2)}) copy-start(bf16[1,256,1024]{2,1,0:T(8,128)(2,1)} %param.10) | copy-start | bytes 1572868
  20.0 17.7 %copy-start = (bf16[1024,2048]{1,0:T(8,128)(2,1)S(1)}, bf16[1024,2048]{1,0:T(8,128)(2,1)}, u32[]{:S(2)}) copy-start(bf16[1024,2048]{1,0:T(8,128)(2,1)} %r_4_.5) | copy-start | bytes 12582916
  21.4 16.4 %copy-start.7 = (f32[2048]{0:T(1024)S(1)}, f32[2048]{0:T(1024)}, u32[]{:S(2)}) copy-start(f32[2048]{0:T(1024)} %param.16) | copy-start | bytes 24580
  22.0 15.2 %collective-permute-start.9 = (bf16[128,1024]{1,0:T(8,128)(2,1)S(1)}, bf16[128,1024]{1,0:T(8,128)(2,1)S(1)}, u32[]{:S(2)}, u32[]{:S(2)}) collective-permute-start(bf16[128,1024]{1,0:T(8,128)(2,1)S(1)} %get-tuple-element.40), channel_id=1, source_target_pairs={{0,1},{1,2},{2,3},{3,0},{4,5},{5,6},{6,7},{7,4},{8,9},{9,10},{10,1... | collective-permute-start | bytes 786440 | tf_op jit(solution)/shard_map/ppermute | solution.py:49
  22.4 14.8 %collective-permute-start.10 = (bf16[128,1024]{1,0:T(8,128)(2,1)S(1)}, bf16[128,1024]{1,0:T(8,128)(2,1)S(1)}, u32[]{:S(2)}, u32[]{:S(2)}) collective-permute-start(bf16[128,1024]{1,0:T(8,128)(2,1)S(1)} %get-tuple-element.41), channel_id=1, source_target_pairs={{0,2},{1,3},{2,0},{3,1},{4,6},{5,7},{6,4},{7,5},{8,10},{9,11},{10,... | collective-permute-start | bytes 786440 | tf_op jit(solution)/shard_map/ppermute | solution.py:49
  23.9 13.8 %collective-permute-start.11 = (bf16[128,1024]{1,0:T(8,128)(2,1)S(1)}, bf16[128,1024]{1,0:T(8,128)(2,1)S(1)}, u32[]{:S(2)}, u32[]{:S(2)}) collective-permute-start(bf16[128,1024]{1,0:T(8,128)(2,1)S(1)} %get-tuple-element.42), channel_id=1, source_target_pairs={{0,3},{1,0},{2,1},{3,2},{4,7},{5,4},{6,5},{7,6},{8,11},{9,8},{10,9... | collective-permute-start | bytes 786440 | tf_op jit(solution)/shard_map/ppermute | solution.py:49
  34.8 7.6 %collective-permute-start.5 = (bf16[128,1024]{1,0:T(8,128)(2,1)S(1)}, bf16[128,1024]{1,0:T(8,128)(2,1)S(1)}, u32[]{:S(2)}, u32[]{:S(2)}) collective-permute-start(bf16[128,1024]{1,0:T(8,128)(2,1)S(1)} %get-tuple-element.36), channel_id=1, source_target_pairs={{0,1},{1,2},{2,3},{3,0},{4,5},{5,6},{6,7},{7,4},{8,9},{9,10},{10,1... | collective-permute-start | bytes 786440 | tf_op jit(solution)/shard_map/ppermute | solution.py:49
  35.1 8.7 %collective-permute-start.6 = (bf16[128,1024]{1,0:T(8,128)(2,1)S(1)}, bf16[128,1024]{1,0:T(8,128)(2,1)S(1)}, u32[]{:S(2)}, u32[]{:S(2)}) collective-permute-start(bf16[128,1024]{1,0:T(8,128)(2,1)S(1)} %get-tuple-element.37), channel_id=1, source_target_pairs={{0,2},{1,3},{2,0},{3,1},{4,6},{5,7},{6,4},{7,5},{8,10},{9,11},{10,... | collective-permute-start | bytes 786440 | tf_op jit(solution)/shard_map/ppermute | solution.py:49
  37.2 13.2 %collective-permute-start.7 = (bf16[128,1024]{1,0:T(8,128)(2,1)S(1)}, bf16[128,1024]{1,0:T(8,128)(2,1)S(1)}, u32[]{:S(2)}, u32[]{:S(2)}) collective-permute-start(bf16[128,1024]{1,0:T(8,128)(2,1)S(1)} %get-tuple-element.38), channel_id=1, source_target_pairs={{0,3},{1,0},{2,1},{3,2},{4,7},{5,4},{6,5},{7,6},{8,11},{9,8},{10,9... | collective-permute-start | bytes 786440 | tf_op jit(solution)/shard_map/ppermute | solution.py:49
  37.8 12.7 %copy-start.5 = (bf16[2048,1024]{1,0:T(8,128)(2,1)S(1)}, bf16[2048,1024]{1,0:T(8,128)(2,1)}, u32[]{:S(2)}) copy-start(bf16[2048,1024]{1,0:T(8,128)(2,1)} %r_11_.1) | copy-start | bytes 12582916
  37.8 12.7 %copy-start.6 = (bf16[1,256,1024]{2,1,0:T(8,128)(2,1)S(1)}, bf16[1,256,1024]{2,1,0:T(8,128)(2,1)}, u32[]{:S(2)}) copy-start(bf16[1,256,1024]{2,1,0:T(8,128)(2,1)} %param.14) | copy-start | bytes 1572868
  37.8 12.7 %copy-start.8 = (f32[1024]{0:T(1024)S(1)}, f32[1024]{0:T(1024)}, u32[]{:S(2)}) copy-start(f32[1024]{0:T(1024)} %param.19) | copy-start | bytes 12292
  58.1 10.9 %collective-permute-start.13 = (bf16[128,1024]{1,0:T(8,128)(2,1)S(1)}, bf16[128,1024]{1,0:T(8,128)(2,1)S(1)}, u32[]{:S(2)}, u32[]{:S(2)}) collective-permute-start(bf16[128,1024]{1,0:T(8,128)(2,1)S(1)} %get-tuple-element.55), channel_id=1, source_target_pairs={{0,2},{1,3},{2,0},{3,1},{4,6},{5,7},{6,4},{7,5},{8,10},{9,11},{10,... | collective-permute-start | bytes 786440 | tf_op jit(solution)/shard_map/ppermute | solution.py:49
  58.9 16.4 %collective-permute-start.14 = (bf16[128,1024]{1,0:T(8,128)(2,1)S(1)}, bf16[128,1024]{1,0:T(8,128)(2,1)S(1)}, u32[]{:S(2)}, u32[]{:S(2)}) collective-permute-start(bf16[128,1024]{1,0:T(8,128)(2,1)S(1)} %get-tuple-element.56), channel_id=1, source_target_pairs={{0,1},{1,2},{2,3},{3,0},{4,5},{5,6},{6,7},{7,4},{8,9},{9,10},{10,1... | collective-permute-start | bytes 786440 | tf_op jit(solution)/shard_map/ppermute | solution.py:49
  60.2 16.8 %collective-permute-start.12 = (bf16[128,1024]{1,0:T(8,128)(2,1)S(1)}, bf16[128,1024]{1,0:T(8,128)(2,1)S(1)}, u32[]{:S(2)}, u32[]{:S(2)}) collective-permute-start(bf16[128,1024]{1,0:T(8,128)(2,1)S(1)} %get-tuple-element.52.r_6_), channel_id=1, source_target_pairs={{0,3},{1,0},{2,1},{3,2},{4,7},{5,4},{6,5},{7,6},{8,11},{9,8},{10,9... | collective-permute-start | bytes 786440 | tf_op jit(solution)/shard_map/ppermute | solution.py:49
  63.2 17.0 %collective-permute-start.16 = (bf16[128,1152]{1,0:T(8,128)(2,1)S(1)}, bf16[128,1152]{1,0:T(8,128)(2,1)S(1)}, u32[]{:S(2)}, u32[]{:S(2)}) collective-permute-start(bf16[128,1152]{1,0:T(8,128)(2,1)S(1)} %get-tuple-element.59), channel_id=1, source_target_pairs={{66,0},{67,1},{72,2},{73,3},{70,4},{71,5},{76,6},{77,7},{74,8},{75... | collective-permute-start | bytes 884744 | tf_op jit(solution)/shard_map/ppermute | solution.py:59
  66.7 24.8 %collective-permute-start.15 = (bf16[128,1152]{1,0:T(8,128)(2,1)S(1)}, bf16[128,1152]{1,0:T(8,128)(2,1)S(1)}, u32[]{:S(2)}, u32[]{:S(2)}) collective-permute-start(bf16[128,1152]{1,0:T(8,128)(2,1)S(1)} %get-tuple-element.53.r_5_), channel_id=1, source_target_pairs={{65,0},{66,1},{67,2},{72,3},{69,4},{70,5},{71,6},{76,7},{73,8},{74... | collective-permute-start | bytes 884744 | tf_op jit(solution)/shard_map/ppermute | solution.py:59
  69.0 22.6 %collective-permute-start.17 = (bf16[128,1152]{1,0:T(8,128)(2,1)S(1)}, bf16[128,1152]{1,0:T(8,128)(2,1)S(1)}, u32[]{:S(2)}, u32[]{:S(2)}) collective-permute-start(bf16[128,1152]{1,0:T(8,128)(2,1)S(1)} %get-tuple-element.60), channel_id=1, source_target_pairs={{67,0},{72,1},{73,2},{74,3},{71,4},{76,5},{77,6},{78,7},{75,8},{80... | collective-permute-start | bytes 884744 | tf_op jit(solution)/shard_map/ppermute | solution.py:59
  75.3 16.6 %collective-permute-start.18 = (bf16[256,1024]{1,0:T(8,128)(2,1)S(1)}, bf16[256,1024]{1,0:T(8,128)(2,1)S(1)}, u32[]{:S(2)}, u32[]{:S(2)}) collective-permute-start(bf16[256,1024]{1,0:T(8,128)(2,1)S(1)} %get-tuple-element.61), channel_id=1, source_target_pairs={{0,64},{1,65},{2,66},{3,67},{4,68},{5,69},{6,70},{7,71},{8,72},{9,... | collective-permute-start | bytes 1572872 | tf_op jit(solution)/shard_map/ppermute | solution.py:43
  77.0 1.6 %copy-start.3 = (bf16[1024,1024]{1,0:T(8,128)(2,1)S(1)}, bf16[1024,1024]{1,0:T(8,128)(2,1)}, u32[]{:S(2)}) copy-start(bf16[1024,1024]{1,0:T(8,128)(2,1)} %sw_ref.1) | copy-start | bytes 6291460
  78.0 24.8 %collective-permute-start.19 = (bf16[256,1024]{1,0:T(8,128)(2,1)S(1)}, bf16[256,1024]{1,0:T(8,128)(2,1)S(1)}, u32[]{:S(2)}, u32[]{:S(2)}) collective-permute-start(bf16[256,1024]{1,0:T(8,128)(2,1)S(1)} %shard_map.120._), channel_id=1, source_target_pairs={{0,124},{1,125},{2,126},{3,127},{4,64},{5,65},{6,66},{7,67},{8,68}... | collective-permute-start | bytes 1572872 | tf_op jit(solution)/shard_map/ppermute | solution.py:43

commit v12 on v11

--- a/solution.py
+++ b/solution.py
@@ -71,7 +71,7 @@
     return pl.ds(pl.multiple_of(index * block, block), block)
 
 
-def pick_near_kernel(block, place_ref, m1, m2, m3, rows_ref, _, *outs):
+def pick_near_kernel(block, place_ref, m1, m2, m3, rows_ref, *outs):
     for d, (meta, out) in enumerate(zip((m1, m2, m3), outs), 1):
         p = lax.rem(place_ref[0] + d, LINE)
         out[...] = rows_ref[at_block(meta[0, near(p, d)], block), :]
@@ -95,7 +95,7 @@
     return [0, LINE] + [near(p, d) for d in range(1, LINE)] + [far(p, d) for d in range(1, LINE)]
 
 
-def tiles_kernel(block, place_ref, lists_ref, counts_ref, x_ref, sw_ref, tiles_ref, tiles_t_ref, self_ref):
+def tiles_kernel(block, place_ref, lists_ref, counts_ref, x_ref, sw_ref, _, tiles_ref, tiles_t_ref, self_ref):
     for i, o in enumerate(slots(place_ref[0])):
         first, second = lists_ref[o, 0], lists_ref[o, 1]
         at = pl.ds(pl.multiple_of((o * 2 + second) * block, block), block)
@@ -138,8 +138,8 @@
 
 
 def layer_kernel(
-    block, live_ref, got_a, got_b, got_c, q_ref, qb_ref, tiles_ref, acc_ref, deg_ref, self_ref, up_ref, nb_ref, ob_ref, tt_ref,
-    msg_ref, g_ref, gpool_ref, pre_ref, last_ref, near1, near2, near3, pooled_ref, gn_ref,
+    block, live_ref, place_ref, lists_ref, got_a, got_b, got_c, q_ref, qb_ref, tiles_ref, acc_ref, deg_ref, self_ref, up_ref, nb_ref, ob_ref, tt_ref,
+    msg_ref, g_ref, gpool_ref, pre_ref, last_ref, near1, near2, near3, far1, pooled_ref, gn_ref,
 ):
     rows, width = self_ref.shape
     hidden = nb_ref.shape[0]
@@ -174,10 +174,17 @@
         gpool_ref[:, cols] = (dot(g, nb_ref[cols, :], 1, 1) * inv_deg).astype(BF16)
 
     def store(cols, part):
-        for i, out in enumerate((near1, near2, near3)):
+        for i, out in enumerate((near1, near2, near3, far1)):
             out[:, cols] = part[i * block : (i + 1) * block].astype(BF16)
 
-    back_dot(2 * block, tt_ref, gpool_ref, [msg_ref[2 * block :, :]], q_ref, gn_ref, store)
+    mark_block(place_ref, lists_ref, 1, far1, width)
+    messages = [msg_ref[2 * block :, :], last_ref[:block, :]]
+    back_dot(2 * block, tt_ref, gpool_ref, messages, q_ref, gn_ref, store)
+
+
+def mark_block(place_ref, lists_ref, d, out, width):
+    which = lists_ref[far(place_ref[0], d), 1].astype(F32)
+    out[:, width:] = jnp.full((out.shape[0], out.shape[1] - width), which, F32).astype(BF16)
 
 
 def back_dot(first, tt_ref, gpool_ref, messages, q_ref, gn_ref, store):
@@ -202,10 +209,9 @@
         for i, out in enumerate(outs):
             out[:, cols] = part[i * block : (i + 1) * block].astype(BF16)
 
-    for d, out in enumerate(outs, 1):
-        which = lists_ref[far(place_ref[0], d), 1].astype(F32)
-        out[:, width:] = jnp.full((block, 128), which, F32).astype(BF16)
-    back_dot((1 + LINE) * block, tt_ref, gpool_ref, [msg_ref[...]], q_ref, gn_ref, store)
+    for d, out in enumerate(outs, 2):
+        mark_block(place_ref, lists_ref, d, out, width)
+    back_dot((2 + LINE) * block, tt_ref, gpool_ref, [msg_ref[block:, :]], q_ref, gn_ref, store)
 
 
 def back_own_kernel(block, lists_ref, tt_ref, gpool_ref, msg_ref, q_ref, _, same_ref, below_ref, gn_ref):
@@ -279,18 +285,11 @@
     later, *metas = lax.optimization_barrier((marked, *metas))
     below2 = swap_rows(later, 2 * LINE)
     scalars = [SMEM] * (1 + len(steps))
-    tiles, tiles_t, self_pre = call(
-        lambda *r: tiles_kernel(block, *r),
-        [((rows, reach * block), BF16), ((reach * block, rows), BF16), ((rows, width), F32)],
-        (place, lists, counts, x, sw),
-        [SMEM] * 2 + [VMEM] * 3,
-        flops=2 * rows * width * width,
-    )
     sent = call(
         lambda *r: pick_near_kernel(block, *r),
         [one] * len(steps),
-        (place, *metas, below, tiles),
-        scalars + [VMEM, HELD],
+        (place, *metas, below),
+        scalars + [VMEM],
     )
     got_near = [along(b, d) for d, b in zip(steps, sent)]
     sent = call(
@@ -300,6 +299,13 @@
         scalars + [VMEM] * 2,
     )
     got_far = [along(b, d) for d, b in zip(steps, sent)]
+    tiles, tiles_t, self_pre = call(
+        lambda *r: tiles_kernel(block, *r),
+        [((rows, reach * block), BF16), ((reach * block, rows), BF16), ((rows, width), F32)],
+        (place, lists, counts, x, sw, sent[0]),
+        [SMEM] * 2 + [VMEM] * 3 + [HELD],
+        flops=2 * rows * width * width,
+    )
     split = 1 + LINE
 
     def message(first, last, ins, specs):
@@ -315,25 +321,24 @@
     msg_a, acc, deg = message(
         0, split, (lists, same, below, *got_near, q, qb, tiles), [SMEM] + [VMEM] * 8
     )
-    gn = pltpu.VMEM((3 * block, hidden), BF16)
-    g, gpool, pre, msg_b, *near_back = call(
+    g, gpool, pre, msg_b, *near_back, far_first = call(
         lambda *r: layer_kernel(block, *r),
-        [two, ((rows, hidden), BF16), ((rows, width), F32), ((3 * block, hidden), BF16)] + [one] * 3,
-        (live, *got_far, q, qb, tiles, acc, deg, self_pre, up, nb, ob, tiles_t, msg_a),
-        [SMEM] + [VMEM] * 14,
-        scratch=[pltpu.VMEM((rows, hidden), BF16), gn],
+        [two, ((rows, hidden), BF16), ((rows, width), F32), ((3 * block, hidden), BF16)] + [one] * 3 + [((block, width + 128), BF16)],
+        (live, place, lists, *got_far, q, qb, tiles, acc, deg, self_pre, up, nb, ob, tiles_t, msg_a),
+        [SMEM] * 3 + [VMEM] * 14,
+        scratch=[pltpu.VMEM((rows, hidden), BF16), pltpu.VMEM((4 * block, hidden), BF16)],
         flops=8 * MICROSECOND,
     )
     back_near = [along(b, -d) for d, b in zip(steps, near_back)]
     far_back = call(
         lambda *r: back_far_kernel(block, *r),
-        [((block, width + 128), BF16)] * 3,
+        [((block, width + 128), BF16)] * 2,
         (place, lists, tiles_t, gpool, msg_b, q, near_back[0]),
         [SMEM] * 2 + [VMEM] * 4 + [HELD],
-        scratch=[gn],
+        scratch=[pltpu.VMEM((2 * block, hidden), BF16)],
         flops=2 * MICROSECOND,
     )
-    back_far = [straight_back(b, d) for d, b in zip(steps, far_back)]
+    back_far = [straight_back(b, d) for d, b in zip(steps, (far_first, *far_back))]
     own_same, own_below = call(
         lambda *r: back_own_kernel(block, *r),
         [two, one],

time: 105 us -> 104 us (level)
  waiting for transfers between devices: 44.5 us -> 40.8 us
  Pallas kernels: 23.7 us -> 26.6 us
  local copies, waits for them, and re-layouts: 6.26 us -> 4.18 us
  starting transfers between devices: 26.7 us -> 28.1 us
    ppermute x12, waiting for transfers between devices: 12.1 us -> 6.26 us  [along(): return lax.ppermute(x, 'dom', pairs)]
    ppermute x3, waiting for transfers between devices: 11.4 us -> 14.5 us  [straight_back(): return lax.ppermute(x, ('side', 'dom'), pairs)]
    pallas_call x11, Pallas kernels: 23.7 us -> 26.6 us  [call(): pl.pallas_call(kernel, out_shape=[jax.ShapeDtypeStruct(s, d) for s, d in...]
    ppermute x12, starting transfers between devices: 9.02 us -> 11.2 us  [along(): return lax.ppermute(x, 'dom', pairs)]
    unnamed x18, local copies, waits for them, and re-layouts: 4.82 us -> 2.74 us
    ppermute x5, starting transfers between devices: 7.8 us -> 6.63 us  [swap_rows(): return lax.ppermute(x, ('side', 'dom'), pairs)]
  transfers between devices with their start and end apart: 20 -> 20, of which waited for: 8 -> 7; matrix products, arithmetic and copies ran while one was open for 1% -> 1% of each run, Pallas kernels for 15% -> 16%
where the time goes in v12:
time: 104 us; the launch traced here: 103 us
  waiting for transfers between devices  40.8 us (39%)
  starting transfers between devices  28.1 us (27%)
  Pallas kernels  26.6 us (26%)
  local copies, waits for them, and re-layouts  4.18 us (4%)
  other arithmetic  1.96 us (2%)
  between operations  1.61 us (2%)
    pallas_call x11, Pallas kernels, call(): pl.pallas_call(kernel, out_shape=[jax.ShapeDtypeStruct(s, d) for s, d in...  26.6 us
    ppermute x5, waiting for transfers between devices, swap_rows(): return lax.ppermute(x, ('side', 'dom'), pairs)  20.1 us
    ppermute x3, waiting for transfers between devices, straight_back(): return lax.ppermute(x, ('side', 'dom'), pairs)  14.5 us
    ppermute x12, starting transfers between devices, along(): return lax.ppermute(x, 'dom', pairs)  11.2 us
    ppermute x3, starting transfers between devices, straight_back(): return lax.ppermute(x, ('side', 'dom'), pairs)  10.2 us
    ppermute x5, starting transfers between devices, swap_rows(): return lax.ppermute(x, ('side', 'dom'), pairs)  6.63 us
    ppermute x12, waiting for transfers between devices, along(): return lax.ppermute(x, 'dom', pairs)  6.26 us
    unnamed x18, local copies, waits for them, and re-layouts  2.74 us
  transfers between devices with their start and end apart: 20, of which 7 were waited for; matrix products, arithmetic and copies ran while one was open for 1% of the time, Pallas kernels for 16%

profile of v12, /device:TPU:7, one launch (start us, length us, event | category | flops | bytes accessed | tf_op | source)
XLA Modules:
  0.0 103.2 jit_solution(14442085827380607639)
XLA Ops:
  1.5 2.0 %broadcast_select_fusion = bf16[256,1024]{1,0:T(8,128)(2,1)} fusion(pred[256]{0:T(512)(128)(4,1)S(1)} %iota_compare_fusion, bf16[1,256,1024]{2,1,0:T(8,128)(2,1)} %param.10), kind=kLoop, calls=%fused_computation | loop fusion | flops 262144 | bytes 1048832 | tf_op jit(solution)/shard_map/jit(_where)/select_n | solution.py:277
  3.4 1.9 %collective-permute-start.8 = (bf16[256,1024]{1,0:T(8,128)(2,1)}, bf16[256,1024]{1,0:T(8,128)(2,1)S(1)}, u32[]{:S(2)}, u32[]{:S(2)}) collective-permute-start(bf16[256,1024]{1,0:T(8,128)(2,1)} %broadcast_select_fusion), channel_id=1, source_target_pairs={{0,68},{1,69},{2,70},{3,71},{4,72},{5,73},{6,74},{7,75},{8,76},{9,... | collective-permute-start | bytes 1572872 | tf_op jit(solution)/shard_map/ppermute | solution.py:43
  5.3 0.7 slice_bitcast_fusion
  6.2 2.2 %collective-permute-start.1 = (s32[1,128]{1,0:T(1,128)S(1)}, s32[1,128]{1,0:T(1,128)S(1)}, u32[]{:S(2)}, u32[]{:S(2)}) collective-permute-start(s32[1,128]{1,0:T(1,128)S(1)} %pad_bitcast_fusion), channel_id=1, source_target_pairs={{0,2},{1,3},{2,0},{3,1},{4,6},{5,7},{6,4},{7,5},{8,10},{9,11},{10,... | collective-permute-start | bytes 1544 | tf_op jit(solution)/shard_map/ppermute | solution.py:49
  8.7 1.4 %collective-permute-done.1.r_2_.r_3_ = s32[1,128]{1,0:T(1,128)S(1)} collective-permute-done((s32[1,128]{1,0:T(1,128)S(1)}, s32[1,128]{1,0:T(1,128)S(1)}, u32[]{:S(2)}, u32[]{:S(2)}) %collective-permute-start.1) | collective-permute-done | bytes 544 | tf_op jit(solution)/shard_map/ppermute | solution.py:49
  10.1 2.1 %collective-permute-done.r_1_.r_2_ = s32[1,128]{1,0:T(1,128)S(1)} collective-permute-done((s32[1,128]{1,0:T(1,128)S(1)}, s32[1,128]{1,0:T(1,128)S(1)}, u32[]{:S(2)}, u32[]{:S(2)}) %collective-permute-start) | collective-permute-done | bytes 544 | tf_op jit(solution)/shard_map/ppermute | solution.py:49
  12.2 3.7 %collective-permute-start.4 = (bf16[256,1024]{1,0:T(8,128)(2,1)}, bf16[256,1024]{1,0:T(8,128)(2,1)}, u32[]{:S(2)}, u32[]{:S(2)}) collective-permute-start(bf16[256,1024]{1,0:T(8,128)(2,1)} %broadcast_select_fusion), channel_id=1, source_target_pairs={{0,72},{1,73},{2,74},{3,75},{4,76},{5,77},{6,78},{7,79},{8,80},{9,... | collective-permute-start | bytes 1572872 | tf_op jit(solution)/shard_map/ppermute | solution.py:43
  15.9 6.1 %collective-permute-done.8.r_4_.r_2_ = bf16[256,1024]{1,0:T(8,128)(2,1)S(1)} collective-permute-done((bf16[256,1024]{1,0:T(8,128)(2,1)}, bf16[256,1024]{1,0:T(8,128)(2,1)S(1)}, u32[]{:S(2)}, u32[]{:S(2)}) %collective-permute-start.8) | collective-permute-done | bytes 524320 | tf_op jit(solution)/shard_map/ppermute | solution.py:43
  22.0 1.5 %shard_map.115 = (bf16[128,1024]{1,0:T(8,128)(2,1)}, bf16[128,1024]{1,0:T(8,128)(2,1)}, bf16[128,1024]{1,0:T(8,128)(2,1)}) custom-call(s32[1]{0:T(128)} %bitcast.1.r_0_.r_1_, s32[1,128]{1,0:T(1,128)S(1)} %collective-permute-done.r_1_.r_2_, s32[1,128]{1,0:T(1,128)S(1)} %collective-permute-done.1.r_2_.r_3_, s32[1,128]{1,0:T(1,128)S(1)} %collective-permute-done.2.r_3_.r_4_, ...), custom_call_target="tpu_custom_call" | custom-call | bytes 1048576 | tf_op jit(solution)/shard_map/pallas_call | solution.py:25
  23.7 2.1 %collective-permute-start.10 = (bf16[128,1024]{1,0:T(8,128)(2,1)}, bf16[128,1024]{1,0:T(8,128)(2,1)}, u32[]{:S(2)}, u32[]{:S(2)}) collective-permute-start(bf16[128,1024]{1,0:T(8,128)(2,1)} %get-tuple-element.41), channel_id=1, source_target_pairs={{0,2},{1,3},{2,0},{3,1},{4,6},{5,7},{6,4},{7,5},{8,10},{9,11},{10,... | collective-permute-start | bytes 786440 | tf_op jit(solution)/shard_map/ppermute | solution.py:49
  25.8 0.8 copy.14.r_1_.r_0_.r_2_
  26.6 8.8 %collective-permute-done.4.r_5_ = bf16[256,1024]{1,0:T(8,128)(2,1)} collective-permute-done((bf16[256,1024]{1,0:T(8,128)(2,1)}, bf16[256,1024]{1,0:T(8,128)(2,1)}, u32[]{:S(2)}, u32[]{:S(2)}) %collective-permute-start.4) | collective-permute-done | bytes 524320 | tf_op jit(solution)/shard_map/ppermute | solution.py:43
  35.4 1.3 %shard_map.113 = (bf16[128,1024]{1,0:T(8,128)(2,1)S(1)}, bf16[128,1024]{1,0:T(8,128)(2,1)S(1)}, bf16[128,1024]{1,0:T(8,128)(2,1)S(1)}) custom-call(s32[1]{0:T(128)} %bitcast.1.r_0_.r_1_, s32[1,128]{1,0:T(1,128)S(1)} %collective-permute-done.r_1_.r_2_, s32[1,128]{1,0:T(1,128)S(1)} %collective-permute-done.1.r_2_.r_3_, ...), custom_call_target="tpu_custom_call" | custom-call | bytes 1048576 | tf_op jit(solution)/shard_map/pallas_call | solution.py:25
  36.7 1.2 %collective-permute-start.6 = (bf16[128,1024]{1,0:T(8,128)(2,1)S(1)}, bf16[128,1024]{1,0:T(8,128)(2,1)S(1)}, u32[]{:S(2)}, u32[]{:S(2)}) collective-permute-start(bf16[128,1024]{1,0:T(8,128)(2,1)S(1)} %get-tuple-element.37), channel_id=1, source_target_pairs={{0,2},{1,3},{2,0},{3,1},{4,6},{5,7},{6,4},{7,5},{8,10},{9,11},{10,... | collective-permute-start | bytes 786440 | tf_op jit(solution)/shard_map/ppermute | solution.py:49
  37.9 1.8 %collective-permute-start.5 = (bf16[128,1024]{1,0:T(8,128)(2,1)S(1)}, bf16[128,1024]{1,0:T(8,128)(2,1)S(1)}, u32[]{:S(2)}, u32[]{:S(2)}) collective-permute-start(bf16[128,1024]{1,0:T(8,128)(2,1)S(1)} %get-tuple-element.36.r_5_), channel_id=1, source_target_pairs={{0,1},{1,2},{2,3},{3,0},{4,5},{5,6},{6,7},{7,4},{8,9},{9,10},{10,1... | collective-permute-start | bytes 786440 | tf_op jit(solution)/shard_map/ppermute | solution.py:49
  39.7 1.6 %copy-done.3 = bf16[1024,1024]{1,0:T(8,128)(2,1)S(1)} copy-done((bf16[1024,1024]{1,0:T(8,128)(2,1)S(1)}, bf16[1024,1024]{1,0:T(8,128)(2,1)}, u32[]{:S(2)}) %copy-start.3) | copy-done | bytes 2097176
  41.3 1.3 %shard_map.114 = (bf16[256,1024]{1,0:T(8,128)(2,1)S(1)}, bf16[1024,256]{1,0:T(8,128)(2,1)S(1)}, f32[256,1024]{1,0:T(8,128)S(1)}) custom-call(s32[1]{0:T(128)} %bitcast.1.r_0_.r_1_, s32[8,2]{1,0:T(8,128)S(1)} %copy.14.r_1_.r_0_.r_2_, s32[256,2048]{1,0:T(8,128)S(1)} %bitcast.21, bf16[256,1024]{1,0:T(8,128)(2,1)S(1)} %bitcast.20, ...), custom_call_target="tpu_custom_call" | custom-call | flops 536870912 | bytes 1048576 | tf_op jit(solution)/shard_map/pallas_call | solution.py:25
  43.5 5.3 %shard_map.116 = (bf16[640,2048]{1,0:T(8,128)(2,1)S(1)}, f32[256,2048]{1,0:T(8,128)S(1)}, f32[256,128]{1,0:T(8,128)S(1)}) custom-call(s32[8,2]{1,0:T(8,128)S(1)} %copy.14.r_1_.r_0_.r_2_, bf16[256,1024]{1,0:T(8,128)(2,1)} %collective-permute-done.3.r_4_.r_1_, bf16[256,1024]{1,0:T(8,128)(2,1)S(1)} %collective-permute-done.8.r_4_.r_2_, ...), custom_call_target="tpu_custom_call" | custom-call | flops 3355443200 | bytes 1048576 | tf_op jit(solution)/shard_map/pallas_call | solution.py:25
  48.9 2.7 %collective-permute-done.7.r_5_ = bf16[128,1024]{1,0:T(8,128)(2,1)S(1)} collective-permute-done((bf16[128,1024]{1,0:T(8,128)(2,1)S(1)}, bf16[128,1024]{1,0:T(8,128)(2,1)S(1)}, u32[]{:S(2)}, u32[]{:S(2)}) %collective-permute-start.7) | collective-permute-done | bytes 262176 | tf_op jit(solution)/shard_map/ppermute | solution.py:49
  51.6 8.9 %shard_map.117 = (bf16[256,1024]{1,0:T(8,128)(2,1)S(1)}, bf16[256,2048]{1,0:T(8,128)(2,1)S(1)}, f32[256,1024]{1,0:T(8,128)S(1)}, bf16[384,2048]{1,0:T(8,128)(2,1...) custom-call(s32[1]{0:T(128)} %bitcast.16.r_0_, ...), custom_call_target="tpu_custom_call" | custom-call | flops 8000000000 | bytes 1048576 | tf_op jit(solution)/shard_map/pallas_call | solution.py:25
  60.5 1.7 %collective-permute-start.13 = (bf16[128,1024]{1,0:T(8,128)(2,1)S(1)}, bf16[128,1024]{1,0:T(8,128)(2,1)S(1)}, u32[]{:S(2)}, u32[]{:S(2)}) collective-permute-start(bf16[128,1024]{1,0:T(8,128)(2,1)S(1)} %get-tuple-element.55), channel_id=1, source_target_pairs={{0,2},{1,3},{2,0},{3,1},{4,6},{5,7},{6,4},{7,5},{8,10},{9,11},{10,... | collective-permute-start | bytes 786440 | tf_op jit(solution)/shard_map/ppermute | solution.py:49
  62.7 1.0 collective-permute-start.12
  63.7 1.5 %collective-permute-start.15 = (bf16[128,1152]{1,0:T(8,128)(2,1)S(1)}, bf16[128,1152]{1,0:T(8,128)(2,1)S(1)}, u32[]{:S(2)}, u32[]{:S(2)}) collective-permute-start(bf16[128,1152]{1,0:T(8,128)(2,1)S(1)} %get-tuple-element.59), channel_id=1, source_target_pairs={{65,0},{66,1},{67,2},{72,3},{69,4},{70,5},{71,6},{76,7},{73,8},{74... | collective-permute-start | bytes 884744 | tf_op jit(solution)/shard_map/ppermute | solution.py:59
  65.3 2.2 %shard_map.118 = (bf16[128,1152]{1,0:T(8,128)(2,1)S(1)}, bf16[128,1152]{1,0:T(8,128)(2,1)S(1)}) custom-call(s32[1]{0:T(128)} %bitcast.1.r_0_.r_1_, s32[8,2]{1,0:T(8,128)S(1)} %copy.14.r_1_.r_0_.r_2_, bf16[1024,256]{1,0:T(8,128)(2,1)S(1)} %get-tuple-element.46.r_15_.r_2_.r_1_, bf16[256,2048]{1,0:T(8,128)(2,1)S(1)} %get-tuple-element.50.r_3_.r_2_, ...), custom_call_target="tpu_custom_call" | custom-call | flops 2000000000 | bytes 1048576 | tf_op jit(solution)/shard_map/pallas_call | solution.py:25
  67.4 2.1 %collective-permute-start.16 = (bf16[128,1152]{1,0:T(8,128)(2,1)S(1)}, bf16[128,1152]{1,0:T(8,128)(2,1)S(1)}, u32[]{:S(2)}, u32[]{:S(2)}) collective-permute-start(bf16[128,1152]{1,0:T(8,128)(2,1)S(1)} %get-tuple-element.53.r_5_), channel_id=1, source_target_pairs={{66,0},{67,1},{72,2},{73,3},{70,4},{71,5},{76,6},{77,7},{74,8},{75... | collective-permute-start | bytes 884744 | tf_op jit(solution)/shard_map/ppermute | solution.py:59
  69.6 2.2 %shard_map.119 = (bf16[256,1024]{1,0:T(8,128)(2,1)S(1)}, bf16[128,1024]{1,0:T(8,128)(2,1)S(1)}) custom-call(s32[8,2]{1,0:T(8,128)S(1)} %copy.14.r_1_.r_0_.r_2_, bf16[1024,256]{1,0:T(8,128)(2,1)S(1)} %get-tuple-element.46.r_15_.r_2_.r_1_, bf16[256,2048]{1,0:T(8,128)(2,1)S(1)} %get-tuple-element.50.r_3_.r_2_, ...), custom_call_target="tpu_custom_call" | custom-call | flops 2000000000 | bytes 1048576 | tf_op jit(solution)/shard_map/pallas_call | solution.py:25
  71.8 6.6 %collective-permute-start.17 = (bf16[128,1152]{1,0:T(8,128)(2,1)S(1)}, bf16[128,1152]{1,0:T(8,128)(2,1)S(1)}, u32[]{:S(2)}, u32[]{:S(2)}) collective-permute-start(bf16[128,1152]{1,0:T(8,128)(2,1)S(1)} %get-tuple-element.60), channel_id=1, source_target_pairs={{67,0},{72,1},{73,2},{74,3},{71,4},{76,5},{77,6},{78,7},{75,8},{80... | collective-permute-start | bytes 884744 | tf_op jit(solution)/shard_map/ppermute | solution.py:59
  79.0 0.9 shard_map.120._
  80.6 1.6 %shard_map.121 = (f32[256,1024]{1,0:T(8,128)S(1)}, bf16[256,1024]{1,0:T(8,128)(2,1)}) custom-call(s32[1]{0:T(128)} %bitcast.17.live_ref, bf16[256,1024]{1,0:T(8,128)(2,1)S(1)} %get-tuple-element.48.g_ref, bf16[1024,1024]{1,0:T(8,128)(2,1)S(1)} %copy-done.4, f32[256,1024]{1,0:T(8,128)S(1)} %get-tuple-element.49.pre_ref, bf16[256,1024]{1,0:T(8,128)(2,1)S(1)} %shard_map.120._), custom_call_target="tpu_custom_call" | custom-call | flops 2000000000 | bytes 1048576 | tf_op jit(solution)/shard_map/pallas_call | solution.py:25
  82.2 14.5 %collective-permute-done.15.c1 = bf16[128,1152]{1,0:T(8,128)(2,1)S(1)} collective-permute-done((bf16[128,1152]{1,0:T(8,128)(2,1)S(1)}, bf16[128,1152]{1,0:T(8,128)(2,1)S(1)}, u32[]{:S(2)}, u32[]{:S(2)}) %collective-permute-start.15) | collective-permute-done | bytes 294944 | tf_op jit(solution)/shard_map/ppermute | solution.py:59
  97.0 5.2 %collective-permute-done.19.below_ref = bf16[256,1024]{1,0:T(8,128)(2,1)S(1)} collective-permute-done((bf16[256,1024]{1,0:T(8,128)(2,1)S(1)}, bf16[256,1024]{1,0:T(8,128)(2,1)S(1)}, u32[]{:S(2)}, u32[]{:S(2)}) %collective-permute-start.19) | collective-permute-done | bytes 524320 | tf_op jit(solution)/shard_map/ppermute | solution.py:43
  102.2 1.0 shard_map.123
  (42 shorter events, 3.7 us)
Async XLA Ops:
  0.6 39.1 %copy-start.1 = (bf16[1,256,1024]{2,1,0:T(8,128)(2,1)S(1)}, bf16[1,256,1024]{2,1,0:T(8,128)(2,1)}, u32[]{:S(2)}) copy-start(bf16[1,256,1024]{2,1,0:T(8,128)(2,1)} %param.10) | copy-start | bytes 1572868
  0.6 39.1 %copy-start.2 = (s32[1,256,2048]{2,1,0:T(8,128)S(1)}, s32[1,256,2048]{2,1,0:T(8,128)}, u32[]{:S(2)}) copy-start(s32[1,256,2048]{2,1,0:T(8,128)} %param.13) | copy-start | bytes 6291460
  3.4 18.6 %collective-permute-start.8 = (bf16[256,1024]{1,0:T(8,128)(2,1)}, bf16[256,1024]{1,0:T(8,128)(2,1)S(1)}, u32[]{:S(2)}, u32[]{:S(2)}) collective-permute-start(bf16[256,1024]{1,0:T(8,128)(2,1)} %broadcast_select_fusion), channel_id=1, source_target_pairs={{0,68},{1,69},{2,70},{3,71},{4,72},{5,73},{6,74},{7,75},{8,76},{9,... | collective-permute-start | bytes 1572872 | tf_op jit(solution)/shard_map/ppermute | solution.py:43
  6.0 2.7 %collective-permute-start.2 = (s32[1,128]{1,0:T(1,128)S(1)}, s32[1,128]{1,0:T(1,128)S(1)}, u32[]{:S(2)}, u32[]{:S(2)}) collective-permute-start(s32[1,128]{1,0:T(1,128)S(1)} %pad_bitcast_fusion), channel_id=1, source_target_pairs={{0,1},{1,2},{2,3},{3,0},{4,5},{5,6},{6,7},{7,4},{8,9},{9,10},{10,1... | collective-permute-start | bytes 1544 | tf_op jit(solution)/shard_map/ppermute | solution.py:49
  6.2 3.9 %collective-permute-start.1 = (s32[1,128]{1,0:T(1,128)S(1)}, s32[1,128]{1,0:T(1,128)S(1)}, u32[]{:S(2)}, u32[]{:S(2)}) collective-permute-start(s32[1,128]{1,0:T(1,128)S(1)} %pad_bitcast_fusion), channel_id=1, source_target_pairs={{0,2},{1,3},{2,0},{3,1},{4,6},{5,7},{6,4},{7,5},{8,10},{9,11},{10,... | collective-permute-start | bytes 1544 | tf_op jit(solution)/shard_map/ppermute | solution.py:49
  8.3 3.9 %collective-permute-start = (s32[1,128]{1,0:T(1,128)S(1)}, s32[1,128]{1,0:T(1,128)S(1)}, u32[]{:S(2)}, u32[]{:S(2)}) collective-permute-start(s32[1,128]{1,0:T(1,128)S(1)} %pad_bitcast_fusion), channel_id=1, source_target_pairs={{0,3},{1,0},{2,1},{3,2},{4,7},{5,4},{6,5},{7,6},{8,11},{9,8},{10,9... | collective-permute-start | bytes 1544 | tf_op jit(solution)/shard_map/ppermute | solution.py:49
  8.3 18.3 %collective-permute-start.3 = (bf16[256,1024]{1,0:T(8,128)(2,1)}, bf16[256,1024]{1,0:T(8,128)(2,1)}, u32[]{:S(2)}, u32[]{:S(2)}) collective-permute-start(bf16[256,1024]{1,0:T(8,128)(2,1)} %broadcast_select_fusion), channel_id=1, source_target_pairs={{0,64},{1,65},{2,66},{3,67},{4,68},{5,69},{6,70},{7,71},{8,72},{9,... | collective-permute-start | bytes 1572872 | tf_op jit(solution)/shard_map/ppermute | solution.py:43
  12.2 23.2 %collective-permute-start.4 = (bf16[256,1024]{1,0:T(8,128)(2,1)}, bf16[256,1024]{1,0:T(8,128)(2,1)}, u32[]{:S(2)}, u32[]{:S(2)}) collective-permute-start(bf16[256,1024]{1,0:T(8,128)(2,1)} %broadcast_select_fusion), channel_id=1, source_target_pairs={{0,72},{1,73},{2,74},{3,75},{4,76},{5,77},{6,78},{7,79},{8,80},{9,... | collective-permute-start | bytes 1572872 | tf_op jit(solution)/shard_map/ppermute | solution.py:43
  23.5 19.2 %collective-permute-start.9 = (bf16[128,1024]{1,0:T(8,128)(2,1)}, bf16[128,1024]{1,0:T(8,128)(2,1)S(1)}, u32[]{:S(2)}, u32[]{:S(2)}) collective-permute-start(bf16[128,1024]{1,0:T(8,128)(2,1)} %get-tuple-element.40), channel_id=1, source_target_pairs={{0,1},{1,2},{2,3},{3,0},{4,5},{5,6},{6,7},{7,4},{8,9},{9,10},{10,1... | collective-permute-start | bytes 786440 | tf_op jit(solution)/shard_map/ppermute | solution.py:49
  23.7 19.2 %collective-permute-start.10 = (bf16[128,1024]{1,0:T(8,128)(2,1)}, bf16[128,1024]{1,0:T(8,128)(2,1)}, u32[]{:S(2)}, u32[]{:S(2)}) collective-permute-start(bf16[128,1024]{1,0:T(8,128)(2,1)} %get-tuple-element.41), channel_id=1, source_target_pairs={{0,2},{1,3},{2,0},{3,1},{4,6},{5,7},{6,4},{7,5},{8,10},{9,11},{10,... | collective-permute-start | bytes 786440 | tf_op jit(solution)/shard_map/ppermute | solution.py:49
  25.8 17.1 %collective-permute-start.11 = (bf16[128,1024]{1,0:T(8,128)(2,1)}, bf16[128,1024]{1,0:T(8,128)(2,1)}, u32[]{:S(2)}, u32[]{:S(2)}) collective-permute-start(bf16[128,1024]{1,0:T(8,128)(2,1)} %get-tuple-element.42), channel_id=1, source_target_pairs={{0,3},{1,0},{2,1},{3,2},{4,7},{5,4},{6,5},{7,6},{8,11},{9,8},{10,9... | collective-permute-start | bytes 786440 | tf_op jit(solution)/shard_map/ppermute | solution.py:49
  36.7 12.2 %collective-permute-start.6 = (bf16[128,1024]{1,0:T(8,128)(2,1)S(1)}, bf16[128,1024]{1,0:T(8,128)(2,1)S(1)}, u32[]{:S(2)}, u32[]{:S(2)}) collective-permute-start(bf16[128,1024]{1,0:T(8,128)(2,1)S(1)} %get-tuple-element.37), channel_id=1, source_target_pairs={{0,2},{1,3},{2,0},{3,1},{4,6},{5,7},{6,4},{7,5},{8,10},{9,11},{10,... | collective-permute-start | bytes 786440 | tf_op jit(solution)/shard_map/ppermute | solution.py:49
  37.9 13.7 %collective-permute-start.5 = (bf16[128,1024]{1,0:T(8,128)(2,1)S(1)}, bf16[128,1024]{1,0:T(8,128)(2,1)S(1)}, u32[]{:S(2)}, u32[]{:S(2)}) collective-permute-start(bf16[128,1024]{1,0:T(8,128)(2,1)S(1)} %get-tuple-element.36.r_5_), channel_id=1, source_target_pairs={{0,1},{1,2},{2,3},{3,0},{4,5},{5,6},{6,7},{7,4},{8,9},{9,10},{10,1... | collective-permute-start | bytes 786440 | tf_op jit(solution)/shard_map/ppermute | solution.py:49
  39.7 1.6 %copy-start.3 = (bf16[1024,1024]{1,0:T(8,128)(2,1)S(1)}, bf16[1024,1024]{1,0:T(8,128)(2,1)}, u32[]{:S(2)}) copy-start(bf16[1024,1024]{1,0:T(8,128)(2,1)} %sw_ref.1) | copy-start | bytes 6291460
  41.3 2.2 %copy-start = (bf16[1024,2048]{1,0:T(8,128)(2,1)S(1)}, bf16[1024,2048]{1,0:T(8,128)(2,1)}, u32[]{:S(2)}) copy-start(bf16[1024,2048]{1,0:T(8,128)(2,1)} %r_4_.3) | copy-start | bytes 12582916
  41.3 2.2 %copy-start.7 = (f32[2048]{0:T(1024)S(1)}, f32[2048]{0:T(1024)}, u32[]{:S(2)}) copy-start(f32[2048]{0:T(1024)} %param.16) | copy-start | bytes 24580
  42.7 8.9 %collective-permute-start.7 = (bf16[128,1024]{1,0:T(8,128)(2,1)S(1)}, bf16[128,1024]{1,0:T(8,128)(2,1)S(1)}, u32[]{:S(2)}, u32[]{:S(2)}) collective-permute-start(bf16[128,1024]{1,0:T(8,128)(2,1)S(1)} %get-tuple-element.38), channel_id=1, source_target_pairs={{0,3},{1,0},{2,1},{3,2},{4,7},{5,4},{6,5},{7,6},{8,11},{9,8},{10,9... | collective-permute-start | bytes 786440 | tf_op jit(solution)/shard_map/ppermute | solution.py:49
  43.5 8.1 %copy-start.5 = (bf16[2048,1024]{1,0:T(8,128)(2,1)S(1)}, bf16[2048,1024]{1,0:T(8,128)(2,1)}, u32[]{:S(2)}) copy-start(bf16[2048,1024]{1,0:T(8,128)(2,1)} %r_13_.1) | copy-start | bytes 12582916
  43.5 8.1 %copy-start.6 = (bf16[1,256,1024]{2,1,0:T(8,128)(2,1)S(1)}, bf16[1,256,1024]{2,1,0:T(8,128)(2,1)}, u32[]{:S(2)}) copy-start(bf16[1,256,1024]{2,1,0:T(8,128)(2,1)} %param.14) | copy-start | bytes 1572868
  43.5 8.1 %copy-start.8 = (f32[1024]{0:T(1024)S(1)}, f32[1024]{0:T(1024)}, u32[]{:S(2)}) copy-start(f32[1024]{0:T(1024)} %param.19) | copy-start | bytes 12292
  60.5 11.3 %collective-permute-start.13 = (bf16[128,1024]{1,0:T(8,128)(2,1)S(1)}, bf16[128,1024]{1,0:T(8,128)(2,1)S(1)}, u32[]{:S(2)}, u32[]{:S(2)}) collective-permute-start(bf16[128,1024]{1,0:T(8,128)(2,1)S(1)} %get-tuple-element.55), channel_id=1, source_target_pairs={{0,2},{1,3},{2,0},{3,1},{4,6},{5,7},{6,4},{7,5},{8,10},{9,11},{10,... | collective-permute-start | bytes 786440 | tf_op jit(solution)/shard_map/ppermute | solution.py:49
  62.3 16.1 %collective-permute-start.14 = (bf16[128,1024]{1,0:T(8,128)(2,1)S(1)}, bf16[128,1024]{1,0:T(8,128)(2,1)S(1)}, u32[]{:S(2)}, u32[]{:S(2)}) collective-permute-start(bf16[128,1024]{1,0:T(8,128)(2,1)S(1)} %get-tuple-element.56), channel_id=1, source_target_pairs={{0,1},{1,2},{2,3},{3,0},{4,5},{5,6},{6,7},{7,4},{8,9},{9,10},{10,1... | collective-permute-start | bytes 786440 | tf_op jit(solution)/shard_map/ppermute | solution.py:49
  62.7 16.3 %collective-permute-start.12 = (bf16[128,1024]{1,0:T(8,128)(2,1)S(1)}, bf16[128,1024]{1,0:T(8,128)(2,1)S(1)}, u32[]{:S(2)}, u32[]{:S(2)}) collective-permute-start(bf16[128,1024]{1,0:T(8,128)(2,1)S(1)} %get-tuple-element.52.r_6_), channel_id=1, source_target_pairs={{0,3},{1,0},{2,1},{3,2},{4,7},{5,4},{6,5},{7,6},{8,11},{9,8},{10,9... | collective-permute-start | bytes 786440 | tf_op jit(solution)/shard_map/ppermute | solution.py:49
  63.7 32.9 %collective-permute-start.15 = (bf16[128,1152]{1,0:T(8,128)(2,1)S(1)}, bf16[128,1152]{1,0:T(8,128)(2,1)S(1)}, u32[]{:S(2)}, u32[]{:S(2)}) collective-permute-start(bf16[128,1152]{1,0:T(8,128)(2,1)S(1)} %get-tuple-element.59), channel_id=1, source_target_pairs={{65,0},{66,1},{67,2},{72,3},{69,4},{70,5},{71,6},{76,7},{73,8},{74... | collective-permute-start | bytes 884744 | tf_op jit(solution)/shard_map/ppermute | solution.py:59
  67.4 29.2 %collective-permute-start.16 = (bf16[128,1152]{1,0:T(8,128)(2,1)S(1)}, bf16[128,1152]{1,0:T(8,128)(2,1)S(1)}, u32[]{:S(2)}, u32[]{:S(2)}) collective-permute-start(bf16[128,1152]{1,0:T(8,128)(2,1)S(1)} %get-tuple-element.53.r_5_), channel_id=1, source_target_pairs={{66,0},{67,1},{72,2},{73,3},{70,4},{71,5},{76,6},{77,7},{74,8},{75... | collective-permute-start | bytes 884744 | tf_op jit(solution)/shard_map/ppermute | solution.py:59
  71.8 24.8 %collective-permute-start.17 = (bf16[128,1152]{1,0:T(8,128)(2,1)S(1)}, bf16[128,1152]{1,0:T(8,128)(2,1)S(1)}, u32[]{:S(2)}, u32[]{:S(2)}) collective-permute-start(bf16[128,1152]{1,0:T(8,128)(2,1)S(1)} %get-tuple-element.60), channel_id=1, source_target_pairs={{67,0},{72,1},{73,2},{74,3},{71,4},{76,5},{77,6},{78,7},{75,8},{80... | collective-permute-start | bytes 884744 | tf_op jit(solution)/shard_map/ppermute | solution.py:59
  78.4 18.6 %collective-permute-start.18 = (bf16[256,1024]{1,0:T(8,128)(2,1)S(1)}, bf16[256,1024]{1,0:T(8,128)(2,1)S(1)}, u32[]{:S(2)}, u32[]{:S(2)}) collective-permute-start(bf16[256,1024]{1,0:T(8,128)(2,1)S(1)} %get-tuple-element.61), channel_id=1, source_target_pairs={{0,64},{1,65},{2,66},{3,67},{4,68},{5,69},{6,70},{7,71},{8,72},{9,... | collective-permute-start | bytes 1572872 | tf_op jit(solution)/shard_map/ppermute | solution.py:43
  79.0 1.6 %copy-start.4 = (bf16[1024,1024]{1,0:T(8,128)(2,1)S(1)}, bf16[1024,1024]{1,0:T(8,128)(2,1)}, u32[]{:S(2)}) copy-start(bf16[1024,1024]{1,0:T(8,128)(2,1)} %sw_ref.1) | copy-start | bytes 6291460
  79.9 22.3 %collective-permute-start.19 = (bf16[256,1024]{1,0:T(8,128)(2,1)S(1)}, bf16[256,1024]{1,0:T(8,128)(2,1)S(1)}, u32[]{:S(2)}, u32[]{:S(2)}) collective-permute-start(bf16[256,1024]{1,0:T(8,128)(2,1)S(1)} %shard_map.120._), channel_id=1, source_target_pairs={{0,124},{1,125},{2,126},{3,127},{4,64},{5,65},{6,66},{7,67},{8,68}... | collective-permute-start | bytes 1572872 | tf_op jit(solution)/shard_map/ppermute | solution.py:43

commit v13 on v12

--- a/solution.py
+++ b/solution.py
@@ -56,6 +56,26 @@
         for j in range(count):
             to = j + d if j % LINE + d < LINE else j + d + LINE
             pairs.append(((1 - s) * count + to % count, s * count + j))
+    return lax.ppermute(x, ("side", "dom"), pairs)
+
+
+def two_back(x):
+    count = lax.axis_size("dom")
+    pairs = [
+        (s * count + j, (1 - s) * count + (j - 2 * LINE) % count)
+        for s in range(2)
+        for j in range(0, count, LINE)
+    ]
+    return lax.ppermute(x, ("side", "dom"), pairs)
+
+
+def turn(x):
+    count = lax.axis_size("dom")
+    pairs = []
+    for s in range(2):
+        for j in range(count):
+            to = (1 - s) * count + j - 1 if j % LINE else s * count + j + LINE - 1
+            pairs.append((s * count + j, to))
     return lax.ppermute(x, ("side", "dom"), pairs)
 
 
@@ -246,6 +266,16 @@
     out_ref[...] = total[...].astype(BF16)
 
 
+def join_kernel(place_ref, mine_ref, sent_ref, out_ref):
+    @pl.when(place_ref[0] == 0)
+    def _():
+        out_ref[...] = sent_ref[...]
+
+    @pl.when(place_ref[0] > 0)
+    def _():
+        out_ref[...] = mine_ref[...]
+
+
 def place_kernel(gself_ref, c1, c2, c3, total_ref):
     block, width = c1.shape[0], gself_ref.shape[1]
     first, second = gself_ref[:block, :], gself_ref[block:, :]
@@ -338,7 +368,14 @@
         scratch=[pltpu.VMEM((2 * block, hidden), BF16)],
         flops=2 * MICROSECOND,
     )
-    back_far = [straight_back(b, d) for d, b in zip(steps, (far_first, *far_back))]
+    (joined,) = call(
+        join_kernel,
+        [((block, width + 128), BF16)],
+        (place, far_first, two_back(far_first)),
+        [SMEM] + [VMEM] * 2,
+    )
+    back_far = [turn(joined)]
+    back_far += [straight_back(b, d) for d, b in zip(steps[1:], far_back)]
     own_same, own_below = call(
         lambda *r: back_own_kernel(block, *r),
         [two, one],

time: 104 us -> 101 us (0.971)
  the two profiles are of different devices: /device:TPU:7 before, /device:TPU:1 now
where the time goes in v13:
time: 101 us; the launch traced here: 100 us
  starting transfers between devices  42.5 us (42%)
  Pallas kernels  26.6 us (26%)
  waiting for transfers between devices  24.5 us (24%)
  local copies, waits for them, and re-layouts  3.07 us (3%)
  other arithmetic  1.96 us (2%)
  between operations  1.64 us (2%)
    pallas_call x12, Pallas kernels, call(): pl.pallas_call(kernel, out_shape=[jax.ShapeDtypeStruct(s, d) for s, d in...  26.6 us
    ppermute x12, starting transfers between devices, along(): return lax.ppermute(x, 'dom', pairs)  19.5 us
    ppermute x5, waiting for transfers between devices, swap_rows(): return lax.ppermute(x, ('side', 'dom'), pairs)  17.6 us
    ppermute x5, starting transfers between devices, swap_rows(): return lax.ppermute(x, ('side', 'dom'), pairs)  12.2 us
    ppermute x1, starting transfers between devices, two_back(): return lax.ppermute(x, ('side', 'dom'), pairs)  7.74 us
    ppermute x2, waiting for transfers between devices, straight_back(): return lax.ppermute(x, ('side', 'dom'), pairs)  4.65 us
    ppermute x1, starting transfers between devices, turn(): return lax.ppermute(x, ('side', 'dom'), pairs)  2.65 us
    ppermute x12, waiting for transfers between devices, along(): return lax.ppermute(x, 'dom', pairs)  2.23 us
  transfers between devices with their start and end apart: 21, of which 7 were waited for; matrix products, arithmetic and copies ran while one was open for 1% of the time, Pallas kernels for 17%

profile of v13, /device:TPU:1, one launch (start us, length us, event | category | flops | bytes accessed | tf_op | source)
XLA Modules:
  0.0 100.3 jit_solution(4850795404453858879)
XLA Ops:
  1.5 2.0 %broadcast_select_fusion = bf16[256,1024]{1,0:T(8,128)(2,1)} fusion(pred[256]{0:T(512)(128)(4,1)S(1)} %iota_compare_fusion, bf16[1,256,1024]{2,1,0:T(8,128)(2,1)} %param.10), kind=kLoop, calls=%fused_computation | loop fusion | flops 262144 | bytes 1048832 | tf_op jit(solution)/shard_map/jit(_where)/select_n | solution.py:307
  3.4 2.7 %collective-permute-start.8 = (bf16[256,1024]{1,0:T(8,128)(2,1)}, bf16[256,1024]{1,0:T(8,128)(2,1)S(1)}, u32[]{:S(2)}, u32[]{:S(2)}) collective-permute-start(bf16[256,1024]{1,0:T(8,128)(2,1)} %broadcast_select_fusion), channel_id=1, source_target_pairs={{0,68},{1,69},{2,70},{3,71},{4,72},{5,73},{6,74},{7,75},{8,76},{9,... | collective-permute-start | bytes 1572872 | tf_op jit(solution)/shard_map/ppermute | solution.py:43
  6.8 1.2 %collective-permute-start.2 = (s32[1,128]{1,0:T(1,128)S(1)}, s32[1,128]{1,0:T(1,128)S(1)}, u32[]{:S(2)}, u32[]{:S(2)}) collective-permute-start(s32[1,128]{1,0:T(1,128)S(1)} %pad_bitcast_fusion), channel_id=1, source_target_pairs={{0,1},{1,2},{2,3},{3,0},{4,5},{5,6},{6,7},{7,4},{8,9},{9,10},{10,1... | collective-permute-start | bytes 1544 | tf_op jit(solution)/shard_map/ppermute | solution.py:49
  8.0 2.5 %collective-permute-start.1 = (s32[1,128]{1,0:T(1,128)S(1)}, s32[1,128]{1,0:T(1,128)S(1)}, u32[]{:S(2)}, u32[]{:S(2)}) collective-permute-start(s32[1,128]{1,0:T(1,128)S(1)} %pad_bitcast_fusion), channel_id=1, source_target_pairs={{0,2},{1,3},{2,0},{3,1},{4,6},{5,7},{6,4},{7,5},{8,10},{9,11},{10,... | collective-permute-start | bytes 1544 | tf_op jit(solution)/shard_map/ppermute | solution.py:49
  10.5 1.2 %collective-permute-start = (s32[1,128]{1,0:T(1,128)S(1)}, s32[1,128]{1,0:T(1,128)S(1)}, u32[]{:S(2)}, u32[]{:S(2)}) collective-permute-start(s32[1,128]{1,0:T(1,128)S(1)} %pad_bitcast_fusion), channel_id=1, source_target_pairs={{0,3},{1,0},{2,1},{3,2},{4,7},{5,4},{6,5},{7,6},{8,11},{9,8},{10,9... | collective-permute-start | bytes 1544 | tf_op jit(solution)/shard_map/ppermute | solution.py:49
  13.2 3.7 %collective-permute-start.4 = (bf16[256,1024]{1,0:T(8,128)(2,1)}, bf16[256,1024]{1,0:T(8,128)(2,1)}, u32[]{:S(2)}, u32[]{:S(2)}) collective-permute-start(bf16[256,1024]{1,0:T(8,128)(2,1)} %broadcast_select_fusion), channel_id=1, source_target_pairs={{0,72},{1,73},{2,74},{3,75},{4,76},{5,77},{6,78},{7,79},{8,80},{9,... | collective-permute-start | bytes 1572872 | tf_op jit(solution)/shard_map/ppermute | solution.py:43
  16.9 6.0 %collective-permute-done.8.r_4_.r_2_ = bf16[256,1024]{1,0:T(8,128)(2,1)S(1)} collective-permute-done((bf16[256,1024]{1,0:T(8,128)(2,1)}, bf16[256,1024]{1,0:T(8,128)(2,1)S(1)}, u32[]{:S(2)}, u32[]{:S(2)}) %collective-permute-start.8) | collective-permute-done | bytes 524320 | tf_op jit(solution)/shard_map/ppermute | solution.py:43
  22.8 1.5 %shard_map.115 = (bf16[128,1024]{1,0:T(8,128)(2,1)}, bf16[128,1024]{1,0:T(8,128)(2,1)}, bf16[128,1024]{1,0:T(8,128)(2,1)}) custom-call(s32[1]{0:T(128)} %bitcast.1.r_0_.r_1_.place_ref, s32[1,128]{1,0:T(1,128)S(1)} %collective-permute-done.r_1_.r_2_, s32[1,128]{1,0:T(1,128)S(1)} %collective-permute-done.1.r_2_.r_3_, ...), custom_call_target="tpu_custom_call" | custom-call | bytes 1048576 | tf_op jit(solution)/shard_map/pallas_call | solution.py:25
  24.3 1.2 %collective-permute-start.9 = (bf16[128,1024]{1,0:T(8,128)(2,1)}, bf16[128,1024]{1,0:T(8,128)(2,1)S(1)}, u32[]{:S(2)}, u32[]{:S(2)}) collective-permute-start(bf16[128,1024]{1,0:T(8,128)(2,1)} %get-tuple-element.40), channel_id=1, source_target_pairs={{0,1},{1,2},{2,3},{3,0},{4,5},{5,6},{6,7},{7,4},{8,9},{9,10},{10,1... | collective-permute-start | bytes 786440 | tf_op jit(solution)/shard_map/ppermute | solution.py:49
  25.5 2.5 %collective-permute-start.10 = (bf16[128,1024]{1,0:T(8,128)(2,1)}, bf16[128,1024]{1,0:T(8,128)(2,1)}, u32[]{:S(2)}, u32[]{:S(2)}) collective-permute-start(bf16[128,1024]{1,0:T(8,128)(2,1)} %get-tuple-element.41), channel_id=1, source_target_pairs={{0,2},{1,3},{2,0},{3,1},{4,6},{5,7},{6,4},{7,5},{8,10},{9,11},{10,... | collective-permute-start | bytes 786440 | tf_op jit(solution)/shard_map/ppermute | solution.py:49
  28.0 1.2 %collective-permute-start.11 = (bf16[128,1024]{1,0:T(8,128)(2,1)}, bf16[128,1024]{1,0:T(8,128)(2,1)}, u32[]{:S(2)}, u32[]{:S(2)}) collective-permute-start(bf16[128,1024]{1,0:T(8,128)(2,1)} %get-tuple-element.42), channel_id=1, source_target_pairs={{0,3},{1,0},{2,1},{3,2},{4,7},{5,4},{6,5},{7,6},{8,11},{9,8},{10,9... | collective-permute-start | bytes 786440 | tf_op jit(solution)/shard_map/ppermute | solution.py:49
  29.9 6.3 %collective-permute-done.4.r_5_ = bf16[256,1024]{1,0:T(8,128)(2,1)} collective-permute-done((bf16[256,1024]{1,0:T(8,128)(2,1)}, bf16[256,1024]{1,0:T(8,128)(2,1)}, u32[]{:S(2)}, u32[]{:S(2)}) %collective-permute-start.4) | collective-permute-done | bytes 524320 | tf_op jit(solution)/shard_map/ppermute | solution.py:43
  36.2 1.3 %shard_map.113 = (bf16[128,1024]{1,0:T(8,128)(2,1)S(1)}, bf16[128,1024]{1,0:T(8,128)(2,1)S(1)}, bf16[128,1024]{1,0:T(8,128)(2,1)S(1)}) custom-call(s32[1]{0:T(128)} %bitcast.1.r_0_.r_1_.place_ref, s32[1,128]{1,0:T(1,128)S(1)} %collective-permute-done.r_1_.r_2_, s32[1,128]{1,0:T(1,128)S(1)} %collective-permute-done.1.r_2_.r_3_, ...), custom_call_target="tpu_custom_call" | custom-call | bytes 1048576 | tf_op jit(solution)/shard_map/pallas_call | solution.py:25
  37.5 2.8 %collective-permute-start.6 = (bf16[128,1024]{1,0:T(8,128)(2,1)S(1)}, bf16[128,1024]{1,0:T(8,128)(2,1)S(1)}, u32[]{:S(2)}, u32[]{:S(2)}) collective-permute-start(bf16[128,1024]{1,0:T(8,128)(2,1)S(1)} %get-tuple-element.37), channel_id=1, source_target_pairs={{0,2},{1,3},{2,0},{3,1},{4,6},{5,7},{6,4},{7,5},{8,10},{9,11},{10,... | collective-permute-start | bytes 786440 | tf_op jit(solution)/shard_map/ppermute | solution.py:49
  40.7 1.6 %copy-done.3 = bf16[1024,1024]{1,0:T(8,128)(2,1)S(1)} copy-done((bf16[1024,1024]{1,0:T(8,128)(2,1)S(1)}, bf16[1024,1024]{1,0:T(8,128)(2,1)}, u32[]{:S(2)}) %copy-start.3) | copy-done | bytes 2097176
  42.3 1.3 %shard_map.114 = (bf16[256,1024]{1,0:T(8,128)(2,1)S(1)}, bf16[1024,256]{1,0:T(8,128)(2,1)S(1)}, f32[256,1024]{1,0:T(8,128)S(1)}) custom-call(s32[1]{0:T(128)} %bitcast.1.r_0_.r_1_.place_ref, s32[8,2]{1,0:T(8,128)S(1)} %copy.14.r_1_.r_0_.r_2_, s32[256,2048]{1,0:T(8,128)S(1)} %bitcast.21, bf16[256,1024]{1,0:T(8,128)(2,1)S(1)} %bitcast.20, ...), custom_call_target="tpu_custom_call" | custom-call | flops 536870912 | bytes 1048576 | tf_op jit(solution)/shard_map/pallas_call | solution.py:25
  43.6 2.6 %collective-permute-start.7 = (bf16[128,1024]{1,0:T(8,128)(2,1)S(1)}, bf16[128,1024]{1,0:T(8,128)(2,1)S(1)}, u32[]{:S(2)}, u32[]{:S(2)}) collective-permute-start(bf16[128,1024]{1,0:T(8,128)(2,1)S(1)} %get-tuple-element.38), channel_id=1, source_target_pairs={{0,3},{1,0},{2,1},{3,2},{4,7},{5,4},{6,5},{7,6},{8,11},{9,8},{10,9... | collective-permute-start | bytes 786440 | tf_op jit(solution)/shard_map/ppermute | solution.py:49
  46.3 5.3 %shard_map.116 = (bf16[640,2048]{1,0:T(8,128)(2,1)S(1)}, f32[256,2048]{1,0:T(8,128)S(1)}, f32[256,128]{1,0:T(8,128)S(1)}) custom-call(s32[8,2]{1,0:T(8,128)S(1)} %copy.14.r_1_.r_0_.r_2_, bf16[256,1024]{1,0:T(8,128)(2,1)} %collective-permute-done.3.r_4_.r_1_, bf16[256,1024]{1,0:T(8,128)(2,1)S(1)} %collective-permute-done.8.r_4_.r_2_, ...), custom_call_target="tpu_custom_call" | custom-call | flops 3355443200 | bytes 1048576 | tf_op jit(solution)/shard_map/pallas_call | solution.py:25
  53.0 8.9 %shard_map.117 = (bf16[256,1024]{1,0:T(8,128)(2,1)S(1)}, bf16[256,2048]{1,0:T(8,128)(2,1)S(1)}, f32[256,1024]{1,0:T(8,128)S(1)}, bf16[384,2048]{1,0:T(8,128)(2,1...) custom-call(s32[1]{0:T(128)} %bitcast.16.r_0_, ...), custom_call_target="tpu_custom_call" | custom-call | flops 8000000000 | bytes 1048576 | tf_op jit(solution)/shard_map/pallas_call | solution.py:25
  61.9 1.5 %collective-permute-start.13 = (bf16[128,1024]{1,0:T(8,128)(2,1)S(1)}, bf16[128,1024]{1,0:T(8,128)(2,1)S(1)}, u32[]{:S(2)}, u32[]{:S(2)}) collective-permute-start(bf16[128,1024]{1,0:T(8,128)(2,1)S(1)} %get-tuple-element.55), channel_id=1, source_target_pairs={{0,2},{1,3},{2,0},{3,1},{4,6},{5,7},{6,4},{7,5},{8,10},{9,11},{10,... | collective-permute-start | bytes 786440 | tf_op jit(solution)/shard_map/ppermute | solution.py:49
  63.3 1.1 %collective-permute-start.14 = (bf16[128,1024]{1,0:T(8,128)(2,1)S(1)}, bf16[128,1024]{1,0:T(8,128)(2,1)S(1)}, u32[]{:S(2)}, u32[]{:S(2)}) collective-permute-start(bf16[128,1024]{1,0:T(8,128)(2,1)S(1)} %get-tuple-element.56), channel_id=1, source_target_pairs={{0,1},{1,2},{2,3},{3,0},{4,5},{5,6},{6,7},{7,4},{8,9},{9,10},{10,1... | collective-permute-start | bytes 786440 | tf_op jit(solution)/shard_map/ppermute | solution.py:49
  64.5 1.5 %collective-permute-start.12 = (bf16[128,1024]{1,0:T(8,128)(2,1)S(1)}, bf16[128,1024]{1,0:T(8,128)(2,1)S(1)}, u32[]{:S(2)}, u32[]{:S(2)}) collective-permute-start(bf16[128,1024]{1,0:T(8,128)(2,1)S(1)} %get-tuple-element.52.r_6_), channel_id=1, source_target_pairs={{0,3},{1,0},{2,1},{3,2},{4,7},{5,4},{6,5},{7,6},{8,11},{9,8},{10,9... | collective-permute-start | bytes 786440 | tf_op jit(solution)/shard_map/ppermute | solution.py:49
  66.0 7.7 %collective-permute-start.15 = (bf16[128,1152]{1,0:T(8,128)(2,1)S(1)}, bf16[128,1152]{1,0:T(8,128)(2,1)S(1)}, u32[]{:S(2)}, u32[]{:S(2)}) collective-permute-start(bf16[128,1152]{1,0:T(8,128)(2,1)S(1)} %get-tuple-element.59.mine_ref), channel_id=1, source_target_pairs={{0,120},{4,124},{8,64},{12,68},{16,72},{20,76},{24,80},{28,84},{32... | collective-permute-start | bytes 884744 | tf_op jit(solution)/shard_map/ppermute | solution.py:69
  73.8 2.2 %shard_map.118 = (bf16[128,1152]{1,0:T(8,128)(2,1)S(1)}, bf16[128,1152]{1,0:T(8,128)(2,1)S(1)}) custom-call(s32[1]{0:T(128)} %bitcast.1.r_0_.r_1_.place_ref, s32[8,2]{1,0:T(8,128)S(1)} %copy.14.r_1_.r_0_.r_2_, bf16[1024,256]{1,0:T(8,128)(2,1)S(1)} %get-tuple-element.46.r_15_.r_2_.r_1_, bf16[256,2048]{1,0:T(8,128)(2,1)S(1)} %get-tuple-element.50.r_3_.r_2_, ...), custom_call_target="tpu_custom_call" | custom-call | flops 2000000000 | bytes 1048576 | tf_op jit(solution)/shard_map/pallas_call | solution.py:25
  76.2 2.2 %shard_map.119 = (bf16[256,1024]{1,0:T(8,128)(2,1)S(1)}, bf16[128,1024]{1,0:T(8,128)(2,1)S(1)}) custom-call(s32[8,2]{1,0:T(8,128)S(1)} %copy.14.r_1_.r_0_.r_2_, bf16[1024,256]{1,0:T(8,128)(2,1)S(1)} %get-tuple-element.46.r_15_.r_2_.r_1_, bf16[256,2048]{1,0:T(8,128)(2,1)S(1)} %get-tuple-element.50.r_3_.r_2_, ...), custom_call_target="tpu_custom_call" | custom-call | flops 2000000000 | bytes 1048576 | tf_op jit(solution)/shard_map/pallas_call | solution.py:25
  78.6 2.5 %collective-permute-start.19 = (bf16[256,1024]{1,0:T(8,128)(2,1)S(1)}, bf16[256,1024]{1,0:T(8,128)(2,1)S(1)}, u32[]{:S(2)}, u32[]{:S(2)}) collective-permute-start(bf16[256,1024]{1,0:T(8,128)(2,1)S(1)} %get-tuple-element.61), channel_id=1, source_target_pairs={{0,64},{1,65},{2,66},{3,67},{4,68},{5,69},{6,70},{7,71},{8,72},{9,... | collective-permute-start | bytes 1572872 | tf_op jit(solution)/shard_map/ppermute | solution.py:43
  81.1 2.6 %collective-permute-start.16 = (bf16[128,1152]{1,0:T(8,128)(2,1)S(1)}, bf16[128,1152]{1,0:T(8,128)(2,1)S(1)}, u32[]{:S(2)}, u32[]{:S(2)}) collective-permute-start(bf16[128,1152]{1,0:T(8,128)(2,1)S(1)} %shard_map.122), channel_id=1, source_target_pairs={{0,3},{1,64},{2,65},{3,66},{4,7},{5,68},{6,69},{7,70},{8,11},{9,72... | collective-permute-start | bytes 884744 | tf_op jit(solution)/shard_map/ppermute | solution.py:79
  84.7 2.7 %collective-permute-start.20 = (bf16[256,1024]{1,0:T(8,128)(2,1)S(1)}, bf16[256,1024]{1,0:T(8,128)(2,1)S(1)}, u32[]{:S(2)}, u32[]{:S(2)}) collective-permute-start(bf16[256,1024]{1,0:T(8,128)(2,1)S(1)} %shard_map.120._), channel_id=1, source_target_pairs={{0,124},{1,125},{2,126},{3,127},{4,64},{5,65},{6,66},{7,67},{8,68}... | collective-permute-start | bytes 1572872 | tf_op jit(solution)/shard_map/ppermute | solution.py:43
  87.4 1.6 %shard_map.121 = (f32[256,1024]{1,0:T(8,128)S(1)}, bf16[256,1024]{1,0:T(8,128)(2,1)}) custom-call(s32[1]{0:T(128)} %bitcast.17.live_ref, bf16[256,1024]{1,0:T(8,128)(2,1)S(1)} %get-tuple-element.48.g_ref, bf16[1024,1024]{1,0:T(8,128)(2,1)S(1)} %copy-done.4, f32[256,1024]{1,0:T(8,128)S(1)} %get-tuple-element.49.pre_ref, bf16[256,1024]{1,0:T(8,128)(2,1)S(1)} %shard_map.120._), custom_call_target="tpu_custom_call" | custom-call | flops 2000000000 | bytes 1048576 | tf_op jit(solution)/shard_map/pallas_call | solution.py:25
  88.9 4.6 %collective-permute-done.18.c3 = bf16[128,1152]{1,0:T(8,128)(2,1)S(1)} collective-permute-done((bf16[128,1152]{1,0:T(8,128)(2,1)S(1)}, bf16[128,1152]{1,0:T(8,128)(2,1)S(1)}, u32[]{:S(2)}, u32[]{:S(2)}) %collective-permute-start.18) | collective-permute-done | bytes 294944 | tf_op jit(solution)/shard_map/ppermute | solution.py:59
  93.9 5.3 %collective-permute-done.20.below_ref = bf16[256,1024]{1,0:T(8,128)(2,1)S(1)} collective-permute-done((bf16[256,1024]{1,0:T(8,128)(2,1)S(1)}, bf16[256,1024]{1,0:T(8,128)(2,1)S(1)}, u32[]{:S(2)}, u32[]{:S(2)}) %collective-permute-start.20) | collective-permute-done | bytes 524320 | tf_op jit(solution)/shard_map/ppermute | solution.py:43
  99.3 1.0 shard_map.124
  (45 shorter events, 6.4 us)
Async XLA Ops:
  0.6 40.0 %copy-start.1 = (bf16[1,256,1024]{2,1,0:T(8,128)(2,1)S(1)}, bf16[1,256,1024]{2,1,0:T(8,128)(2,1)}, u32[]{:S(2)}) copy-start(bf16[1,256,1024]{2,1,0:T(8,128)(2,1)} %param.10) | copy-start | bytes 1572868
  0.6 40.0 %copy-start.2 = (s32[1,256,2048]{2,1,0:T(8,128)S(1)}, s32[1,256,2048]{2,1,0:T(8,128)}, u32[]{:S(2)}) copy-start(s32[1,256,2048]{2,1,0:T(8,128)} %param.13) | copy-start | bytes 6291460
  3.4 19.4 %collective-permute-start.8 = (bf16[256,1024]{1,0:T(8,128)(2,1)}, bf16[256,1024]{1,0:T(8,128)(2,1)S(1)}, u32[]{:S(2)}, u32[]{:S(2)}) collective-permute-start(bf16[256,1024]{1,0:T(8,128)(2,1)} %broadcast_select_fusion), channel_id=1, source_target_pairs={{0,68},{1,69},{2,70},{3,71},{4,72},{5,73},{6,74},{7,75},{8,76},{9,... | collective-permute-start | bytes 1572872 | tf_op jit(solution)/shard_map/ppermute | solution.py:43
  6.8 5.5 %collective-permute-start.2 = (s32[1,128]{1,0:T(1,128)S(1)}, s32[1,128]{1,0:T(1,128)S(1)}, u32[]{:S(2)}, u32[]{:S(2)}) collective-permute-start(s32[1,128]{1,0:T(1,128)S(1)} %pad_bitcast_fusion), channel_id=1, source_target_pairs={{0,1},{1,2},{2,3},{3,0},{4,5},{5,6},{6,7},{7,4},{8,9},{9,10},{10,1... | collective-permute-start | bytes 1544 | tf_op jit(solution)/shard_map/ppermute | solution.py:49
  8.0 4.3 %collective-permute-start.1 = (s32[1,128]{1,0:T(1,128)S(1)}, s32[1,128]{1,0:T(1,128)S(1)}, u32[]{:S(2)}, u32[]{:S(2)}) collective-permute-start(s32[1,128]{1,0:T(1,128)S(1)} %pad_bitcast_fusion), channel_id=1, source_target_pairs={{0,2},{1,3},{2,0},{3,1},{4,6},{5,7},{6,4},{7,5},{8,10},{9,11},{10,... | collective-permute-start | bytes 1544 | tf_op jit(solution)/shard_map/ppermute | solution.py:49
  10.5 2.7 %collective-permute-start = (s32[1,128]{1,0:T(1,128)S(1)}, s32[1,128]{1,0:T(1,128)S(1)}, u32[]{:S(2)}, u32[]{:S(2)}) collective-permute-start(s32[1,128]{1,0:T(1,128)S(1)} %pad_bitcast_fusion), channel_id=1, source_target_pairs={{0,3},{1,0},{2,1},{3,2},{4,7},{5,4},{6,5},{7,6},{8,11},{9,8},{10,9... | collective-permute-start | bytes 1544 | tf_op jit(solution)/shard_map/ppermute | solution.py:49
  11.6 18.3 %collective-permute-start.3 = (bf16[256,1024]{1,0:T(8,128)(2,1)}, bf16[256,1024]{1,0:T(8,128)(2,1)}, u32[]{:S(2)}, u32[]{:S(2)}) collective-permute-start(bf16[256,1024]{1,0:T(8,128)(2,1)} %broadcast_select_fusion), channel_id=1, source_target_pairs={{0,64},{1,65},{2,66},{3,67},{4,68},{5,69},{6,70},{7,71},{8,72},{9,... | collective-permute-start | bytes 1572872 | tf_op jit(solution)/shard_map/ppermute | solution.py:43
  13.2 23.0 %collective-permute-start.4 = (bf16[256,1024]{1,0:T(8,128)(2,1)}, bf16[256,1024]{1,0:T(8,128)(2,1)}, u32[]{:S(2)}, u32[]{:S(2)}) collective-permute-start(bf16[256,1024]{1,0:T(8,128)(2,1)} %broadcast_select_fusion), channel_id=1, source_target_pairs={{0,72},{1,73},{2,74},{3,75},{4,76},{5,77},{6,78},{7,79},{8,80},{9,... | collective-permute-start | bytes 1572872 | tf_op jit(solution)/shard_map/ppermute | solution.py:43
  24.3 19.3 %collective-permute-start.9 = (bf16[128,1024]{1,0:T(8,128)(2,1)}, bf16[128,1024]{1,0:T(8,128)(2,1)S(1)}, u32[]{:S(2)}, u32[]{:S(2)}) collective-permute-start(bf16[128,1024]{1,0:T(8,128)(2,1)} %get-tuple-element.40), channel_id=1, source_target_pairs={{0,1},{1,2},{2,3},{3,0},{4,5},{5,6},{6,7},{7,4},{8,9},{9,10},{10,1... | collective-permute-start | bytes 786440 | tf_op jit(solution)/shard_map/ppermute | solution.py:49
  25.5 20.7 %collective-permute-start.10 = (bf16[128,1024]{1,0:T(8,128)(2,1)}, bf16[128,1024]{1,0:T(8,128)(2,1)}, u32[]{:S(2)}, u32[]{:S(2)}) collective-permute-start(bf16[128,1024]{1,0:T(8,128)(2,1)} %get-tuple-element.41), channel_id=1, source_target_pairs={{0,2},{1,3},{2,0},{3,1},{4,6},{5,7},{6,4},{7,5},{8,10},{9,11},{10,... | collective-permute-start | bytes 786440 | tf_op jit(solution)/shard_map/ppermute | solution.py:49
  28.0 18.2 %collective-permute-start.11 = (bf16[128,1024]{1,0:T(8,128)(2,1)}, bf16[128,1024]{1,0:T(8,128)(2,1)}, u32[]{:S(2)}, u32[]{:S(2)}) collective-permute-start(bf16[128,1024]{1,0:T(8,128)(2,1)} %get-tuple-element.42), channel_id=1, source_target_pairs={{0,3},{1,0},{2,1},{3,2},{4,7},{5,4},{6,5},{7,6},{8,11},{9,8},{10,9... | collective-permute-start | bytes 786440 | tf_op jit(solution)/shard_map/ppermute | solution.py:49
  37.5 14.1 %collective-permute-start.6 = (bf16[128,1024]{1,0:T(8,128)(2,1)S(1)}, bf16[128,1024]{1,0:T(8,128)(2,1)S(1)}, u32[]{:S(2)}, u32[]{:S(2)}) collective-permute-start(bf16[128,1024]{1,0:T(8,128)(2,1)S(1)} %get-tuple-element.37), channel_id=1, source_target_pairs={{0,2},{1,3},{2,0},{3,1},{4,6},{5,7},{6,4},{7,5},{8,10},{9,11},{10,... | collective-permute-start | bytes 786440 | tf_op jit(solution)/shard_map/ppermute | solution.py:49
  40.3 12.6 %collective-permute-start.5 = (bf16[128,1024]{1,0:T(8,128)(2,1)S(1)}, bf16[128,1024]{1,0:T(8,128)(2,1)S(1)}, u32[]{:S(2)}, u32[]{:S(2)}) collective-permute-start(bf16[128,1024]{1,0:T(8,128)(2,1)S(1)} %get-tuple-element.36.r_5_), channel_id=1, source_target_pairs={{0,1},{1,2},{2,3},{3,0},{4,5},{5,6},{6,7},{7,4},{8,9},{9,10},{10,1... | collective-permute-start | bytes 786440 | tf_op jit(solution)/shard_map/ppermute | solution.py:49
  40.7 1.6 %copy-start.3 = (bf16[1024,1024]{1,0:T(8,128)(2,1)S(1)}, bf16[1024,1024]{1,0:T(8,128)(2,1)}, u32[]{:S(2)}) copy-start(bf16[1024,1024]{1,0:T(8,128)(2,1)} %sw_ref.1) | copy-start | bytes 6291460
  42.3 4.0 %copy-start = (bf16[1024,2048]{1,0:T(8,128)(2,1)S(1)}, bf16[1024,2048]{1,0:T(8,128)(2,1)}, u32[]{:S(2)}) copy-start(bf16[1024,2048]{1,0:T(8,128)(2,1)} %r_4_.3) | copy-start | bytes 12582916
  42.3 4.0 %copy-start.7 = (f32[2048]{0:T(1024)S(1)}, f32[2048]{0:T(1024)}, u32[]{:S(2)}) copy-start(f32[2048]{0:T(1024)} %param.16) | copy-start | bytes 24580
  43.6 8.7 %collective-permute-start.7 = (bf16[128,1024]{1,0:T(8,128)(2,1)S(1)}, bf16[128,1024]{1,0:T(8,128)(2,1)S(1)}, u32[]{:S(2)}, u32[]{:S(2)}) collective-permute-start(bf16[128,1024]{1,0:T(8,128)(2,1)S(1)} %get-tuple-element.38), channel_id=1, source_target_pairs={{0,3},{1,0},{2,1},{3,2},{4,7},{5,4},{6,5},{7,6},{8,11},{9,8},{10,9... | collective-permute-start | bytes 786440 | tf_op jit(solution)/shard_map/ppermute | solution.py:49
  46.2 6.7 %copy-start.5 = (bf16[2048,1024]{1,0:T(8,128)(2,1)S(1)}, bf16[2048,1024]{1,0:T(8,128)(2,1)}, u32[]{:S(2)}) copy-start(bf16[2048,1024]{1,0:T(8,128)(2,1)} %r_13_.1) | copy-start | bytes 12582916
  46.3 6.7 %copy-start.6 = (bf16[1,256,1024]{2,1,0:T(8,128)(2,1)S(1)}, bf16[1,256,1024]{2,1,0:T(8,128)(2,1)}, u32[]{:S(2)}) copy-start(bf16[1,256,1024]{2,1,0:T(8,128)(2,1)} %param.14) | copy-start | bytes 1572868
  46.3 6.7 %copy-start.8 = (f32[1024]{0:T(1024)S(1)}, f32[1024]{0:T(1024)}, u32[]{:S(2)}) copy-start(f32[1024]{0:T(1024)} %param.19) | copy-start | bytes 12292
  61.9 16.7 %collective-permute-start.13 = (bf16[128,1024]{1,0:T(8,128)(2,1)S(1)}, bf16[128,1024]{1,0:T(8,128)(2,1)S(1)}, u32[]{:S(2)}, u32[]{:S(2)}) collective-permute-start(bf16[128,1024]{1,0:T(8,128)(2,1)S(1)} %get-tuple-element.55), channel_id=1, source_target_pairs={{0,2},{1,3},{2,0},{3,1},{4,6},{5,7},{6,4},{7,5},{8,10},{9,11},{10,... | collective-permute-start | bytes 786440 | tf_op jit(solution)/shard_map/ppermute | solution.py:49
  63.3 17.8 %collective-permute-start.14 = (bf16[128,1024]{1,0:T(8,128)(2,1)S(1)}, bf16[128,1024]{1,0:T(8,128)(2,1)S(1)}, u32[]{:S(2)}, u32[]{:S(2)}) collective-permute-start(bf16[128,1024]{1,0:T(8,128)(2,1)S(1)} %get-tuple-element.56), channel_id=1, source_target_pairs={{0,1},{1,2},{2,3},{3,0},{4,5},{5,6},{6,7},{7,4},{8,9},{9,10},{10,1... | collective-permute-start | bytes 786440 | tf_op jit(solution)/shard_map/ppermute | solution.py:49
  64.5 19.3 %collective-permute-start.12 = (bf16[128,1024]{1,0:T(8,128)(2,1)S(1)}, bf16[128,1024]{1,0:T(8,128)(2,1)S(1)}, u32[]{:S(2)}, u32[]{:S(2)}) collective-permute-start(bf16[128,1024]{1,0:T(8,128)(2,1)S(1)} %get-tuple-element.52.r_6_), channel_id=1, source_target_pairs={{0,3},{1,0},{2,1},{3,2},{4,7},{5,4},{6,5},{7,6},{8,11},{9,8},{10,9... | collective-permute-start | bytes 786440 | tf_op jit(solution)/shard_map/ppermute | solution.py:49
  66.0 12.5 %collective-permute-start.15 = (bf16[128,1152]{1,0:T(8,128)(2,1)S(1)}, bf16[128,1152]{1,0:T(8,128)(2,1)S(1)}, u32[]{:S(2)}, u32[]{:S(2)}) collective-permute-start(bf16[128,1152]{1,0:T(8,128)(2,1)S(1)} %get-tuple-element.59.mine_ref), channel_id=1, source_target_pairs={{0,120},{4,124},{8,64},{12,68},{16,72},{20,76},{24,80},{28,84},{32... | collective-permute-start | bytes 884744 | tf_op jit(solution)/shard_map/ppermute | solution.py:69
  75.9 17.6 %collective-permute-start.17 = (bf16[128,1152]{1,0:T(8,128)(2,1)S(1)}, bf16[128,1152]{1,0:T(8,128)(2,1)S(1)}, u32[]{:S(2)}, u32[]{:S(2)}) collective-permute-start(bf16[128,1152]{1,0:T(8,128)(2,1)S(1)} %get-tuple-element.53.r_5_), channel_id=1, source_target_pairs={{66,0},{67,1},{72,2},{73,3},{70,4},{71,5},{76,6},{77,7},{74,8},{75... | collective-permute-start | bytes 884744 | tf_op jit(solution)/shard_map/ppermute | solution.py:59
  78.5 15.1 %collective-permute-start.18 = (bf16[128,1152]{1,0:T(8,128)(2,1)S(1)}, bf16[128,1152]{1,0:T(8,128)(2,1)S(1)}, u32[]{:S(2)}, u32[]{:S(2)}) collective-permute-start(bf16[128,1152]{1,0:T(8,128)(2,1)S(1)} %get-tuple-element.60), channel_id=1, source_target_pairs={{67,0},{72,1},{73,2},{74,3},{71,4},{76,5},{77,6},{78,7},{75,8},{80... | collective-permute-start | bytes 884744 | tf_op jit(solution)/shard_map/ppermute | solution.py:59
  78.6 15.3 %collective-permute-start.19 = (bf16[256,1024]{1,0:T(8,128)(2,1)S(1)}, bf16[256,1024]{1,0:T(8,128)(2,1)S(1)}, u32[]{:S(2)}, u32[]{:S(2)}) collective-permute-start(bf16[256,1024]{1,0:T(8,128)(2,1)S(1)} %get-tuple-element.61), channel_id=1, source_target_pairs={{0,64},{1,65},{2,66},{3,67},{4,68},{5,69},{6,70},{7,71},{8,72},{9,... | collective-permute-start | bytes 1572872 | tf_op jit(solution)/shard_map/ppermute | solution.py:43
  81.1 12.5 %collective-permute-start.16 = (bf16[128,1152]{1,0:T(8,128)(2,1)S(1)}, bf16[128,1152]{1,0:T(8,128)(2,1)S(1)}, u32[]{:S(2)}, u32[]{:S(2)}) collective-permute-start(bf16[128,1152]{1,0:T(8,128)(2,1)S(1)} %shard_map.122), channel_id=1, source_target_pairs={{0,3},{1,64},{2,65},{3,66},{4,7},{5,68},{6,69},{7,70},{8,11},{9,72... | collective-permute-start | bytes 884744 | tf_op jit(solution)/shard_map/ppermute | solution.py:79
  83.7 3.6 %copy-start.4 = (bf16[1024,1024]{1,0:T(8,128)(2,1)S(1)}, bf16[1024,1024]{1,0:T(8,128)(2,1)}, u32[]{:S(2)}) copy-start(bf16[1024,1024]{1,0:T(8,128)(2,1)} %sw_ref.1) | copy-start | bytes 6291460
  84.7 14.6 %collective-permute-start.20 = (bf16[256,1024]{1,0:T(8,128)(2,1)S(1)}, bf16[256,1024]{1,0:T(8,128)(2,1)S(1)}, u32[]{:S(2)}, u32[]{:S(2)}) collective-permute-start(bf16[256,1024]{1,0:T(8,128)(2,1)S(1)} %shard_map.120._), channel_id=1, source_target_pairs={{0,124},{1,125},{2,126},{3,127},{4,64},{5,65},{6,66},{7,67},{8,68}... | collective-permute-start | bytes 1572872 | tf_op jit(solution)/shard_map/ppermute | solution.py:43

commit v14 on v13

--- a/solution.py
+++ b/solution.py
@@ -91,7 +91,7 @@
     return pl.ds(pl.multiple_of(index * block, block), block)
 
 
-def pick_near_kernel(block, place_ref, m1, m2, m3, rows_ref, *outs):
+def pick_near_kernel(block, place_ref, m1, m2, m3, rows_ref, _, *outs):
     for d, (meta, out) in enumerate(zip((m1, m2, m3), outs), 1):
         p = lax.rem(place_ref[0] + d, LINE)
         out[...] = rows_ref[at_block(meta[0, near(p, d)], block), :]
@@ -115,7 +115,7 @@
     return [0, LINE] + [near(p, d) for d in range(1, LINE)] + [far(p, d) for d in range(1, LINE)]
 
 
-def tiles_kernel(block, place_ref, lists_ref, counts_ref, x_ref, sw_ref, _, tiles_ref, tiles_t_ref, self_ref):
+def tiles_kernel(block, place_ref, lists_ref, counts_ref, x_ref, sw_ref, tiles_ref, tiles_t_ref, self_ref):
     for i, o in enumerate(slots(place_ref[0])):
         first, second = lists_ref[o, 0], lists_ref[o, 1]
         at = pl.ds(pl.multiple_of((o * 2 + second) * block, block), block)
@@ -315,11 +315,18 @@
     later, *metas = lax.optimization_barrier((marked, *metas))
     below2 = swap_rows(later, 2 * LINE)
     scalars = [SMEM] * (1 + len(steps))
+    tiles, tiles_t, self_pre = call(
+        lambda *r: tiles_kernel(block, *r),
+        [((rows, reach * block), BF16), ((reach * block, rows), BF16), ((rows, width), F32)],
+        (place, lists, counts, x, sw),
+        [SMEM] * 2 + [VMEM] * 3,
+        flops=2 * rows * width * width,
+    )
     sent = call(
         lambda *r: pick_near_kernel(block, *r),
         [one] * len(steps),
-        (place, *metas, below),
-        scalars + [VMEM],
+        (place, *metas, below, tiles),
+        scalars + [VMEM, HELD],
     )
     got_near = [along(b, d) for d, b in zip(steps, sent)]
     sent = call(
@@ -329,13 +336,6 @@
         scalars + [VMEM] * 2,
     )
     got_far = [along(b, d) for d, b in zip(steps, sent)]
-    tiles, tiles_t, self_pre = call(
-        lambda *r: tiles_kernel(block, *r),
-        [((rows, reach * block), BF16), ((reach * block, rows), BF16), ((rows, width), F32)],
-        (place, lists, counts, x, sw, sent[0]),
-        [SMEM] * 2 + [VMEM] * 3 + [HELD],
-        flops=2 * rows * width * width,
-    )
     split = 1 + LINE
 
     def message(first, last, ins, specs):

time: 101 us -> 100 us (0.990)
  the two profiles are of different devices: /device:TPU:1 before, /device:TPU:7 now
where the time goes in v14:
time: 100 us; the launch traced here: 98.7 us
  waiting for transfers between devices  36.7 us (37%)
  starting transfers between devices  29.5 us (30%)
  Pallas kernels  24.3 us (24%)
  local copies, waits for them, and re-layouts  5.69 us (6%)
  between operations  1.48 us (1%)
  other arithmetic  1.16 us (1%)
    pallas_call x12, Pallas kernels, call(): pl.pallas_call(kernel, out_shape=[jax.ShapeDtypeStruct(s, d) for s, d in...  24.3 us
    ppermute x5, waiting for transfers between devices, swap_rows(): return lax.ppermute(x, ('side', 'dom'), pairs)  20 us
    ppermute x12, waiting for transfers between devices, along(): return lax.ppermute(x, 'dom', pairs)  12.1 us
    ppermute x2, starting transfers between devices, straight_back(): return lax.ppermute(x, ('side', 'dom'), pairs)  11.3 us
    ppermute x12, starting transfers between devices, along(): return lax.ppermute(x, 'dom', pairs)  9.02 us
    ppermute x5, starting transfers between devices, swap_rows(): return lax.ppermute(x, ('side', 'dom'), pairs)  7.51 us
    unnamed x18, local copies, waits for them, and re-layouts  4.25 us
    ppermute x2, waiting for transfers between devices, straight_back(): return lax.ppermute(x, ('side', 'dom'), pairs)  3.98 us
  transfers between devices with their start and end apart: 21, of which 9 were waited for; matrix products, arithmetic and copies ran while one was open for 1% of the time, Pallas kernels for 15%

profile of v14, /device:TPU:7, one launch (start us, length us, event | category | flops | bytes accessed | tf_op | source)
XLA Modules:
  0.0 98.7 jit_solution(532133827778322221)
XLA Ops:
  1.3 1.2 %broadcast_select_fusion = bf16[256,1024]{1,0:T(8,128)(2,1)S(1)} fusion(pred[256]{0:T(512)(128)(4,1)S(1)} %iota_compare_fusion, bf16[1,256,1024]{2,1,0:T(8,128)(2,1)} %param.10), kind=kLoop, calls=%fused_computation | loop fusion | flops 262144 | bytes 1048832 | tf_op jit(solution)/shard_map/jit(_where)/select_n | solution.py:307
  2.5 1.9 %collective-permute-start.8 = (bf16[256,1024]{1,0:T(8,128)(2,1)S(1)}, bf16[256,1024]{1,0:T(8,128)(2,1)S(1)}, u32[]{:S(2)}, u32[]{:S(2)}) collective-permute-start(bf16[256,1024]{1,0:T(8,128)(2,1)S(1)} %broadcast_select_fusion), channel_id=1, source_target_pairs={{0,68},{1,69},{2,70},{3,71},{4,72},{5,73},{6,74},{7,75},{8,76},{9,... | collective-permute-start | bytes 1572872 | tf_op jit(solution)/shard_map/ppermute | solution.py:43
  4.4 0.7 slice_bitcast_fusion
  5.3 2.2 %collective-permute-start.1 = (s32[1,128]{1,0:T(1,128)S(1)}, s32[1,128]{1,0:T(1,128)S(1)}, u32[]{:S(2)}, u32[]{:S(2)}) collective-permute-start(s32[1,128]{1,0:T(1,128)S(1)} %pad_bitcast_fusion), channel_id=1, source_target_pairs={{0,2},{1,3},{2,0},{3,1},{4,6},{5,7},{6,4},{7,5},{8,10},{9,11},{10,... | collective-permute-start | bytes 1544 | tf_op jit(solution)/shard_map/ppermute | solution.py:49
  7.8 1.4 %collective-permute-done.1.r_2_.r_3_ = s32[1,128]{1,0:T(1,128)S(1)} collective-permute-done((s32[1,128]{1,0:T(1,128)S(1)}, s32[1,128]{1,0:T(1,128)S(1)}, u32[]{:S(2)}, u32[]{:S(2)}) %collective-permute-start.1) | collective-permute-done | bytes 544 | tf_op jit(solution)/shard_map/ppermute | solution.py:49
  9.2 2.1 %collective-permute-done.r_1_.r_2_ = s32[1,128]{1,0:T(1,128)S(1)} collective-permute-done((s32[1,128]{1,0:T(1,128)S(1)}, s32[1,128]{1,0:T(1,128)S(1)}, u32[]{:S(2)}, u32[]{:S(2)}) %collective-permute-start) | collective-permute-done | bytes 544 | tf_op jit(solution)/shard_map/ppermute | solution.py:49
  11.3 3.7 %collective-permute-start.4 = (bf16[256,1024]{1,0:T(8,128)(2,1)S(1)}, bf16[256,1024]{1,0:T(8,128)(2,1)S(1)}, u32[]{:S(2)}, u32[]{:S(2)}) collective-permute-start(bf16[256,1024]{1,0:T(8,128)(2,1)S(1)} %broadcast_select_fusion), channel_id=1, source_target_pairs={{0,72},{1,73},{2,74},{3,75},{4,76},{5,77},{6,78},{7,79},{8,80},{9,... | collective-permute-start | bytes 1572872 | tf_op jit(solution)/shard_map/ppermute | solution.py:43
  15.1 0.8 copy.14.r_1_.r_0_.r_2_
  15.8 1.6 %copy-done.1 = s32[1,256,2048]{2,1,0:T(8,128)S(1)} copy-done((s32[1,256,2048]{2,1,0:T(8,128)S(1)}, s32[1,256,2048]{2,1,0:T(8,128)}, u32[]{:S(2)}) %copy-start.1) | copy-done | bytes 2097176
  17.4 1.6 %copy-done.2 = bf16[1024,1024]{1,0:T(8,128)(2,1)S(1)} copy-done((bf16[1024,1024]{1,0:T(8,128)(2,1)S(1)}, bf16[1024,1024]{1,0:T(8,128)(2,1)}, u32[]{:S(2)}) %copy-start.2) | copy-done | bytes 2097176
  19.0 1.0 %copy-done.4 = bf16[1,256,1024]{2,1,0:T(8,128)(2,1)S(1)} copy-done((bf16[1,256,1024]{2,1,0:T(8,128)(2,1)S(1)}, bf16[1,256,1024]{2,1,0:T(8,128)(2,1)}, u32[]{:S(2)}) %copy-start.4) | copy-done | bytes 524312
  20.0 1.3 %shard_map.114 = (bf16[256,1024]{1,0:T(8,128)(2,1)S(1)}, bf16[1024,256]{1,0:T(8,128)(2,1)S(1)}, f32[256,1024]{1,0:T(8,128)S(1)}) custom-call(s32[1]{0:T(128)} %bitcast.1.r_0_.r_1_.place_ref, s32[8,2]{1,0:T(8,128)S(1)} %copy.14.r_1_.r_0_.r_2_, s32[256,2048]{1,0:T(8,128)S(1)} %bitcast.20, bf16[256,1024]{1,0:T(8,128)(2,1)S(1)} %bitcast.21, ...), custom_call_target="tpu_custom_call" | custom-call | flops 536870912 | bytes 1048576 | tf_op jit(solution)/shard_map/pallas_call | solution.py:25
  22.4 1.6 %collective-permute-start.10 = (bf16[128,1024]{1,0:T(8,128)(2,1)S(1)}, bf16[128,1024]{1,0:T(8,128)(2,1)S(1)}, u32[]{:S(2)}, u32[]{:S(2)}) collective-permute-start(bf16[128,1024]{1,0:T(8,128)(2,1)S(1)} %get-tuple-element.41), channel_id=1, source_target_pairs={{0,2},{1,3},{2,0},{3,1},{4,6},{5,7},{6,4},{7,5},{8,10},{9,11},{10,... | collective-permute-start | bytes 786440 | tf_op jit(solution)/shard_map/ppermute | solution.py:49
  24.0 10.2 %collective-permute-done.4.r_5_ = bf16[256,1024]{1,0:T(8,128)(2,1)S(1)} collective-permute-done((bf16[256,1024]{1,0:T(8,128)(2,1)S(1)}, bf16[256,1024]{1,0:T(8,128)(2,1)S(1)}, u32[]{:S(2)}, u32[]{:S(2)}) %collective-permute-start.4) | collective-permute-done | bytes 524320 | tf_op jit(solution)/shard_map/ppermute | solution.py:43
  35.1 2.1 %collective-permute-start.6 = (bf16[128,1024]{1,0:T(8,128)(2,1)S(1)}, bf16[128,1024]{1,0:T(8,128)(2,1)S(1)}, u32[]{:S(2)}, u32[]{:S(2)}) collective-permute-start(bf16[128,1024]{1,0:T(8,128)(2,1)S(1)} %get-tuple-element.37), channel_id=1, source_target_pairs={{0,2},{1,3},{2,0},{3,1},{4,6},{5,7},{6,4},{7,5},{8,10},{9,11},{10,... | collective-permute-start | bytes 786440 | tf_op jit(solution)/shard_map/ppermute | solution.py:49
  37.8 4.6 %shard_map.116 = (bf16[640,2048]{1,0:T(8,128)(2,1)S(1)}, f32[256,2048]{1,0:T(8,128)S(1)}, f32[256,128]{1,0:T(8,128)S(1)}) custom-call(s32[8,2]{1,0:T(8,128)S(1)} %copy.14.r_1_.r_0_.r_2_, bf16[256,1024]{1,0:T(8,128)(2,1)S(1)} %collective-permute-done.3.r_4_.r_1_, bf16[256,1024]{1,0:T(8,128)(2,1)S(1)} %collective-permute-done.8.r_4_.r_2_, ...), custom_call_target="tpu_custom_call" | custom-call | flops 3355443200 | bytes 1048576 | tf_op jit(solution)/shard_map/pallas_call | solution.py:25
  42.4 1.4 %collective-permute-done.6.r_4_ = bf16[128,1024]{1,0:T(8,128)(2,1)S(1)} collective-permute-done((bf16[128,1024]{1,0:T(8,128)(2,1)S(1)}, bf16[128,1024]{1,0:T(8,128)(2,1)S(1)}, u32[]{:S(2)}, u32[]{:S(2)}) %collective-permute-start.6) | collective-permute-done | bytes 262176 | tf_op jit(solution)/shard_map/ppermute | solution.py:49
  43.8 6.6 %collective-permute-done.7.r_5_ = bf16[128,1024]{1,0:T(8,128)(2,1)S(1)} collective-permute-done((bf16[128,1024]{1,0:T(8,128)(2,1)S(1)}, bf16[128,1024]{1,0:T(8,128)(2,1)S(1)}, u32[]{:S(2)}, u32[]{:S(2)}) %collective-permute-start.7) | collective-permute-done | bytes 262176 | tf_op jit(solution)/shard_map/ppermute | solution.py:49
  50.5 8.8 %shard_map.117 = (bf16[256,1024]{1,0:T(8,128)(2,1)S(1)}, bf16[256,2048]{1,0:T(8,128)(2,1)S(1)}, f32[256,1024]{1,0:T(8,128)S(1)}, bf16[384,2048]{1,0:T(8,128)(2,1...) custom-call(s32[1]{0:T(128)} %bitcast.16.r_0_, ...), custom_call_target="tpu_custom_call" | custom-call | flops 8000000000 | bytes 1048576 | tf_op jit(solution)/shard_map/pallas_call | solution.py:25
  59.3 0.8 collective-permute-start.13
  60.1 1.3 %collective-permute-start.14 = (bf16[128,1024]{1,0:T(8,128)(2,1)S(1)}, bf16[128,1024]{1,0:T(8,128)(2,1)S(1)}, u32[]{:S(2)}, u32[]{:S(2)}) collective-permute-start(bf16[128,1024]{1,0:T(8,128)(2,1)S(1)} %get-tuple-element.56), channel_id=1, source_target_pairs={{0,1},{1,2},{2,3},{3,0},{4,5},{5,6},{6,7},{7,4},{8,9},{9,10},{10,1... | collective-permute-start | bytes 786440 | tf_op jit(solution)/shard_map/ppermute | solution.py:49
  62.3 2.2 %shard_map.118 = (bf16[128,1152]{1,0:T(8,128)(2,1)S(1)}, bf16[128,1152]{1,0:T(8,128)(2,1)S(1)}) custom-call(s32[1]{0:T(128)} %bitcast.1.r_0_.r_1_.place_ref, s32[8,2]{1,0:T(8,128)S(1)} %copy.14.r_1_.r_0_.r_2_, bf16[1024,256]{1,0:T(8,128)(2,1)S(1)} %get-tuple-element.46.r_15_.r_2_.r_1_, bf16[256,2048]{1,0:T(8,128)(2,1)S(1)} %get-tuple-element.50.r_3_.r_2_, ...), custom_call_target="tpu_custom_call" | custom-call | flops 2000000000 | bytes 1048576 | tf_op jit(solution)/shard_map/pallas_call | solution.py:25
  64.5 3.7 %collective-permute-start.17 = (bf16[128,1152]{1,0:T(8,128)(2,1)S(1)}, bf16[128,1152]{1,0:T(8,128)(2,1)S(1)}, u32[]{:S(2)}, u32[]{:S(2)}) collective-permute-start(bf16[128,1152]{1,0:T(8,128)(2,1)S(1)} %get-tuple-element.53.r_5_), channel_id=1, source_target_pairs={{66,0},{67,1},{72,2},{73,3},{70,4},{71,5},{76,6},{77,7},{74,8},{75... | collective-permute-start | bytes 884744 | tf_op jit(solution)/shard_map/ppermute | solution.py:59
  68.2 2.2 %shard_map.119 = (bf16[256,1024]{1,0:T(8,128)(2,1)S(1)}, bf16[128,1024]{1,0:T(8,128)(2,1)S(1)}) custom-call(s32[8,2]{1,0:T(8,128)S(1)} %copy.14.r_1_.r_0_.r_2_, bf16[1024,256]{1,0:T(8,128)(2,1)S(1)} %get-tuple-element.46.r_15_.r_2_.r_1_, bf16[256,2048]{1,0:T(8,128)(2,1)S(1)} %get-tuple-element.50.r_3_.r_2_, ...), custom_call_target="tpu_custom_call" | custom-call | flops 2000000000 | bytes 1048576 | tf_op jit(solution)/shard_map/pallas_call | solution.py:25
  70.5 7.6 %collective-permute-start.18 = (bf16[128,1152]{1,0:T(8,128)(2,1)S(1)}, bf16[128,1152]{1,0:T(8,128)(2,1)S(1)}, u32[]{:S(2)}, u32[]{:S(2)}) collective-permute-start(bf16[128,1152]{1,0:T(8,128)(2,1)S(1)} %get-tuple-element.60), channel_id=1, source_target_pairs={{67,0},{72,1},{73,2},{74,3},{71,4},{76,5},{77,6},{78,7},{75,8},{80... | collective-permute-start | bytes 884744 | tf_op jit(solution)/shard_map/ppermute | solution.py:59
  78.2 1.0 collective-permute-start.16
  79.1 0.9 shard_map.120._
  80.1 1.4 %collective-permute-start.20 = (bf16[256,1024]{1,0:T(8,128)(2,1)S(1)}, bf16[256,1024]{1,0:T(8,128)(2,1)S(1)}, u32[]{:S(2)}, u32[]{:S(2)}) collective-permute-start(bf16[256,1024]{1,0:T(8,128)(2,1)S(1)} %shard_map.120._), channel_id=1, source_target_pairs={{0,124},{1,125},{2,126},{3,127},{4,64},{5,65},{6,66},{7,67},{8,68}... | collective-permute-start | bytes 1572872 | tf_op jit(solution)/shard_map/ppermute | solution.py:43
  81.5 1.6 %shard_map.121 = (f32[256,1024]{1,0:T(8,128)S(1)}, bf16[256,1024]{1,0:T(8,128)(2,1)}) custom-call(s32[1]{0:T(128)} %bitcast.17.live_ref, bf16[256,1024]{1,0:T(8,128)(2,1)S(1)} %get-tuple-element.48.g_ref, bf16[1024,1024]{1,0:T(8,128)(2,1)S(1)} %copy-done.3, f32[256,1024]{1,0:T(8,128)S(1)} %get-tuple-element.49.pre_ref, bf16[256,1024]{1,0:T(8,128)(2,1)S(1)} %shard_map.120._), custom_call_target="tpu_custom_call" | custom-call | flops 2000000000 | bytes 1048576 | tf_op jit(solution)/shard_map/pallas_call | solution.py:25
  83.0 4.0 %collective-permute-done.18.c3 = bf16[128,1152]{1,0:T(8,128)(2,1)S(1)} collective-permute-done((bf16[128,1152]{1,0:T(8,128)(2,1)S(1)}, bf16[128,1152]{1,0:T(8,128)(2,1)S(1)}, u32[]{:S(2)}, u32[]{:S(2)}) %collective-permute-start.18) | collective-permute-done | bytes 294944 | tf_op jit(solution)/shard_map/ppermute | solution.py:59
  88.0 9.7 %collective-permute-done.20.below_ref = bf16[256,1024]{1,0:T(8,128)(2,1)S(1)} collective-permute-done((bf16[256,1024]{1,0:T(8,128)(2,1)S(1)}, bf16[256,1024]{1,0:T(8,128)(2,1)S(1)}, u32[]{:S(2)}, u32[]{:S(2)}) %collective-permute-start.20) | collective-permute-done | bytes 524320 | tf_op jit(solution)/shard_map/ppermute | solution.py:43
  97.7 1.0 %shard_map.124 = bf16[256,1024]{1,0:T(8,128)(2,1)} custom-call(s32[1]{0:T(128)} %bitcast.18.live_ref, f32[256,1024]{1,0:T(8,128)S(1)} %shard_map.123.total_ref, bf16[256,1024]{1,0:T(8,128)(2,1)S(1)} %collective-permute-done.19.same_ref, bf16[256,1024]{1,0:T(8,128)(2,1)S(1)} %collective-permute-done.20.below_ref), custom_call_target="tpu_custom_call" | custom-call | bytes 1048576 | tf_op jit(solution)/shard_map/pallas_call | solution.py:25
  (45 shorter events, 5.0 us)
Async XLA Ops:
  2.5 18.9 %collective-permute-start.8 = (bf16[256,1024]{1,0:T(8,128)(2,1)S(1)}, bf16[256,1024]{1,0:T(8,128)(2,1)S(1)}, u32[]{:S(2)}, u32[]{:S(2)}) collective-permute-start(bf16[256,1024]{1,0:T(8,128)(2,1)S(1)} %broadcast_select_fusion), channel_id=1, source_target_pairs={{0,68},{1,69},{2,70},{3,71},{4,72},{5,73},{6,74},{7,75},{8,76},{9,... | collective-permute-start | bytes 1572872 | tf_op jit(solution)/shard_map/ppermute | solution.py:43
  5.1 2.7 %collective-permute-start.2 = (s32[1,128]{1,0:T(1,128)S(1)}, s32[1,128]{1,0:T(1,128)S(1)}, u32[]{:S(2)}, u32[]{:S(2)}) collective-permute-start(s32[1,128]{1,0:T(1,128)S(1)} %pad_bitcast_fusion), channel_id=1, source_target_pairs={{0,1},{1,2},{2,3},{3,0},{4,5},{5,6},{6,7},{7,4},{8,9},{9,10},{10,1... | collective-permute-start | bytes 1544 | tf_op jit(solution)/shard_map/ppermute | solution.py:49
  5.3 3.9 %collective-permute-start.1 = (s32[1,128]{1,0:T(1,128)S(1)}, s32[1,128]{1,0:T(1,128)S(1)}, u32[]{:S(2)}, u32[]{:S(2)}) collective-permute-start(s32[1,128]{1,0:T(1,128)S(1)} %pad_bitcast_fusion), channel_id=1, source_target_pairs={{0,2},{1,3},{2,0},{3,1},{4,6},{5,7},{6,4},{7,5},{8,10},{9,11},{10,... | collective-permute-start | bytes 1544 | tf_op jit(solution)/shard_map/ppermute | solution.py:49
  7.4 3.9 %collective-permute-start = (s32[1,128]{1,0:T(1,128)S(1)}, s32[1,128]{1,0:T(1,128)S(1)}, u32[]{:S(2)}, u32[]{:S(2)}) collective-permute-start(s32[1,128]{1,0:T(1,128)S(1)} %pad_bitcast_fusion), channel_id=1, source_target_pairs={{0,3},{1,0},{2,1},{3,2},{4,7},{5,4},{6,5},{7,6},{8,11},{9,8},{10,9... | collective-permute-start | bytes 1544 | tf_op jit(solution)/shard_map/ppermute | solution.py:49
  7.4 16.5 %collective-permute-start.3 = (bf16[256,1024]{1,0:T(8,128)(2,1)S(1)}, bf16[256,1024]{1,0:T(8,128)(2,1)S(1)}, u32[]{:S(2)}, u32[]{:S(2)}) collective-permute-start(bf16[256,1024]{1,0:T(8,128)(2,1)S(1)} %broadcast_select_fusion), channel_id=1, source_target_pairs={{0,64},{1,65},{2,66},{3,67},{4,68},{5,69},{6,70},{7,71},{8,72},{9,... | collective-permute-start | bytes 1572872 | tf_op jit(solution)/shard_map/ppermute | solution.py:43
  11.3 22.8 %collective-permute-start.4 = (bf16[256,1024]{1,0:T(8,128)(2,1)S(1)}, bf16[256,1024]{1,0:T(8,128)(2,1)S(1)}, u32[]{:S(2)}, u32[]{:S(2)}) collective-permute-start(bf16[256,1024]{1,0:T(8,128)(2,1)S(1)} %broadcast_select_fusion), channel_id=1, source_target_pairs={{0,72},{1,73},{2,74},{3,75},{4,76},{5,77},{6,78},{7,79},{8,80},{9,... | collective-permute-start | bytes 1572872 | tf_op jit(solution)/shard_map/ppermute | solution.py:43
  15.8 1.6 %copy-start.1 = (s32[1,256,2048]{2,1,0:T(8,128)S(1)}, s32[1,256,2048]{2,1,0:T(8,128)}, u32[]{:S(2)}) copy-start(s32[1,256,2048]{2,1,0:T(8,128)} %param.13) | copy-start | bytes 6291460
  17.4 1.6 %copy-start.2 = (bf16[1024,1024]{1,0:T(8,128)(2,1)S(1)}, bf16[1024,1024]{1,0:T(8,128)(2,1)}, u32[]{:S(2)}) copy-start(bf16[1024,1024]{1,0:T(8,128)(2,1)} %sw_ref.1) | copy-start | bytes 6291460
  19.0 1.0 %copy-start.4 = (bf16[1,256,1024]{2,1,0:T(8,128)(2,1)S(1)}, bf16[1,256,1024]{2,1,0:T(8,128)(2,1)}, u32[]{:S(2)}) copy-start(bf16[1,256,1024]{2,1,0:T(8,128)(2,1)} %param.10) | copy-start | bytes 1572868
  20.0 17.7 %copy-start = (bf16[1024,2048]{1,0:T(8,128)(2,1)S(1)}, bf16[1024,2048]{1,0:T(8,128)(2,1)}, u32[]{:S(2)}) copy-start(bf16[1024,2048]{1,0:T(8,128)(2,1)} %r_4_.3) | copy-start | bytes 12582916
  21.4 16.4 %copy-start.7 = (f32[2048]{0:T(1024)S(1)}, f32[2048]{0:T(1024)}, u32[]{:S(2)}) copy-start(f32[2048]{0:T(1024)} %param.16) | copy-start | bytes 24580
  22.0 15.2 %collective-permute-start.9 = (bf16[128,1024]{1,0:T(8,128)(2,1)S(1)}, bf16[128,1024]{1,0:T(8,128)(2,1)S(1)}, u32[]{:S(2)}, u32[]{:S(2)}) collective-permute-start(bf16[128,1024]{1,0:T(8,128)(2,1)S(1)} %get-tuple-element.40), channel_id=1, source_target_pairs={{0,1},{1,2},{2,3},{3,0},{4,5},{5,6},{6,7},{7,4},{8,9},{9,10},{10,1... | collective-permute-start | bytes 786440 | tf_op jit(solution)/shard_map/ppermute | solution.py:49
  22.4 14.8 %collective-permute-start.10 = (bf16[128,1024]{1,0:T(8,128)(2,1)S(1)}, bf16[128,1024]{1,0:T(8,128)(2,1)S(1)}, u32[]{:S(2)}, u32[]{:S(2)}) collective-permute-start(bf16[128,1024]{1,0:T(8,128)(2,1)S(1)} %get-tuple-element.41), channel_id=1, source_target_pairs={{0,2},{1,3},{2,0},{3,1},{4,6},{5,7},{6,4},{7,5},{8,10},{9,11},{10,... | collective-permute-start | bytes 786440 | tf_op jit(solution)/shard_map/ppermute | solution.py:49
  23.9 13.8 %collective-permute-start.11 = (bf16[128,1024]{1,0:T(8,128)(2,1)S(1)}, bf16[128,1024]{1,0:T(8,128)(2,1)S(1)}, u32[]{:S(2)}, u32[]{:S(2)}) collective-permute-start(bf16[128,1024]{1,0:T(8,128)(2,1)S(1)} %get-tuple-element.42), channel_id=1, source_target_pairs={{0,3},{1,0},{2,1},{3,2},{4,7},{5,4},{6,5},{7,6},{8,11},{9,8},{10,9... | collective-permute-start | bytes 786440 | tf_op jit(solution)/shard_map/ppermute | solution.py:49
  34.8 7.6 %collective-permute-start.5 = (bf16[128,1024]{1,0:T(8,128)(2,1)S(1)}, bf16[128,1024]{1,0:T(8,128)(2,1)S(1)}, u32[]{:S(2)}, u32[]{:S(2)}) collective-permute-start(bf16[128,1024]{1,0:T(8,128)(2,1)S(1)} %get-tuple-element.36), channel_id=1, source_target_pairs={{0,1},{1,2},{2,3},{3,0},{4,5},{5,6},{6,7},{7,4},{8,9},{9,10},{10,1... | collective-permute-start | bytes 786440 | tf_op jit(solution)/shard_map/ppermute | solution.py:49
  35.1 8.7 %collective-permute-start.6 = (bf16[128,1024]{1,0:T(8,128)(2,1)S(1)}, bf16[128,1024]{1,0:T(8,128)(2,1)S(1)}, u32[]{:S(2)}, u32[]{:S(2)}) collective-permute-start(bf16[128,1024]{1,0:T(8,128)(2,1)S(1)} %get-tuple-element.37), channel_id=1, source_target_pairs={{0,2},{1,3},{2,0},{3,1},{4,6},{5,7},{6,4},{7,5},{8,10},{9,11},{10,... | collective-permute-start | bytes 786440 | tf_op jit(solution)/shard_map/ppermute | solution.py:49
  37.2 13.2 %collective-permute-start.7 = (bf16[128,1024]{1,0:T(8,128)(2,1)S(1)}, bf16[128,1024]{1,0:T(8,128)(2,1)S(1)}, u32[]{:S(2)}, u32[]{:S(2)}) collective-permute-start(bf16[128,1024]{1,0:T(8,128)(2,1)S(1)} %get-tuple-element.38), channel_id=1, source_target_pairs={{0,3},{1,0},{2,1},{3,2},{4,7},{5,4},{6,5},{7,6},{8,11},{9,8},{10,9... | collective-permute-start | bytes 786440 | tf_op jit(solution)/shard_map/ppermute | solution.py:49
  37.8 12.7 %copy-start.5 = (bf16[2048,1024]{1,0:T(8,128)(2,1)S(1)}, bf16[2048,1024]{1,0:T(8,128)(2,1)}, u32[]{:S(2)}) copy-start(bf16[2048,1024]{1,0:T(8,128)(2,1)} %r_13_.1) | copy-start | bytes 12582916
  37.8 12.7 %copy-start.6 = (bf16[1,256,1024]{2,1,0:T(8,128)(2,1)S(1)}, bf16[1,256,1024]{2,1,0:T(8,128)(2,1)}, u32[]{:S(2)}) copy-start(bf16[1,256,1024]{2,1,0:T(8,128)(2,1)} %param.14) | copy-start | bytes 1572868
  37.8 12.7 %copy-start.8 = (f32[1024]{0:T(1024)S(1)}, f32[1024]{0:T(1024)}, u32[]{:S(2)}) copy-start(f32[1024]{0:T(1024)} %param.19) | copy-start | bytes 12292
  59.3 18.7 %collective-permute-start.13 = (bf16[128,1024]{1,0:T(8,128)(2,1)S(1)}, bf16[128,1024]{1,0:T(8,128)(2,1)S(1)}, u32[]{:S(2)}, u32[]{:S(2)}) collective-permute-start(bf16[128,1024]{1,0:T(8,128)(2,1)S(1)} %get-tuple-element.55), channel_id=1, source_target_pairs={{0,2},{1,3},{2,0},{3,1},{4,6},{5,7},{6,4},{7,5},{8,10},{9,11},{10,... | collective-permute-start | bytes 786440 | tf_op jit(solution)/shard_map/ppermute | solution.py:49
  60.1 18.0 %collective-permute-start.14 = (bf16[128,1024]{1,0:T(8,128)(2,1)S(1)}, bf16[128,1024]{1,0:T(8,128)(2,1)S(1)}, u32[]{:S(2)}, u32[]{:S(2)}) collective-permute-start(bf16[128,1024]{1,0:T(8,128)(2,1)S(1)} %get-tuple-element.56), channel_id=1, source_target_pairs={{0,1},{1,2},{2,3},{3,0},{4,5},{5,6},{6,7},{7,4},{8,9},{9,10},{10,1... | collective-permute-start | bytes 786440 | tf_op jit(solution)/shard_map/ppermute | solution.py:49
  61.4 17.7 %collective-permute-start.12 = (bf16[128,1024]{1,0:T(8,128)(2,1)S(1)}, bf16[128,1024]{1,0:T(8,128)(2,1)S(1)}, u32[]{:S(2)}, u32[]{:S(2)}) collective-permute-start(bf16[128,1024]{1,0:T(8,128)(2,1)S(1)} %get-tuple-element.52.r_6_), channel_id=1, source_target_pairs={{0,3},{1,0},{2,1},{3,2},{4,7},{5,4},{6,5},{7,6},{8,11},{9,8},{10,9... | collective-permute-start | bytes 786440 | tf_op jit(solution)/shard_map/ppermute | solution.py:49
  61.6 8.8 %collective-permute-start.15 = (bf16[128,1152]{1,0:T(8,128)(2,1)S(1)}, bf16[128,1152]{1,0:T(8,128)(2,1)S(1)}, u32[]{:S(2)}, u32[]{:S(2)}) collective-permute-start(bf16[128,1152]{1,0:T(8,128)(2,1)S(1)} %get-tuple-element.59.mine_ref), channel_id=1, source_target_pairs={{0,120},{4,124},{8,64},{12,68},{16,72},{20,76},{24,80},{28,84},{32... | collective-permute-start | bytes 884744 | tf_op jit(solution)/shard_map/ppermute | solution.py:69
  64.5 22.5 %collective-permute-start.17 = (bf16[128,1152]{1,0:T(8,128)(2,1)S(1)}, bf16[128,1152]{1,0:T(8,128)(2,1)S(1)}, u32[]{:S(2)}, u32[]{:S(2)}) collective-permute-start(bf16[128,1152]{1,0:T(8,128)(2,1)S(1)} %get-tuple-element.53.r_5_), channel_id=1, source_target_pairs={{66,0},{67,1},{72,2},{73,3},{70,4},{71,5},{76,6},{77,7},{74,8},{75... | collective-permute-start | bytes 884744 | tf_op jit(solution)/shard_map/ppermute | solution.py:59
  70.5 16.6 %collective-permute-start.18 = (bf16[128,1152]{1,0:T(8,128)(2,1)S(1)}, bf16[128,1152]{1,0:T(8,128)(2,1)S(1)}, u32[]{:S(2)}, u32[]{:S(2)}) collective-permute-start(bf16[128,1152]{1,0:T(8,128)(2,1)S(1)} %get-tuple-element.60), channel_id=1, source_target_pairs={{67,0},{72,1},{73,2},{74,3},{71,4},{76,5},{77,6},{78,7},{75,8},{80... | collective-permute-start | bytes 884744 | tf_op jit(solution)/shard_map/ppermute | solution.py:59
  78.1 9.9 %collective-permute-start.19 = (bf16[256,1024]{1,0:T(8,128)(2,1)S(1)}, bf16[256,1024]{1,0:T(8,128)(2,1)S(1)}, u32[]{:S(2)}, u32[]{:S(2)}) collective-permute-start(bf16[256,1024]{1,0:T(8,128)(2,1)S(1)} %get-tuple-element.61), channel_id=1, source_target_pairs={{0,64},{1,65},{2,66},{3,67},{4,68},{5,69},{6,70},{7,71},{8,72},{9,... | collective-permute-start | bytes 1572872 | tf_op jit(solution)/shard_map/ppermute | solution.py:43
  78.2 9.5 %collective-permute-start.16 = (bf16[128,1152]{1,0:T(8,128)(2,1)S(1)}, bf16[128,1152]{1,0:T(8,128)(2,1)S(1)}, u32[]{:S(2)}, u32[]{:S(2)}) collective-permute-start(bf16[128,1152]{1,0:T(8,128)(2,1)S(1)} %shard_map.122), channel_id=1, source_target_pairs={{0,3},{1,64},{2,65},{3,66},{4,7},{5,68},{6,69},{7,70},{8,11},{9,72... | collective-permute-start | bytes 884744 | tf_op jit(solution)/shard_map/ppermute | solution.py:79
  79.1 2.3 %copy-start.3 = (bf16[1024,1024]{1,0:T(8,128)(2,1)S(1)}, bf16[1024,1024]{1,0:T(8,128)(2,1)}, u32[]{:S(2)}) copy-start(bf16[1024,1024]{1,0:T(8,128)(2,1)} %sw_ref.1) | copy-start | bytes 6291460
  80.1 17.7 %collective-permute-start.20 = (bf16[256,1024]{1,0:T(8,128)(2,1)S(1)}, bf16[256,1024]{1,0:T(8,128)(2,1)S(1)}, u32[]{:S(2)}, u32[]{:S(2)}) collective-permute-start(bf16[256,1024]{1,0:T(8,128)(2,1)S(1)} %shard_map.120._), channel_id=1, source_target_pairs={{0,124},{1,125},{2,126},{3,127},{4,64},{5,65},{6,66},{7,67},{8,68}... | collective-permute-start | bytes 1572872 | tf_op jit(solution)/shard_map/ppermute | solution.py:43

commit v15 on v14

--- a/solution.py
+++ b/solution.py
@@ -147,7 +147,7 @@
     deg_ref[...] = deg + deg_in[...] if first else deg
     keep = keep[:, :1]
     hidden = q_ref.shape[1]
-    step = 512
+    step = 1024
     for n in range(hidden // step):
         cols = slice(n * step, (n + 1) * step)
         pre = dot(x, q_ref[:, cols]) + qb_ref[:, cols]
@@ -163,7 +163,7 @@
 ):
     rows, width = self_ref.shape
     hidden = nb_ref.shape[0]
-    step = 512
+    step = 1024
     x = jnp.concatenate([got_a[...], got_b[...], got_c[...]], axis=0)
     keep = x[:, :128].astype(F32) < LIMIT
     tiles = tiles_ref[:, -3 * block :]
@@ -210,7 +210,7 @@
 def back_dot(first, tt_ref, gpool_ref, messages, q_ref, gn_ref, store):
     rows = gn_ref.shape[0]
     tt = tt_ref[first : first + rows, :]
-    step = 512
+    step = 1024
     for n in range(gpool_ref.shape[1] // step):
         cols = slice(n * step, (n + 1) * step)
         live = jnp.concatenate([m[:, cols] for m in messages], axis=0).astype(F32) > 0
@@ -247,7 +247,7 @@
 
 def own_rows_kernel(live_ref, g_ref, sw_ref, pre_ref, _, gself_ref, emb_ref):
     rows, width = pre_ref.shape
-    step = 512
+    step = 1024
     for n in range(width // step):
         cols = slice(n * step, (n + 1) * step)
         gself_ref[:, cols] = dot(g_ref[...], sw_ref[cols, :], 1, 1)

time: 100 us -> 99.8 us (level)
  no operation moved by 1% of the time
where the time goes in v15:
time: 99.8 us; the launch traced here: 98.4 us
  waiting for transfers between devices  36.6 us (37%)
  starting transfers between devices  29.5 us (30%)
  Pallas kernels  23.9 us (24%)
  local copies, waits for them, and re-layouts  5.69 us (6%)
  between operations  1.48 us (1%)
  other arithmetic  1.16 us (1%)
    pallas_call x12, Pallas kernels, call(): pl.pallas_call(kernel, out_shape=[jax.ShapeDtypeStruct(s, d) for s, d in...  23.9 us
    ppermute x5, waiting for transfers between devices, swap_rows(): return lax.ppermute(x, ('side', 'dom'), pairs)  20 us
    ppermute x12, waiting for transfers between devices, along(): return lax.ppermute(x, 'dom', pairs)  12.1 us
    ppermute x2, starting transfers between devices, straight_back(): return lax.ppermute(x, ('side', 'dom'), pairs)  11.3 us
    ppermute x12, starting transfers between devices, along(): return lax.ppermute(x, 'dom', pairs)  9.02 us
    ppermute x5, starting transfers between devices, swap_rows(): return lax.ppermute(x, ('side', 'dom'), pairs)  7.5 us
    unnamed x18, local copies, waits for them, and re-layouts  4.25 us
    ppermute x2, waiting for transfers between devices, straight_back(): return lax.ppermute(x, ('side', 'dom'), pairs)  3.99 us
  transfers between devices with their start and end apart: 21, of which 9 were waited for; matrix products, arithmetic and copies ran while one was open for 1% of the time, Pallas kernels for 15%

profile of v15, /device:TPU:7, one launch (start us, length us, event | category | flops | bytes accessed | tf_op | source)
XLA Modules:
  0.0 98.4 jit_solution(2274264166668083722)
XLA Ops:
  1.3 1.2 %broadcast_select_fusion = bf16[256,1024]{1,0:T(8,128)(2,1)S(1)} fusion(pred[256]{0:T(512)(128)(4,1)S(1)} %iota_compare_fusion, bf16[1,256,1024]{2,1,0:T(8,128)(2,1)} %param.10), kind=kLoop, calls=%fused_computation | loop fusion | flops 262144 | bytes 1048832 | tf_op jit(solution)/shard_map/jit(_where)/select_n | solution.py:307
  2.5 1.9 %collective-permute-start.8 = (bf16[256,1024]{1,0:T(8,128)(2,1)S(1)}, bf16[256,1024]{1,0:T(8,128)(2,1)S(1)}, u32[]{:S(2)}, u32[]{:S(2)}) collective-permute-start(bf16[256,1024]{1,0:T(8,128)(2,1)S(1)} %broadcast_select_fusion), channel_id=1, source_target_pairs={{0,68},{1,69},{2,70},{3,71},{4,72},{5,73},{6,74},{7,75},{8,76},{9,... | collective-permute-start | bytes 1572872 | tf_op jit(solution)/shard_map/ppermute | solution.py:43
  4.4 0.7 slice_bitcast_fusion
  5.3 2.2 %collective-permute-start.1 = (s32[1,128]{1,0:T(1,128)S(1)}, s32[1,128]{1,0:T(1,128)S(1)}, u32[]{:S(2)}, u32[]{:S(2)}) collective-permute-start(s32[1,128]{1,0:T(1,128)S(1)} %pad_bitcast_fusion), channel_id=1, source_target_pairs={{0,2},{1,3},{2,0},{3,1},{4,6},{5,7},{6,4},{7,5},{8,10},{9,11},{10,... | collective-permute-start | bytes 1544 | tf_op jit(solution)/shard_map/ppermute | solution.py:49
  7.8 1.4 %collective-permute-done.1.r_2_.r_3_ = s32[1,128]{1,0:T(1,128)S(1)} collective-permute-done((s32[1,128]{1,0:T(1,128)S(1)}, s32[1,128]{1,0:T(1,128)S(1)}, u32[]{:S(2)}, u32[]{:S(2)}) %collective-permute-start.1) | collective-permute-done | bytes 544 | tf_op jit(solution)/shard_map/ppermute | solution.py:49
  9.2 2.1 %collective-permute-done.r_1_.r_2_ = s32[1,128]{1,0:T(1,128)S(1)} collective-permute-done((s32[1,128]{1,0:T(1,128)S(1)}, s32[1,128]{1,0:T(1,128)S(1)}, u32[]{:S(2)}, u32[]{:S(2)}) %collective-permute-start) | collective-permute-done | bytes 544 | tf_op jit(solution)/shard_map/ppermute | solution.py:49
  11.3 3.7 %collective-permute-start.4 = (bf16[256,1024]{1,0:T(8,128)(2,1)S(1)}, bf16[256,1024]{1,0:T(8,128)(2,1)S(1)}, u32[]{:S(2)}, u32[]{:S(2)}) collective-permute-start(bf16[256,1024]{1,0:T(8,128)(2,1)S(1)} %broadcast_select_fusion), channel_id=1, source_target_pairs={{0,72},{1,73},{2,74},{3,75},{4,76},{5,77},{6,78},{7,79},{8,80},{9,... | collective-permute-start | bytes 1572872 | tf_op jit(solution)/shard_map/ppermute | solution.py:43
  15.1 0.8 copy.14.r_1_.r_0_.r_2_
  15.8 1.6 %copy-done.1 = s32[1,256,2048]{2,1,0:T(8,128)S(1)} copy-done((s32[1,256,2048]{2,1,0:T(8,128)S(1)}, s32[1,256,2048]{2,1,0:T(8,128)}, u32[]{:S(2)}) %copy-start.1) | copy-done | bytes 2097176
  17.4 1.6 %copy-done.2 = bf16[1024,1024]{1,0:T(8,128)(2,1)S(1)} copy-done((bf16[1024,1024]{1,0:T(8,128)(2,1)S(1)}, bf16[1024,1024]{1,0:T(8,128)(2,1)}, u32[]{:S(2)}) %copy-start.2) | copy-done | bytes 2097176
  19.0 1.0 %copy-done.4 = bf16[1,256,1024]{2,1,0:T(8,128)(2,1)S(1)} copy-done((bf16[1,256,1024]{2,1,0:T(8,128)(2,1)S(1)}, bf16[1,256,1024]{2,1,0:T(8,128)(2,1)}, u32[]{:S(2)}) %copy-start.4) | copy-done | bytes 524312
  20.0 1.3 %shard_map.114 = (bf16[256,1024]{1,0:T(8,128)(2,1)S(1)}, bf16[1024,256]{1,0:T(8,128)(2,1)S(1)}, f32[256,1024]{1,0:T(8,128)S(1)}) custom-call(s32[1]{0:T(128)} %bitcast.1.r_0_.r_1_.place_ref, s32[8,2]{1,0:T(8,128)S(1)} %copy.14.r_1_.r_0_.r_2_, s32[256,2048]{1,0:T(8,128)S(1)} %bitcast.20, bf16[256,1024]{1,0:T(8,128)(2,1)S(1)} %bitcast.21, ...), custom_call_target="tpu_custom_call" | custom-call | flops 536870912 | bytes 1048576 | tf_op jit(solution)/shard_map/pallas_call | solution.py:25
  22.4 1.6 %collective-permute-start.10 = (bf16[128,1024]{1,0:T(8,128)(2,1)S(1)}, bf16[128,1024]{1,0:T(8,128)(2,1)S(1)}, u32[]{:S(2)}, u32[]{:S(2)}) collective-permute-start(bf16[128,1024]{1,0:T(8,128)(2,1)S(1)} %get-tuple-element.41), channel_id=1, source_target_pairs={{0,2},{1,3},{2,0},{3,1},{4,6},{5,7},{6,4},{7,5},{8,10},{9,11},{10,... | collective-permute-start | bytes 786440 | tf_op jit(solution)/shard_map/ppermute | solution.py:49
  24.0 10.2 %collective-permute-done.4.r_5_ = bf16[256,1024]{1,0:T(8,128)(2,1)S(1)} collective-permute-done((bf16[256,1024]{1,0:T(8,128)(2,1)S(1)}, bf16[256,1024]{1,0:T(8,128)(2,1)S(1)}, u32[]{:S(2)}, u32[]{:S(2)}) %collective-permute-start.4) | collective-permute-done | bytes 524320 | tf_op jit(solution)/shard_map/ppermute | solution.py:43
  35.1 2.1 %collective-permute-start.6 = (bf16[128,1024]{1,0:T(8,128)(2,1)S(1)}, bf16[128,1024]{1,0:T(8,128)(2,1)S(1)}, u32[]{:S(2)}, u32[]{:S(2)}) collective-permute-start(bf16[128,1024]{1,0:T(8,128)(2,1)S(1)} %get-tuple-element.37), channel_id=1, source_target_pairs={{0,2},{1,3},{2,0},{3,1},{4,6},{5,7},{6,4},{7,5},{8,10},{9,11},{10,... | collective-permute-start | bytes 786440 | tf_op jit(solution)/shard_map/ppermute | solution.py:49
  37.8 4.6 %shard_map.116 = (bf16[640,2048]{1,0:T(8,128)(2,1)S(1)}, f32[256,2048]{1,0:T(8,128)S(1)}, f32[256,128]{1,0:T(8,128)S(1)}) custom-call(s32[8,2]{1,0:T(8,128)S(1)} %copy.14.r_1_.r_0_.r_2_, bf16[256,1024]{1,0:T(8,128)(2,1)S(1)} %collective-permute-done.3.r_4_.r_1_, bf16[256,1024]{1,0:T(8,128)(2,1)S(1)} %collective-permute-done.8.r_4_.r_2_, ...), custom_call_target="tpu_custom_call" | custom-call | flops 3355443200 | bytes 1048576 | tf_op jit(solution)/shard_map/pallas_call | solution.py:25
  42.4 1.4 %collective-permute-done.6.r_4_ = bf16[128,1024]{1,0:T(8,128)(2,1)S(1)} collective-permute-done((bf16[128,1024]{1,0:T(8,128)(2,1)S(1)}, bf16[128,1024]{1,0:T(8,128)(2,1)S(1)}, u32[]{:S(2)}, u32[]{:S(2)}) %collective-permute-start.6) | collective-permute-done | bytes 262176 | tf_op jit(solution)/shard_map/ppermute | solution.py:49
  43.8 6.6 %collective-permute-done.7.r_5_ = bf16[128,1024]{1,0:T(8,128)(2,1)S(1)} collective-permute-done((bf16[128,1024]{1,0:T(8,128)(2,1)S(1)}, bf16[128,1024]{1,0:T(8,128)(2,1)S(1)}, u32[]{:S(2)}, u32[]{:S(2)}) %collective-permute-start.7) | collective-permute-done | bytes 262176 | tf_op jit(solution)/shard_map/ppermute | solution.py:49
  50.5 8.5 %shard_map.117 = (bf16[256,1024]{1,0:T(8,128)(2,1)S(1)}, bf16[256,2048]{1,0:T(8,128)(2,1)S(1)}, f32[256,1024]{1,0:T(8,128)S(1)}, bf16[384,2048]{1,0:T(8,128)(2,1...) custom-call(s32[1]{0:T(128)} %bitcast.16.r_0_, ...), custom_call_target="tpu_custom_call" | custom-call | flops 8000000000 | bytes 1048576 | tf_op jit(solution)/shard_map/pallas_call | solution.py:25
  59.0 0.8 collective-permute-start.13
  59.8 1.3 %collective-permute-start.14 = (bf16[128,1024]{1,0:T(8,128)(2,1)S(1)}, bf16[128,1024]{1,0:T(8,128)(2,1)S(1)}, u32[]{:S(2)}, u32[]{:S(2)}) collective-permute-start(bf16[128,1024]{1,0:T(8,128)(2,1)S(1)} %get-tuple-element.56), channel_id=1, source_target_pairs={{0,1},{1,2},{2,3},{3,0},{4,5},{5,6},{6,7},{7,4},{8,9},{9,10},{10,1... | collective-permute-start | bytes 786440 | tf_op jit(solution)/shard_map/ppermute | solution.py:49
  61.9 2.2 %shard_map.118 = (bf16[128,1152]{1,0:T(8,128)(2,1)S(1)}, bf16[128,1152]{1,0:T(8,128)(2,1)S(1)}) custom-call(s32[1]{0:T(128)} %bitcast.1.r_0_.r_1_.place_ref, s32[8,2]{1,0:T(8,128)S(1)} %copy.14.r_1_.r_0_.r_2_, bf16[1024,256]{1,0:T(8,128)(2,1)S(1)} %get-tuple-element.46.r_15_.r_2_.r_1_, bf16[256,2048]{1,0:T(8,128)(2,1)S(1)} %get-tuple-element.50.r_3_.r_2_, ...), custom_call_target="tpu_custom_call" | custom-call | flops 2000000000 | bytes 1048576 | tf_op jit(solution)/shard_map/pallas_call | solution.py:25
  64.1 3.7 %collective-permute-start.17 = (bf16[128,1152]{1,0:T(8,128)(2,1)S(1)}, bf16[128,1152]{1,0:T(8,128)(2,1)S(1)}, u32[]{:S(2)}, u32[]{:S(2)}) collective-permute-start(bf16[128,1152]{1,0:T(8,128)(2,1)S(1)} %get-tuple-element.53.r_5_), channel_id=1, source_target_pairs={{66,0},{67,1},{72,2},{73,3},{70,4},{71,5},{76,6},{77,7},{74,8},{75... | collective-permute-start | bytes 884744 | tf_op jit(solution)/shard_map/ppermute | solution.py:59
  67.8 2.2 %shard_map.119 = (bf16[256,1024]{1,0:T(8,128)(2,1)S(1)}, bf16[128,1024]{1,0:T(8,128)(2,1)S(1)}) custom-call(s32[8,2]{1,0:T(8,128)S(1)} %copy.14.r_1_.r_0_.r_2_, bf16[1024,256]{1,0:T(8,128)(2,1)S(1)} %get-tuple-element.46.r_15_.r_2_.r_1_, bf16[256,2048]{1,0:T(8,128)(2,1)S(1)} %get-tuple-element.50.r_3_.r_2_, ...), custom_call_target="tpu_custom_call" | custom-call | flops 2000000000 | bytes 1048576 | tf_op jit(solution)/shard_map/pallas_call | solution.py:25
  70.1 7.6 %collective-permute-start.18 = (bf16[128,1152]{1,0:T(8,128)(2,1)S(1)}, bf16[128,1152]{1,0:T(8,128)(2,1)S(1)}, u32[]{:S(2)}, u32[]{:S(2)}) collective-permute-start(bf16[128,1152]{1,0:T(8,128)(2,1)S(1)} %get-tuple-element.60), channel_id=1, source_target_pairs={{67,0},{72,1},{73,2},{74,3},{71,4},{76,5},{77,6},{78,7},{75,8},{80... | collective-permute-start | bytes 884744 | tf_op jit(solution)/shard_map/ppermute | solution.py:59
  77.8 1.0 collective-permute-start.16
  78.8 0.9 shard_map.120._
  79.7 1.4 %collective-permute-start.20 = (bf16[256,1024]{1,0:T(8,128)(2,1)S(1)}, bf16[256,1024]{1,0:T(8,128)(2,1)S(1)}, u32[]{:S(2)}, u32[]{:S(2)}) collective-permute-start(bf16[256,1024]{1,0:T(8,128)(2,1)S(1)} %shard_map.120._), channel_id=1, source_target_pairs={{0,124},{1,125},{2,126},{3,127},{4,64},{5,65},{6,66},{7,67},{8,68}... | collective-permute-start | bytes 1572872 | tf_op jit(solution)/shard_map/ppermute | solution.py:43
  81.1 1.5 %shard_map.121 = (f32[256,1024]{1,0:T(8,128)S(1)}, bf16[256,1024]{1,0:T(8,128)(2,1)}) custom-call(s32[1]{0:T(128)} %bitcast.17.live_ref, bf16[256,1024]{1,0:T(8,128)(2,1)S(1)} %get-tuple-element.48.g_ref, bf16[1024,1024]{1,0:T(8,128)(2,1)S(1)} %copy-done.3, f32[256,1024]{1,0:T(8,128)S(1)} %get-tuple-element.49.pre_ref, bf16[256,1024]{1,0:T(8,128)(2,1)S(1)} %shard_map.120._), custom_call_target="tpu_custom_call" | custom-call | flops 2000000000 | bytes 1048576 | tf_op jit(solution)/shard_map/pallas_call | solution.py:25
  82.7 4.0 %collective-permute-done.18.c3 = bf16[128,1152]{1,0:T(8,128)(2,1)S(1)} collective-permute-done((bf16[128,1152]{1,0:T(8,128)(2,1)S(1)}, bf16[128,1152]{1,0:T(8,128)(2,1)S(1)}, u32[]{:S(2)}, u32[]{:S(2)}) %collective-permute-start.18) | collective-permute-done | bytes 294944 | tf_op jit(solution)/shard_map/ppermute | solution.py:59
  87.6 9.7 %collective-permute-done.20.below_ref = bf16[256,1024]{1,0:T(8,128)(2,1)S(1)} collective-permute-done((bf16[256,1024]{1,0:T(8,128)(2,1)S(1)}, bf16[256,1024]{1,0:T(8,128)(2,1)S(1)}, u32[]{:S(2)}, u32[]{:S(2)}) %collective-permute-start.20) | collective-permute-done | bytes 524320 | tf_op jit(solution)/shard_map/ppermute | solution.py:43
  97.4 1.0 %shard_map.124 = bf16[256,1024]{1,0:T(8,128)(2,1)} custom-call(s32[1]{0:T(128)} %bitcast.18.live_ref, f32[256,1024]{1,0:T(8,128)S(1)} %shard_map.123.total_ref, bf16[256,1024]{1,0:T(8,128)(2,1)S(1)} %collective-permute-done.19.same_ref, bf16[256,1024]{1,0:T(8,128)(2,1)S(1)} %collective-permute-done.20.below_ref), custom_call_target="tpu_custom_call" | custom-call | bytes 1048576 | tf_op jit(solution)/shard_map/pallas_call | solution.py:25
  (45 shorter events, 5.0 us)
Async XLA Ops:
  2.5 18.9 %collective-permute-start.8 = (bf16[256,1024]{1,0:T(8,128)(2,1)S(1)}, bf16[256,1024]{1,0:T(8,128)(2,1)S(1)}, u32[]{:S(2)}, u32[]{:S(2)}) collective-permute-start(bf16[256,1024]{1,0:T(8,128)(2,1)S(1)} %broadcast_select_fusion), channel_id=1, source_target_pairs={{0,68},{1,69},{2,70},{3,71},{4,72},{5,73},{6,74},{7,75},{8,76},{9,... | collective-permute-start | bytes 1572872 | tf_op jit(solution)/shard_map/ppermute | solution.py:43
  5.1 2.7 %collective-permute-start.2 = (s32[1,128]{1,0:T(1,128)S(1)}, s32[1,128]{1,0:T(1,128)S(1)}, u32[]{:S(2)}, u32[]{:S(2)}) collective-permute-start(s32[1,128]{1,0:T(1,128)S(1)} %pad_bitcast_fusion), channel_id=1, source_target_pairs={{0,1},{1,2},{2,3},{3,0},{4,5},{5,6},{6,7},{7,4},{8,9},{9,10},{10,1... | collective-permute-start | bytes 1544 | tf_op jit(solution)/shard_map/ppermute | solution.py:49
  5.3 3.9 %collective-permute-start.1 = (s32[1,128]{1,0:T(1,128)S(1)}, s32[1,128]{1,0:T(1,128)S(1)}, u32[]{:S(2)}, u32[]{:S(2)}) collective-permute-start(s32[1,128]{1,0:T(1,128)S(1)} %pad_bitcast_fusion), channel_id=1, source_target_pairs={{0,2},{1,3},{2,0},{3,1},{4,6},{5,7},{6,4},{7,5},{8,10},{9,11},{10,... | collective-permute-start | bytes 1544 | tf_op jit(solution)/shard_map/ppermute | solution.py:49
  7.4 3.9 %collective-permute-start = (s32[1,128]{1,0:T(1,128)S(1)}, s32[1,128]{1,0:T(1,128)S(1)}, u32[]{:S(2)}, u32[]{:S(2)}) collective-permute-start(s32[1,128]{1,0:T(1,128)S(1)} %pad_bitcast_fusion), channel_id=1, source_target_pairs={{0,3},{1,0},{2,1},{3,2},{4,7},{5,4},{6,5},{7,6},{8,11},{9,8},{10,9... | collective-permute-start | bytes 1544 | tf_op jit(solution)/shard_map/ppermute | solution.py:49
  7.4 16.5 %collective-permute-start.3 = (bf16[256,1024]{1,0:T(8,128)(2,1)S(1)}, bf16[256,1024]{1,0:T(8,128)(2,1)S(1)}, u32[]{:S(2)}, u32[]{:S(2)}) collective-permute-start(bf16[256,1024]{1,0:T(8,128)(2,1)S(1)} %broadcast_select_fusion), channel_id=1, source_target_pairs={{0,64},{1,65},{2,66},{3,67},{4,68},{5,69},{6,70},{7,71},{8,72},{9,... | collective-permute-start | bytes 1572872 | tf_op jit(solution)/shard_map/ppermute | solution.py:43
  11.3 22.8 %collective-permute-start.4 = (bf16[256,1024]{1,0:T(8,128)(2,1)S(1)}, bf16[256,1024]{1,0:T(8,128)(2,1)S(1)}, u32[]{:S(2)}, u32[]{:S(2)}) collective-permute-start(bf16[256,1024]{1,0:T(8,128)(2,1)S(1)} %broadcast_select_fusion), channel_id=1, source_target_pairs={{0,72},{1,73},{2,74},{3,75},{4,76},{5,77},{6,78},{7,79},{8,80},{9,... | collective-permute-start | bytes 1572872 | tf_op jit(solution)/shard_map/ppermute | solution.py:43
  15.8 1.6 %copy-start.1 = (s32[1,256,2048]{2,1,0:T(8,128)S(1)}, s32[1,256,2048]{2,1,0:T(8,128)}, u32[]{:S(2)}) copy-start(s32[1,256,2048]{2,1,0:T(8,128)} %param.13) | copy-start | bytes 6291460
  17.4 1.6 %copy-start.2 = (bf16[1024,1024]{1,0:T(8,128)(2,1)S(1)}, bf16[1024,1024]{1,0:T(8,128)(2,1)}, u32[]{:S(2)}) copy-start(bf16[1024,1024]{1,0:T(8,128)(2,1)} %sw_ref.1) | copy-start | bytes 6291460
  19.0 1.0 %copy-start.4 = (bf16[1,256,1024]{2,1,0:T(8,128)(2,1)S(1)}, bf16[1,256,1024]{2,1,0:T(8,128)(2,1)}, u32[]{:S(2)}) copy-start(bf16[1,256,1024]{2,1,0:T(8,128)(2,1)} %param.10) | copy-start | bytes 1572868
  20.0 17.7 %copy-start = (bf16[1024,2048]{1,0:T(8,128)(2,1)S(1)}, bf16[1024,2048]{1,0:T(8,128)(2,1)}, u32[]{:S(2)}) copy-start(bf16[1024,2048]{1,0:T(8,128)(2,1)} %r_4_.3) | copy-start | bytes 12582916
  21.4 16.4 %copy-start.7 = (f32[2048]{0:T(1024)S(1)}, f32[2048]{0:T(1024)}, u32[]{:S(2)}) copy-start(f32[2048]{0:T(1024)} %param.16) | copy-start | bytes 24580
  22.0 15.2 %collective-permute-start.9 = (bf16[128,1024]{1,0:T(8,128)(2,1)S(1)}, bf16[128,1024]{1,0:T(8,128)(2,1)S(1)}, u32[]{:S(2)}, u32[]{:S(2)}) collective-permute-start(bf16[128,1024]{1,0:T(8,128)(2,1)S(1)} %get-tuple-element.40), channel_id=1, source_target_pairs={{0,1},{1,2},{2,3},{3,0},{4,5},{5,6},{6,7},{7,4},{8,9},{9,10},{10,1... | collective-permute-start | bytes 786440 | tf_op jit(solution)/shard_map/ppermute | solution.py:49
  22.4 14.8 %collective-permute-start.10 = (bf16[128,1024]{1,0:T(8,128)(2,1)S(1)}, bf16[128,1024]{1,0:T(8,128)(2,1)S(1)}, u32[]{:S(2)}, u32[]{:S(2)}) collective-permute-start(bf16[128,1024]{1,0:T(8,128)(2,1)S(1)} %get-tuple-element.41), channel_id=1, source_target_pairs={{0,2},{1,3},{2,0},{3,1},{4,6},{5,7},{6,4},{7,5},{8,10},{9,11},{10,... | collective-permute-start | bytes 786440 | tf_op jit(solution)/shard_map/ppermute | solution.py:49
  23.9 13.8 %collective-permute-start.11 = (bf16[128,1024]{1,0:T(8,128)(2,1)S(1)}, bf16[128,1024]{1,0:T(8,128)(2,1)S(1)}, u32[]{:S(2)}, u32[]{:S(2)}) collective-permute-start(bf16[128,1024]{1,0:T(8,128)(2,1)S(1)} %get-tuple-element.42), channel_id=1, source_target_pairs={{0,3},{1,0},{2,1},{3,2},{4,7},{5,4},{6,5},{7,6},{8,11},{9,8},{10,9... | collective-permute-start | bytes 786440 | tf_op jit(solution)/shard_map/ppermute | solution.py:49
  34.8 7.6 %collective-permute-start.5 = (bf16[128,1024]{1,0:T(8,128)(2,1)S(1)}, bf16[128,1024]{1,0:T(8,128)(2,1)S(1)}, u32[]{:S(2)}, u32[]{:S(2)}) collective-permute-start(bf16[128,1024]{1,0:T(8,128)(2,1)S(1)} %get-tuple-element.36), channel_id=1, source_target_pairs={{0,1},{1,2},{2,3},{3,0},{4,5},{5,6},{6,7},{7,4},{8,9},{9,10},{10,1... | collective-permute-start | bytes 786440 | tf_op jit(solution)/shard_map/ppermute | solution.py:49
  35.1 8.7 %collective-permute-start.6 = (bf16[128,1024]{1,0:T(8,128)(2,1)S(1)}, bf16[128,1024]{1,0:T(8,128)(2,1)S(1)}, u32[]{:S(2)}, u32[]{:S(2)}) collective-permute-start(bf16[128,1024]{1,0:T(8,128)(2,1)S(1)} %get-tuple-element.37), channel_id=1, source_target_pairs={{0,2},{1,3},{2,0},{3,1},{4,6},{5,7},{6,4},{7,5},{8,10},{9,11},{10,... | collective-permute-start | bytes 786440 | tf_op jit(solution)/shard_map/ppermute | solution.py:49
  37.2 13.2 %collective-permute-start.7 = (bf16[128,1024]{1,0:T(8,128)(2,1)S(1)}, bf16[128,1024]{1,0:T(8,128)(2,1)S(1)}, u32[]{:S(2)}, u32[]{:S(2)}) collective-permute-start(bf16[128,1024]{1,0:T(8,128)(2,1)S(1)} %get-tuple-element.38), channel_id=1, source_target_pairs={{0,3},{1,0},{2,1},{3,2},{4,7},{5,4},{6,5},{7,6},{8,11},{9,8},{10,9... | collective-permute-start | bytes 786440 | tf_op jit(solution)/shard_map/ppermute | solution.py:49
  37.8 12.7 %copy-start.5 = (bf16[2048,1024]{1,0:T(8,128)(2,1)S(1)}, bf16[2048,1024]{1,0:T(8,128)(2,1)}, u32[]{:S(2)}) copy-start(bf16[2048,1024]{1,0:T(8,128)(2,1)} %r_13_.1) | copy-start | bytes 12582916
  37.8 12.7 %copy-start.6 = (bf16[1,256,1024]{2,1,0:T(8,128)(2,1)S(1)}, bf16[1,256,1024]{2,1,0:T(8,128)(2,1)}, u32[]{:S(2)}) copy-start(bf16[1,256,1024]{2,1,0:T(8,128)(2,1)} %param.14) | copy-start | bytes 1572868
  37.8 12.7 %copy-start.8 = (f32[1024]{0:T(1024)S(1)}, f32[1024]{0:T(1024)}, u32[]{:S(2)}) copy-start(f32[1024]{0:T(1024)} %param.19) | copy-start | bytes 12292
  59.0 18.7 %collective-permute-start.13 = (bf16[128,1024]{1,0:T(8,128)(2,1)S(1)}, bf16[128,1024]{1,0:T(8,128)(2,1)S(1)}, u32[]{:S(2)}, u32[]{:S(2)}) collective-permute-start(bf16[128,1024]{1,0:T(8,128)(2,1)S(1)} %get-tuple-element.55), channel_id=1, source_target_pairs={{0,2},{1,3},{2,0},{3,1},{4,6},{5,7},{6,4},{7,5},{8,10},{9,11},{10,... | collective-permute-start | bytes 786440 | tf_op jit(solution)/shard_map/ppermute | solution.py:49
  59.8 18.0 %collective-permute-start.14 = (bf16[128,1024]{1,0:T(8,128)(2,1)S(1)}, bf16[128,1024]{1,0:T(8,128)(2,1)S(1)}, u32[]{:S(2)}, u32[]{:S(2)}) collective-permute-start(bf16[128,1024]{1,0:T(8,128)(2,1)S(1)} %get-tuple-element.56), channel_id=1, source_target_pairs={{0,1},{1,2},{2,3},{3,0},{4,5},{5,6},{6,7},{7,4},{8,9},{9,10},{10,1... | collective-permute-start | bytes 786440 | tf_op jit(solution)/shard_map/ppermute | solution.py:49
  61.1 17.7 %collective-permute-start.12 = (bf16[128,1024]{1,0:T(8,128)(2,1)S(1)}, bf16[128,1024]{1,0:T(8,128)(2,1)S(1)}, u32[]{:S(2)}, u32[]{:S(2)}) collective-permute-start(bf16[128,1024]{1,0:T(8,128)(2,1)S(1)} %get-tuple-element.52.r_6_), channel_id=1, source_target_pairs={{0,3},{1,0},{2,1},{3,2},{4,7},{5,4},{6,5},{7,6},{8,11},{9,8},{10,9... | collective-permute-start | bytes 786440 | tf_op jit(solution)/shard_map/ppermute | solution.py:49
  61.3 8.8 %collective-permute-start.15 = (bf16[128,1152]{1,0:T(8,128)(2,1)S(1)}, bf16[128,1152]{1,0:T(8,128)(2,1)S(1)}, u32[]{:S(2)}, u32[]{:S(2)}) collective-permute-start(bf16[128,1152]{1,0:T(8,128)(2,1)S(1)} %get-tuple-element.59.mine_ref), channel_id=1, source_target_pairs={{0,120},{4,124},{8,64},{12,68},{16,72},{20,76},{24,80},{28,84},{32... | collective-permute-start | bytes 884744 | tf_op jit(solution)/shard_map/ppermute | solution.py:69
  64.1 22.5 %collective-permute-start.17 = (bf16[128,1152]{1,0:T(8,128)(2,1)S(1)}, bf16[128,1152]{1,0:T(8,128)(2,1)S(1)}, u32[]{:S(2)}, u32[]{:S(2)}) collective-permute-start(bf16[128,1152]{1,0:T(8,128)(2,1)S(1)} %get-tuple-element.53.r_5_), channel_id=1, source_target_pairs={{66,0},{67,1},{72,2},{73,3},{70,4},{71,5},{76,6},{77,7},{74,8},{75... | collective-permute-start | bytes 884744 | tf_op jit(solution)/shard_map/ppermute | solution.py:59
  70.1 16.6 %collective-permute-start.18 = (bf16[128,1152]{1,0:T(8,128)(2,1)S(1)}, bf16[128,1152]{1,0:T(8,128)(2,1)S(1)}, u32[]{:S(2)}, u32[]{:S(2)}) collective-permute-start(bf16[128,1152]{1,0:T(8,128)(2,1)S(1)} %get-tuple-element.60), channel_id=1, source_target_pairs={{67,0},{72,1},{73,2},{74,3},{71,4},{76,5},{77,6},{78,7},{75,8},{80... | collective-permute-start | bytes 884744 | tf_op jit(solution)/shard_map/ppermute | solution.py:59
  77.7 9.9 %collective-permute-start.19 = (bf16[256,1024]{1,0:T(8,128)(2,1)S(1)}, bf16[256,1024]{1,0:T(8,128)(2,1)S(1)}, u32[]{:S(2)}, u32[]{:S(2)}) collective-permute-start(bf16[256,1024]{1,0:T(8,128)(2,1)S(1)} %get-tuple-element.61), channel_id=1, source_target_pairs={{0,64},{1,65},{2,66},{3,67},{4,68},{5,69},{6,70},{7,71},{8,72},{9,... | collective-permute-start | bytes 1572872 | tf_op jit(solution)/shard_map/ppermute | solution.py:43
  77.8 9.5 %collective-permute-start.16 = (bf16[128,1152]{1,0:T(8,128)(2,1)S(1)}, bf16[128,1152]{1,0:T(8,128)(2,1)S(1)}, u32[]{:S(2)}, u32[]{:S(2)}) collective-permute-start(bf16[128,1152]{1,0:T(8,128)(2,1)S(1)} %shard_map.122), channel_id=1, source_target_pairs={{0,3},{1,64},{2,65},{3,66},{4,7},{5,68},{6,69},{7,70},{8,11},{9,72... | collective-permute-start | bytes 884744 | tf_op jit(solution)/shard_map/ppermute | solution.py:79
  78.8 2.3 %copy-start.3 = (bf16[1024,1024]{1,0:T(8,128)(2,1)S(1)}, bf16[1024,1024]{1,0:T(8,128)(2,1)}, u32[]{:S(2)}) copy-start(bf16[1024,1024]{1,0:T(8,128)(2,1)} %sw_ref.1) | copy-start | bytes 6291460
  79.7 17.7 %collective-permute-start.20 = (bf16[256,1024]{1,0:T(8,128)(2,1)S(1)}, bf16[256,1024]{1,0:T(8,128)(2,1)S(1)}, u32[]{:S(2)}, u32[]{:S(2)}) collective-permute-start(bf16[256,1024]{1,0:T(8,128)(2,1)S(1)} %shard_map.120._), channel_id=1, source_target_pairs={{0,124},{1,125},{2,126},{3,127},{4,64},{5,65},{6,66},{7,67},{8,68}... | collective-permute-start | bytes 1572872 | tf_op jit(solution)/shard_map/ppermute | solution.py:43
